TPU v7x, 256 devices: a whole 4x4x8 slice. The times are simulated.
256 devices in a mesh: blk: 64 (over z, y, core), smp: 4 (over x).
Axes of the slice: x: 4, y: 4, z: 8, core: 2. Of those that a mesh axis runs over, the one named last changes fastest.
Arguments:
- forward_samples: bfloat16 [256, 524288], P('smp', 'blk'), may hold values from -0.375 to 0.375
- adjoint_samples: bfloat16 [256, 131072], P('smp', 'blk'), may hold values from -0.125 to 0.125
- probe_values: bfloat16 [131072, 192], P('blk'), may hold values from -6 to 6
- owners: int32 [131072, 1], P('blk'), may hold values from 0 to 63; in each aligned block of 2048 rows (0 to 2047, 2048 to 4095, ...) at most 64 rows name the same one
- block_ranks: int32 [64], P('blk'), may hold values from 64 to 256
- twiddle: float32 [2, 524288], P(None, 'blk'), may hold values from -1.2 to 1.2
Outputs:
- applied: bfloat16 [192, 524288], P('smp', 'blk')
Inputs may be any that keep to these rules, and one draw needn't show every extreme that they name: `owners`: in the rows of one block index no owner block is named more than 64 times.
All inputs are finite; a program needn't handle non-finite values.
Results may differ from a plain program's by a relative error of at most 0.005.
Values may be sent and summed in bfloat16 or wider, within the bound.
No kernel may reach another device: no remote copies, remote signals or barrier semaphores. Data moves between devices by JAX's collectives and lax.ppermute only.
A program may use at most 64 MiB of HBM per device.

v0:
```python
import jax
import jax.numpy as jnp
from jax import lax
from jax.sharding import PartitionSpec as P


def partner_2(block, axis, stride):
    count = lax.axis_size(axis)
    route = []
    for low in range(count):
        high = low | 1 << stride
        if high != low and high < count:
            route += [(low, high), (high, low)]
    return lax.ppermute(block, axis, route)


def body(forward_samples, adjoint_samples, probe_values, owners, block_ranks, twiddle):
    blk_count = lax.axis_size("blk")
    sample_local = adjoint_samples.shape[0]
    row_count = adjoint_samples.shape[1]
    vector_count = probe_values.shape[1]
    vector_local = vector_count // lax.axis_size("smp")
    owner_ids = owners[:, 0]
    stacked = jnp.concatenate([adjoint_samples.T, probe_values], axis=1)
    capacity = max(2, 2 * row_count // blk_count)
    onehot = (owner_ids[:, None] == jnp.arange(blk_count, dtype=jnp.int32)[None, :]).astype(
        jnp.int32
    )
    earlier = jnp.cumsum(onehot, axis=0) - onehot
    slot_ids = jnp.sum(earlier * onehot, axis=1)
    targets = owner_ids * capacity + slot_ids
    placing = (
        jnp.arange(blk_count * capacity, dtype=jnp.int32)[:, None] == targets[None, :]
    ).astype(jnp.bfloat16)
    outgoing = jnp.dot(placing, stacked, preferred_element_type=jnp.float32).astype(jnp.bfloat16)
    arrived = lax.all_to_all(outgoing, "blk", split_axis=0, concat_axis=0, tiled=True)
    coeffs = lax.dot_general(
        arrived[:, :sample_local],
        arrived[:, sample_local:],
        (((0,), (0,)), ((), ())),
        preferred_element_type=jnp.float32,
    )
    sample_ids = lax.axis_index("smp") * sample_local + jnp.arange(sample_local, dtype=jnp.int32)
    keep_samples = (sample_ids < block_ranks[0]).astype(jnp.float32)
    weights = (coeffs * keep_samples[:, None]).astype(jnp.bfloat16)
    vector_start = lax.axis_index("smp") * vector_local
    weight_piece = lax.all_gather(weights, "smp", axis=0, tiled=True)
    sample_piece = lax.all_gather(forward_samples, "smp", axis=0, tiled=True)
    columns = lax.dynamic_slice_in_dim(weight_piece, vector_start, vector_local, 1)
    field = lax.dot_general(
        columns, sample_piece, (((0,), (0,)), ((), ())), preferred_element_type=jnp.float32
    )
    top_bit = blk_count.bit_length() - 2
    for level_index in range(twiddle.shape[0]):
        partner = partner_2(field, "blk", top_bit - level_index)
        field = field + twiddle[level_index][None, :] * partner
    return field.astype(jnp.bfloat16)


def solution(mesh):
    in_specs = (
        P("smp", "blk"),
        P("smp", "blk"),
        P("blk", None),
        P("blk", None),
        P("blk"),
        P(None, "blk"),
    )
    out_specs = P("smp", "blk")
    return jax.shard_map(body, mesh=mesh, in_specs=in_specs, out_specs=out_specs, check_vma=False)
```

profile of v0, /device:TPU:40, one launch (start us, length us, event | category | flops | bytes accessed | tf_op | source)
XLA Modules:
  0.0 259.7 jit_solution(4066551883589560715)
XLA Ops:
  6.5 0.0 all-gather.2.cloned.1.call-start
  6.5 0.7 all-gather.2.cloned.1.call-update
  7.3 0.0 copy-start
  7.3 0.8 fusion.18
  8.1 0.0 copy-start.2
  8.1 0.0 copy-start.3
  8.1 18.1 %reduce-window.6 = s32[64,16,128]{2,1,0:T(8,128)S(1)} reduce-window(s32[64,16,128]{2,1,0:T(8,128)S(1)} %fusion.18, s32[]{:T(128)} %constant.6.clone.1), window={size=1x1x128 pad=0_0x0_0x127_0}, to_apply=%region_0.0 | reduce-window | flops 16646144 | bytes 1048580 | tf_op jit(solution)/shard_map/reduce-window
  26.2 0.2 slice.24
  26.4 0.4 copy.9
  26.9 0.2 reduce-window.9
  27.1 0.2 broadcast_add_fusion
  27.3 0.0 copy-done
  27.3 0.3 fusion.17
  27.6 0.0 copy-done.2
  27.6 0.0 copy-done.3
  27.6 7.4 %fusion.2 = bf16[4096,256]{1,0:T(8,128)(2,1)} fusion(s32[2048]{0:T(1024)S(1)} %multiply_add_fusion.1, bf16[2048,192]{0,1:T(8,128)(2,1)S(1)} %copy-done.2, bf16[2048,64]{0,1:T(8,128)(2,1)S(1)} %bitcast.40), kind=kOutput, calls=%fused_computation.3 | convolution fusion | flops 4306501632 | bytes 3153920 | tf_op jit(solution)/shard_map/dot_general | solution.py:35
  35.0 11.7 %all-to-all-start = ((bf16[64,64,256]{2,1,0:T(8,128)(2,1)}), bf16[64,64,256]{2,1,0:T(8,128)(2,1)S(1)}, u32[]{:S(2)}, u32[]{:S(2)}) async-start(bf16[64,64,256]{2,1,0:T(8,128)(2,1)} %bitcast.31), calls=%async_computation | async-start | bytes 4194304 | tf_op jit(solution)/shard_map/all_to_all | solution.py:36
  47.3 49.8 %all-to-all-done = bf16[64,64,256]{2,1,0:T(8,128)(2,1)S(1)} async-done(((bf16[64,64,256]{2,1,0:T(8,128)(2,1)}), bf16[64,64,256]{2,1,0:T(8,128)(2,1)S(1)}, u32[]{:S(2)}, u32[]{:S(2)}) %all-to-all-start) | async-done | bytes 2097184 | tf_op jit(solution)/shard_map/all_to_all | solution.py:36
  97.1 1.1 fusion.8
  98.2 12.3 %all_gather.6 = bf16[256,192]{1,0:T(8,128)(2,1)S(1)} all-gather(bf16[64,192]{1,0:T(8,128)(2,1)S(1)} %fusion.8), channel_id=1, replica_groups=mesh['blk'=64,'smp'=4] {'smp'}, dimensions={0}, use_global_device_ids=true | all-gather | bytes 122880 | tf_op jit(solution)/shard_map/all_gather | solution.py:47
  110.5 0.0 copy-start.1
  110.5 0.0 all-gather.2.cloned.1.call-done
  110.5 3.2 %fusion.19 = f32[48,8192]{1,0:T(8,128)S(1)} fusion(bf16[256,8192]{1,0:T(8,128)(2,1)} %all-gather.2.cloned.1.call-done, bf16[256,192]{1,0:T(8,128)(2,1)S(1)} %all_gather.6, s32[]{:T(128)S(6)} %select_n.3), kind=kOutput, calls=%fused_computation.22 | convolution fusion | flops 201326592 | bytes 5832708 | tf_op jit(solution)/shard_map/dot_general | solution.py:50
  113.7 1.8 collective-permute-start
  115.5 0.0 copy-done.1
  115.5 0.1 fusion.23
  115.5 69.0 %collective-permute-done = f32[48,8192]{1,0:T(8,128)S(1)} collective-permute-done((f32[48,8192]{1,0:T(8,128)S(1)}, f32[48,8192]{1,0:T(8,128)S(1)}, u32[]{:S(2)}, u32[]{:S(2)}) %collective-permute-start) | collective-permute-done | bytes 1572896 | tf_op jit(solution)/shard_map/ppermute | solution.py:14
  184.5 0.2 multiply_add_fusion
  184.7 0.1 collective-permute-start.1
  184.8 67.0 %collective-permute-done.1 = f32[48,8192]{1,0:T(8,128)S(1)} collective-permute-done((f32[48,8192]{1,0:T(8,128)S(1)}, f32[48,8192]{1,0:T(8,128)S(1)}, u32[]{:S(2)}, u32[]{:S(2)}) %collective-permute-start.1) | collective-permute-done | bytes 1572896 | tf_op jit(solution)/shard_map/ppermute | solution.py:14
  251.8 1.0 add_convert_fusion
  (2 shorter events, 0.0 us)
Async XLA Ops:
  6.5 104.0 %all-gather.2.cloned.1.call-start = ((), (), s32[]{:S(2)}) async-start(), calls=%async_computation.1 | async-start | bytes 5242880 | tf_op jit(solution)/shard_map/all_gather | solution.py:48
  7.3 20.0 %copy-start = (s32[2048,1]{0,1:T(1,128)S(1)}, s32[2048,1]{0,1:T(1,128)}, u32[]{:S(2)}) copy-start(s32[2048,1]{0,1:T(1,128)} %param.9) | copy-start | bytes 24580
  8.1 19.5 %copy-start.2 = (bf16[2048,192]{0,1:T(8,128)(2,1)S(1)}, bf16[2048,192]{0,1:T(8,128)(2,1)}, u32[]{:S(2)}) copy-start(bf16[2048,192]{0,1:T(8,128)(2,1)} %param.8) | copy-start | bytes 2359300
  8.1 19.5 %copy-start.3 = (bf16[64,2048]{1,0:T(8,128)(2,1)S(1)}, bf16[64,2048]{1,0:T(8,128)(2,1)}, u32[]{:S(2)}) copy-start(bf16[64,2048]{1,0:T(8,128)(2,1)} %param.7) | copy-start | bytes 786436
  35.0 62.1 %all-to-all-start = ((bf16[64,64,256]{2,1,0:T(8,128)(2,1)}), bf16[64,64,256]{2,1,0:T(8,128)(2,1)S(1)}, u32[]{:S(2)}, u32[]{:S(2)}) async-start(bf16[64,64,256]{2,1,0:T(8,128)(2,1)} %bitcast.31), calls=%async_computation | async-start | bytes 4194304 | tf_op jit(solution)/shard_map/all_to_all | solution.py:36
  110.5 5.0 %copy-start.1 = (f32[2,8192]{1,0:T(2,128)S(1)}, f32[2,8192]{1,0:T(2,128)}, u32[]{:S(2)}) copy-start(f32[2,8192]{1,0:T(2,128)} %param.11) | copy-start | bytes 196612
  113.7 70.9 %collective-permute-start = (f32[48,8192]{1,0:T(8,128)S(1)}, f32[48,8192]{1,0:T(8,128)S(1)}, u32[]{:S(2)}, u32[]{:S(2)}) collective-permute-start(f32[48,8192]{1,0:T(8,128)S(1)} %fusion.19), channel_id=1, source_target_pairs={{0,128},{128,0},{4,132},{132,4},{8,136},{136,8},{12,140},{140,12},... | collective-permute-start | bytes 4718600 | tf_op jit(solution)/shard_map/ppermute | solution.py:14
  184.7 67.1 %collective-permute-start.1 = (f32[48,8192]{1,0:T(8,128)S(1)}, f32[48,8192]{1,0:T(8,128)S(1)}, u32[]{:S(2)}, u32[]{:S(2)}) collective-permute-start(f32[48,8192]{1,0:T(8,128)S(1)} %multiply_add_fusion), channel_id=1, source_target_pairs={{0,64},{64,0},{4,68},{68,4},{8,72},{72,8},{12,76},{76,12},{16,80},... | collective-permute-start | bytes 4718600 | tf_op jit(solution)/shard_map/ppermute | solution.py:14
Sparse Core Ops, SparseCore 0:
  9.2 53.3 all-gather.1
where the time goes:
time: 263 us; the launch traced here: 260 us
  waiting for transfers between devices  187 us (71%)
  other arithmetic  20.8 us (8%)
  between operations  14.1 us (5%)
  starting transfers between devices  13.5 us (5%)
  blocking collectives  12.3 us (5%)
  matrix products  11.7 us (4%)
    ppermute x2, waiting for transfers between devices, partner_2(): return lax.ppermute(block, axis, route)  136 us
    all_to_all x1, waiting for transfers between devices, body(): lax.all_to_all(outgoing, 'blk', split_axis=0, concat_axis=0, tiled=True)  49.8 us
    another operation x3, other arithmetic  18.5 us
    all_gather x1, blocking collectives, body(): weight_piece = lax.all_gather(weights, 'smp', axis=0, tiled=True)  12.3 us
    all_to_all x1, starting transfers between devices, body(): lax.all_to_all(outgoing, 'blk', split_axis=0, concat_axis=0, tiled=True)  11.7 us
    dot_general x1, matrix products, body(): jnp.dot(placing, stacked, preferred_element_type=jnp.float32)  7.43 us
  transfers between devices with their start and end apart: 4, of which 3 were waited for; matrix products, arithmetic and copies ran while one was open for 11% of the time, Pallas kernels for 0%

commit v1 on v0

v1 whole, which is shorter than its diff:
```python
import functools

import jax
import jax.numpy as jnp
from jax import lax
from jax.experimental import pallas as pl
from jax.experimental.pallas import tpu as pltpu
from jax.sharding import Mesh, PartitionSpec as P

GROUP = ("zg", "smp")
Z_AXES = ("zg", "zl")
BLK = ("zg", "zl", "y", "core")
STEP = 8


def partial_kernel(parity_ref, owners_ref, adjoint_ref, probes_ref, out_ref, masked, wide):
    step = pl.program_id(0)
    samples = adjoint_ref.shape[0]
    vectors = probes_ref.shape[0]

    @pl.when(step == 0)
    def _():
        wide[:vectors, :] = probes_ref[...]
        wide[vectors:, :] = probes_ref[128:, :]

    own = owners_ref[...]
    adjoint = adjoint_ref[...]
    y_count = pl.num_programs(0)
    for z in range(STEP):
        owner = (z * y_count + step) * 2 + parity_ref[0]
        hot = jnp.where(own == owner, 1.0, 0.0).astype(jnp.bfloat16)
        masked[z * samples:(z + 1) * samples, :] = adjoint * hot
    product = lax.dot_general(
        masked[...], wide[...], (((1,), (1,)), ((), ())), preferred_element_type=jnp.float32
    )
    half = samples // 2
    low = lax.broadcasted_iota(jnp.int32, (half, 128), 1) < 64
    for z in range(STEP):
        block = product[z * samples:(z + 1) * samples, :]
        out_ref[0, z, :samples, :] = block[:, :128]
        out_ref[0, z, samples:, :] = jnp.where(low, block[:half, 128:], block[half:, 128:])


def partial_coeffs(parity, owners, adjoint, probes):
    samples, rows = adjoint.shape
    vectors = probes.shape[0]
    y_count = lax.axis_size("y")
    packed = samples * vectors // 128
    return pl.pallas_call(
        partial_kernel,
        grid=(y_count,),
        in_specs=[
            pl.BlockSpec(memory_space=pltpu.SMEM),
            pl.BlockSpec((1, rows), lambda i: (0, 0)),
            pl.BlockSpec((samples, rows), lambda i: (0, 0)),
            pl.BlockSpec((vectors, rows), lambda i: (0, 0)),
        ],
        out_specs=pl.BlockSpec((1, STEP, packed, 128), lambda i: (i, 0, 0, 0)),
        out_shape=jax.ShapeDtypeStruct((y_count, STEP, packed, 128), jnp.float32),
        scratch_shapes=[
            pltpu.VMEM((STEP * samples, rows), jnp.bfloat16),
            pltpu.VMEM((256, rows), jnp.bfloat16),
        ],
        compiler_params=pltpu.CompilerParams(vmem_limit_bytes=24 * 1024 * 1024),
        cost_estimate=pl.CostEstimate(
            flops=2 * y_count * STEP * samples * rows * 256,
            bytes_accessed=3 * 1024 * 1024,
            transcendentals=0,
        ),
    )(parity, owners, adjoint, probes)


def field_kernel(weights_ref, samples_ref, twiddle_ref, out_ref, field):
    blocks = twiddle_ref.shape[0]
    parts = weights_ref.shape[0] // blocks
    samples = samples_ref.shape[1]
    half = samples // 2
    vectors = field.shape[1]
    for c in range(blocks):
        grid = samples_ref[c * parts:(c + 1) * parts].reshape(parts * samples, -1)
        head = [weights_ref[c * parts + p, :samples, :] for p in range(parts)]
        tail = []
        for p in range(parts):
            rest = weights_ref[c * parts + p, samples:, :]
            tail += [rest[:, :64], rest[:, 64:]]
        head = jnp.concatenate(head, axis=0)
        tail = jnp.concatenate(tail, axis=0)
        field[c, :128, :] = lax.dot_general(
            head, grid, (((0,), (0,)), ((), ())), preferred_element_type=jnp.float32
        )
        field[c, 128:, :] = lax.dot_general(
            tail, grid, (((0,), (0,)), ((), ())), preferred_element_type=jnp.float32
        )
    share = vectors // parts
    for p in range(parts):
        rows = slice(p * share, (p + 1) * share)
        level = [field[c, rows, :] for c in range(blocks)]
        for index, distance in enumerate((2, 1)):
            level = [
                level[c] + twiddle_ref[c, index:index + 1, :] * level[c ^ distance]
                for c in range(blocks)
            ]
        for c in range(blocks):
            out_ref[c * parts + p] = level[c].astype(jnp.bfloat16)


def butterfly(weights, samples, twiddle, vectors):
    pieces, _, points = samples.shape
    share = vectors * twiddle.shape[0] // pieces
    return pl.pallas_call(
        field_kernel,
        out_shape=jax.ShapeDtypeStruct((pieces, share, points), jnp.bfloat16),
        in_specs=[pl.BlockSpec(memory_space=pltpu.VMEM)] * 3,
        out_specs=pl.BlockSpec(memory_space=pltpu.VMEM),
        scratch_shapes=[pltpu.VMEM((twiddle.shape[0], vectors, points), jnp.float32)],
        compiler_params=pltpu.CompilerParams(vmem_limit_bytes=24 * 1024 * 1024),
        cost_estimate=pl.CostEstimate(
            flops=2 * pieces * 64 * vectors * points,
            bytes_accessed=3 * 1024 * 1024,
            transcendentals=0,
        ),
    )(weights, samples, twiddle)


def body(forward_samples, adjoint_samples, probe_values, owners, block_ranks, twiddle):
    groups = lax.axis_size("zg")
    parts = lax.axis_size("smp")
    samples, points = forward_samples.shape
    vectors = probe_values.shape[1]
    members = groups * parts
    smp = lax.axis_index("smp")
    core = lax.axis_index("core")

    pieces = forward_samples.reshape(samples, members, points // members).transpose(1, 0, 2)
    pieces = lax.all_to_all(pieces, GROUP, 0, 0, tiled=True)
    factors = twiddle.reshape(twiddle.shape[0], groups, parts, points // members)
    factors = lax.dynamic_index_in_dim(factors, smp, 2, keepdims=False).transpose(1, 0, 2)
    factors = lax.all_to_all(factors, "zg", 0, 0, tiled=True)

    own, probes = owners.T, probe_values.T
    sent = partial_coeffs((1 - core)[None], own, adjoint_samples, probes)
    came = lax.ppermute(sent, "core", [(0, 1), (1, 0)])
    kept = partial_coeffs(core[None], own, adjoint_samples, probes)
    sums = (kept + came).astype(jnp.bfloat16)
    sums = lax.all_to_all(sums, "y", 0, 0, tiled=True)
    sums = jnp.sum(sums.astype(jnp.float32), axis=0).astype(jnp.bfloat16)
    sums = lax.all_to_all(sums, Z_AXES, 0, 0, tiled=True)
    coeffs = jnp.sum(sums.astype(jnp.float32), axis=0)

    row = lax.broadcasted_iota(jnp.int32, coeffs.shape, 0)
    lane = lax.broadcasted_iota(jnp.int32, coeffs.shape, 1)
    tail = row - samples + jnp.where(lane < 64, 0, samples // 2)
    sample = smp * samples + jnp.where(row < samples, row, tail)
    weights = jnp.where(sample < block_ranks[0], coeffs, 0.0).astype(jnp.bfloat16)
    weights = jnp.broadcast_to(weights[None], (members,) + weights.shape)
    weights = lax.all_to_all(weights, GROUP, 0, 0, tiled=True)

    result = butterfly(weights, pieces, factors, vectors)
    result = lax.all_to_all(result, GROUP, 0, 0, tiled=True)
    return result.transpose(1, 0, 2).reshape(vectors // parts, points)


def solution(mesh):
    grid = Mesh(mesh.devices.reshape(4, 2, 4, 2, 4), BLK + ("smp",))
    in_specs = (
        P("smp", BLK),
        P("smp", BLK),
        P(BLK, None),
        P(BLK, None),
        P(BLK),
        P(None, BLK),
    )
    out_specs = P("smp", BLK)
    return jax.shard_map(body, mesh=grid, in_specs=in_specs, out_specs=out_specs, check_vma=False)
```

time: 263 us -> 130 us (0.49)
  waiting for transfers between devices: 187 us -> 50.1 us
  blocking collectives: 12.3 us -> 41.4 us
  other arithmetic: 20.8 us -> 2.07 us
  between operations: 14.1 us -> 0.78 us
  matrix products: 11.7 us -> 0 us
  starting transfers between devices: 13.5 us -> 21.8 us
  Pallas kernels: 0 us -> 6.98 us
  local copies, waits for them, and re-layouts: 0.71 us -> 5.59 us
    ppermute x2 -> x1, waiting for transfers between devices: 136 us -> 0.24 us  [body(): came = lax.ppermute(sent, 'core', [(0, 1), (1, 0)])]
    all_to_all x0 -> x2, blocking collectives: none -> 41.4 us  [the longest x1 23.9 us: body(): result = lax.all_to_all(result, GROUP, 0, 0, tiled=True)]
    another operation x3 -> x0, other arithmetic: 18.5 us -> none
    all_gather x1 -> x0, blocking collectives: 12.3 us -> none  [body(): weight_piece = lax.all_gather(weights, 'smp', axis=0, tiled=True)]
    dot_general x3 -> x0, matrix products: 11.7 us -> none  [the longest x1 7.43 us: body(): jnp.dot(placing, stacked, preferred_element_type=jnp.float32)]
    all_to_all x1 -> x4, starting transfers between devices: 11.7 us -> 21.7 us  [the longest x1 7.56 us: body(): factors = lax.all_to_all(factors, 'zg', 0, 0, tiled=True)]
    pallas_call x0 -> x3, Pallas kernels: none -> 6.98 us  [the longest x2 6.22 us: partial_coeffs(): pl.pallas_call(partial_kernel, grid=(y_count,), in_specs=[pl.BlockSpec(me...]
    unnamed x8 -> x17, local copies, waits for them, and re-layouts: 0.02 us -> 3.41 us
  transfers between devices with their start and end apart: 4 -> 5, of which waited for: 3 -> 5; matrix products, arithmetic and copies ran while one was open for 11% -> 2% of each run, Pallas kernels for 0% -> 2%
where the time goes in v1:
time: 130 us; the launch traced here: 129 us
  waiting for transfers between devices  50.1 us (39%)
  blocking collectives  41.4 us (32%)
  starting transfers between devices  21.8 us (17%)
  Pallas kernels  6.98 us (5%)
  local copies, waits for them, and re-layouts  5.59 us (4%)
  other arithmetic  2.07 us (2%)
    all_to_all x1, waiting for transfers between devices, body(): pieces = lax.all_to_all(pieces, GROUP, 0, 0, tiled=True)  25.1 us
    all_to_all x1, blocking collectives, body(): result = lax.all_to_all(result, GROUP, 0, 0, tiled=True)  23.9 us
    all_to_all x1, blocking collectives, body(): weights = lax.all_to_all(weights, GROUP, 0, 0, tiled=True)  17.5 us
    all_to_all x1, waiting for transfers between devices, body(): sums = lax.all_to_all(sums, 'y', 0, 0, tiled=True)  10.5 us
    all_to_all x1, starting transfers between devices, body(): factors = lax.all_to_all(factors, 'zg', 0, 0, tiled=True)  7.56 us
    all_to_all x1, waiting for transfers between devices, body(): sums = lax.all_to_all(sums, Z_AXES, 0, 0, tiled=True)  7.26 us
    all_to_all x1, waiting for transfers between devices, body(): factors = lax.all_to_all(factors, 'zg', 0, 0, tiled=True)  6.96 us
    pallas_call x2, Pallas kernels, partial_coeffs(): pl.pallas_call(partial_kernel, grid=(y_count,), in_specs=[pl.BlockSpec(me...  6.22 us
  transfers between devices with their start and end apart: 5, of which 5 were waited for; matrix products, arithmetic and copies ran while one was open for 2% of the time, Pallas kernels for 2%

profile of v1, /device:TPU:40, one launch (start us, length us, event | category | flops | bytes accessed | tf_op | source)
XLA Modules:
  0.0 128.7 jit_solution(7107995102122155896)
XLA Ops:
  0.0 0.0 copy-start
  0.0 1.1 copy-done
  1.1 0.0 copy-start.2
  1.1 0.9 copy-done.2
  2.1 0.0 copy-start.4
  2.1 0.7 copy-done.4
  2.8 0.0 copy-start.1
  2.8 0.0 copy-start.3
  2.8 0.0 copy-start.5
  2.8 3.1 %shard_map.65 = f32[4,8,96,128]{3,2,1,0:T(8,128)S(1)} custom-call(s32[1]{0:T(128)} %bitcast.4.parity_ref, s32[1,2048]{1,0:T(1,128)S(1)} %bitcast.23, bf16[64,2048]{1,0:T(8,128)(2,1)S(1)} %copy-done.2, bf16[192,2048]{1,0:T(8,128)(2,1)S(1)} %bitcast.21), custom_call_target="tpu_custom_call" | custom-call | flops 2147483648 | bytes 3145728 | tf_op jit(solution)/shard_map/pallas_call | solution.py:49
  5.9 0.1 collective-permute-start
  6.0 0.0 copy-done.1
  6.0 0.0 copy-done.3
  6.0 0.0 copy-done.5
  6.0 3.1 %shard_map.64 = f32[4,8,96,128]{3,2,1,0:T(8,128)S(1)} custom-call(s32[1]{0:T(128)} %bitcast.1.parity_ref, s32[1,2048]{1,0:T(1,128)S(1)} %bitcast.24, bf16[64,2048]{1,0:T(8,128)(2,1)S(1)} %copy-done.3, bf16[192,2048]{1,0:T(8,128)(2,1)S(1)} %bitcast.22), custom_call_target="tpu_custom_call" | custom-call | flops 2147483648 | bytes 3145728 | tf_op jit(solution)/shard_map/pallas_call | solution.py:49
  9.2 0.2 collective-permute-done
  9.4 1.1 add_convert_fusion
  10.5 0.0 copy-start.7
  10.5 0.0 copy-start.6
  10.5 5.0 %all-to-all-start = ((bf16[4,8,96,128]{3,2,1,0:T(8,128)(2,1)}), bf16[4,8,96,128]{3,2,1,0:T(8,128)(2,1)S(1)}, u32[]{:S(2)}, u32[]{:S(2)}) async-start(bf16[4,8,96,128]{3,2,1,0:T(8,128)(2,1)} %add_convert_fusion), calls=%async_computation | async-start | bytes 1572864 | tf_op jit(solution)/shard_map/all_to_all | solution.py:145
  15.6 0.0 copy-done.7
  15.6 0.1 reshape.54
  15.7 0.6 copy.20
  16.3 10.5 %all-to-all-done = bf16[4,8,96,128]{3,2,1,0:T(8,128)(2,1)S(1)} async-done(((bf16[4,8,96,128]{3,2,1,0:T(8,128)(2,1)}), bf16[4,8,96,128]{3,2,1,0:T(8,128)(2,1)S(1)}, u32[]{:S(2)}, u32[]{:S(2)}) %all-to-all-start) | async-done | bytes 786464 | tf_op jit(solution)/shard_map/all_to_all | solution.py:145
  26.8 7.6 %all-to-all-start.4 = ((f32[4,2,512]{2,1,0:T(2,128)}), f32[4,2,512]{2,1,0:T(2,128)S(1)}, u32[]{:S(2)}, u32[]{:S(2)}) async-start(f32[4,2,512]{2,1,0:T(2,128)} %bitcast.19), calls=%async_computation.4 | async-start | bytes 32768 | tf_op jit(solution)/shard_map/all_to_all | solution.py:138
  34.4 0.8 reduce_sum.21
  35.2 7.0 %all-to-all-done.4.twiddle_ref = f32[4,2,512]{2,1,0:T(2,128)S(1)} async-done(((f32[4,2,512]{2,1,0:T(2,128)}), f32[4,2,512]{2,1,0:T(2,128)S(1)}, u32[]{:S(2)}, u32[]{:S(2)}) %all-to-all-start.4) | async-done | bytes 16416 | tf_op jit(solution)/shard_map/all_to_all | solution.py:138
  42.1 4.3 %all-to-all-start.1 = ((bf16[8,96,128]{2,1,0:T(8,128)(2,1)}), bf16[8,96,128]{2,1,0:T(8,128)(2,1)S(1)}, u32[]{:S(2)}, u32[]{:S(2)}) async-start(bf16[8,96,128]{2,1,0:T(8,128)(2,1)} %reduce_sum.21), calls=%async_computation.1 | async-start | bytes 393216 | tf_op jit(solution)/shard_map/all_to_all | solution.py:147
  46.4 0.0 copy-done.6
  46.4 1.1 copy.19
  47.5 7.3 %all-to-all-done.1 = bf16[8,96,128]{2,1,0:T(8,128)(2,1)S(1)} async-done(((bf16[8,96,128]{2,1,0:T(8,128)(2,1)}), bf16[8,96,128]{2,1,0:T(8,128)(2,1)S(1)}, u32[]{:S(2)}, u32[]{:S(2)}) %all-to-all-start.1) | async-done | bytes 196640 | tf_op jit(solution)/shard_map/all_to_all | solution.py:147
  54.8 4.8 %all-to-all-start.3 = ((bf16[16,64,512]{2,1,0:T(8,128)(2,1)}), bf16[16,64,512]{2,1,0:T(8,128)(2,1)S(1)}, u32[]{:S(2)}, u32[]{:S(2)}) async-start(bf16[16,64,512]{2,1,0:T(8,128)(2,1)} %bitcast.18), calls=%async_computation.3 | async-start | bytes 2097152 | tf_op jit(solution)/shard_map/all_to_all | solution.py:135
  60.3 0.1 select_convert_fusion
  60.4 25.1 %all-to-all-done.3.samples_ref = bf16[16,64,512]{2,1,0:T(8,128)(2,1)S(1)} async-done(((bf16[16,64,512]{2,1,0:T(8,128)(2,1)}), bf16[16,64,512]{2,1,0:T(8,128)(2,1)S(1)}, u32[]{:S(2)}, u32[]{:S(2)}) %all-to-all-start.3) | async-done | bytes 1048608 | tf_op jit(solution)/shard_map/all_to_all | solution.py:135
  85.5 0.1 broadcast_in_dim.29
  85.6 17.5 %all_to_all.30.weights_ref = bf16[16,96,128]{2,1,0:T(8,128)(2,1)S(1)} all-to-all(bf16[16,96,128]{2,1,0:T(8,128)(2,1)S(1)} %broadcast_in_dim.29), channel_id=1, replica_groups=mesh['zg'=4,'zl'=2,'y'=4,'core'=2,'smp'=4] {'zg','smp'}, dimensions={0} | all-to-all | bytes 786432 | tf_op jit(solution)/shard_map/all_to_all | solution.py:156
  103.0 0.8 shard_map.66
  103.8 23.9 %all_to_all.31 = bf16[16,48,512]{2,1,0:T(8,128)(2,1)S(1)} all-to-all(bf16[16,48,512]{2,1,0:T(8,128)(2,1)S(1)} %shard_map.66), channel_id=1, replica_groups=mesh['zg'=4,'zl'=2,'y'=4,'core'=2,'smp'=4] {'zg','smp'}, dimensions={0} | all-to-all | bytes 1572864 | tf_op jit(solution)/shard_map/all_to_all | solution.py:159
  127.7 1.0 copy.16
  (5 shorter events, 0.1 us)
Async XLA Ops:
  0.0 1.1 copy-start
  1.1 0.9 copy-start.2
  2.1 0.7 copy-start.4
  2.8 3.2 %copy-start.1 = (bf16[2048,192]{0,1:T(8,128)(2,1)S(1)}, bf16[2048,192]{0,1:T(8,128)(2,1)}, u32[]{:S(2)}) copy-start(bf16[2048,192]{0,1:T(8,128)(2,1)} %param.8) | copy-start | bytes 2359300
  2.8 3.2 %copy-start.3 = (bf16[64,2048]{1,0:T(8,128)(2,1)S(1)}, bf16[64,2048]{1,0:T(8,128)(2,1)}, u32[]{:S(2)}) copy-start(bf16[64,2048]{1,0:T(8,128)(2,1)} %adjoint_ref.3) | copy-start | bytes 786436
  2.8 3.2 %copy-start.5 = (s32[2048,1]{0,1:T(1,128)S(1)}, s32[2048,1]{0,1:T(1,128)}, u32[]{:S(2)}) copy-start(s32[2048,1]{0,1:T(1,128)} %param.9) | copy-start | bytes 24580
  5.9 3.5 %collective-permute-start = (f32[4,8,96,128]{3,2,1,0:T(8,128)S(1)}, f32[4,8,96,128]{3,2,1,0:T(8,128)S(1)}, u32[]{:S(2)}, u32[]{:S(2)}) collective-permute-start(f32[4,8,96,128]{3,2,1,0:T(8,128)S(1)} %shard_map.65), channel_id=1, source_target_pairs={{0,4},{4,0},{1,5},{5,1},{2,6},{6,2},{3,7},{7,3},{8,12},{12,8},{9,1... | collective-permute-start | bytes 4718600 | tf_op jit(solution)/shard_map/ppermute | solution.py:142
  10.5 5.0 %copy-start.7 = (f32[2,8192]{1,0:T(2,128)S(1)}, f32[2,8192]{1,0:T(2,128)}, u32[]{:S(2)}) copy-start(f32[2,8192]{1,0:T(2,128)} %param.11) | copy-start | bytes 196612
  10.5 35.9 %copy-start.6 = (bf16[64,8192]{1,0:T(8,128)(2,1)S(1)}, bf16[64,8192]{1,0:T(8,128)(2,1)}, u32[]{:S(2)}) copy-start(bf16[64,8192]{1,0:T(8,128)(2,1)} %param.6) | copy-start | bytes 3145732
  10.5 16.3 %all-to-all-start = ((bf16[4,8,96,128]{3,2,1,0:T(8,128)(2,1)}), bf16[4,8,96,128]{3,2,1,0:T(8,128)(2,1)S(1)}, u32[]{:S(2)}, u32[]{:S(2)}) async-start(bf16[4,8,96,128]{3,2,1,0:T(8,128)(2,1)} %add_convert_fusion), calls=%async_computation | async-start | bytes 1572864 | tf_op jit(solution)/shard_map/all_to_all | solution.py:145
  26.8 15.3 %all-to-all-start.4 = ((f32[4,2,512]{2,1,0:T(2,128)}), f32[4,2,512]{2,1,0:T(2,128)S(1)}, u32[]{:S(2)}, u32[]{:S(2)}) async-start(f32[4,2,512]{2,1,0:T(2,128)} %bitcast.19), calls=%async_computation.4 | async-start | bytes 32768 | tf_op jit(solution)/shard_map/all_to_all | solution.py:138
  42.1 12.6 %all-to-all-start.1 = ((bf16[8,96,128]{2,1,0:T(8,128)(2,1)}), bf16[8,96,128]{2,1,0:T(8,128)(2,1)S(1)}, u32[]{:S(2)}, u32[]{:S(2)}) async-start(bf16[8,96,128]{2,1,0:T(8,128)(2,1)} %reduce_sum.21), calls=%async_computation.1 | async-start | bytes 393216 | tf_op jit(solution)/shard_map/all_to_all | solution.py:147
  54.8 30.7 %all-to-all-start.3 = ((bf16[16,64,512]{2,1,0:T(8,128)(2,1)}), bf16[16,64,512]{2,1,0:T(8,128)(2,1)S(1)}, u32[]{:S(2)}, u32[]{:S(2)}) async-start(bf16[16,64,512]{2,1,0:T(8,128)(2,1)} %bitcast.18), calls=%async_computation.3 | async-start | bytes 2097152 | tf_op jit(solution)/shard_map/all_to_all | solution.py:135

commit v2 on v1

v2 whole, which is shorter than its diff:
```python
import jax
import jax.numpy as jnp
from jax import lax
from jax.experimental import pallas as pl
from jax.experimental.pallas import tpu as pltpu
from jax.sharding import Mesh, PartitionSpec as P

GROUP = ("zg", "smp")
Z_AXES = ("zg", "zl")
BLK = ("zg", "zl", "y", "core")
MIB = 1024 * 1024
VMEM = pl.BlockSpec(memory_space=pltpu.VMEM)
SMEM = pl.BlockSpec(memory_space=pltpu.SMEM)


def partial_kernel(place_ref, owners_ref, adjoint_ref, probes_ref, out_ref, masked, wide):
    step = pl.program_id(0)
    y_count = pl.num_programs(0)
    z_count = out_ref.shape[1]
    samples = adjoint_ref.shape[0]
    vectors = probes_ref.shape[0]

    @pl.when(step == 0)
    def _():
        wide[:vectors, :] = probes_ref[...]
        wide[vectors:, :] = probes_ref[128:, :]

    own = owners_ref[...]
    adjoint = adjoint_ref[...]
    y = lax.rem(place_ref[1] + step, y_count)
    for offset in range(z_count):
        z = lax.rem(place_ref[0] + offset, z_count)
        owner = (z * y_count + y) * 2 + place_ref[2]
        hot = jnp.where(own == owner, 1.0, 0.0).astype(jnp.bfloat16)
        masked[offset * samples:(offset + 1) * samples, :] = adjoint * hot
    product = lax.dot_general(
        masked[...], wide[...], (((1,), (1,)), ((), ())), preferred_element_type=jnp.float32
    )
    half = samples // 2
    low = lax.broadcasted_iota(jnp.int32, (half, 128), 1) < 64
    for offset in range(z_count):
        block = product[offset * samples:(offset + 1) * samples, :]
        out_ref[0, offset, :samples, :] = block[:, :128]
        out_ref[0, offset, samples:, :] = jnp.where(low, block[:half, 128:], block[half:, 128:])


def partial_coeffs(place, owners, adjoint, probes):
    samples, rows = adjoint.shape
    vectors = probes.shape[0]
    y_count, z_count = lax.axis_size("y"), lax.axis_size(Z_AXES)
    packed = samples * vectors // 128
    return pl.pallas_call(
        partial_kernel,
        grid=(y_count,),
        in_specs=[
            SMEM,
            pl.BlockSpec((1, rows), lambda i: (0, 0)),
            pl.BlockSpec((samples, rows), lambda i: (0, 0)),
            pl.BlockSpec((vectors, rows), lambda i: (0, 0)),
        ],
        out_specs=pl.BlockSpec((1, z_count, packed, 128), lambda i: (i, 0, 0, 0)),
        out_shape=jax.ShapeDtypeStruct((y_count, z_count, packed, 128), jnp.float32),
        scratch_shapes=[
            pltpu.VMEM((z_count * samples, rows), jnp.bfloat16),
            pltpu.VMEM((256, rows), jnp.bfloat16),
        ],
        compiler_params=pltpu.CompilerParams(vmem_limit_bytes=24 * MIB),
        cost_estimate=pl.CostEstimate(
            flops=2 * y_count * z_count * samples * rows * 256,
            bytes_accessed=3 * MIB,
            transcendentals=0,
        ),
    )(place, owners, adjoint, probes)


def local_call(kernel, out_shape, *args, smem=0, scratch=(), flops=0):
    return pl.pallas_call(
        kernel,
        out_shape=out_shape,
        in_specs=[SMEM] * smem + [VMEM] * (len(args) - smem),
        out_specs=jax.tree.map(lambda _: VMEM, out_shape),
        scratch_shapes=list(scratch),
        compiler_params=pltpu.CompilerParams(vmem_limit_bytes=24 * MIB),
        cost_estimate=pl.CostEstimate(flops=flops, bytes_accessed=2 * MIB, transcendentals=0),
    )(*args)


def merge_kernel(kept_ref, came_ref, own_ref, *out_refs):
    own_ref[...] = kept_ref[0] + came_ref[0]
    for offset, out_ref in enumerate(out_refs, 1):
        out_ref[...] = (kept_ref[offset] + came_ref[offset]).astype(out_ref.dtype)


def spread_kernel(count, *refs):
    total = refs[0][...]
    for ref in refs[1:count]:
        total = total + ref[...].astype(jnp.float32)
    for offset, out_ref in enumerate(refs[count:]):
        out_ref[...] = total[offset].astype(out_ref.dtype)


def weights_kernel(place_ref, *refs):
    total = refs[0][...]
    for ref in refs[1:-1]:
        total = total + ref[...].astype(jnp.float32)
    samples = total.shape[0] * 2 // 3
    row = lax.broadcasted_iota(jnp.int32, total.shape, 0)
    lane = lax.broadcasted_iota(jnp.int32, total.shape, 1)
    tail = row - samples + jnp.where(lane < 64, 0, samples // 2)
    sample = place_ref[0] * samples + jnp.where(row < samples, row, tail)
    refs[-1][...] = jnp.where(sample < place_ref[1], total, 0.0).astype(jnp.bfloat16)


def field_kernel(blocks, parts, place_ref, samples_ref, *refs):
    twiddle_refs, weight_refs = refs[:blocks], refs[blocks:-2]
    out_ref, field = refs[-2:]
    zg, smp = place_ref[0], place_ref[1]
    samples, points = samples_ref.shape[1:]
    vectors = field.shape[1]
    for c in range(blocks):
        block = zg ^ c
        grid, head, tail = [], [], []
        for p in range(parts):
            grid.append(samples_ref[block * parts + lax.rem(smp - p + parts, parts)])
            weights = weight_refs[c * parts + p]
            head.append(weights[:samples, :])
            rest = weights[samples:, :]
            tail += [rest[:, :64], rest[:, 64:]]
        grid = jnp.concatenate(grid, axis=0)
        head = jnp.concatenate(head, axis=0)
        tail = jnp.concatenate(tail, axis=0)
        field[c, :128, :] = lax.dot_general(
            head, grid, (((0,), (0,)), ((), ())), preferred_element_type=jnp.float32
        )
        field[c, 128:, :] = lax.dot_general(
            tail, grid, (((0,), (0,)), ((), ())), preferred_element_type=jnp.float32
        )
    share = vectors // parts
    for p in range(parts):
        rows = slice(p * share, (p + 1) * share)
        level = [field[c, rows, :] for c in range(blocks)]
        for index, distance in enumerate((2, 1)):
            level = [
                level[c] + twiddle_refs[c][index:index + 1, :] * level[c ^ distance]
                for c in range(blocks)
            ]
        for c in range(blocks):
            out_ref[(zg ^ c) * parts + p] = level[c].astype(jnp.bfloat16)


def turn(x, axis, offset):
    count = lax.axis_size(axis)
    return lax.ppermute(x, axis, [(i, (i + offset) % count) for i in range(count)])


def body(forward_samples, adjoint_samples, probe_values, owners, block_ranks, twiddle):
    groups, parts = lax.axis_size("zg"), lax.axis_size("smp")
    y_count, z_count = lax.axis_size("y"), lax.axis_size(Z_AXES)
    samples, points = forward_samples.shape
    vectors = probe_values.shape[1]
    members = groups * parts
    piece = points // members
    zg, smp = lax.axis_index("zg"), lax.axis_index("smp")
    z, y, core = lax.axis_index(Z_AXES), lax.axis_index("y"), lax.axis_index("core")

    pieces = forward_samples.reshape(samples, members, piece).transpose(1, 0, 2)
    pieces = lax.all_to_all(pieces, GROUP, 0, 0, tiled=True)
    factors = []
    for c in range(groups):
        start = ((zg ^ c) * parts + smp) * piece
        part = lax.dynamic_slice_in_dim(twiddle, start, piece, 1)
        factors.append(lax.ppermute(part, "zg", [(i, i ^ c) for i in range(groups)]) if c else part)

    own, probes = owners.T, probe_values.T
    sent = partial_coeffs(jnp.stack([z, y, 1 - core]), own, adjoint_samples, probes)
    came = lax.ppermute(sent, "core", [(0, 1), (1, 0)])
    kept = partial_coeffs(jnp.stack([z, y, core]), own, adjoint_samples, probes)
    packed = kept.shape[2:]
    shapes = [jax.ShapeDtypeStruct((z_count,) + packed, jnp.float32)]
    shapes += [jax.ShapeDtypeStruct((z_count,) + packed, jnp.bfloat16)] * (y_count - 1)
    sums = local_call(merge_kernel, shapes, kept, came)
    sums = [sums[0]] + [turn(sums[i], "y", i) for i in range(1, y_count)]
    shapes = [jax.ShapeDtypeStruct(packed, jnp.float32)]
    shapes += [jax.ShapeDtypeStruct(packed, jnp.bfloat16)] * (z_count - 1)
    sums = local_call(lambda *refs: spread_kernel(y_count, *refs), shapes, *sums)
    sums = [sums[0]] + [turn(sums[i], Z_AXES, i) for i in range(1, z_count)]
    weights = local_call(
        weights_kernel,
        jax.ShapeDtypeStruct(packed, jnp.bfloat16),
        jnp.stack([smp, block_ranks[0]]),
        *sums,
        smem=1,
    )
    every = []
    for c in range(groups):
        for p in range(parts):
            route = [
                (i, (i // parts ^ c) * parts + (i + p) % parts) for i in range(members)
            ]
            every.append(lax.ppermute(weights, GROUP, route) if c or p else weights)

    result = local_call(
        lambda *refs: field_kernel(groups, parts, *refs),
        jax.ShapeDtypeStruct((members, vectors // parts, piece), jnp.bfloat16),
        jnp.stack([zg, smp]),
        pieces,
        *factors,
        *every,
        smem=1,
        scratch=[pltpu.VMEM((groups, vectors, piece), jnp.float32)],
        flops=2 * members * samples * vectors * piece,
    )
    result = lax.all_to_all(result, GROUP, 0, 0, tiled=True)
    return result.transpose(1, 0, 2).reshape(vectors // parts, points)


def solution(mesh):
    grid = Mesh(mesh.devices.reshape(4, 2, 4, 2, 4), BLK + ("smp",))
    in_specs = (
        P("smp", BLK),
        P("smp", BLK),
        P(BLK, None),
        P(BLK, None),
        P(BLK),
        P(None, BLK),
    )
    out_specs = P("smp", BLK)
    return jax.shard_map(body, mesh=grid, in_specs=in_specs, out_specs=out_specs, check_vma=False)
```

time: 130 us -> 135 us (1.038)
  starting transfers between devices: 21.8 us -> 75.3 us
  waiting for transfers between devices: 50.1 us -> 16.2 us
  blocking collectives: 41.4 us -> 24.1 us
  Pallas kernels: 6.98 us -> 11 us
  other arithmetic: 2.07 us -> 0.3 us
    ppermute x0 -> x28, starting transfers between devices: none -> 65 us  [the longest x15 38.8 us: body(): every.append(lax.ppermute(weights, GROUP, route) if c or p else weights)]
    all_to_all x1, waiting for transfers between devices: 25.1 us -> 0.01 us  [body(): pieces = lax.all_to_all(pieces, GROUP, 0, 0, tiled=True)]
    all_to_all x3 -> x0, waiting for transfers between devices: 24.7 us -> none  [the longest x1 10.5 us: body(): sums = lax.all_to_all(sums, 'y', 0, 0, tiled=True)]
    all_to_all x1 -> x0, blocking collectives: 17.5 us -> none  [body(): weights = lax.all_to_all(weights, GROUP, 0, 0, tiled=True)]
    all_to_all x3 -> x0, starting transfers between devices: 16.9 us -> none  [the longest x1 7.56 us: body(): factors = lax.all_to_all(factors, 'zg', 0, 0, tiled=True)]
    ppermute x0 -> x28, waiting for transfers between devices: none -> 16.2 us  [the longest x10 13.2 us: turn(): lax.ppermute(x, axis, [(i, (i + offset) % count) for i in range(count)])]
    all_to_all x1, starting transfers between devices: 4.77 us -> 10.3 us  [body(): pieces = lax.all_to_all(pieces, GROUP, 0, 0, tiled=True)]
    pallas_call x3 -> x6, Pallas kernels: 6.98 us -> 11 us  [the longest x2 8.09 us: partial_coeffs(): pl.pallas_call(partial_kernel, grid=(y_count,), in_specs=[SMEM, pl.BlockS...]
  transfers between devices with their start and end apart: 5 -> 30, of which waited for: 5 -> 8; matrix products, arithmetic and copies ran while one was open for 2% -> 2% of each run, Pallas kernels for 2% -> 4%
where the time goes in v2:
time: 135 us; the launch traced here: 134 us
  starting transfers between devices  75.3 us (56%)
  blocking collectives  24.1 us (18%)
  waiting for transfers between devices  16.2 us (12%)
  Pallas kernels  11 us (8%)
  local copies, waits for them, and re-layouts  6.52 us (5%)
    ppermute x15, starting transfers between devices, body(): every.append(lax.ppermute(weights, GROUP, route) if c or p else weights)  38.8 us
    all_to_all x1, blocking collectives, body(): result = lax.all_to_all(result, GROUP, 0, 0, tiled=True)  24.1 us
    ppermute x10, starting transfers between devices, turn(): lax.ppermute(x, axis, [(i, (i + offset) % count) for i in range(count)])  19.8 us
    ppermute x10, waiting for transfers between devices, turn(): lax.ppermute(x, axis, [(i, (i + offset) % count) for i in range(count)])  13.2 us
    all_to_all x1, starting transfers between devices, body(): pieces = lax.all_to_all(pieces, GROUP, 0, 0, tiled=True)  10.3 us
    pallas_call x2, Pallas kernels, partial_coeffs(): pl.pallas_call(partial_kernel, grid=(y_count,), in_specs=[SMEM, pl.BlockS...  8.09 us
    ppermute x3, starting transfers between devices, body(): lax.ppermute(part, 'zg', [(i, i ^ c) for i in range(groups)])  6.5 us
    unnamed x14, local copies, waits for them, and re-layouts  3.74 us
  transfers between devices with their start and end apart: 30, of which 8 were waited for; matrix products, arithmetic and copies ran while one was open for 2% of the time, Pallas kernels for 4%

profile of v2, /device:TPU:40, one launch (start us, length us, event | category | flops | bytes accessed | tf_op | source)
XLA Modules:
  0.0 134.2 jit_solution(1198830391780922315)
XLA Ops:
  0.1 1.1 copy-done
  1.2 0.9 copy-done.2
  2.2 0.7 copy-done.4
  2.9 4.4 %shard_map.65 = f32[4,8,96,128]{3,2,1,0:T(8,128)} custom-call(s32[3]{0:T(128)S(1)} %pad_add_fusion.4.place_ref, s32[1,2048]{1,0:T(1,128)S(1)} %bitcast.20, bf16[64,2048]{1,0:T(8,128)(2,1)S(1)} %copy-done.2, bf16[192,2048]{1,0:T(8,128)(2,1)S(1)} %bitcast.18), custom_call_target="tpu_custom_call" | custom-call | flops 2147483648 | bytes 3145728 | tf_op jit(solution)/shard_map/pallas_call | solution.py:52
  7.3 1.1 copy.12
  8.4 10.3 %all-to-all-start = ((bf16[16,64,512]{2,1,0:T(8,128)(2,1)}), bf16[16,64,512]{2,1,0:T(8,128)(2,1)S(1)}, u32[]{:S(2)}, u32[]{:S(2)}) async-start(bf16[16,64,512]{2,1,0:T(8,128)(2,1)} %bitcast.22), calls=%async_computation | async-start | bytes 2097152 | tf_op jit(solution)/shard_map/all_to_all | solution.py:167
  18.7 0.9 copy-done.3
  19.7 3.7 %shard_map.64.kept_ref = f32[4,8,96,128]{3,2,1,0:T(8,128)S(1)} custom-call(s32[3]{0:T(128)S(1)} %pad_add_fusion.2.place_ref, s32[1,2048]{1,0:T(1,128)S(1)} %bitcast.21, bf16[64,2048]{1,0:T(8,128)(2,1)S(1)} %copy-done.3, bf16[192,2048]{1,0:T(8,128)(2,1)S(1)} %bitcast.19), custom_call_target="tpu_custom_call" | custom-call | flops 2147483648 | bytes 3145728 | tf_op jit(solution)/shard_map/pallas_call | solution.py:52
  23.4 0.9 shard_map.66
  24.3 1.6 %collective-permute-start.4 = (bf16[8,96,128]{2,1,0:T(8,128)(2,1)}, bf16[8,96,128]{2,1,0:T(8,128)(2,1)S(1)}, u32[]{:S(2)}, u32[]{:S(2)}) collective-permute-start(bf16[8,96,128]{2,1,0:T(8,128)(2,1)} %get-tuple-element.18), channel_id=1, source_target_pairs={{0,8},{8,16},{16,24},{24,0},{1,9},{9,17},{17,25},{25,1},{2,10},{10... | collective-permute-start | bytes 589832 | tf_op jit(solution)/shard_map/ppermute | solution.py:153
  25.9 0.9 collective-permute-start.5
  26.8 2.4 %collective-permute-start.6 = (bf16[8,96,128]{2,1,0:T(8,128)(2,1)S(1)}, bf16[8,96,128]{2,1,0:T(8,128)(2,1)S(1)}, u32[]{:S(2)}, u32[]{:S(2)}) collective-permute-start(bf16[8,96,128]{2,1,0:T(8,128)(2,1)S(1)} %get-tuple-element.20), channel_id=1, source_target_pairs={{0,24},{8,0},{16,8},{24,16},{1,25},{9,1},{17,9},{25,17},{2,26},{10... | collective-permute-start | bytes 589832 | tf_op jit(solution)/shard_map/ppermute | solution.py:153
  29.2 3.0 %collective-permute-done.4.refs_1_ = bf16[8,96,128]{2,1,0:T(8,128)(2,1)S(1)} collective-permute-done((bf16[8,96,128]{2,1,0:T(8,128)(2,1)}, bf16[8,96,128]{2,1,0:T(8,128)(2,1)S(1)}, u32[]{:S(2)}, u32[]{:S(2)}) %collective-permute-start.4) | collective-permute-done | bytes 196640 | tf_op jit(solution)/shard_map/ppermute | solution.py:153
  32.3 2.9 %collective-permute-done.5.refs_2_ = bf16[8,96,128]{2,1,0:T(8,128)(2,1)S(1)} collective-permute-done((bf16[8,96,128]{2,1,0:T(8,128)(2,1)S(1)}, bf16[8,96,128]{2,1,0:T(8,128)(2,1)S(1)}, u32[]{:S(2)}, u32[]{:S(2)}) %collective-permute-start.5) | collective-permute-done | bytes 196640 | tf_op jit(solution)/shard_map/ppermute | solution.py:153
  35.2 2.4 %collective-permute-done.6.refs_3_ = bf16[8,96,128]{2,1,0:T(8,128)(2,1)S(1)} collective-permute-done((bf16[8,96,128]{2,1,0:T(8,128)(2,1)S(1)}, bf16[8,96,128]{2,1,0:T(8,128)(2,1)S(1)}, u32[]{:S(2)}, u32[]{:S(2)}) %collective-permute-start.6) | collective-permute-done | bytes 196640 | tf_op jit(solution)/shard_map/ppermute | solution.py:153
  37.7 5.6 %collective-permute-start.10 = (bf16[96,128]{1,0:T(8,128)(2,1)S(1)}, bf16[96,128]{1,0:T(8,128)(2,1)S(1)}, u32[]{:S(2)}, u32[]{:S(2)}) collective-permute-start(bf16[96,128]{1,0:T(8,128)(2,1)S(1)} %get-tuple-element.25), channel_id=1, source_target_pairs={{0,128},{32,160},{64,192},{96,224},{128,0},{160,32},{192,64},{224,... | collective-permute-start | bytes 73736 | tf_op jit(solution)/shard_map/ppermute | solution.py:153
  43.3 1.0 collective-permute-start.11
  44.7 3.3 %collective-permute-start.13 = (bf16[96,128]{1,0:T(8,128)(2,1)S(1)}, bf16[96,128]{1,0:T(8,128)(2,1)S(1)}, u32[]{:S(2)}, u32[]{:S(2)}) collective-permute-start(bf16[96,128]{1,0:T(8,128)(2,1)S(1)} %get-tuple-element.28), channel_id=1, source_target_pairs={{0,224},{32,0},{64,32},{96,64},{128,96},{160,128},{192,160},{224,1... | collective-permute-start | bytes 73736 | tf_op jit(solution)/shard_map/ppermute | solution.py:153
  48.0 0.7 constant_dynamic-slice_fusion
  49.4 0.9 collective-permute-done.10.refs_4_
  50.3 1.7 %collective-permute-start = (f32[2,512]{1,0:T(2,128)S(1)}, f32[2,512]{1,0:T(2,128)S(1)}, u32[]{:S(2)}, u32[]{:S(2)}) collective-permute-start(f32[2,512]{1,0:T(2,128)S(1)} %get-tuple-element.30), channel_id=1, source_target_pairs={{0,64},{64,0},{128,192},{192,128},{1,65},{65,1},{129,193},{193,129... | collective-permute-start | bytes 12296 | tf_op jit(solution)/shard_map/ppermute | solution.py:172
  52.0 3.6 %collective-permute-start.1 = (f32[2,512]{1,0:T(2,128)S(1)}, f32[2,512]{1,0:T(2,128)S(1)}, u32[]{:S(2)}, u32[]{:S(2)}) collective-permute-start(f32[2,512]{1,0:T(2,128)S(1)} %get-tuple-element.32), channel_id=1, source_target_pairs={{0,128},{64,192},{128,0},{192,64},{1,129},{65,193},{129,1},{193,65... | collective-permute-start | bytes 12296 | tf_op jit(solution)/shard_map/ppermute | solution.py:172
  55.5 1.2 collective-permute-start.2
  56.8 1.7 %collective-permute-start.8 = (bf16[96,128]{1,0:T(8,128)(2,1)S(1)}, bf16[96,128]{1,0:T(8,128)(2,1)S(1)}, u32[]{:S(2)}, u32[]{:S(2)}) collective-permute-start(bf16[96,128]{1,0:T(8,128)(2,1)S(1)} %get-tuple-element.23), channel_id=1, source_target_pairs={{0,64},{32,96},{64,128},{96,160},{128,192},{160,224},{192,0},{224,... | collective-permute-start | bytes 73736 | tf_op jit(solution)/shard_map/ppermute | solution.py:153
  58.5 2.8 %collective-permute-start.9 = (bf16[96,128]{1,0:T(8,128)(2,1)S(1)}, bf16[96,128]{1,0:T(8,128)(2,1)S(1)}, u32[]{:S(2)}, u32[]{:S(2)}) collective-permute-start(bf16[96,128]{1,0:T(8,128)(2,1)S(1)} %get-tuple-element.24), channel_id=1, source_target_pairs={{0,96},{32,128},{64,160},{96,192},{128,224},{160,0},{192,32},{224,... | collective-permute-start | bytes 73736 | tf_op jit(solution)/shard_map/ppermute | solution.py:153
  61.4 1.4 %collective-permute-done.8.refs_2_ = bf16[96,128]{1,0:T(8,128)(2,1)S(1)} collective-permute-done((bf16[96,128]{1,0:T(8,128)(2,1)S(1)}, bf16[96,128]{1,0:T(8,128)(2,1)S(1)}, u32[]{:S(2)}, u32[]{:S(2)}) %collective-permute-start.8) | collective-permute-done | bytes 24608 | tf_op jit(solution)/shard_map/ppermute | solution.py:153
  62.7 2.6 %collective-permute-done.9.refs_3_ = bf16[96,128]{1,0:T(8,128)(2,1)S(1)} collective-permute-done((bf16[96,128]{1,0:T(8,128)(2,1)S(1)}, bf16[96,128]{1,0:T(8,128)(2,1)S(1)}, u32[]{:S(2)}, u32[]{:S(2)}) %collective-permute-start.9) | collective-permute-done | bytes 24608 | tf_op jit(solution)/shard_map/ppermute | solution.py:153
  65.3 0.6 shard_map.68.refs_6_
  65.9 1.7 %collective-permute-start.14 = (bf16[96,128]{1,0:T(8,128)(2,1)S(1)}, bf16[96,128]{1,0:T(8,128)(2,1)S(1)}, u32[]{:S(2)}, u32[]{:S(2)}) collective-permute-start(bf16[96,128]{1,0:T(8,128)(2,1)S(1)} %shard_map.68.refs_6_), channel_id=1, source_target_pairs={{0,1},{1,2},{2,3},{3,0},{64,65},{65,66},{66,67},{67,64},{128,129},... | collective-permute-start | bytes 73736 | tf_op jit(solution)/shard_map/ppermute | solution.py:200
  67.6 2.7 %collective-permute-start.15 = (bf16[96,128]{1,0:T(8,128)(2,1)S(1)}, bf16[96,128]{1,0:T(8,128)(2,1)S(1)}, u32[]{:S(2)}, u32[]{:S(2)}) collective-permute-start(bf16[96,128]{1,0:T(8,128)(2,1)S(1)} %shard_map.68.refs_6_), channel_id=1, source_target_pairs={{0,2},{1,3},{2,0},{3,1},{64,66},{65,67},{66,64},{67,65},{128,130},... | collective-permute-start | bytes 73736 | tf_op jit(solution)/shard_map/ppermute | solution.py:200
  70.3 1.5 %collective-permute-start.16 = (bf16[96,128]{1,0:T(8,128)(2,1)S(1)}, bf16[96,128]{1,0:T(8,128)(2,1)S(1)}, u32[]{:S(2)}, u32[]{:S(2)}) collective-permute-start(bf16[96,128]{1,0:T(8,128)(2,1)S(1)} %shard_map.68.refs_6_), channel_id=1, source_target_pairs={{0,3},{1,0},{2,1},{3,2},{64,67},{65,64},{66,65},{67,66},{128,131},... | collective-permute-start | bytes 73736 | tf_op jit(solution)/shard_map/ppermute | solution.py:200
  71.8 1.1 collective-permute-start.17
  72.9 1.8 %collective-permute-start.18 = (bf16[96,128]{1,0:T(8,128)(2,1)S(1)}, bf16[96,128]{1,0:T(8,128)(2,1)S(1)}, u32[]{:S(2)}, u32[]{:S(2)}) collective-permute-start(bf16[96,128]{1,0:T(8,128)(2,1)S(1)} %shard_map.68.refs_6_), channel_id=1, source_target_pairs={{0,65},{1,66},{2,67},{3,64},{64,1},{65,2},{66,3},{67,0},{128,193},... | collective-permute-start | bytes 73736 | tf_op jit(solution)/shard_map/ppermute | solution.py:200
  74.7 1.6 %collective-permute-start.19 = (bf16[96,128]{1,0:T(8,128)(2,1)S(1)}, bf16[96,128]{1,0:T(8,128)(2,1)S(1)}, u32[]{:S(2)}, u32[]{:S(2)}) collective-permute-start(bf16[96,128]{1,0:T(8,128)(2,1)S(1)} %shard_map.68.refs_6_), channel_id=1, source_target_pairs={{0,66},{1,67},{2,64},{3,65},{64,2},{65,3},{66,0},{67,1},{128,194},... | collective-permute-start | bytes 73736 | tf_op jit(solution)/shard_map/ppermute | solution.py:200
  76.3 2.9 %collective-permute-start.20 = (bf16[96,128]{1,0:T(8,128)(2,1)S(1)}, bf16[96,128]{1,0:T(8,128)(2,1)S(1)}, u32[]{:S(2)}, u32[]{:S(2)}) collective-permute-start(bf16[96,128]{1,0:T(8,128)(2,1)S(1)} %shard_map.68.refs_6_), channel_id=1, source_target_pairs={{0,67},{1,64},{2,65},{3,66},{64,3},{65,0},{66,1},{67,2},{128,195},... | collective-permute-start | bytes 73736 | tf_op jit(solution)/shard_map/ppermute | solution.py:200
  79.1 3.8 %collective-permute-start.21 = (bf16[96,128]{1,0:T(8,128)(2,1)S(1)}, bf16[96,128]{1,0:T(8,128)(2,1)S(1)}, u32[]{:S(2)}, u32[]{:S(2)}) collective-permute-start(bf16[96,128]{1,0:T(8,128)(2,1)S(1)} %shard_map.68.refs_6_), channel_id=1, source_target_pairs={{0,128},{1,129},{2,130},{3,131},{64,192},{65,193},{66,194},{67,195... | collective-permute-start | bytes 73736 | tf_op jit(solution)/shard_map/ppermute | solution.py:200
  83.0 1.9 %collective-permute-start.22 = (bf16[96,128]{1,0:T(8,128)(2,1)S(1)}, bf16[96,128]{1,0:T(8,128)(2,1)S(1)}, u32[]{:S(2)}, u32[]{:S(2)}) collective-permute-start(bf16[96,128]{1,0:T(8,128)(2,1)S(1)} %shard_map.68.refs_6_), channel_id=1, source_target_pairs={{0,129},{1,130},{2,131},{3,128},{64,193},{65,194},{66,195},{67,192... | collective-permute-start | bytes 73736 | tf_op jit(solution)/shard_map/ppermute | solution.py:200
  84.9 5.8 %collective-permute-start.23 = (bf16[96,128]{1,0:T(8,128)(2,1)S(1)}, bf16[96,128]{1,0:T(8,128)(2,1)S(1)}, u32[]{:S(2)}, u32[]{:S(2)}) collective-permute-start(bf16[96,128]{1,0:T(8,128)(2,1)S(1)} %shard_map.68.refs_6_), channel_id=1, source_target_pairs={{0,130},{1,131},{2,128},{3,129},{64,194},{65,195},{66,192},{67,193... | collective-permute-start | bytes 73736 | tf_op jit(solution)/shard_map/ppermute | solution.py:200
  90.7 4.2 %collective-permute-start.24 = (bf16[96,128]{1,0:T(8,128)(2,1)S(1)}, bf16[96,128]{1,0:T(8,128)(2,1)S(1)}, u32[]{:S(2)}, u32[]{:S(2)}) collective-permute-start(bf16[96,128]{1,0:T(8,128)(2,1)S(1)} %shard_map.68.refs_6_), channel_id=1, source_target_pairs={{0,131},{1,128},{2,129},{3,130},{64,195},{65,192},{66,193},{67,194... | collective-permute-start | bytes 73736 | tf_op jit(solution)/shard_map/ppermute | solution.py:200
  94.9 1.6 %collective-permute-start.25 = (bf16[96,128]{1,0:T(8,128)(2,1)S(1)}, bf16[96,128]{1,0:T(8,128)(2,1)S(1)}, u32[]{:S(2)}, u32[]{:S(2)}) collective-permute-start(bf16[96,128]{1,0:T(8,128)(2,1)S(1)} %shard_map.68.refs_6_), channel_id=1, source_target_pairs={{0,192},{1,193},{2,194},{3,195},{64,128},{65,129},{66,130},{67,131... | collective-permute-start | bytes 73736 | tf_op jit(solution)/shard_map/ppermute | solution.py:200
  96.5 1.4 %collective-permute-start.26 = (bf16[96,128]{1,0:T(8,128)(2,1)S(1)}, bf16[96,128]{1,0:T(8,128)(2,1)S(1)}, u32[]{:S(2)}, u32[]{:S(2)}) collective-permute-start(bf16[96,128]{1,0:T(8,128)(2,1)S(1)} %shard_map.68.refs_6_), channel_id=1, source_target_pairs={{0,193},{1,194},{2,195},{3,192},{64,129},{65,130},{66,131},{67,128... | collective-permute-start | bytes 73736 | tf_op jit(solution)/shard_map/ppermute | solution.py:200
  97.9 3.1 %collective-permute-start.27 = (bf16[96,128]{1,0:T(8,128)(2,1)S(1)}, bf16[96,128]{1,0:T(8,128)(2,1)S(1)}, u32[]{:S(2)}, u32[]{:S(2)}) collective-permute-start(bf16[96,128]{1,0:T(8,128)(2,1)S(1)} %shard_map.68.refs_6_), channel_id=1, source_target_pairs={{0,194},{1,195},{2,192},{3,193},{64,130},{65,131},{66,128},{67,129... | collective-permute-start | bytes 73736 | tf_op jit(solution)/shard_map/ppermute | solution.py:200
  100.9 3.8 %collective-permute-start.28 = (bf16[96,128]{1,0:T(8,128)(2,1)S(1)}, bf16[96,128]{1,0:T(8,128)(2,1)S(1)}, u32[]{:S(2)}, u32[]{:S(2)}) collective-permute-start(bf16[96,128]{1,0:T(8,128)(2,1)S(1)} %shard_map.68.refs_6_), channel_id=1, source_target_pairs={{0,195},{1,192},{2,193},{3,194},{64,131},{65,128},{66,129},{67,130... | collective-permute-start | bytes 73736 | tf_op jit(solution)/shard_map/ppermute | solution.py:200
  104.8 1.4 %collective-permute-done.27.refs_20_ = bf16[96,128]{1,0:T(8,128)(2,1)S(1)} collective-permute-done((bf16[96,128]{1,0:T(8,128)(2,1)S(1)}, bf16[96,128]{1,0:T(8,128)(2,1)S(1)}, u32[]{:S(2)}, u32[]{:S(2)}) %collective-permute-start.27) | collective-permute-done | bytes 24608 | tf_op jit(solution)/shard_map/ppermute | solution.py:200
  106.2 1.6 %collective-permute-done.28.refs_21_ = bf16[96,128]{1,0:T(8,128)(2,1)S(1)} collective-permute-done((bf16[96,128]{1,0:T(8,128)(2,1)S(1)}, bf16[96,128]{1,0:T(8,128)(2,1)S(1)}, u32[]{:S(2)}, u32[]{:S(2)}) %collective-permute-start.28) | collective-permute-done | bytes 24608 | tf_op jit(solution)/shard_map/ppermute | solution.py:200
  107.8 1.3 shard_map.69
  109.1 24.1 %all_to_all.10 = bf16[16,48,512]{2,1,0:T(8,128)(2,1)S(1)} all-to-all(bf16[16,48,512]{2,1,0:T(8,128)(2,1)S(1)} %shard_map.69), channel_id=1, replica_groups=mesh['zg'=4,'zl'=2,'y'=4,'core'=2,'smp'=4] {'zg','smp'}, dimensions={0} | all-to-all | bytes 1572864 | tf_op jit(solution)/shard_map/all_to_all | solution.py:213
  133.2 1.0 copy.10
  (40 shorter events, 0.8 us)
Async XLA Ops:
  0.1 1.1 copy-start
  1.2 0.9 copy-start.2
  2.2 0.7 copy-start.4
  2.9 4.4 %copy-start.6 = (bf16[64,8192]{1,0:T(8,128)(2,1)S(1)}, bf16[64,8192]{1,0:T(8,128)(2,1)}, u32[]{:S(2)}) copy-start(bf16[64,8192]{1,0:T(8,128)(2,1)} %param.6) | copy-start | bytes 3145732
  7.3 16.1 %collective-permute-start.3 = (f32[4,8,96,128]{3,2,1,0:T(8,128)}, f32[4,8,96,128]{3,2,1,0:T(8,128)S(1)}, u32[]{:S(2)}, u32[]{:S(2)}) collective-permute-start(f32[4,8,96,128]{3,2,1,0:T(8,128)} %shard_map.65), channel_id=1, source_target_pairs={{0,4},{4,0},{1,5},{5,1},{2,6},{6,2},{3,7},{7,3},{8,12},{12,8},{9,1... | collective-permute-start | bytes 4718600 | tf_op jit(solution)/shard_map/ppermute | solution.py:176
  8.4 10.4 %copy-start.1 = (bf16[2048,192]{0,1:T(8,128)(2,1)S(1)}, bf16[2048,192]{0,1:T(8,128)(2,1)}, u32[]{:S(2)}) copy-start(bf16[2048,192]{0,1:T(8,128)(2,1)} %param.8) | copy-start | bytes 2359300
  8.4 10.4 %copy-start.5 = (s32[2048,1]{0,1:T(1,128)S(1)}, s32[2048,1]{0,1:T(1,128)}, u32[]{:S(2)}) copy-start(s32[2048,1]{0,1:T(1,128)} %param.9) | copy-start | bytes 24580
  8.4 99.4 %all-to-all-start = ((bf16[16,64,512]{2,1,0:T(8,128)(2,1)}), bf16[16,64,512]{2,1,0:T(8,128)(2,1)S(1)}, u32[]{:S(2)}, u32[]{:S(2)}) async-start(bf16[16,64,512]{2,1,0:T(8,128)(2,1)} %bitcast.22), calls=%async_computation | async-start | bytes 2097152 | tf_op jit(solution)/shard_map/all_to_all | solution.py:167
  18.7 1.0 copy-start.3
  24.3 7.9 %collective-permute-start.4 = (bf16[8,96,128]{2,1,0:T(8,128)(2,1)}, bf16[8,96,128]{2,1,0:T(8,128)(2,1)S(1)}, u32[]{:S(2)}, u32[]{:S(2)}) collective-permute-start(bf16[8,96,128]{2,1,0:T(8,128)(2,1)} %get-tuple-element.18), channel_id=1, source_target_pairs={{0,8},{8,16},{16,24},{24,0},{1,9},{9,17},{17,25},{25,1},{2,10},{10... | collective-permute-start | bytes 589832 | tf_op jit(solution)/shard_map/ppermute | solution.py:153
  25.9 9.3 %collective-permute-start.5 = (bf16[8,96,128]{2,1,0:T(8,128)(2,1)S(1)}, bf16[8,96,128]{2,1,0:T(8,128)(2,1)S(1)}, u32[]{:S(2)}, u32[]{:S(2)}) collective-permute-start(bf16[8,96,128]{2,1,0:T(8,128)(2,1)S(1)} %get-tuple-element.19), channel_id=1, source_target_pairs={{0,16},{8,24},{16,0},{24,8},{1,17},{9,25},{17,1},{25,9},{2,18},{10... | collective-permute-start | bytes 589832 | tf_op jit(solution)/shard_map/ppermute | solution.py:153
  26.8 10.8 %collective-permute-start.6 = (bf16[8,96,128]{2,1,0:T(8,128)(2,1)S(1)}, bf16[8,96,128]{2,1,0:T(8,128)(2,1)S(1)}, u32[]{:S(2)}, u32[]{:S(2)}) collective-permute-start(bf16[8,96,128]{2,1,0:T(8,128)(2,1)S(1)} %get-tuple-element.20), channel_id=1, source_target_pairs={{0,24},{8,0},{16,8},{24,16},{1,25},{9,1},{17,9},{25,17},{2,26},{10... | collective-permute-start | bytes 589832 | tf_op jit(solution)/shard_map/ppermute | solution.py:153
  37.7 12.6 %collective-permute-start.10 = (bf16[96,128]{1,0:T(8,128)(2,1)S(1)}, bf16[96,128]{1,0:T(8,128)(2,1)S(1)}, u32[]{:S(2)}, u32[]{:S(2)}) collective-permute-start(bf16[96,128]{1,0:T(8,128)(2,1)S(1)} %get-tuple-element.25), channel_id=1, source_target_pairs={{0,128},{32,160},{64,192},{96,224},{128,0},{160,32},{192,64},{224,... | collective-permute-start | bytes 73736 | tf_op jit(solution)/shard_map/ppermute | solution.py:153
  43.3 8.7 %collective-permute-start.11 = (bf16[96,128]{1,0:T(8,128)(2,1)S(1)}, bf16[96,128]{1,0:T(8,128)(2,1)S(1)}, u32[]{:S(2)}, u32[]{:S(2)}) collective-permute-start(bf16[96,128]{1,0:T(8,128)(2,1)S(1)} %get-tuple-element.26), channel_id=1, source_target_pairs={{0,160},{32,192},{64,224},{96,0},{128,32},{160,64},{192,96},{224,1... | collective-permute-start | bytes 73736 | tf_op jit(solution)/shard_map/ppermute | solution.py:153
  44.3 11.2 %collective-permute-start.12 = (bf16[96,128]{1,0:T(8,128)(2,1)S(1)}, bf16[96,128]{1,0:T(8,128)(2,1)S(1)}, u32[]{:S(2)}, u32[]{:S(2)}) collective-permute-start(bf16[96,128]{1,0:T(8,128)(2,1)S(1)} %get-tuple-element.27), channel_id=1, source_target_pairs={{0,192},{32,224},{64,0},{96,32},{128,64},{160,96},{192,128},{224,1... | collective-permute-start | bytes 73736 | tf_op jit(solution)/shard_map/ppermute | solution.py:153
  44.7 12.1 %collective-permute-start.13 = (bf16[96,128]{1,0:T(8,128)(2,1)S(1)}, bf16[96,128]{1,0:T(8,128)(2,1)S(1)}, u32[]{:S(2)}, u32[]{:S(2)}) collective-permute-start(bf16[96,128]{1,0:T(8,128)(2,1)S(1)} %get-tuple-element.28), channel_id=1, source_target_pairs={{0,224},{32,0},{64,32},{96,64},{128,96},{160,128},{192,160},{224,1... | collective-permute-start | bytes 73736 | tf_op jit(solution)/shard_map/ppermute | solution.py:153
  48.0 10.5 %collective-permute-start.7 = (bf16[96,128]{1,0:T(8,128)(2,1)S(1)}, bf16[96,128]{1,0:T(8,128)(2,1)S(1)}, u32[]{:S(2)}, u32[]{:S(2)}) collective-permute-start(bf16[96,128]{1,0:T(8,128)(2,1)S(1)} %get-tuple-element.22), channel_id=1, source_target_pairs={{0,32},{32,64},{64,96},{96,128},{128,160},{160,192},{192,224},{224... | collective-permute-start | bytes 73736 | tf_op jit(solution)/shard_map/ppermute | solution.py:153
  50.3 20.0 %collective-permute-start = (f32[2,512]{1,0:T(2,128)S(1)}, f32[2,512]{1,0:T(2,128)S(1)}, u32[]{:S(2)}, u32[]{:S(2)}) collective-permute-start(f32[2,512]{1,0:T(2,128)S(1)} %get-tuple-element.30), channel_id=1, source_target_pairs={{0,64},{64,0},{128,192},{192,128},{1,65},{65,1},{129,193},{193,129... | collective-permute-start | bytes 12296 | tf_op jit(solution)/shard_map/ppermute | solution.py:172
  52.0 19.8 %collective-permute-start.1 = (f32[2,512]{1,0:T(2,128)S(1)}, f32[2,512]{1,0:T(2,128)S(1)}, u32[]{:S(2)}, u32[]{:S(2)}) collective-permute-start(f32[2,512]{1,0:T(2,128)S(1)} %get-tuple-element.32), channel_id=1, source_target_pairs={{0,128},{64,192},{128,0},{192,64},{1,129},{65,193},{129,1},{193,65... | collective-permute-start | bytes 12296 | tf_op jit(solution)/shard_map/ppermute | solution.py:172
  55.5 17.4 %collective-permute-start.2 = (f32[2,512]{1,0:T(2,128)S(1)}, f32[2,512]{1,0:T(2,128)S(1)}, u32[]{:S(2)}, u32[]{:S(2)}) collective-permute-start(f32[2,512]{1,0:T(2,128)S(1)} %get-tuple-element.29), channel_id=1, source_target_pairs={{0,192},{64,128},{128,64},{192,0},{1,193},{65,129},{129,65},{193,1... | collective-permute-start | bytes 12296 | tf_op jit(solution)/shard_map/ppermute | solution.py:172
  56.8 5.9 %collective-permute-start.8 = (bf16[96,128]{1,0:T(8,128)(2,1)S(1)}, bf16[96,128]{1,0:T(8,128)(2,1)S(1)}, u32[]{:S(2)}, u32[]{:S(2)}) collective-permute-start(bf16[96,128]{1,0:T(8,128)(2,1)S(1)} %get-tuple-element.23), channel_id=1, source_target_pairs={{0,64},{32,96},{64,128},{96,160},{128,192},{160,224},{192,0},{224,... | collective-permute-start | bytes 73736 | tf_op jit(solution)/shard_map/ppermute | solution.py:153
  58.5 6.8 %collective-permute-start.9 = (bf16[96,128]{1,0:T(8,128)(2,1)S(1)}, bf16[96,128]{1,0:T(8,128)(2,1)S(1)}, u32[]{:S(2)}, u32[]{:S(2)}) collective-permute-start(bf16[96,128]{1,0:T(8,128)(2,1)S(1)} %get-tuple-element.24), channel_id=1, source_target_pairs={{0,96},{32,128},{64,160},{96,192},{128,224},{160,0},{192,32},{224,... | collective-permute-start | bytes 73736 | tf_op jit(solution)/shard_map/ppermute | solution.py:153
  65.9 8.8 %collective-permute-start.14 = (bf16[96,128]{1,0:T(8,128)(2,1)S(1)}, bf16[96,128]{1,0:T(8,128)(2,1)S(1)}, u32[]{:S(2)}, u32[]{:S(2)}) collective-permute-start(bf16[96,128]{1,0:T(8,128)(2,1)S(1)} %shard_map.68.refs_6_), channel_id=1, source_target_pairs={{0,1},{1,2},{2,3},{3,0},{64,65},{65,66},{66,67},{67,64},{128,129},... | collective-permute-start | bytes 73736 | tf_op jit(solution)/shard_map/ppermute | solution.py:200
  67.6 8.7 %collective-permute-start.15 = (bf16[96,128]{1,0:T(8,128)(2,1)S(1)}, bf16[96,128]{1,0:T(8,128)(2,1)S(1)}, u32[]{:S(2)}, u32[]{:S(2)}) collective-permute-start(bf16[96,128]{1,0:T(8,128)(2,1)S(1)} %shard_map.68.refs_6_), channel_id=1, source_target_pairs={{0,2},{1,3},{2,0},{3,1},{64,66},{65,67},{66,64},{67,65},{128,130},... | collective-permute-start | bytes 73736 | tf_op jit(solution)/shard_map/ppermute | solution.py:200
  70.3 8.8 %collective-permute-start.16 = (bf16[96,128]{1,0:T(8,128)(2,1)S(1)}, bf16[96,128]{1,0:T(8,128)(2,1)S(1)}, u32[]{:S(2)}, u32[]{:S(2)}) collective-permute-start(bf16[96,128]{1,0:T(8,128)(2,1)S(1)} %shard_map.68.refs_6_), channel_id=1, source_target_pairs={{0,3},{1,0},{2,1},{3,2},{64,67},{65,64},{66,65},{67,66},{128,131},... | collective-permute-start | bytes 73736 | tf_op jit(solution)/shard_map/ppermute | solution.py:200
  71.8 11.2 %collective-permute-start.17 = (bf16[96,128]{1,0:T(8,128)(2,1)S(1)}, bf16[96,128]{1,0:T(8,128)(2,1)S(1)}, u32[]{:S(2)}, u32[]{:S(2)}) collective-permute-start(bf16[96,128]{1,0:T(8,128)(2,1)S(1)} %shard_map.68.refs_6_), channel_id=1, source_target_pairs={{0,64},{1,65},{2,66},{3,67},{64,0},{65,1},{66,2},{67,3},{128,192},... | collective-permute-start | bytes 73736 | tf_op jit(solution)/shard_map/ppermute | solution.py:200
  72.9 12.0 %collective-permute-start.18 = (bf16[96,128]{1,0:T(8,128)(2,1)S(1)}, bf16[96,128]{1,0:T(8,128)(2,1)S(1)}, u32[]{:S(2)}, u32[]{:S(2)}) collective-permute-start(bf16[96,128]{1,0:T(8,128)(2,1)S(1)} %shard_map.68.refs_6_), channel_id=1, source_target_pairs={{0,65},{1,66},{2,67},{3,64},{64,1},{65,2},{66,3},{67,0},{128,193},... | collective-permute-start | bytes 73736 | tf_op jit(solution)/shard_map/ppermute | solution.py:200
  74.7 16.0 %collective-permute-start.19 = (bf16[96,128]{1,0:T(8,128)(2,1)S(1)}, bf16[96,128]{1,0:T(8,128)(2,1)S(1)}, u32[]{:S(2)}, u32[]{:S(2)}) collective-permute-start(bf16[96,128]{1,0:T(8,128)(2,1)S(1)} %shard_map.68.refs_6_), channel_id=1, source_target_pairs={{0,66},{1,67},{2,64},{3,65},{64,2},{65,3},{66,0},{67,1},{128,194},... | collective-permute-start | bytes 73736 | tf_op jit(solution)/shard_map/ppermute | solution.py:200
  76.3 18.7 %collective-permute-start.20 = (bf16[96,128]{1,0:T(8,128)(2,1)S(1)}, bf16[96,128]{1,0:T(8,128)(2,1)S(1)}, u32[]{:S(2)}, u32[]{:S(2)}) collective-permute-start(bf16[96,128]{1,0:T(8,128)(2,1)S(1)} %shard_map.68.refs_6_), channel_id=1, source_target_pairs={{0,67},{1,64},{2,65},{3,66},{64,3},{65,0},{66,1},{67,2},{128,195},... | collective-permute-start | bytes 73736 | tf_op jit(solution)/shard_map/ppermute | solution.py:200
  79.1 17.4 %collective-permute-start.21 = (bf16[96,128]{1,0:T(8,128)(2,1)S(1)}, bf16[96,128]{1,0:T(8,128)(2,1)S(1)}, u32[]{:S(2)}, u32[]{:S(2)}) collective-permute-start(bf16[96,128]{1,0:T(8,128)(2,1)S(1)} %shard_map.68.refs_6_), channel_id=1, source_target_pairs={{0,128},{1,129},{2,130},{3,131},{64,192},{65,193},{66,194},{67,195... | collective-permute-start | bytes 73736 | tf_op jit(solution)/shard_map/ppermute | solution.py:200
  83.0 14.9 %collective-permute-start.22 = (bf16[96,128]{1,0:T(8,128)(2,1)S(1)}, bf16[96,128]{1,0:T(8,128)(2,1)S(1)}, u32[]{:S(2)}, u32[]{:S(2)}) collective-permute-start(bf16[96,128]{1,0:T(8,128)(2,1)S(1)} %shard_map.68.refs_6_), channel_id=1, source_target_pairs={{0,129},{1,130},{2,131},{3,128},{64,193},{65,194},{66,195},{67,192... | collective-permute-start | bytes 73736 | tf_op jit(solution)/shard_map/ppermute | solution.py:200
  84.9 16.0 %collective-permute-start.23 = (bf16[96,128]{1,0:T(8,128)(2,1)S(1)}, bf16[96,128]{1,0:T(8,128)(2,1)S(1)}, u32[]{:S(2)}, u32[]{:S(2)}) collective-permute-start(bf16[96,128]{1,0:T(8,128)(2,1)S(1)} %shard_map.68.refs_6_), channel_id=1, source_target_pairs={{0,130},{1,131},{2,128},{3,129},{64,194},{65,195},{66,192},{67,193... | collective-permute-start | bytes 73736 | tf_op jit(solution)/shard_map/ppermute | solution.py:200
  90.7 14.1 %collective-permute-start.24 = (bf16[96,128]{1,0:T(8,128)(2,1)S(1)}, bf16[96,128]{1,0:T(8,128)(2,1)S(1)}, u32[]{:S(2)}, u32[]{:S(2)}) collective-permute-start(bf16[96,128]{1,0:T(8,128)(2,1)S(1)} %shard_map.68.refs_6_), channel_id=1, source_target_pairs={{0,131},{1,128},{2,129},{3,130},{64,195},{65,192},{66,193},{67,194... | collective-permute-start | bytes 73736 | tf_op jit(solution)/shard_map/ppermute | solution.py:200
  94.9 9.9 %collective-permute-start.25 = (bf16[96,128]{1,0:T(8,128)(2,1)S(1)}, bf16[96,128]{1,0:T(8,128)(2,1)S(1)}, u32[]{:S(2)}, u32[]{:S(2)}) collective-permute-start(bf16[96,128]{1,0:T(8,128)(2,1)S(1)} %shard_map.68.refs_6_), channel_id=1, source_target_pairs={{0,192},{1,193},{2,194},{3,195},{64,128},{65,129},{66,130},{67,131... | collective-permute-start | bytes 73736 | tf_op jit(solution)/shard_map/ppermute | solution.py:200
  96.5 8.3 %collective-permute-start.26 = (bf16[96,128]{1,0:T(8,128)(2,1)S(1)}, bf16[96,128]{1,0:T(8,128)(2,1)S(1)}, u32[]{:S(2)}, u32[]{:S(2)}) collective-permute-start(bf16[96,128]{1,0:T(8,128)(2,1)S(1)} %shard_map.68.refs_6_), channel_id=1, source_target_pairs={{0,193},{1,194},{2,195},{3,192},{64,129},{65,130},{66,131},{67,128... | collective-permute-start | bytes 73736 | tf_op jit(solution)/shard_map/ppermute | solution.py:200
  97.9 8.3 %collective-permute-start.27 = (bf16[96,128]{1,0:T(8,128)(2,1)S(1)}, bf16[96,128]{1,0:T(8,128)(2,1)S(1)}, u32[]{:S(2)}, u32[]{:S(2)}) collective-permute-start(bf16[96,128]{1,0:T(8,128)(2,1)S(1)} %shard_map.68.refs_6_), channel_id=1, source_target_pairs={{0,194},{1,195},{2,192},{3,193},{64,130},{65,131},{66,128},{67,129... | collective-permute-start | bytes 73736 | tf_op jit(solution)/shard_map/ppermute | solution.py:200
  100.9 6.8 %collective-permute-start.28 = (bf16[96,128]{1,0:T(8,128)(2,1)S(1)}, bf16[96,128]{1,0:T(8,128)(2,1)S(1)}, u32[]{:S(2)}, u32[]{:S(2)}) collective-permute-start(bf16[96,128]{1,0:T(8,128)(2,1)S(1)} %shard_map.68.refs_6_), channel_id=1, source_target_pairs={{0,195},{1,192},{2,193},{3,194},{64,131},{65,128},{66,129},{67,130... | collective-permute-start | bytes 73736 | tf_op jit(solution)/shard_map/ppermute | solution.py:200

commit v3 on v2

--- a/solution.py
+++ b/solution.py
@@ -27,10 +27,9 @@
 
     own = owners_ref[...]
     adjoint = adjoint_ref[...]
-    y = lax.rem(place_ref[1] + step, y_count)
+    y = lax.rem(place_ref[0] + step, y_count)
     for offset in range(z_count):
-        z = lax.rem(place_ref[0] + offset, z_count)
-        owner = (z * y_count + y) * 2 + place_ref[2]
+        owner = (offset * y_count + y) * 2 + place_ref[1]
         hot = jnp.where(own == owner, 1.0, 0.0).astype(jnp.bfloat16)
         masked[offset * samples:(offset + 1) * samples, :] = adjoint * hot
     product = lax.dot_general(
@@ -91,42 +90,54 @@
         out_ref[...] = (kept_ref[offset] + came_ref[offset]).astype(out_ref.dtype)
 
 
-def spread_kernel(count, *refs):
-    total = refs[0][...]
-    for ref in refs[1:count]:
-        total = total + ref[...].astype(jnp.float32)
-    for offset, out_ref in enumerate(refs[count:]):
-        out_ref[...] = total[offset].astype(out_ref.dtype)
-
-
-def weights_kernel(place_ref, *refs):
+def gather_kernel(*refs):
     total = refs[0][...]
     for ref in refs[1:-1]:
         total = total + ref[...].astype(jnp.float32)
-    samples = total.shape[0] * 2 // 3
+    refs[-1][...] = total.astype(refs[-1].dtype)
+
+
+def weights_kernel(place_ref, sums_ref, twiddle_ref, out_ref):
+    members, rows, lanes = out_ref.shape
+    levels, points = twiddle_ref.shape
+    packed = sums_ref.shape[1]
+    samples = packed * 2 // 3
+    total = jnp.sum(sums_ref[...].astype(jnp.float32), axis=0)
     row = lax.broadcasted_iota(jnp.int32, total.shape, 0)
     lane = lax.broadcasted_iota(jnp.int32, total.shape, 1)
     tail = row - samples + jnp.where(lane < 64, 0, samples // 2)
     sample = place_ref[0] * samples + jnp.where(row < samples, row, tail)
-    refs[-1][...] = jnp.where(sample < place_ref[1], total, 0.0).astype(jnp.bfloat16)
-
-
-def field_kernel(blocks, parts, place_ref, samples_ref, *refs):
-    twiddle_refs, weight_refs = refs[:blocks], refs[blocks:-2]
-    out_ref, field = refs[-2:]
-    zg, smp = place_ref[0], place_ref[1]
-    samples, points = samples_ref.shape[1:]
-    vectors = field.shape[1]
+    weights = jnp.where(sample < place_ref[1], total, 0.0).astype(jnp.bfloat16)
+    for member in range(members):
+        out_ref[member, :packed, :] = weights
+        start = pl.multiple_of(member * (points // members) + place_ref[0] * lanes, lanes)
+        left = twiddle_ref[:, pl.ds(start, lanes)]
+        terms = []
+        for _ in range(3):
+            term = left.astype(jnp.bfloat16).astype(jnp.float32)
+            left = left - term
+            terms.append(term)
+        terms.append(jnp.zeros((rows - packed - 3 * levels, lanes), jnp.float32))
+        out_ref[member, packed:, :] = jnp.concatenate(terms, axis=0).astype(jnp.bfloat16)
+
+
+def field_kernel(samples_ref, weights_ref, out_ref, field):
+    blocks, vectors, points = field.shape
+    parts = samples_ref.shape[0] // blocks
+    samples = samples_ref.shape[1]
+    packed = samples * vectors // 128
+    factors = []
     for c in range(blocks):
-        block = zg ^ c
-        grid, head, tail = [], [], []
+        head, tail, columns = [], [], []
         for p in range(parts):
-            grid.append(samples_ref[block * parts + lax.rem(smp - p + parts, parts)])
-            weights = weight_refs[c * parts + p]
-            head.append(weights[:samples, :])
-            rest = weights[samples:, :]
+            piece = c * parts + p
+            head.append(weights_ref[piece, :samples, :])
+            rest = weights_ref[piece, samples:packed, :]
             tail += [rest[:, :64], rest[:, 64:]]
-        grid = jnp.concatenate(grid, axis=0)
+            terms = weights_ref[piece, packed:, :].astype(jnp.float32)
+            columns.append(terms[0:2] + terms[2:4] + terms[4:6])
+        factors.append(jnp.concatenate(columns, axis=1))
+        grid = samples_ref[c * parts:(c + 1) * parts].reshape(parts * samples, points)
         head = jnp.concatenate(head, axis=0)
         tail = jnp.concatenate(tail, axis=0)
         field[c, :128, :] = lax.dot_general(
@@ -141,11 +152,11 @@
         level = [field[c, rows, :] for c in range(blocks)]
         for index, distance in enumerate((2, 1)):
             level = [
-                level[c] + twiddle_refs[c][index:index + 1, :] * level[c ^ distance]
+                level[c] + factors[c][index:index + 1, :] * level[c ^ distance]
                 for c in range(blocks)
             ]
         for c in range(blocks):
-            out_ref[(zg ^ c) * parts + p] = level[c].astype(jnp.bfloat16)
+            out_ref[c * parts + p] = level[c].astype(jnp.bfloat16)
 
 
 def turn(x, axis, offset):
@@ -155,58 +166,44 @@
 
 def body(forward_samples, adjoint_samples, probe_values, owners, block_ranks, twiddle):
     groups, parts = lax.axis_size("zg"), lax.axis_size("smp")
-    y_count, z_count = lax.axis_size("y"), lax.axis_size(Z_AXES)
+    y_count = lax.axis_size("y")
     samples, points = forward_samples.shape
     vectors = probe_values.shape[1]
     members = groups * parts
     piece = points // members
-    zg, smp = lax.axis_index("zg"), lax.axis_index("smp")
-    z, y, core = lax.axis_index(Z_AXES), lax.axis_index("y"), lax.axis_index("core")
+    smp = lax.axis_index("smp")
+    y, core = lax.axis_index("y"), lax.axis_index("core")
 
     pieces = forward_samples.reshape(samples, members, piece).transpose(1, 0, 2)
+    own, probes = owners.T, probe_values.T
+    pieces, own = lax.optimization_barrier((pieces, own))
     pieces = lax.all_to_all(pieces, GROUP, 0, 0, tiled=True)
-    factors = []
-    for c in range(groups):
-        start = ((zg ^ c) * parts + smp) * piece
-        part = lax.dynamic_slice_in_dim(twiddle, start, piece, 1)
-        factors.append(lax.ppermute(part, "zg", [(i, i ^ c) for i in range(groups)]) if c else part)
-
-    own, probes = owners.T, probe_values.T
-    sent = partial_coeffs(jnp.stack([z, y, 1 - core]), own, adjoint_samples, probes)
+
+    sent = partial_coeffs(jnp.stack([y, 1 - core]), own, adjoint_samples, probes)
     came = lax.ppermute(sent, "core", [(0, 1), (1, 0)])
-    kept = partial_coeffs(jnp.stack([z, y, core]), own, adjoint_samples, probes)
-    packed = kept.shape[2:]
-    shapes = [jax.ShapeDtypeStruct((z_count,) + packed, jnp.float32)]
-    shapes += [jax.ShapeDtypeStruct((z_count,) + packed, jnp.bfloat16)] * (y_count - 1)
+    kept = partial_coeffs(jnp.stack([y, core]), own, adjoint_samples, probes)
+    shape = kept.shape[1:]
+    shapes = [jax.ShapeDtypeStruct(shape, jnp.float32)]
+    shapes += [jax.ShapeDtypeStruct(shape, jnp.bfloat16)] * (y_count - 1)
     sums = local_call(merge_kernel, shapes, kept, came)
     sums = [sums[0]] + [turn(sums[i], "y", i) for i in range(1, y_count)]
-    shapes = [jax.ShapeDtypeStruct(packed, jnp.float32)]
-    shapes += [jax.ShapeDtypeStruct(packed, jnp.bfloat16)] * (z_count - 1)
-    sums = local_call(lambda *refs: spread_kernel(y_count, *refs), shapes, *sums)
-    sums = [sums[0]] + [turn(sums[i], Z_AXES, i) for i in range(1, z_count)]
+    sums = local_call(gather_kernel, jax.ShapeDtypeStruct(shape, jnp.bfloat16), *sums)
+    sums, pieces = lax.optimization_barrier((sums, pieces))
+    sums = lax.all_to_all(sums, Z_AXES, 0, 0, tiled=True)
     weights = local_call(
         weights_kernel,
-        jax.ShapeDtypeStruct(packed, jnp.bfloat16),
+        jax.ShapeDtypeStruct((members, shape[1] + 16, shape[2]), jnp.bfloat16),
         jnp.stack([smp, block_ranks[0]]),
-        *sums,
+        sums,
+        twiddle,
         smem=1,
     )
-    every = []
-    for c in range(groups):
-        for p in range(parts):
-            route = [
-                (i, (i // parts ^ c) * parts + (i + p) % parts) for i in range(members)
-            ]
-            every.append(lax.ppermute(weights, GROUP, route) if c or p else weights)
-
+    weights = lax.all_to_all(weights, GROUP, 0, 0, tiled=True)
     result = local_call(
-        lambda *refs: field_kernel(groups, parts, *refs),
+        field_kernel,
         jax.ShapeDtypeStruct((members, vectors // parts, piece), jnp.bfloat16),
-        jnp.stack([zg, smp]),
         pieces,
-        *factors,
-        *every,
-        smem=1,
+        weights,
         scratch=[pltpu.VMEM((groups, vectors, piece), jnp.float32)],
         flops=2 * members * samples * vectors * piece,
     )

time: 135 us -> 102 us (0.76)
  starting transfers between devices: 75.3 us -> 19.8 us
  blocking collectives: 24.1 us -> 44.3 us
  waiting for transfers between devices: 16.2 us -> 23 us
  local copies, waits for them, and re-layouts: 6.52 us -> 3.28 us
    ppermute x18 -> x0, starting transfers between devices: 45.3 us -> none  [the longest x15 38.8 us: body(): every.append(lax.ppermute(weights, GROUP, route) if c or p else weights)]
    all_to_all x0 -> x1, blocking collectives: none -> 18.6 us  [body(): weights = lax.all_to_all(weights, GROUP, 0, 0, tiled=True)]
    ppermute x10 -> x3, starting transfers between devices: 19.8 us -> 5 us  [turn(): lax.ppermute(x, axis, [(i, (i + offset) % count) for i in range(count)])]
    all_to_all x0 -> x1, waiting for transfers between devices: none -> 7.56 us  [body(): sums = lax.all_to_all(sums, Z_AXES, 0, 0, tiled=True)]
    all_to_all x1, waiting for transfers between devices: 0.01 us -> 6.76 us  [body(): pieces = lax.all_to_all(pieces, GROUP, 0, 0, tiled=True)]
    all_to_all x0 -> x1, starting transfers between devices: none -> 4.49 us  [body(): sums = lax.all_to_all(sums, Z_AXES, 0, 0, tiled=True)]
    ppermute x10 -> x3, waiting for transfers between devices: 13.2 us -> 8.7 us  [turn(): lax.ppermute(x, axis, [(i, (i + offset) % count) for i in range(count)])]
    unnamed x14 -> x8, local copies, waits for them, and re-layouts: 3.74 us -> 0.01 us
  transfers between devices with their start and end apart: 30 -> 6, of which waited for: 8 -> 5; matrix products, arithmetic and copies ran while one was open for 2% -> 0% of each run, Pallas kernels for 4% -> 8%
where the time goes in v3:
time: 102 us; the launch traced here: 101 us
  blocking collectives  44.3 us (43%)
  waiting for transfers between devices  23 us (23%)
  starting transfers between devices  19.8 us (19%)
  Pallas kernels  9.71 us (10%)
  local copies, waits for them, and re-layouts  3.28 us (3%)
    all_to_all x1, blocking collectives, body(): result = lax.all_to_all(result, GROUP, 0, 0, tiled=True)  25.7 us
    all_to_all x1, blocking collectives, body(): weights = lax.all_to_all(weights, GROUP, 0, 0, tiled=True)  18.6 us
    all_to_all x1, starting transfers between devices, body(): pieces = lax.all_to_all(pieces, GROUP, 0, 0, tiled=True)  10.3 us
    ppermute x3, waiting for transfers between devices, turn(): lax.ppermute(x, axis, [(i, (i + offset) % count) for i in range(count)])  8.7 us
    all_to_all x1, waiting for transfers between devices, body(): sums = lax.all_to_all(sums, Z_AXES, 0, 0, tiled=True)  7.56 us
    pallas_call x2, Pallas kernels, partial_coeffs(): pl.pallas_call(partial_kernel, grid=(y_count,), in_specs=[SMEM, pl.BlockS...  7.34 us
    all_to_all x1, waiting for transfers between devices, body(): pieces = lax.all_to_all(pieces, GROUP, 0, 0, tiled=True)  6.76 us
    ppermute x3, starting transfers between devices, turn(): lax.ppermute(x, axis, [(i, (i + offset) % count) for i in range(count)])  5 us
  transfers between devices with their start and end apart: 6, of which 5 were waited for; matrix products, arithmetic and copies ran while one was open for 0% of the time, Pallas kernels for 8%

profile of v3, /device:TPU:40, one launch (start us, length us, event | category | flops | bytes accessed | tf_op | source)
XLA Modules:
  0.0 101.2 jit_solution(5688570550982115151)
XLA Ops:
  0.0 2.3 %copy.12 = bf16[8,16,8,512]{3,2,0,1:T(8,128)(2,1)} copy(bf16[8,16,8,512]{3,2,1,0:T(8,128)(2,1)} %bitcast.21) | data formatting | bytes 2097152 | tf_op jit(solution)/shard_map/reshape | solution.py:177
  2.3 0.0 copy-start.1
  2.3 0.0 copy-start.2
  2.3 0.0 copy-start.3
  2.3 10.3 %all-to-all-start = ((bf16[16,64,512]{2,1,0:T(8,128)(2,1)}), bf16[16,64,512]{2,1,0:T(8,128)(2,1)S(1)}, u32[]{:S(2)}, u32[]{:S(2)}) async-start(bf16[16,64,512]{2,1,0:T(8,128)(2,1)} %bitcast.15), calls=%async_computation | async-start | bytes 2097152 | tf_op jit(solution)/shard_map/all_to_all | solution.py:180
  12.6 0.1 pad_add_fusion.1.place_ref
  12.7 0.0 copy-done.1
  12.7 0.0 copy-done.2
  12.7 0.0 copy-done.3
  12.7 3.7 %shard_map.65 = f32[4,8,96,128]{3,2,1,0:T(8,128)S(1)} custom-call(s32[2]{0:T(128)S(1)} %pad_add_fusion.1.place_ref, s32[1,2048]{1,0:T(1,128)S(1)} %bitcast.18, bf16[64,2048]{1,0:T(8,128)(2,1)S(1)} %copy-done.2, bf16[192,2048]{1,0:T(8,128)(2,1)S(1)} %bitcast.16), custom_call_target="tpu_custom_call" | custom-call | flops 2147483648 | bytes 3145728 | tf_op jit(solution)/shard_map/pallas_call | solution.py:51
  16.4 0.1 collective-permute-start
  16.5 0.1 pad_add_fusion.place_ref
  16.5 3.7 %shard_map.64.kept_ref = f32[4,8,96,128]{3,2,1,0:T(8,128)S(1)} custom-call(s32[2]{0:T(128)S(1)} %pad_add_fusion.place_ref, s32[1,2048]{1,0:T(1,128)S(1)} %bitcast.19, bf16[64,2048]{1,0:T(8,128)(2,1)S(1)} %copy-done.2, bf16[192,2048]{1,0:T(8,128)(2,1)S(1)} %bitcast.17), custom_call_target="tpu_custom_call" | custom-call | flops 2147483648 | bytes 3145728 | tf_op jit(solution)/shard_map/pallas_call | solution.py:51
  20.2 0.0 collective-permute-done.came_ref
  20.2 0.3 shard_map.66
  20.5 0.0 copy-start
  20.5 1.7 %collective-permute-start.1 = (bf16[8,96,128]{2,1,0:T(8,128)(2,1)S(1)}, bf16[8,96,128]{2,1,0:T(8,128)(2,1)S(1)}, u32[]{:S(2)}, u32[]{:S(2)}) collective-permute-start(bf16[8,96,128]{2,1,0:T(8,128)(2,1)S(1)} %get-tuple-element.15), channel_id=1, source_target_pairs={{0,8},{8,16},{16,24},{24,0},{1,9},{9,17},{17,25},{25,1},{2,10},{10... | collective-permute-start | bytes 589832 | tf_op jit(solution)/shard_map/ppermute | solution.py:164
  22.1 1.0 collective-permute-start.2
  23.1 2.4 %collective-permute-start.3 = (bf16[8,96,128]{2,1,0:T(8,128)(2,1)S(1)}, bf16[8,96,128]{2,1,0:T(8,128)(2,1)S(1)}, u32[]{:S(2)}, u32[]{:S(2)}) collective-permute-start(bf16[8,96,128]{2,1,0:T(8,128)(2,1)S(1)} %get-tuple-element.17), channel_id=1, source_target_pairs={{0,24},{8,0},{16,8},{24,16},{1,25},{9,1},{17,9},{25,17},{2,26},{10... | collective-permute-start | bytes 589832 | tf_op jit(solution)/shard_map/ppermute | solution.py:164
  25.5 2.8 %collective-permute-done.1.refs_1_ = bf16[8,96,128]{2,1,0:T(8,128)(2,1)S(1)} collective-permute-done((bf16[8,96,128]{2,1,0:T(8,128)(2,1)S(1)}, bf16[8,96,128]{2,1,0:T(8,128)(2,1)S(1)}, u32[]{:S(2)}, u32[]{:S(2)}) %collective-permute-start.1) | collective-permute-done | bytes 196640 | tf_op jit(solution)/shard_map/ppermute | solution.py:164
  28.3 3.2 %collective-permute-done.2.refs_2_ = bf16[8,96,128]{2,1,0:T(8,128)(2,1)S(1)} collective-permute-done((bf16[8,96,128]{2,1,0:T(8,128)(2,1)S(1)}, bf16[8,96,128]{2,1,0:T(8,128)(2,1)S(1)}, u32[]{:S(2)}, u32[]{:S(2)}) %collective-permute-start.2) | collective-permute-done | bytes 196640 | tf_op jit(solution)/shard_map/ppermute | solution.py:164
  31.4 2.8 %collective-permute-done.3.refs_3_ = bf16[8,96,128]{2,1,0:T(8,128)(2,1)S(1)} collective-permute-done((bf16[8,96,128]{2,1,0:T(8,128)(2,1)S(1)}, bf16[8,96,128]{2,1,0:T(8,128)(2,1)S(1)}, u32[]{:S(2)}, u32[]{:S(2)}) %collective-permute-start.3) | collective-permute-done | bytes 196640 | tf_op jit(solution)/shard_map/ppermute | solution.py:164
  34.2 0.8 shard_map.67
  35.0 6.8 %all-to-all-done.samples_ref = bf16[16,64,512]{2,1,0:T(8,128)(2,1)S(1)} async-done(((bf16[16,64,512]{2,1,0:T(8,128)(2,1)}), bf16[16,64,512]{2,1,0:T(8,128)(2,1)S(1)}, u32[]{:S(2)}, u32[]{:S(2)}) %all-to-all-start) | async-done | bytes 1048608 | tf_op jit(solution)/shard_map/all_to_all | solution.py:180
  41.7 4.5 %all-to-all-start.1 = ((bf16[8,96,128]{2,1,0:T(8,128)(2,1)}), bf16[8,96,128]{2,1,0:T(8,128)(2,1)S(1)}, u32[]{:S(2)}, u32[]{:S(2)}) async-start(bf16[8,96,128]{2,1,0:T(8,128)(2,1)} %shard_map.67), calls=%async_computation.1 | async-start | bytes 393216 | tf_op jit(solution)/shard_map/all_to_all | solution.py:192
  46.9 0.1 pad_add_fusion.2.place_ref
  46.9 7.6 %all-to-all-done.1.sums_ref = bf16[8,96,128]{2,1,0:T(8,128)(2,1)S(1)} async-done(((bf16[8,96,128]{2,1,0:T(8,128)(2,1)}), bf16[8,96,128]{2,1,0:T(8,128)(2,1)S(1)}, u32[]{:S(2)}, u32[]{:S(2)}) %all-to-all-start.1) | async-done | bytes 196640 | tf_op jit(solution)/shard_map/all_to_all | solution.py:192
  54.5 0.0 copy-done
  54.5 0.6 shard_map.68
  55.1 18.6 %all_to_all.20.weights_ref = bf16[16,112,128]{2,1,0:T(8,128)(2,1)S(1)} all-to-all(bf16[16,112,128]{2,1,0:T(8,128)(2,1)S(1)} %shard_map.68), channel_id=1, replica_groups=mesh['zg'=4,'zl'=2,'y'=4,'core'=2,'smp'=4] {'zg','smp'}, dimensions={0} | all-to-all | bytes 917504 | tf_op jit(solution)/shard_map/all_to_all | solution.py:201
  73.8 0.8 shard_map.69
  74.5 25.7 %all_to_all.21 = bf16[16,48,512]{2,1,0:T(8,128)(2,1)S(1)} all-to-all(bf16[16,48,512]{2,1,0:T(8,128)(2,1)S(1)} %shard_map.69), channel_id=1, replica_groups=mesh['zg'=4,'zl'=2,'y'=4,'core'=2,'smp'=4] {'zg','smp'}, dimensions={0} | all-to-all | bytes 1572864 | tf_op jit(solution)/shard_map/all_to_all | solution.py:210
  100.2 1.0 copy.10
Async XLA Ops:
  2.3 10.4 %copy-start.1 = (bf16[2048,192]{0,1:T(8,128)(2,1)S(1)}, bf16[2048,192]{0,1:T(8,128)(2,1)}, u32[]{:S(2)}) copy-start(bf16[2048,192]{0,1:T(8,128)(2,1)} %param.8) | copy-start | bytes 2359300
  2.3 10.4 %copy-start.2 = (bf16[64,2048]{1,0:T(8,128)(2,1)S(1)}, bf16[64,2048]{1,0:T(8,128)(2,1)}, u32[]{:S(2)}) copy-start(bf16[64,2048]{1,0:T(8,128)(2,1)} %adjoint_ref.3) | copy-start | bytes 786436
  2.3 10.4 %copy-start.3 = (s32[2048,1]{0,1:T(1,128)S(1)}, s32[2048,1]{0,1:T(1,128)}, u32[]{:S(2)}) copy-start(s32[2048,1]{0,1:T(1,128)} %param.9) | copy-start | bytes 24580
  2.3 39.4 %all-to-all-start = ((bf16[16,64,512]{2,1,0:T(8,128)(2,1)}), bf16[16,64,512]{2,1,0:T(8,128)(2,1)S(1)}, u32[]{:S(2)}, u32[]{:S(2)}) async-start(bf16[16,64,512]{2,1,0:T(8,128)(2,1)} %bitcast.15), calls=%async_computation | async-start | bytes 2097152 | tf_op jit(solution)/shard_map/all_to_all | solution.py:180
  16.4 3.9 %collective-permute-start = (f32[4,8,96,128]{3,2,1,0:T(8,128)S(1)}, f32[4,8,96,128]{3,2,1,0:T(8,128)S(1)}, u32[]{:S(2)}, u32[]{:S(2)}) collective-permute-start(f32[4,8,96,128]{3,2,1,0:T(8,128)S(1)} %shard_map.65), channel_id=1, source_target_pairs={{0,4},{4,0},{1,5},{5,1},{2,6},{6,2},{3,7},{7,3},{8,12},{12,8},{9,1... | collective-permute-start | bytes 4718600 | tf_op jit(solution)/shard_map/ppermute | solution.py:183
  20.5 34.0 %copy-start = (f32[2,8192]{1,0:T(2,128)S(1)}, f32[2,8192]{1,0:T(2,128)}, u32[]{:S(2)}) copy-start(f32[2,8192]{1,0:T(2,128)} %twiddle_ref.1) | copy-start | bytes 196612
  20.5 7.8 %collective-permute-start.1 = (bf16[8,96,128]{2,1,0:T(8,128)(2,1)S(1)}, bf16[8,96,128]{2,1,0:T(8,128)(2,1)S(1)}, u32[]{:S(2)}, u32[]{:S(2)}) collective-permute-start(bf16[8,96,128]{2,1,0:T(8,128)(2,1)S(1)} %get-tuple-element.15), channel_id=1, source_target_pairs={{0,8},{8,16},{16,24},{24,0},{1,9},{9,17},{17,25},{25,1},{2,10},{10... | collective-permute-start | bytes 589832 | tf_op jit(solution)/shard_map/ppermute | solution.py:164
  22.1 9.3 %collective-permute-start.2 = (bf16[8,96,128]{2,1,0:T(8,128)(2,1)S(1)}, bf16[8,96,128]{2,1,0:T(8,128)(2,1)S(1)}, u32[]{:S(2)}, u32[]{:S(2)}) collective-permute-start(bf16[8,96,128]{2,1,0:T(8,128)(2,1)S(1)} %get-tuple-element.16), channel_id=1, source_target_pairs={{0,16},{8,24},{16,0},{24,8},{1,17},{9,25},{17,1},{25,9},{2,18},{10... | collective-permute-start | bytes 589832 | tf_op jit(solution)/shard_map/ppermute | solution.py:164
  23.1 11.1 %collective-permute-start.3 = (bf16[8,96,128]{2,1,0:T(8,128)(2,1)S(1)}, bf16[8,96,128]{2,1,0:T(8,128)(2,1)S(1)}, u32[]{:S(2)}, u32[]{:S(2)}) collective-permute-start(bf16[8,96,128]{2,1,0:T(8,128)(2,1)S(1)} %get-tuple-element.17), channel_id=1, source_target_pairs={{0,24},{8,0},{16,8},{24,16},{1,25},{9,1},{17,9},{25,17},{2,26},{10... | collective-permute-start | bytes 589832 | tf_op jit(solution)/shard_map/ppermute | solution.py:164
  41.7 12.8 %all-to-all-start.1 = ((bf16[8,96,128]{2,1,0:T(8,128)(2,1)}), bf16[8,96,128]{2,1,0:T(8,128)(2,1)S(1)}, u32[]{:S(2)}, u32[]{:S(2)}) async-start(bf16[8,96,128]{2,1,0:T(8,128)(2,1)} %shard_map.67), calls=%async_computation.1 | async-start | bytes 393216 | tf_op jit(solution)/shard_map/all_to_all | solution.py:192

commit v4 on v3

--- a/solution.py
+++ b/solution.py
@@ -90,51 +90,75 @@
         out_ref[...] = (kept_ref[offset] + came_ref[offset]).astype(out_ref.dtype)
 
 
-def gather_kernel(*refs):
-    total = refs[0][...]
-    for ref in refs[1:-1]:
-        total = total + ref[...].astype(jnp.float32)
-    refs[-1][...] = total.astype(refs[-1].dtype)
-
-
-def weights_kernel(place_ref, sums_ref, twiddle_ref, out_ref):
-    members, rows, lanes = out_ref.shape
+def halve_kernel(place_ref, *refs):
+    kept_ref, sent_ref = refs[-2:]
+    for block in range(kept_ref.shape[0]):
+        for parity, out_ref in ((place_ref[0], kept_ref), (1 - place_ref[0], sent_ref)):
+            z = block * 2 + parity
+            total = refs[0][z]
+            for ref in refs[1:-2]:
+                total = total + ref[z].astype(jnp.float32)
+            out_ref[block] = total.astype(out_ref.dtype)
+
+
+def offer_kernel(place_ref, kept_ref, came_ref, twiddle_ref, own_ref, out_ref):
+    blocks, packed, lanes = kept_ref.shape
     levels, points = twiddle_ref.shape
-    packed = sums_ref.shape[1]
+    piece = points // (blocks * blocks)
+    total = kept_ref[...] + came_ref[...].astype(jnp.float32)
+    own_ref[...] = total
+    total = total.astype(jnp.bfloat16).reshape(blocks * packed, lanes)
+    rank = jnp.full((8 - 3 * levels, lanes), place_ref[1].astype(jnp.float32))
+    for block in range(blocks):
+        out_ref[block, :blocks * packed, :] = total
+        start = (block * blocks + place_ref[0]) * piece
+        rows = []
+        for column in range(piece // lanes):
+            left = twiddle_ref[:, pl.ds(pl.multiple_of(start + column * lanes, lanes), lanes)]
+            for _ in range(3):
+                term = left.astype(jnp.bfloat16).astype(jnp.float32)
+                left = left - term
+                rows.append(term)
+            rows.append(rank)
+        out_ref[block, blocks * packed:, :] = jnp.concatenate(rows, axis=0).astype(jnp.bfloat16)
+
+
+def weights_kernel(place_ref, own_ref, offers_ref, out_ref):
+    blocks, packed, lanes = own_ref.shape
     samples = packed * 2 // 3
-    total = jnp.sum(sums_ref[...].astype(jnp.float32), axis=0)
-    row = lax.broadcasted_iota(jnp.int32, total.shape, 0)
-    lane = lax.broadcasted_iota(jnp.int32, total.shape, 1)
+    row = lax.broadcasted_iota(jnp.int32, (packed, lanes), 0)
+    lane = lax.broadcasted_iota(jnp.int32, (packed, lanes), 1)
     tail = row - samples + jnp.where(lane < 64, 0, samples // 2)
-    sample = place_ref[0] * samples + jnp.where(row < samples, row, tail)
-    weights = jnp.where(sample < place_ref[1], total, 0.0).astype(jnp.bfloat16)
-    for member in range(members):
-        out_ref[member, :packed, :] = weights
-        start = pl.multiple_of(member * (points // members) + place_ref[0] * lanes, lanes)
-        left = twiddle_ref[:, pl.ds(start, lanes)]
-        terms = []
-        for _ in range(3):
-            term = left.astype(jnp.bfloat16).astype(jnp.float32)
-            left = left - term
-            terms.append(term)
-        terms.append(jnp.zeros((rows - packed - 3 * levels, lanes), jnp.float32))
-        out_ref[member, packed:, :] = jnp.concatenate(terms, axis=0).astype(jnp.bfloat16)
-
-
-def field_kernel(samples_ref, weights_ref, out_ref, field):
+    sample = place_ref[1] * samples + jnp.where(row < samples, row, tail)
+    sample = sample.astype(jnp.float32)
+    for block in range(blocks):
+        total = own_ref[block]
+        for other in range(1, blocks):
+            partner = place_ref[0] ^ other
+            total = total + offers_ref[partner, block * packed:(block + 1) * packed, :].astype(
+                jnp.float32
+            )
+        extra = offers_ref[block, blocks * packed:, :].astype(jnp.float32)
+        weights = jnp.where(sample < extra[6:7], total, 0.0).astype(jnp.bfloat16)
+        for part in range(out_ref.shape[0]):
+            out_ref[part, block] = weights
+
+
+def field_kernel(samples_ref, offers_ref, weights_ref, out_ref, field):
     blocks, vectors, points = field.shape
     parts = samples_ref.shape[0] // blocks
     samples = samples_ref.shape[1]
-    packed = samples * vectors // 128
+    packed = weights_ref.shape[2]
     factors = []
     for c in range(blocks):
         head, tail, columns = [], [], []
         for p in range(parts):
-            piece = c * parts + p
-            head.append(weights_ref[piece, :samples, :])
-            rest = weights_ref[piece, samples:packed, :]
+            head.append(weights_ref[p, c, :samples, :])
+            rest = weights_ref[p, c, samples:, :]
             tail += [rest[:, :64], rest[:, 64:]]
-            terms = weights_ref[piece, packed:, :].astype(jnp.float32)
+        extra = offers_ref[c, blocks * packed:, :].astype(jnp.float32)
+        for column in range(extra.shape[0] // 8):
+            terms = extra[column * 8:column * 8 + 8]
             columns.append(terms[0:2] + terms[2:4] + terms[4:6])
         factors.append(jnp.concatenate(columns, axis=1))
         grid = samples_ref[c * parts:(c + 1) * parts].reshape(parts * samples, points)
@@ -187,22 +211,32 @@
     shapes += [jax.ShapeDtypeStruct(shape, jnp.bfloat16)] * (y_count - 1)
     sums = local_call(merge_kernel, shapes, kept, came)
     sums = [sums[0]] + [turn(sums[i], "y", i) for i in range(1, y_count)]
-    sums = local_call(gather_kernel, jax.ShapeDtypeStruct(shape, jnp.bfloat16), *sums)
-    sums, pieces = lax.optimization_barrier((sums, pieces))
-    sums = lax.all_to_all(sums, Z_AXES, 0, 0, tiled=True)
+    shape = (groups,) + shape[1:]
+    shapes = [jax.ShapeDtypeStruct(shape, jnp.float32), jax.ShapeDtypeStruct(shape, jnp.bfloat16)]
+    zl = lax.axis_index("zl")
+    kept, sent = local_call(halve_kernel, shapes, zl[None], *sums, smem=1)
+    came = lax.ppermute(sent, "zl", [(0, 1), (1, 0)])
+    rows = groups * shape[1] + 8 * piece // shape[2]
+    shapes = [jax.ShapeDtypeStruct(shape, jnp.float32)]
+    shapes += [jax.ShapeDtypeStruct((groups, rows, shape[2]), jnp.bfloat16)]
+    place = jnp.stack([smp, block_ranks[0]])
+    partial, offers = local_call(offer_kernel, shapes, place, kept, came, twiddle, smem=1)
+    offers, pieces = lax.optimization_barrier((offers, pieces))
+    offers = lax.all_to_all(offers, "zg", 0, 0, tiled=True)
     weights = local_call(
         weights_kernel,
-        jax.ShapeDtypeStruct((members, shape[1] + 16, shape[2]), jnp.bfloat16),
-        jnp.stack([smp, block_ranks[0]]),
-        sums,
-        twiddle,
+        jax.ShapeDtypeStruct((parts,) + shape, jnp.bfloat16),
+        jnp.stack([lax.axis_index("zg"), smp]),
+        partial,
+        offers,
         smem=1,
     )
-    weights = lax.all_to_all(weights, GROUP, 0, 0, tiled=True)
+    weights = lax.all_to_all(weights, "smp", 0, 0, tiled=True)
     result = local_call(
         field_kernel,
         jax.ShapeDtypeStruct((members, vectors // parts, piece), jnp.bfloat16),
         pieces,
+        offers,
         weights,
         scratch=[pltpu.VMEM((groups, vectors, piece), jnp.float32)],
         flops=2 * members * samples * vectors * piece,

time: 102 us -> 99.1 us (0.972)
  the two profiles are of different devices: /device:TPU:40 before, /device:TPU:56 now
where the time goes in v4:
time: 99.1 us; the launch traced here: 98.8 us
  blocking collectives  36.7 us (37%)
  waiting for transfers between devices  28 us (28%)
  starting transfers between devices  19.3 us (19%)
  Pallas kernels  10.4 us (10%)
  local copies, waits for them, and re-layouts  3.29 us (3%)
    all_to_all x1, blocking collectives, body(): result = lax.all_to_all(result, GROUP, 0, 0, tiled=True)  25.1 us
    all_to_all x1, waiting for transfers between devices, body(): offers = lax.all_to_all(offers, 'zg', 0, 0, tiled=True)  12.6 us
    all_to_all x1, blocking collectives, body(): weights = lax.all_to_all(weights, 'smp', 0, 0, tiled=True)  11.6 us
    all_to_all x1, starting transfers between devices, body(): pieces = lax.all_to_all(pieces, GROUP, 0, 0, tiled=True)  10.3 us
    ppermute x3, waiting for transfers between devices, turn(): lax.ppermute(x, axis, [(i, (i + offset) % count) for i in range(count)])  9.65 us
    pallas_call x2, Pallas kernels, partial_coeffs(): pl.pallas_call(partial_kernel, grid=(y_count,), in_specs=[SMEM, pl.BlockS...  7.34 us
    ppermute x1, waiting for transfers between devices, body(): came = lax.ppermute(sent, 'zl', [(0, 1), (1, 0)])  5.72 us
    all_to_all x1, starting transfers between devices, body(): offers = lax.all_to_all(offers, 'zg', 0, 0, tiled=True)  5.02 us
  transfers between devices with their start and end apart: 7, of which 5 were waited for; matrix products, arithmetic and copies ran while one was open for 0% of the time, Pallas kernels for 9%

profile of v4, /device:TPU:56, one launch (start us, length us, event | category | flops | bytes accessed | tf_op | source)
XLA Modules:
  0.0 98.8 jit_solution(9984892068833605481)
XLA Ops:
  0.0 2.3 %copy.12 = bf16[8,16,8,512]{3,2,0,1:T(8,128)(2,1)} copy(bf16[8,16,8,512]{3,2,1,0:T(8,128)(2,1)} %bitcast.23) | data formatting | bytes 2097152 | tf_op jit(solution)/shard_map/reshape | solution.py:201
  2.3 0.0 copy-start.1
  2.3 0.0 copy-start.2
  2.3 0.0 copy-start.3
  2.3 10.3 %all-to-all-start = ((bf16[16,64,512]{2,1,0:T(8,128)(2,1)}), bf16[16,64,512]{2,1,0:T(8,128)(2,1)S(1)}, u32[]{:S(2)}, u32[]{:S(2)}) async-start(bf16[16,64,512]{2,1,0:T(8,128)(2,1)} %bitcast.17), calls=%async_computation | async-start | bytes 2097152 | tf_op jit(solution)/shard_map/all_to_all | solution.py:204
  12.6 0.1 pad_add_fusion.2.place_ref
  12.7 0.0 copy-done.1
  12.7 0.0 copy-done.2
  12.7 0.0 copy-done.3
  12.7 3.7 %shard_map.65 = f32[4,8,96,128]{3,2,1,0:T(8,128)S(1)} custom-call(s32[2]{0:T(128)S(1)} %pad_add_fusion.2.place_ref, s32[1,2048]{1,0:T(1,128)S(1)} %bitcast.20, bf16[64,2048]{1,0:T(8,128)(2,1)S(1)} %copy-done.2, bf16[192,2048]{1,0:T(8,128)(2,1)S(1)} %bitcast.18), custom_call_target="tpu_custom_call" | custom-call | flops 2147483648 | bytes 3145728 | tf_op jit(solution)/shard_map/pallas_call | solution.py:51
  16.4 0.1 collective-permute-start
  16.5 0.1 pad_add_fusion.1.place_ref
  16.6 3.7 %shard_map.64.kept_ref = f32[4,8,96,128]{3,2,1,0:T(8,128)S(1)} custom-call(s32[2]{0:T(128)S(1)} %pad_add_fusion.1.place_ref, s32[1,2048]{1,0:T(1,128)S(1)} %bitcast.21, bf16[64,2048]{1,0:T(8,128)(2,1)S(1)} %copy-done.2, bf16[192,2048]{1,0:T(8,128)(2,1)S(1)} %bitcast.19), custom_call_target="tpu_custom_call" | custom-call | flops 2147483648 | bytes 3145728 | tf_op jit(solution)/shard_map/pallas_call | solution.py:51
  20.2 0.0 copy-start
  20.2 0.0 collective-permute-done.came_ref
  20.2 0.3 shard_map.66
  20.5 0.3 collective-permute-start.1
  20.8 2.6 %collective-permute-start.2 = (bf16[8,96,128]{2,1,0:T(8,128)(2,1)S(1)}, bf16[8,96,128]{2,1,0:T(8,128)(2,1)S(1)}, u32[]{:S(2)}, u32[]{:S(2)}) collective-permute-start(bf16[8,96,128]{2,1,0:T(8,128)(2,1)S(1)} %get-tuple-element.20), channel_id=1, source_target_pairs={{0,16},{8,24},{16,0},{24,8},{1,17},{9,25},{17,1},{25,9},{2,18},{10... | collective-permute-start | bytes 589832 | tf_op jit(solution)/shard_map/ppermute | solution.py:188
  23.4 0.0 collective-permute-start.3
  24.0 4.2 %collective-permute-done.1.refs_1_ = bf16[8,96,128]{2,1,0:T(8,128)(2,1)S(1)} collective-permute-done((bf16[8,96,128]{2,1,0:T(8,128)(2,1)S(1)}, bf16[8,96,128]{2,1,0:T(8,128)(2,1)S(1)}, u32[]{:S(2)}, u32[]{:S(2)}) %collective-permute-start.1) | collective-permute-done | bytes 196640 | tf_op jit(solution)/shard_map/ppermute | solution.py:188
  28.3 1.8 %collective-permute-done.2.refs_2_ = bf16[8,96,128]{2,1,0:T(8,128)(2,1)S(1)} collective-permute-done((bf16[8,96,128]{2,1,0:T(8,128)(2,1)S(1)}, bf16[8,96,128]{2,1,0:T(8,128)(2,1)S(1)}, u32[]{:S(2)}, u32[]{:S(2)}) %collective-permute-start.2) | collective-permute-done | bytes 196640 | tf_op jit(solution)/shard_map/ppermute | solution.py:188
  30.1 3.6 %collective-permute-done.3.refs_3_ = bf16[8,96,128]{2,1,0:T(8,128)(2,1)S(1)} collective-permute-done((bf16[8,96,128]{2,1,0:T(8,128)(2,1)S(1)}, bf16[8,96,128]{2,1,0:T(8,128)(2,1)S(1)}, u32[]{:S(2)}, u32[]{:S(2)}) %collective-permute-start.3) | collective-permute-done | bytes 196640 | tf_op jit(solution)/shard_map/ppermute | solution.py:188
  33.7 0.1 shard_map.67
  33.8 1.1 %collective-permute-start.4 = (bf16[4,96,128]{2,1,0:T(8,128)(2,1)S(1)}, bf16[4,96,128]{2,1,0:T(8,128)(2,1)S(1)}, u32[]{:S(2)}, u32[]{:S(2)}) collective-permute-start(bf16[4,96,128]{2,1,0:T(8,128)(2,1)S(1)} %get-tuple-element.23), channel_id=1, source_target_pairs={{0,32},{32,0},{1,33},{33,1},{2,34},{34,2},{3,35},{35,3},{4,36},{36... | collective-permute-start | bytes 294920 | tf_op jit(solution)/shard_map/ppermute | solution.py:218
  34.9 0.1 pad_add_fusion.place_ref
  35.0 5.7 %collective-permute-done.4.came_ref = bf16[4,96,128]{2,1,0:T(8,128)(2,1)S(1)} collective-permute-done((bf16[4,96,128]{2,1,0:T(8,128)(2,1)S(1)}, bf16[4,96,128]{2,1,0:T(8,128)(2,1)S(1)}, u32[]{:S(2)}, u32[]{:S(2)}) %collective-permute-start.4) | collective-permute-done | bytes 98336 | tf_op jit(solution)/shard_map/ppermute | solution.py:218
  40.7 0.0 copy-done
  40.7 1.4 %shard_map.68 = (f32[4,96,128]{2,1,0:T(8,128)S(1)}, bf16[4,416,128]{2,1,0:T(8,128)(2,1)}) custom-call(s32[2]{0:T(128)S(1)} %pad_add_fusion.place_ref, f32[4,96,128]{2,1,0:T(8,128)S(1)} %get-tuple-element.22.kept_ref, bf16[4,96,128]{2,1,0:T(8,128)(2,1)S(1)} %collective-permute-done.4.came_ref, f32[2,8192]{1,0:T(2,128)S(1)} %copy-done), custom_call_target="tpu_custom_call" | custom-call | bytes 2097152 | tf_op jit(solution)/shard_map/pallas_call | solution.py:76
  42.0 0.0 all-to-all-done.samples_ref
  42.0 5.0 %all-to-all-start.1 = ((bf16[4,416,128]{2,1,0:T(8,128)(2,1)}), bf16[4,416,128]{2,1,0:T(8,128)(2,1)S(1)}, u32[]{:S(2)}, u32[]{:S(2)}) async-start(bf16[4,416,128]{2,1,0:T(8,128)(2,1)} %get-tuple-element.27), calls=%async_computation.1 | async-start | bytes 851968 | tf_op jit(solution)/shard_map/all_to_all | solution.py:225
  47.1 0.1 pad_add_fusion.3.place_ref
  47.1 12.6 %all-to-all-done.1.offers_ref = bf16[4,416,128]{2,1,0:T(8,128)(2,1)S(1)} async-done(((bf16[4,416,128]{2,1,0:T(8,128)(2,1)}), bf16[4,416,128]{2,1,0:T(8,128)(2,1)S(1)}, u32[]{:S(2)}, u32[]{:S(2)}) %all-to-all-start.1) | async-done | bytes 426016 | tf_op jit(solution)/shard_map/all_to_all | solution.py:225
  59.7 0.6 shard_map.69
  60.3 11.6 %all_to_all.20.weights_ref = bf16[4,4,96,128]{3,2,1,0:T(8,128)(2,1)S(1)} all-to-all(bf16[4,4,96,128]{3,2,1,0:T(8,128)(2,1)S(1)} %shard_map.69), channel_id=1, replica_groups=mesh['zg'=4,'zl'=2,'y'=4,'core'=2,'smp'=4] {'smp'}, dimensions={0} | all-to-all | bytes 786432 | tf_op jit(solution)/shard_map/all_to_all | solution.py:234
  71.9 0.8 shard_map.70
  72.7 25.1 %all_to_all.21 = bf16[16,48,512]{2,1,0:T(8,128)(2,1)S(1)} all-to-all(bf16[16,48,512]{2,1,0:T(8,128)(2,1)S(1)} %shard_map.70), channel_id=1, replica_groups=mesh['zg'=4,'zl'=2,'y'=4,'core'=2,'smp'=4] {'zg','smp'}, dimensions={0} | all-to-all | bytes 1572864 | tf_op jit(solution)/shard_map/all_to_all | solution.py:244
  97.8 1.0 copy.10
Async XLA Ops:
  2.3 10.4 %copy-start.1 = (bf16[2048,192]{0,1:T(8,128)(2,1)S(1)}, bf16[2048,192]{0,1:T(8,128)(2,1)}, u32[]{:S(2)}) copy-start(bf16[2048,192]{0,1:T(8,128)(2,1)} %param.8) | copy-start | bytes 2359300
  2.3 10.4 %copy-start.2 = (bf16[64,2048]{1,0:T(8,128)(2,1)S(1)}, bf16[64,2048]{1,0:T(8,128)(2,1)}, u32[]{:S(2)}) copy-start(bf16[64,2048]{1,0:T(8,128)(2,1)} %adjoint_ref.3) | copy-start | bytes 786436
  2.3 10.4 %copy-start.3 = (s32[2048,1]{0,1:T(1,128)S(1)}, s32[2048,1]{0,1:T(1,128)}, u32[]{:S(2)}) copy-start(s32[2048,1]{0,1:T(1,128)} %param.9) | copy-start | bytes 24580
  2.3 39.7 %all-to-all-start = ((bf16[16,64,512]{2,1,0:T(8,128)(2,1)}), bf16[16,64,512]{2,1,0:T(8,128)(2,1)S(1)}, u32[]{:S(2)}, u32[]{:S(2)}) async-start(bf16[16,64,512]{2,1,0:T(8,128)(2,1)} %bitcast.17), calls=%async_computation | async-start | bytes 2097152 | tf_op jit(solution)/shard_map/all_to_all | solution.py:204
  16.4 3.9 %collective-permute-start = (f32[4,8,96,128]{3,2,1,0:T(8,128)S(1)}, f32[4,8,96,128]{3,2,1,0:T(8,128)S(1)}, u32[]{:S(2)}, u32[]{:S(2)}) collective-permute-start(f32[4,8,96,128]{3,2,1,0:T(8,128)S(1)} %shard_map.65), channel_id=1, source_target_pairs={{0,4},{4,0},{1,5},{5,1},{2,6},{6,2},{3,7},{7,3},{8,12},{12,8},{9,1... | collective-permute-start | bytes 4718600 | tf_op jit(solution)/shard_map/ppermute | solution.py:207
  20.2 20.5 %copy-start = (f32[2,8192]{1,0:T(2,128)S(1)}, f32[2,8192]{1,0:T(2,128)}, u32[]{:S(2)}) copy-start(f32[2,8192]{1,0:T(2,128)} %twiddle_ref.1) | copy-start | bytes 196612
  20.5 7.8 %collective-permute-start.1 = (bf16[8,96,128]{2,1,0:T(8,128)(2,1)S(1)}, bf16[8,96,128]{2,1,0:T(8,128)(2,1)S(1)}, u32[]{:S(2)}, u32[]{:S(2)}) collective-permute-start(bf16[8,96,128]{2,1,0:T(8,128)(2,1)S(1)} %get-tuple-element.19), channel_id=1, source_target_pairs={{0,8},{8,16},{16,24},{24,0},{1,9},{9,17},{17,25},{25,1},{2,10},{10... | collective-permute-start | bytes 589832 | tf_op jit(solution)/shard_map/ppermute | solution.py:188
  20.8 9.3 %collective-permute-start.2 = (bf16[8,96,128]{2,1,0:T(8,128)(2,1)S(1)}, bf16[8,96,128]{2,1,0:T(8,128)(2,1)S(1)}, u32[]{:S(2)}, u32[]{:S(2)}) collective-permute-start(bf16[8,96,128]{2,1,0:T(8,128)(2,1)S(1)} %get-tuple-element.20), channel_id=1, source_target_pairs={{0,16},{8,24},{16,0},{24,8},{1,17},{9,25},{17,1},{25,9},{2,18},{10... | collective-permute-start | bytes 589832 | tf_op jit(solution)/shard_map/ppermute | solution.py:188
  23.4 10.3 %collective-permute-start.3 = (bf16[8,96,128]{2,1,0:T(8,128)(2,1)S(1)}, bf16[8,96,128]{2,1,0:T(8,128)(2,1)S(1)}, u32[]{:S(2)}, u32[]{:S(2)}) collective-permute-start(bf16[8,96,128]{2,1,0:T(8,128)(2,1)S(1)} %get-tuple-element.21), channel_id=1, source_target_pairs={{0,24},{8,0},{16,8},{24,16},{1,25},{9,1},{17,9},{25,17},{2,26},{10... | collective-permute-start | bytes 589832 | tf_op jit(solution)/shard_map/ppermute | solution.py:188
  33.8 6.9 %collective-permute-start.4 = (bf16[4,96,128]{2,1,0:T(8,128)(2,1)S(1)}, bf16[4,96,128]{2,1,0:T(8,128)(2,1)S(1)}, u32[]{:S(2)}, u32[]{:S(2)}) collective-permute-start(bf16[4,96,128]{2,1,0:T(8,128)(2,1)S(1)} %get-tuple-element.23), channel_id=1, source_target_pairs={{0,32},{32,0},{1,33},{33,1},{2,34},{34,2},{3,35},{35,3},{4,36},{36... | collective-permute-start | bytes 294920 | tf_op jit(solution)/shard_map/ppermute | solution.py:218
  42.0 17.7 %all-to-all-start.1 = ((bf16[4,416,128]{2,1,0:T(8,128)(2,1)}), bf16[4,416,128]{2,1,0:T(8,128)(2,1)S(1)}, u32[]{:S(2)}, u32[]{:S(2)}) async-start(bf16[4,416,128]{2,1,0:T(8,128)(2,1)} %get-tuple-element.27), calls=%async_computation.1 | async-start | bytes 851968 | tf_op jit(solution)/shard_map/all_to_all | solution.py:225

commit v5 on v4

--- a/solution.py
+++ b/solution.py
@@ -101,17 +101,17 @@
             out_ref[block] = total.astype(out_ref.dtype)
 
 
-def offer_kernel(place_ref, kept_ref, came_ref, twiddle_ref, own_ref, out_ref):
+def offer_kernel(place_ref, kept_ref, came_ref, twiddle_ref, own_ref, extra_ref, *refs):
+    out_refs, total = refs[:-1], refs[-1]
+    zg, smp, rank = place_ref[0], place_ref[1], place_ref[2]
     blocks, packed, lanes = kept_ref.shape
     levels, points = twiddle_ref.shape
     piece = points // (blocks * blocks)
-    total = kept_ref[...] + came_ref[...].astype(jnp.float32)
-    own_ref[...] = total
-    total = total.astype(jnp.bfloat16).reshape(blocks * packed, lanes)
-    rank = jnp.full((8 - 3 * levels, lanes), place_ref[1].astype(jnp.float32))
-    for block in range(blocks):
-        out_ref[block, :blocks * packed, :] = total
-        start = (block * blocks + place_ref[0]) * piece
+    total[...] = kept_ref[...] + came_ref[...].astype(jnp.float32)
+    rank = jnp.full((8 - 3 * levels, lanes), rank.astype(jnp.float32))
+    for distance in range(blocks):
+        partner = zg ^ distance
+        start = (partner * blocks + smp) * piece
         rows = []
         for column in range(piece // lanes):
             left = twiddle_ref[:, pl.ds(pl.multiple_of(start + column * lanes, lanes), lanes)]
@@ -120,10 +120,22 @@
                 left = left - term
                 rows.append(term)
             rows.append(rank)
-        out_ref[block, blocks * packed:, :] = jnp.concatenate(rows, axis=0).astype(jnp.bfloat16)
-
-
-def weights_kernel(place_ref, own_ref, offers_ref, out_ref):
+        rows = jnp.concatenate(rows, axis=0).astype(jnp.bfloat16)
+        for block in range(blocks):
+            value = total[partner ^ block]
+            if distance == 0:
+                own_ref[block] = value
+            else:
+                target = slice(block * packed, (block + 1) * packed)
+                out_refs[distance - 1][target, :] = value.astype(jnp.bfloat16)
+        if distance == 0:
+            extra_ref[...] = rows
+        else:
+            out_refs[distance - 1][blocks * packed:, :] = rows
+
+
+def weights_kernel(place_ref, own_ref, extra_ref, *refs):
+    offers, out_ref = refs[:-1], refs[-1]
     blocks, packed, lanes = own_ref.shape
     samples = packed * 2 // 3
     row = lax.broadcasted_iota(jnp.int32, (packed, lanes), 0)
@@ -133,35 +145,35 @@
     sample = sample.astype(jnp.float32)
     for block in range(blocks):
         total = own_ref[block]
-        for other in range(1, blocks):
-            partner = place_ref[0] ^ other
-            total = total + offers_ref[partner, block * packed:(block + 1) * packed, :].astype(
-                jnp.float32
-            )
-        extra = offers_ref[block, blocks * packed:, :].astype(jnp.float32)
-        weights = jnp.where(sample < extra[6:7], total, 0.0).astype(jnp.bfloat16)
-        for part in range(out_ref.shape[0]):
-            out_ref[part, block] = weights
-
-
-def field_kernel(samples_ref, offers_ref, weights_ref, out_ref, field):
-    blocks, vectors, points = field.shape
-    parts = samples_ref.shape[0] // blocks
+        for offer in offers:
+            total = total + offer[block * packed:(block + 1) * packed, :].astype(jnp.float32)
+        extra = offers[block - 1][blocks * packed:, :] if block else extra_ref[...]
+        rank = extra.astype(jnp.float32)[6:7]
+        out_ref[block] = jnp.where(sample < rank, total, 0.0).astype(jnp.bfloat16)
+
+
+def field_kernel(blocks, parts, place_ref, samples_ref, extra_ref, *refs):
+    offers, weight_refs = refs[:blocks - 1], refs[blocks - 1:-2]
+    out_ref, field = refs[-2:]
+    zg, smp = place_ref[0], place_ref[1]
+    vectors, points = field.shape[1:]
     samples = samples_ref.shape[1]
-    packed = weights_ref.shape[2]
+    packed = weight_refs[0].shape[1]
     factors = []
     for c in range(blocks):
-        head, tail, columns = [], [], []
+        head, tail, columns, grid = [], [], [], []
         for p in range(parts):
-            head.append(weights_ref[p, c, :samples, :])
-            rest = weights_ref[p, c, samples:, :]
+            grid.append(samples_ref[(zg ^ c) * parts + lax.rem(smp - p + parts, parts)])
+            head.append(weight_refs[p][c, :samples, :])
+            rest = weight_refs[p][c, samples:, :]
             tail += [rest[:, :64], rest[:, 64:]]
-        extra = offers_ref[c, blocks * packed:, :].astype(jnp.float32)
+        extra = offers[c - 1][blocks * packed:, :] if c else extra_ref[...]
+        extra = extra.astype(jnp.float32)
         for column in range(extra.shape[0] // 8):
             terms = extra[column * 8:column * 8 + 8]
             columns.append(terms[0:2] + terms[2:4] + terms[4:6])
         factors.append(jnp.concatenate(columns, axis=1))
-        grid = samples_ref[c * parts:(c + 1) * parts].reshape(parts * samples, points)
+        grid = jnp.concatenate(grid, axis=0)
         head = jnp.concatenate(head, axis=0)
         tail = jnp.concatenate(tail, axis=0)
         field[c, :128, :] = lax.dot_general(
@@ -180,12 +192,16 @@
                 for c in range(blocks)
             ]
         for c in range(blocks):
-            out_ref[c * parts + p] = level[c].astype(jnp.bfloat16)
-
-
-def turn(x, axis, offset):
+            out_ref[(zg ^ c) * parts + p] = level[c].astype(jnp.bfloat16)
+
+
+def exchange(pieces, axis, route):
     count = lax.axis_size(axis)
-    return lax.ppermute(x, axis, [(i, (i + offset) % count) for i in range(count)])
+    came = {}
+    for offset in sorted(pieces, key=lambda k: abs(k - count // 2)):
+        pairs = [(i, route(i, offset) % count) for i in range(count)]
+        came[offset] = lax.ppermute(pieces[offset], axis, pairs)
+    return [came[offset] for offset in sorted(pieces)]
 
 
 def body(forward_samples, adjoint_samples, probe_values, owners, block_ranks, twiddle):
@@ -210,34 +226,51 @@
     shapes = [jax.ShapeDtypeStruct(shape, jnp.float32)]
     shapes += [jax.ShapeDtypeStruct(shape, jnp.bfloat16)] * (y_count - 1)
     sums = local_call(merge_kernel, shapes, kept, came)
-    sums = [sums[0]] + [turn(sums[i], "y", i) for i in range(1, y_count)]
+    came = exchange(dict(enumerate(sums[1:], 1)), "y", lambda i, k: i + k)
+    sums = [sums[0]] + came
     shape = (groups,) + shape[1:]
     shapes = [jax.ShapeDtypeStruct(shape, jnp.float32), jax.ShapeDtypeStruct(shape, jnp.bfloat16)]
     zl = lax.axis_index("zl")
     kept, sent = local_call(halve_kernel, shapes, zl[None], *sums, smem=1)
     came = lax.ppermute(sent, "zl", [(0, 1), (1, 0)])
-    rows = groups * shape[1] + 8 * piece // shape[2]
+    tail = 8 * piece // shape[2]
     shapes = [jax.ShapeDtypeStruct(shape, jnp.float32)]
-    shapes += [jax.ShapeDtypeStruct((groups, rows, shape[2]), jnp.bfloat16)]
-    place = jnp.stack([smp, block_ranks[0]])
-    partial, offers = local_call(offer_kernel, shapes, place, kept, came, twiddle, smem=1)
-    offers, pieces = lax.optimization_barrier((offers, pieces))
-    offers = lax.all_to_all(offers, "zg", 0, 0, tiled=True)
+    shapes += [jax.ShapeDtypeStruct((tail, shape[2]), jnp.bfloat16)]
+    offer = (groups * shape[1] + tail, shape[2])
+    shapes += [jax.ShapeDtypeStruct(offer, jnp.bfloat16)] * (groups - 1)
+    zg = lax.axis_index("zg")
+    place = jnp.stack([zg, smp, block_ranks[0]])
+    partial, extra, *offers = local_call(
+        offer_kernel,
+        shapes,
+        place,
+        kept,
+        came,
+        twiddle,
+        smem=1,
+        scratch=[pltpu.VMEM(shape, jnp.float32)],
+    )
+    offers = exchange(dict(enumerate(offers, 1)), "zg", lambda i, k: i ^ k)
     weights = local_call(
         weights_kernel,
-        jax.ShapeDtypeStruct((parts,) + shape, jnp.bfloat16),
-        jnp.stack([lax.axis_index("zg"), smp]),
+        jax.ShapeDtypeStruct(shape, jnp.bfloat16),
+        place,
         partial,
-        offers,
+        extra,
+        *offers,
         smem=1,
     )
-    weights = lax.all_to_all(weights, "smp", 0, 0, tiled=True)
+    others = exchange({p: weights for p in range(1, parts)}, "smp", lambda i, k: i + k)
     result = local_call(
-        field_kernel,
+        lambda *refs: field_kernel(groups, parts, *refs),
         jax.ShapeDtypeStruct((members, vectors // parts, piece), jnp.bfloat16),
+        place,
         pieces,
-        offers,
+        extra,
+        *offers,
         weights,
+        *others,
+        smem=1,
         scratch=[pltpu.VMEM((groups, vectors, piece), jnp.float32)],
         flops=2 * members * samples * vectors * piece,
     )

time: 99.1 us -> 102 us (1.029)
  the two profiles are of different devices: /device:TPU:56 before, /device:TPU:40 now
where the time goes in v5:
time: 102 us
  starting transfers between devices  29.2 us (29%)
  blocking collectives  27.8 us (27%)
  waiting for transfers between devices  27.5 us (27%)
  Pallas kernels  11.7 us (11%)
  local copies, waits for them, and re-layouts  4.33 us (4%)
    all_to_all x1, blocking collectives, body(): result = lax.all_to_all(result, GROUP, 0, 0, tiled=True)  27.8 us
    ppermute x9, waiting for transfers between devices, exchange(): came[offset] = lax.ppermute(pieces[offset], axis, pairs)  22.3 us
    ppermute x9, starting transfers between devices, exchange(): came[offset] = lax.ppermute(pieces[offset], axis, pairs)  18 us
    all_to_all x1, starting transfers between devices, body(): pieces = lax.all_to_all(pieces, GROUP, 0, 0, tiled=True)  10.1 us
    pallas_call x2, Pallas kernels, partial_coeffs(): pl.pallas_call(partial_kernel, grid=(y_count,), in_specs=[SMEM, pl.BlockS...  8.1 us
    ppermute x1, waiting for transfers between devices, body(): came = lax.ppermute(sent, 'zl', [(0, 1), (1, 0)])  5.2 us
    pallas_call x5, Pallas kernels, local_call(): pl.pallas_call(kernel, out_shape=out_shape, in_specs=[SMEM] * smem + [VME...  3.57 us
    reshape x1, local copies, waits for them, and re-layouts, body(): pieces = forward_samples.reshape(samples, members, piece).transpose(1, 0, 2)  2.41 us
  transfers between devices with their start and end apart: 12, of which 8 were waited for; matrix products, arithmetic and copies ran while one was open for 0% of the time, Pallas kernels for 6%

profile of v5, /device:TPU:40, one launch (start us, length us, event | category | flops | bytes accessed | tf_op | source)
XLA Modules:
  0.0 101.5 jit_solution(12950467189566767509)
XLA Ops:
  0.0 0.0 copy-start.4
  0.0 0.0 copy-start.1
  0.0 0.0 copy-start.2
  0.0 2.4 %copy.12 = bf16[8,16,8,512]{3,2,0,1:T(8,128)(2,1)} copy(bf16[8,16,8,512]{3,2,1,0:T(8,128)(2,1)} %bitcast.24) | data formatting | bytes 2097152 | tf_op jit(solution)/shard_map/reshape | solution.py:217
  2.4 0.1 pad_add_fusion.2.place_ref
  2.5 0.0 copy-done.4
  2.5 0.0 copy-done.1
  2.5 0.0 copy-done.2
  2.5 4.4 %shard_map.65 = f32[4,8,96,128]{3,2,1,0:T(8,128)} custom-call(s32[2]{0:T(128)S(1)} %pad_add_fusion.2.place_ref, s32[1,2048]{1,0:T(1,128)S(1)} %bitcast.20, bf16[64,2048]{1,0:T(8,128)(2,1)S(1)} %copy-done.2, bf16[192,2048]{1,0:T(8,128)(2,1)S(1)} %bitcast.18), custom_call_target="tpu_custom_call" | custom-call | flops 2147483648 | bytes 3145728 | tf_op jit(solution)/shard_map/pallas_call | solution.py:51
  6.9 0.0 collective-permute-start
  6.9 10.1 %all-to-all-start = ((bf16[16,64,512]{2,1,0:T(8,128)(2,1)}), bf16[16,64,512]{2,1,0:T(8,128)(2,1)S(1)}, u32[]{:S(2)}, u32[]{:S(2)}) async-start(bf16[16,64,512]{2,1,0:T(8,128)(2,1)} %bitcast.22), calls=%async_computation | async-start | bytes 2097152 | tf_op jit(solution)/shard_map/all_to_all | solution.py:220
  17.1 0.1 pad_add_fusion.1.place_ref
  17.2 0.0 copy-start.3
  17.2 0.9 copy-done.3
  18.1 3.7 %shard_map.64.kept_ref = f32[4,8,96,128]{3,2,1,0:T(8,128)S(1)} custom-call(s32[2]{0:T(128)S(1)} %pad_add_fusion.1.place_ref, s32[1,2048]{1,0:T(1,128)S(1)} %bitcast.21, bf16[64,2048]{1,0:T(8,128)(2,1)S(1)} %copy-done.3, bf16[192,2048]{1,0:T(8,128)(2,1)S(1)} %bitcast.19), custom_call_target="tpu_custom_call" | custom-call | flops 2147483648 | bytes 3145728 | tf_op jit(solution)/shard_map/pallas_call | solution.py:51
  21.8 0.0 copy-start
  21.8 0.0 collective-permute-done.came_ref
  21.8 0.9 shard_map.66
  22.8 1.6 %collective-permute-start.1 = (bf16[8,96,128]{2,1,0:T(8,128)(2,1)}, bf16[8,96,128]{2,1,0:T(8,128)(2,1)S(1)}, u32[]{:S(2)}, u32[]{:S(2)}) collective-permute-start(bf16[8,96,128]{2,1,0:T(8,128)(2,1)} %get-tuple-element.21), channel_id=1, source_target_pairs={{0,8},{8,16},{16,24},{24,0},{1,9},{9,17},{17,25},{25,1},{2,10},{10... | collective-permute-start | bytes 589832 | tf_op jit(solution)/shard_map/ppermute | solution.py:203
  24.3 0.9 collective-permute-start.2
  25.3 2.4 %collective-permute-start.3 = (bf16[8,96,128]{2,1,0:T(8,128)(2,1)S(1)}, bf16[8,96,128]{2,1,0:T(8,128)(2,1)S(1)}, u32[]{:S(2)}, u32[]{:S(2)}) collective-permute-start(bf16[8,96,128]{2,1,0:T(8,128)(2,1)S(1)} %get-tuple-element.23), channel_id=1, source_target_pairs={{0,24},{8,0},{16,8},{24,16},{1,25},{9,1},{17,9},{25,17},{2,26},{10... | collective-permute-start | bytes 589832 | tf_op jit(solution)/shard_map/ppermute | solution.py:203
  28.3 2.4 %collective-permute-done.1.refs_1_ = bf16[8,96,128]{2,1,0:T(8,128)(2,1)S(1)} collective-permute-done((bf16[8,96,128]{2,1,0:T(8,128)(2,1)}, bf16[8,96,128]{2,1,0:T(8,128)(2,1)S(1)}, u32[]{:S(2)}, u32[]{:S(2)}) %collective-permute-start.1) | collective-permute-done | bytes 196640 | tf_op jit(solution)/shard_map/ppermute | solution.py:203
  30.7 2.9 %collective-permute-done.2.refs_2_ = bf16[8,96,128]{2,1,0:T(8,128)(2,1)S(1)} collective-permute-done((bf16[8,96,128]{2,1,0:T(8,128)(2,1)S(1)}, bf16[8,96,128]{2,1,0:T(8,128)(2,1)S(1)}, u32[]{:S(2)}, u32[]{:S(2)}) %collective-permute-start.2) | collective-permute-done | bytes 196640 | tf_op jit(solution)/shard_map/ppermute | solution.py:203
  33.6 2.4 %collective-permute-done.3.refs_3_ = bf16[8,96,128]{2,1,0:T(8,128)(2,1)S(1)} collective-permute-done((bf16[8,96,128]{2,1,0:T(8,128)(2,1)S(1)}, bf16[8,96,128]{2,1,0:T(8,128)(2,1)S(1)}, u32[]{:S(2)}, u32[]{:S(2)}) %collective-permute-start.3) | collective-permute-done | bytes 196640 | tf_op jit(solution)/shard_map/ppermute | solution.py:203
  36.0 0.1 shard_map.67
  36.1 1.1 %collective-permute-start.4 = (bf16[4,96,128]{2,1,0:T(8,128)(2,1)S(1)}, bf16[4,96,128]{2,1,0:T(8,128)(2,1)S(1)}, u32[]{:S(2)}, u32[]{:S(2)}) collective-permute-start(bf16[4,96,128]{2,1,0:T(8,128)(2,1)S(1)} %get-tuple-element.25), channel_id=1, source_target_pairs={{0,32},{32,0},{1,33},{33,1},{2,34},{34,2},{3,35},{35,3},{4,36},{36... | collective-permute-start | bytes 294920 | tf_op jit(solution)/shard_map/ppermute | solution.py:235
  37.2 0.1 pad_add_fusion.place_ref.refs_0_
  37.3 5.2 %collective-permute-done.4.came_ref = bf16[4,96,128]{2,1,0:T(8,128)(2,1)S(1)} collective-permute-done((bf16[4,96,128]{2,1,0:T(8,128)(2,1)S(1)}, bf16[4,96,128]{2,1,0:T(8,128)(2,1)S(1)}, u32[]{:S(2)}, u32[]{:S(2)}) %collective-permute-start.4) | collective-permute-done | bytes 98336 | tf_op jit(solution)/shard_map/ppermute | solution.py:235
  42.5 0.0 copy-done
  42.5 0.6 shard_map.68
  43.1 3.6 %collective-permute-start.5 = (bf16[416,128]{1,0:T(8,128)(2,1)S(1)}, bf16[416,128]{1,0:T(8,128)(2,1)S(1)}, u32[]{:S(2)}, u32[]{:S(2)}) collective-permute-start(bf16[416,128]{1,0:T(8,128)(2,1)S(1)} %get-tuple-element.27), channel_id=1, source_target_pairs={{0,64},{64,0},{128,192},{192,128},{1,65},{65,1},{129,193},{193,129... | collective-permute-start | bytes 319496 | tf_op jit(solution)/shard_map/ppermute | solution.py:203
  46.7 4.1 %collective-permute-start.6 = (bf16[416,128]{1,0:T(8,128)(2,1)S(1)}, bf16[416,128]{1,0:T(8,128)(2,1)S(1)}, u32[]{:S(2)}, u32[]{:S(2)}) collective-permute-start(bf16[416,128]{1,0:T(8,128)(2,1)S(1)} %get-tuple-element.28), channel_id=1, source_target_pairs={{0,128},{64,192},{128,0},{192,64},{1,129},{65,193},{129,1},{193,65... | collective-permute-start | bytes 319496 | tf_op jit(solution)/shard_map/ppermute | solution.py:203
  50.8 0.0 collective-permute-start.7
  50.8 0.0 collective-permute-done.5.refs_0_.refs_3_
  50.8 6.1 %collective-permute-done.6.refs_1_.refs_4_ = bf16[416,128]{1,0:T(8,128)(2,1)S(1)} collective-permute-done((bf16[416,128]{1,0:T(8,128)(2,1)S(1)}, bf16[416,128]{1,0:T(8,128)(2,1)S(1)}, u32[]{:S(2)}, u32[]{:S(2)}) %collective-permute-start.6) | collective-permute-done | bytes 106528 | tf_op jit(solution)/shard_map/ppermute | solution.py:203
  56.9 4.0 %collective-permute-done.7.refs_2_.refs_5_ = bf16[416,128]{1,0:T(8,128)(2,1)S(1)} collective-permute-done((bf16[416,128]{1,0:T(8,128)(2,1)S(1)}, bf16[416,128]{1,0:T(8,128)(2,1)S(1)}, u32[]{:S(2)}, u32[]{:S(2)}) %collective-permute-start.7) | collective-permute-done | bytes 106528 | tf_op jit(solution)/shard_map/ppermute | solution.py:203
  60.9 0.6 shard_map.69.refs_6_
  61.5 3.0 %collective-permute-start.10 = (bf16[4,96,128]{2,1,0:T(8,128)(2,1)S(1)}, bf16[4,96,128]{2,1,0:T(8,128)(2,1)S(1)}, u32[]{:S(2)}, u32[]{:S(2)}) collective-permute-start(bf16[4,96,128]{2,1,0:T(8,128)(2,1)S(1)} %shard_map.69.refs_6_), channel_id=1, source_target_pairs={{0,3},{1,0},{2,1},{3,2},{4,7},{5,4},{6,5},{7,6},{8,11},{9,8},{10,9... | collective-permute-start | bytes 294920 | tf_op jit(solution)/shard_map/ppermute | solution.py:203
  64.5 0.0 collective-permute-start.8
  64.5 2.3 %collective-permute-start.9 = (bf16[4,96,128]{2,1,0:T(8,128)(2,1)S(1)}, bf16[4,96,128]{2,1,0:T(8,128)(2,1)S(1)}, u32[]{:S(2)}, u32[]{:S(2)}) collective-permute-start(bf16[4,96,128]{2,1,0:T(8,128)(2,1)S(1)} %shard_map.69.refs_6_), channel_id=1, source_target_pairs={{0,2},{1,3},{2,0},{3,1},{4,6},{5,7},{6,4},{7,5},{8,10},{9,11},{10,... | collective-permute-start | bytes 294920 | tf_op jit(solution)/shard_map/ppermute | solution.py:203
  66.8 0.0 all-to-all-done.refs_1_
  66.8 0.8 collective-permute-done.10.refs_9_
  67.6 3.8 %collective-permute-done.8.refs_7_ = bf16[4,96,128]{2,1,0:T(8,128)(2,1)S(1)} collective-permute-done((bf16[4,96,128]{2,1,0:T(8,128)(2,1)S(1)}, bf16[4,96,128]{2,1,0:T(8,128)(2,1)S(1)}, u32[]{:S(2)}, u32[]{:S(2)}) %collective-permute-start.8) | collective-permute-done | bytes 98336 | tf_op jit(solution)/shard_map/ppermute | solution.py:203
  71.4 0.0 collective-permute-done.9.refs_8_
  71.4 1.3 %shard_map.70 = bf16[16,48,512]{2,1,0:T(8,128)(2,1)S(1)} custom-call(s32[3]{0:T(128)S(1)} %pad_add_fusion.place_ref.refs_0_, bf16[16,64,512]{2,1,0:T(8,128)(2,1)S(1)} %all-to-all-done.refs_1_, bf16[32,128]{1,0:T(8,128)(2,1)S(1)} %get-tuple-element.26.extra_ref.refs_2_, bf16[416,128]{1,0:T(8,128)(2,1)S(1)} %collective-permute-done.5.refs_0_.refs_3_, ...), custom_call_target="tpu_custom_call" | custom-call | flops 201326592 | bytes 2097152 | tf_op jit(solution)/shard_map/pallas_call | solution.py:76
  72.7 27.8 %all_to_all.10 = bf16[16,48,512]{2,1,0:T(8,128)(2,1)S(1)} all-to-all(bf16[16,48,512]{2,1,0:T(8,128)(2,1)S(1)} %shard_map.70), channel_id=1, replica_groups=mesh['zg'=4,'zl'=2,'y'=4,'core'=2,'smp'=4] {'zg','smp'}, dimensions={0} | all-to-all | bytes 1572864 | tf_op jit(solution)/shard_map/all_to_all | solution.py:277
  100.5 1.0 copy.10
Async XLA Ops:
  0.0 2.5 %copy-start.4 = (s32[2048,1]{0,1:T(1,128)S(1)}, s32[2048,1]{0,1:T(1,128)}, u32[]{:S(2)}) copy-start(s32[2048,1]{0,1:T(1,128)} %param.9) | copy-start | bytes 24580
  0.0 2.5 %copy-start.1 = (bf16[2048,192]{0,1:T(8,128)(2,1)S(1)}, bf16[2048,192]{0,1:T(8,128)(2,1)}, u32[]{:S(2)}) copy-start(bf16[2048,192]{0,1:T(8,128)(2,1)} %param.8) | copy-start | bytes 2359300
  0.0 2.5 %copy-start.2 = (bf16[64,2048]{1,0:T(8,128)(2,1)S(1)}, bf16[64,2048]{1,0:T(8,128)(2,1)}, u32[]{:S(2)}) copy-start(bf16[64,2048]{1,0:T(8,128)(2,1)} %adjoint_ref.3) | copy-start | bytes 786436
  6.9 14.9 %collective-permute-start = (f32[4,8,96,128]{3,2,1,0:T(8,128)}, f32[4,8,96,128]{3,2,1,0:T(8,128)S(1)}, u32[]{:S(2)}, u32[]{:S(2)}) collective-permute-start(f32[4,8,96,128]{3,2,1,0:T(8,128)} %shard_map.65), channel_id=1, source_target_pairs={{0,4},{4,0},{1,5},{5,1},{2,6},{6,2},{3,7},{7,3},{8,12},{12,8},{9,1... | collective-permute-start | bytes 4718600 | tf_op jit(solution)/shard_map/ppermute | solution.py:223
  6.9 59.9 %all-to-all-start = ((bf16[16,64,512]{2,1,0:T(8,128)(2,1)}), bf16[16,64,512]{2,1,0:T(8,128)(2,1)S(1)}, u32[]{:S(2)}, u32[]{:S(2)}) async-start(bf16[16,64,512]{2,1,0:T(8,128)(2,1)} %bitcast.22), calls=%async_computation | async-start | bytes 2097152 | tf_op jit(solution)/shard_map/all_to_all | solution.py:220
  17.2 1.0 copy-start.3
  21.8 20.7 %copy-start = (f32[2,8192]{1,0:T(2,128)S(1)}, f32[2,8192]{1,0:T(2,128)}, u32[]{:S(2)}) copy-start(f32[2,8192]{1,0:T(2,128)} %twiddle_ref.1) | copy-start | bytes 196612
  22.8 7.9 %collective-permute-start.1 = (bf16[8,96,128]{2,1,0:T(8,128)(2,1)}, bf16[8,96,128]{2,1,0:T(8,128)(2,1)S(1)}, u32[]{:S(2)}, u32[]{:S(2)}) collective-permute-start(bf16[8,96,128]{2,1,0:T(8,128)(2,1)} %get-tuple-element.21), channel_id=1, source_target_pairs={{0,8},{8,16},{16,24},{24,0},{1,9},{9,17},{17,25},{25,1},{2,10},{10... | collective-permute-start | bytes 589832 | tf_op jit(solution)/shard_map/ppermute | solution.py:203
  24.3 9.3 %collective-permute-start.2 = (bf16[8,96,128]{2,1,0:T(8,128)(2,1)S(1)}, bf16[8,96,128]{2,1,0:T(8,128)(2,1)S(1)}, u32[]{:S(2)}, u32[]{:S(2)}) collective-permute-start(bf16[8,96,128]{2,1,0:T(8,128)(2,1)S(1)} %get-tuple-element.22), channel_id=1, source_target_pairs={{0,16},{8,24},{16,0},{24,8},{1,17},{9,25},{17,1},{25,9},{2,18},{10... | collective-permute-start | bytes 589832 | tf_op jit(solution)/shard_map/ppermute | solution.py:203
  25.3 10.7 %collective-permute-start.3 = (bf16[8,96,128]{2,1,0:T(8,128)(2,1)S(1)}, bf16[8,96,128]{2,1,0:T(8,128)(2,1)S(1)}, u32[]{:S(2)}, u32[]{:S(2)}) collective-permute-start(bf16[8,96,128]{2,1,0:T(8,128)(2,1)S(1)} %get-tuple-element.23), channel_id=1, source_target_pairs={{0,24},{8,0},{16,8},{24,16},{1,25},{9,1},{17,9},{25,17},{2,26},{10... | collective-permute-start | bytes 589832 | tf_op jit(solution)/shard_map/ppermute | solution.py:203
  36.1 6.4 %collective-permute-start.4 = (bf16[4,96,128]{2,1,0:T(8,128)(2,1)S(1)}, bf16[4,96,128]{2,1,0:T(8,128)(2,1)S(1)}, u32[]{:S(2)}, u32[]{:S(2)}) collective-permute-start(bf16[4,96,128]{2,1,0:T(8,128)(2,1)S(1)} %get-tuple-element.25), channel_id=1, source_target_pairs={{0,32},{32,0},{1,33},{33,1},{2,34},{34,2},{3,35},{35,3},{4,36},{36... | collective-permute-start | bytes 294920 | tf_op jit(solution)/shard_map/ppermute | solution.py:235
  43.1 7.7 %collective-permute-start.5 = (bf16[416,128]{1,0:T(8,128)(2,1)S(1)}, bf16[416,128]{1,0:T(8,128)(2,1)S(1)}, u32[]{:S(2)}, u32[]{:S(2)}) collective-permute-start(bf16[416,128]{1,0:T(8,128)(2,1)S(1)} %get-tuple-element.27), channel_id=1, source_target_pairs={{0,64},{64,0},{128,192},{192,128},{1,65},{65,1},{129,193},{193,129... | collective-permute-start | bytes 319496 | tf_op jit(solution)/shard_map/ppermute | solution.py:203
  46.7 10.2 %collective-permute-start.6 = (bf16[416,128]{1,0:T(8,128)(2,1)S(1)}, bf16[416,128]{1,0:T(8,128)(2,1)S(1)}, u32[]{:S(2)}, u32[]{:S(2)}) collective-permute-start(bf16[416,128]{1,0:T(8,128)(2,1)S(1)} %get-tuple-element.28), channel_id=1, source_target_pairs={{0,128},{64,192},{128,0},{192,64},{1,129},{65,193},{129,1},{193,65... | collective-permute-start | bytes 319496 | tf_op jit(solution)/shard_map/ppermute | solution.py:203
  50.8 10.1 %collective-permute-start.7 = (bf16[416,128]{1,0:T(8,128)(2,1)S(1)}, bf16[416,128]{1,0:T(8,128)(2,1)S(1)}, u32[]{:S(2)}, u32[]{:S(2)}) collective-permute-start(bf16[416,128]{1,0:T(8,128)(2,1)S(1)} %get-tuple-element.29), channel_id=1, source_target_pairs={{0,192},{64,128},{128,64},{192,0},{1,193},{65,129},{129,65},{193,1... | collective-permute-start | bytes 319496 | tf_op jit(solution)/shard_map/ppermute | solution.py:203
  61.5 6.1 %collective-permute-start.10 = (bf16[4,96,128]{2,1,0:T(8,128)(2,1)S(1)}, bf16[4,96,128]{2,1,0:T(8,128)(2,1)S(1)}, u32[]{:S(2)}, u32[]{:S(2)}) collective-permute-start(bf16[4,96,128]{2,1,0:T(8,128)(2,1)S(1)} %shard_map.69.refs_6_), channel_id=1, source_target_pairs={{0,3},{1,0},{2,1},{3,2},{4,7},{5,4},{6,5},{7,6},{8,11},{9,8},{10,9... | collective-permute-start | bytes 294920 | tf_op jit(solution)/shard_map/ppermute | solution.py:203
  64.5 6.9 %collective-permute-start.8 = (bf16[4,96,128]{2,1,0:T(8,128)(2,1)S(1)}, bf16[4,96,128]{2,1,0:T(8,128)(2,1)S(1)}, u32[]{:S(2)}, u32[]{:S(2)}) collective-permute-start(bf16[4,96,128]{2,1,0:T(8,128)(2,1)S(1)} %shard_map.69.refs_6_), channel_id=1, source_target_pairs={{0,1},{1,2},{2,3},{3,0},{4,5},{5,6},{6,7},{7,4},{8,9},{9,10},{10,1... | collective-permute-start | bytes 294920 | tf_op jit(solution)/shard_map/ppermute | solution.py:203
  64.5 6.9 %collective-permute-start.9 = (bf16[4,96,128]{2,1,0:T(8,128)(2,1)S(1)}, bf16[4,96,128]{2,1,0:T(8,128)(2,1)S(1)}, u32[]{:S(2)}, u32[]{:S(2)}) collective-permute-start(bf16[4,96,128]{2,1,0:T(8,128)(2,1)S(1)} %shard_map.69.refs_6_), channel_id=1, source_target_pairs={{0,2},{1,3},{2,0},{3,1},{4,6},{5,7},{6,4},{7,5},{8,10},{9,11},{10,... | collective-permute-start | bytes 294920 | tf_op jit(solution)/shard_map/ppermute | solution.py:203

commit v6 on v5

--- a/solution.py
+++ b/solution.py
@@ -250,6 +250,7 @@
         smem=1,
         scratch=[pltpu.VMEM(shape, jnp.float32)],
     )
+    *offers, pieces = lax.optimization_barrier((*offers, pieces))
     offers = exchange(dict(enumerate(offers, 1)), "zg", lambda i, k: i ^ k)
     weights = local_call(
         weights_kernel,

time: 102 us -> 97.6 us (0.957)
  Pallas kernels: 11.7 us -> 10.2 us
  starting transfers between devices: 29.2 us -> 28.1 us
  local copies, waits for them, and re-layouts: 4.33 us -> 3.29 us
    ppermute x9, starting transfers between devices: 18 us -> 16.7 us  [exchange(): came[offset] = lax.ppermute(pieces[offset], axis, pairs)]
  transfers between devices with their start and end apart: 12 -> 12, of which waited for: 8 -> 9; matrix products, arithmetic and copies ran while one was open for 0% -> 0% of each run, Pallas kernels for 6% -> 9%
where the time goes in v6:
time: 97.6 us; the launch traced here: 97 us
  starting transfers between devices  28.1 us (29%)
  waiting for transfers between devices  27.4 us (28%)
  blocking collectives  27.1 us (28%)
  Pallas kernels  10.2 us (10%)
  local copies, waits for them, and re-layouts  3.29 us (3%)
    all_to_all x1, blocking collectives, body(): result = lax.all_to_all(result, GROUP, 0, 0, tiled=True)  27.1 us
    ppermute x9, waiting for transfers between devices, exchange(): came[offset] = lax.ppermute(pieces[offset], axis, pairs)  21.7 us
    ppermute x9, starting transfers between devices, exchange(): came[offset] = lax.ppermute(pieces[offset], axis, pairs)  16.7 us
    all_to_all x1, starting transfers between devices, body(): pieces = lax.all_to_all(pieces, GROUP, 0, 0, tiled=True)  10.3 us
    pallas_call x2, Pallas kernels, partial_coeffs(): pl.pallas_call(partial_kernel, grid=(y_count,), in_specs=[SMEM, pl.BlockS...  7.34 us
    ppermute x1, waiting for transfers between devices, body(): came = lax.ppermute(sent, 'zl', [(0, 1), (1, 0)])  5.09 us
    pallas_call x5, Pallas kernels, local_call(): pl.pallas_call(kernel, out_shape=out_shape, in_specs=[SMEM] * smem + [VME...  2.9 us
    reshape x1, local copies, waits for them, and re-layouts, body(): pieces = forward_samples.reshape(samples, members, piece).transpose(1, 0, 2)  2.32 us
  transfers between devices with their start and end apart: 12, of which 9 were waited for; matrix products, arithmetic and copies ran while one was open for 0% of the time, Pallas kernels for 9%

profile of v6, /device:TPU:40, one launch (start us, length us, event | category | flops | bytes accessed | tf_op | source)
XLA Modules:
  0.0 97.0 jit_solution(8189601255761642526)
XLA Ops:
  0.0 2.3 %copy.12 = bf16[8,16,8,512]{3,2,0,1:T(8,128)(2,1)} copy(bf16[8,16,8,512]{3,2,1,0:T(8,128)(2,1)} %bitcast.23) | data formatting | bytes 2097152 | tf_op jit(solution)/shard_map/reshape | solution.py:217
  2.3 0.0 copy-start.1
  2.3 0.0 copy-start.2
  2.3 0.0 copy-start.3
  2.3 10.3 %all-to-all-start = ((bf16[16,64,512]{2,1,0:T(8,128)(2,1)}), bf16[16,64,512]{2,1,0:T(8,128)(2,1)S(1)}, u32[]{:S(2)}, u32[]{:S(2)}) async-start(bf16[16,64,512]{2,1,0:T(8,128)(2,1)} %bitcast.17), calls=%async_computation | async-start | bytes 2097152 | tf_op jit(solution)/shard_map/all_to_all | solution.py:220
  12.6 0.1 pad_add_fusion.2.place_ref
  12.7 0.0 copy-done.1
  12.7 0.0 copy-done.2
  12.7 0.0 copy-done.3
  12.7 3.7 %shard_map.65 = f32[4,8,96,128]{3,2,1,0:T(8,128)S(1)} custom-call(s32[2]{0:T(128)S(1)} %pad_add_fusion.2.place_ref, s32[1,2048]{1,0:T(1,128)S(1)} %bitcast.20, bf16[64,2048]{1,0:T(8,128)(2,1)S(1)} %copy-done.2, bf16[192,2048]{1,0:T(8,128)(2,1)S(1)} %bitcast.18), custom_call_target="tpu_custom_call" | custom-call | flops 2147483648 | bytes 3145728 | tf_op jit(solution)/shard_map/pallas_call | solution.py:51
  16.4 0.1 collective-permute-start
  16.5 0.1 pad_add_fusion.1.place_ref
  16.5 3.7 %shard_map.64.kept_ref = f32[4,8,96,128]{3,2,1,0:T(8,128)S(1)} custom-call(s32[2]{0:T(128)S(1)} %pad_add_fusion.1.place_ref, s32[1,2048]{1,0:T(1,128)S(1)} %bitcast.21, bf16[64,2048]{1,0:T(8,128)(2,1)S(1)} %copy-done.2, bf16[192,2048]{1,0:T(8,128)(2,1)S(1)} %bitcast.19), custom_call_target="tpu_custom_call" | custom-call | flops 2147483648 | bytes 3145728 | tf_op jit(solution)/shard_map/pallas_call | solution.py:51
  20.2 0.0 copy-start
  20.2 0.0 collective-permute-done.came_ref
  20.2 0.3 shard_map.66
  20.5 1.7 %collective-permute-start.1 = (bf16[8,96,128]{2,1,0:T(8,128)(2,1)S(1)}, bf16[8,96,128]{2,1,0:T(8,128)(2,1)S(1)}, u32[]{:S(2)}, u32[]{:S(2)}) collective-permute-start(bf16[8,96,128]{2,1,0:T(8,128)(2,1)S(1)} %get-tuple-element.24), channel_id=1, source_target_pairs={{0,8},{8,16},{16,24},{24,0},{1,9},{9,17},{17,25},{25,1},{2,10},{10... | collective-permute-start | bytes 589832 | tf_op jit(solution)/shard_map/ppermute | solution.py:203
  22.2 1.0 collective-permute-start.2
  23.1 2.4 %collective-permute-start.3 = (bf16[8,96,128]{2,1,0:T(8,128)(2,1)S(1)}, bf16[8,96,128]{2,1,0:T(8,128)(2,1)S(1)}, u32[]{:S(2)}, u32[]{:S(2)}) collective-permute-start(bf16[8,96,128]{2,1,0:T(8,128)(2,1)S(1)} %get-tuple-element.26), channel_id=1, source_target_pairs={{0,24},{8,0},{16,8},{24,16},{1,25},{9,1},{17,9},{25,17},{2,26},{10... | collective-permute-start | bytes 589832 | tf_op jit(solution)/shard_map/ppermute | solution.py:203
  26.2 2.1 %collective-permute-done.1.refs_1_ = bf16[8,96,128]{2,1,0:T(8,128)(2,1)S(1)} collective-permute-done((bf16[8,96,128]{2,1,0:T(8,128)(2,1)S(1)}, bf16[8,96,128]{2,1,0:T(8,128)(2,1)S(1)}, u32[]{:S(2)}, u32[]{:S(2)}) %collective-permute-start.1) | collective-permute-done | bytes 196640 | tf_op jit(solution)/shard_map/ppermute | solution.py:203
  28.3 3.2 %collective-permute-done.2.refs_2_ = bf16[8,96,128]{2,1,0:T(8,128)(2,1)S(1)} collective-permute-done((bf16[8,96,128]{2,1,0:T(8,128)(2,1)S(1)}, bf16[8,96,128]{2,1,0:T(8,128)(2,1)S(1)}, u32[]{:S(2)}, u32[]{:S(2)}) %collective-permute-start.2) | collective-permute-done | bytes 196640 | tf_op jit(solution)/shard_map/ppermute | solution.py:203
  31.5 2.8 %collective-permute-done.3.refs_3_ = bf16[8,96,128]{2,1,0:T(8,128)(2,1)S(1)} collective-permute-done((bf16[8,96,128]{2,1,0:T(8,128)(2,1)S(1)}, bf16[8,96,128]{2,1,0:T(8,128)(2,1)S(1)}, u32[]{:S(2)}, u32[]{:S(2)}) %collective-permute-start.3) | collective-permute-done | bytes 196640 | tf_op jit(solution)/shard_map/ppermute | solution.py:203
  34.2 0.1 shard_map.67
  34.3 1.1 %collective-permute-start.4 = (bf16[4,96,128]{2,1,0:T(8,128)(2,1)S(1)}, bf16[4,96,128]{2,1,0:T(8,128)(2,1)S(1)}, u32[]{:S(2)}, u32[]{:S(2)}) collective-permute-start(bf16[4,96,128]{2,1,0:T(8,128)(2,1)S(1)} %get-tuple-element.28), channel_id=1, source_target_pairs={{0,32},{32,0},{1,33},{33,1},{2,34},{34,2},{3,35},{35,3},{4,36},{36... | collective-permute-start | bytes 294920 | tf_op jit(solution)/shard_map/ppermute | solution.py:235
  35.4 0.1 pad_add_fusion.place_ref.refs_0_
  35.5 5.1 %collective-permute-done.4.came_ref = bf16[4,96,128]{2,1,0:T(8,128)(2,1)S(1)} collective-permute-done((bf16[4,96,128]{2,1,0:T(8,128)(2,1)S(1)}, bf16[4,96,128]{2,1,0:T(8,128)(2,1)S(1)}, u32[]{:S(2)}, u32[]{:S(2)}) %collective-permute-start.4) | collective-permute-done | bytes 98336 | tf_op jit(solution)/shard_map/ppermute | solution.py:235
  40.6 0.0 copy-done
  40.6 0.6 shard_map.68
  41.2 0.6 all-to-all-done.refs_1_
  41.7 0.8 collective-permute-start.5
  42.6 4.0 %collective-permute-start.6 = (bf16[416,128]{1,0:T(8,128)(2,1)S(1)}, bf16[416,128]{1,0:T(8,128)(2,1)S(1)}, u32[]{:S(2)}, u32[]{:S(2)}) collective-permute-start(bf16[416,128]{1,0:T(8,128)(2,1)S(1)} %get-tuple-element.36), channel_id=1, source_target_pairs={{0,128},{64,192},{128,0},{192,64},{1,129},{65,193},{129,1},{193,65... | collective-permute-start | bytes 319496 | tf_op jit(solution)/shard_map/ppermute | solution.py:203
  46.6 1.7 %collective-permute-start.7 = (bf16[416,128]{1,0:T(8,128)(2,1)S(1)}, bf16[416,128]{1,0:T(8,128)(2,1)S(1)}, u32[]{:S(2)}, u32[]{:S(2)}) collective-permute-start(bf16[416,128]{1,0:T(8,128)(2,1)S(1)} %get-tuple-element.37), channel_id=1, source_target_pairs={{0,192},{64,128},{128,64},{192,0},{1,193},{65,129},{129,65},{193,1... | collective-permute-start | bytes 319496 | tf_op jit(solution)/shard_map/ppermute | solution.py:203
  48.2 0.4 collective-permute-done.5.refs_0_.refs_3_
  48.6 4.5 %collective-permute-done.6.refs_1_.refs_4_ = bf16[416,128]{1,0:T(8,128)(2,1)S(1)} collective-permute-done((bf16[416,128]{1,0:T(8,128)(2,1)S(1)}, bf16[416,128]{1,0:T(8,128)(2,1)S(1)}, u32[]{:S(2)}, u32[]{:S(2)}) %collective-permute-start.6) | collective-permute-done | bytes 106528 | tf_op jit(solution)/shard_map/ppermute | solution.py:203
  53.1 3.9 %collective-permute-done.7.refs_2_.refs_5_ = bf16[416,128]{1,0:T(8,128)(2,1)S(1)} collective-permute-done((bf16[416,128]{1,0:T(8,128)(2,1)S(1)}, bf16[416,128]{1,0:T(8,128)(2,1)S(1)}, u32[]{:S(2)}, u32[]{:S(2)}) %collective-permute-start.7) | collective-permute-done | bytes 106528 | tf_op jit(solution)/shard_map/ppermute | solution.py:203
  57.0 0.6 shard_map.69.refs_6_
  57.6 2.9 %collective-permute-start.10 = (bf16[4,96,128]{2,1,0:T(8,128)(2,1)S(1)}, bf16[4,96,128]{2,1,0:T(8,128)(2,1)S(1)}, u32[]{:S(2)}, u32[]{:S(2)}) collective-permute-start(bf16[4,96,128]{2,1,0:T(8,128)(2,1)S(1)} %shard_map.69.refs_6_), channel_id=1, source_target_pairs={{0,3},{1,0},{2,1},{3,2},{4,7},{5,4},{6,5},{7,6},{8,11},{9,8},{10,9... | collective-permute-start | bytes 294920 | tf_op jit(solution)/shard_map/ppermute | solution.py:203
  60.5 0.0 collective-permute-start.8
  60.5 2.3 %collective-permute-start.9 = (bf16[4,96,128]{2,1,0:T(8,128)(2,1)S(1)}, bf16[4,96,128]{2,1,0:T(8,128)(2,1)S(1)}, u32[]{:S(2)}, u32[]{:S(2)}) collective-permute-start(bf16[4,96,128]{2,1,0:T(8,128)(2,1)S(1)} %shard_map.69.refs_6_), channel_id=1, source_target_pairs={{0,2},{1,3},{2,0},{3,1},{4,6},{5,7},{6,4},{7,5},{8,10},{9,11},{10,... | collective-permute-start | bytes 294920 | tf_op jit(solution)/shard_map/ppermute | solution.py:203
  62.7 0.0 collective-permute-done.10.refs_9_
  62.7 4.9 %collective-permute-done.8.refs_7_ = bf16[4,96,128]{2,1,0:T(8,128)(2,1)S(1)} collective-permute-done((bf16[4,96,128]{2,1,0:T(8,128)(2,1)S(1)}, bf16[4,96,128]{2,1,0:T(8,128)(2,1)S(1)}, u32[]{:S(2)}, u32[]{:S(2)}) %collective-permute-start.8) | collective-permute-done | bytes 98336 | tf_op jit(solution)/shard_map/ppermute | solution.py:203
  67.6 0.0 collective-permute-done.9.refs_8_
  67.6 1.3 %shard_map.70 = bf16[16,48,512]{2,1,0:T(8,128)(2,1)S(1)} custom-call(s32[3]{0:T(128)S(1)} %pad_add_fusion.place_ref.refs_0_, bf16[16,64,512]{2,1,0:T(8,128)(2,1)S(1)} %all-to-all-done.refs_1_, bf16[32,128]{1,0:T(8,128)(2,1)S(1)} %get-tuple-element.34.extra_ref.refs_2_, bf16[416,128]{1,0:T(8,128)(2,1)S(1)} %collective-permute-done.5.refs_0_.refs_3_, ...), custom_call_target="tpu_custom_call" | custom-call | flops 201326592 | bytes 2097152 | tf_op jit(solution)/shard_map/pallas_call | solution.py:76
  69.0 27.1 %all_to_all.10 = bf16[16,48,512]{2,1,0:T(8,128)(2,1)S(1)} all-to-all(bf16[16,48,512]{2,1,0:T(8,128)(2,1)S(1)} %shard_map.70), channel_id=1, replica_groups=mesh['zg'=4,'zl'=2,'y'=4,'core'=2,'smp'=4] {'zg','smp'}, dimensions={0} | all-to-all | bytes 1572864 | tf_op jit(solution)/shard_map/all_to_all | solution.py:278
  96.1 1.0 copy.10
Async XLA Ops:
  2.3 10.4 %copy-start.1 = (bf16[2048,192]{0,1:T(8,128)(2,1)S(1)}, bf16[2048,192]{0,1:T(8,128)(2,1)}, u32[]{:S(2)}) copy-start(bf16[2048,192]{0,1:T(8,128)(2,1)} %param.8) | copy-start | bytes 2359300
  2.3 10.4 %copy-start.2 = (bf16[64,2048]{1,0:T(8,128)(2,1)S(1)}, bf16[64,2048]{1,0:T(8,128)(2,1)}, u32[]{:S(2)}) copy-start(bf16[64,2048]{1,0:T(8,128)(2,1)} %adjoint_ref.3) | copy-start | bytes 786436
  2.3 10.4 %copy-start.3 = (s32[2048,1]{0,1:T(1,128)S(1)}, s32[2048,1]{0,1:T(1,128)}, u32[]{:S(2)}) copy-start(s32[2048,1]{0,1:T(1,128)} %param.9) | copy-start | bytes 24580
  2.3 39.4 %all-to-all-start = ((bf16[16,64,512]{2,1,0:T(8,128)(2,1)}), bf16[16,64,512]{2,1,0:T(8,128)(2,1)S(1)}, u32[]{:S(2)}, u32[]{:S(2)}) async-start(bf16[16,64,512]{2,1,0:T(8,128)(2,1)} %bitcast.17), calls=%async_computation | async-start | bytes 2097152 | tf_op jit(solution)/shard_map/all_to_all | solution.py:220
  16.4 3.9 %collective-permute-start = (f32[4,8,96,128]{3,2,1,0:T(8,128)S(1)}, f32[4,8,96,128]{3,2,1,0:T(8,128)S(1)}, u32[]{:S(2)}, u32[]{:S(2)}) collective-permute-start(f32[4,8,96,128]{3,2,1,0:T(8,128)S(1)} %shard_map.65), channel_id=1, source_target_pairs={{0,4},{4,0},{1,5},{5,1},{2,6},{6,2},{3,7},{7,3},{8,12},{12,8},{9,1... | collective-permute-start | bytes 4718600 | tf_op jit(solution)/shard_map/ppermute | solution.py:223
  20.2 20.4 %copy-start = (f32[2,8192]{1,0:T(2,128)S(1)}, f32[2,8192]{1,0:T(2,128)}, u32[]{:S(2)}) copy-start(f32[2,8192]{1,0:T(2,128)} %twiddle_ref.1) | copy-start | bytes 196612
  20.5 7.8 %collective-permute-start.1 = (bf16[8,96,128]{2,1,0:T(8,128)(2,1)S(1)}, bf16[8,96,128]{2,1,0:T(8,128)(2,1)S(1)}, u32[]{:S(2)}, u32[]{:S(2)}) collective-permute-start(bf16[8,96,128]{2,1,0:T(8,128)(2,1)S(1)} %get-tuple-element.24), channel_id=1, source_target_pairs={{0,8},{8,16},{16,24},{24,0},{1,9},{9,17},{17,25},{25,1},{2,10},{10... | collective-permute-start | bytes 589832 | tf_op jit(solution)/shard_map/ppermute | solution.py:203
  22.2 9.3 %collective-permute-start.2 = (bf16[8,96,128]{2,1,0:T(8,128)(2,1)S(1)}, bf16[8,96,128]{2,1,0:T(8,128)(2,1)S(1)}, u32[]{:S(2)}, u32[]{:S(2)}) collective-permute-start(bf16[8,96,128]{2,1,0:T(8,128)(2,1)S(1)} %get-tuple-element.25), channel_id=1, source_target_pairs={{0,16},{8,24},{16,0},{24,8},{1,17},{9,25},{17,1},{25,9},{2,18},{10... | collective-permute-start | bytes 589832 | tf_op jit(solution)/shard_map/ppermute | solution.py:203
  23.1 11.1 %collective-permute-start.3 = (bf16[8,96,128]{2,1,0:T(8,128)(2,1)S(1)}, bf16[8,96,128]{2,1,0:T(8,128)(2,1)S(1)}, u32[]{:S(2)}, u32[]{:S(2)}) collective-permute-start(bf16[8,96,128]{2,1,0:T(8,128)(2,1)S(1)} %get-tuple-element.26), channel_id=1, source_target_pairs={{0,24},{8,0},{16,8},{24,16},{1,25},{9,1},{17,9},{25,17},{2,26},{10... | collective-permute-start | bytes 589832 | tf_op jit(solution)/shard_map/ppermute | solution.py:203
  34.3 6.2 %collective-permute-start.4 = (bf16[4,96,128]{2,1,0:T(8,128)(2,1)S(1)}, bf16[4,96,128]{2,1,0:T(8,128)(2,1)S(1)}, u32[]{:S(2)}, u32[]{:S(2)}) collective-permute-start(bf16[4,96,128]{2,1,0:T(8,128)(2,1)S(1)} %get-tuple-element.28), channel_id=1, source_target_pairs={{0,32},{32,0},{1,33},{33,1},{2,34},{34,2},{3,35},{35,3},{4,36},{36... | collective-permute-start | bytes 294920 | tf_op jit(solution)/shard_map/ppermute | solution.py:235
  41.7 6.9 %collective-permute-start.5 = (bf16[416,128]{1,0:T(8,128)(2,1)S(1)}, bf16[416,128]{1,0:T(8,128)(2,1)S(1)}, u32[]{:S(2)}, u32[]{:S(2)}) collective-permute-start(bf16[416,128]{1,0:T(8,128)(2,1)S(1)} %get-tuple-element.35), channel_id=1, source_target_pairs={{0,64},{64,0},{128,192},{192,128},{1,65},{65,1},{129,193},{193,129... | collective-permute-start | bytes 319496 | tf_op jit(solution)/shard_map/ppermute | solution.py:203
  42.6 10.5 %collective-permute-start.6 = (bf16[416,128]{1,0:T(8,128)(2,1)S(1)}, bf16[416,128]{1,0:T(8,128)(2,1)S(1)}, u32[]{:S(2)}, u32[]{:S(2)}) collective-permute-start(bf16[416,128]{1,0:T(8,128)(2,1)S(1)} %get-tuple-element.36), channel_id=1, source_target_pairs={{0,128},{64,192},{128,0},{192,64},{1,129},{65,193},{129,1},{193,65... | collective-permute-start | bytes 319496 | tf_op jit(solution)/shard_map/ppermute | solution.py:203
  46.6 10.4 %collective-permute-start.7 = (bf16[416,128]{1,0:T(8,128)(2,1)S(1)}, bf16[416,128]{1,0:T(8,128)(2,1)S(1)}, u32[]{:S(2)}, u32[]{:S(2)}) collective-permute-start(bf16[416,128]{1,0:T(8,128)(2,1)S(1)} %get-tuple-element.37), channel_id=1, source_target_pairs={{0,192},{64,128},{128,64},{192,0},{1,193},{65,129},{129,65},{193,1... | collective-permute-start | bytes 319496 | tf_op jit(solution)/shard_map/ppermute | solution.py:203
  57.6 5.1 %collective-permute-start.10 = (bf16[4,96,128]{2,1,0:T(8,128)(2,1)S(1)}, bf16[4,96,128]{2,1,0:T(8,128)(2,1)S(1)}, u32[]{:S(2)}, u32[]{:S(2)}) collective-permute-start(bf16[4,96,128]{2,1,0:T(8,128)(2,1)S(1)} %shard_map.69.refs_6_), channel_id=1, source_target_pairs={{0,3},{1,0},{2,1},{3,2},{4,7},{5,4},{6,5},{7,6},{8,11},{9,8},{10,9... | collective-permute-start | bytes 294920 | tf_op jit(solution)/shard_map/ppermute | solution.py:203
  60.5 7.2 %collective-permute-start.8 = (bf16[4,96,128]{2,1,0:T(8,128)(2,1)S(1)}, bf16[4,96,128]{2,1,0:T(8,128)(2,1)S(1)}, u32[]{:S(2)}, u32[]{:S(2)}) collective-permute-start(bf16[4,96,128]{2,1,0:T(8,128)(2,1)S(1)} %shard_map.69.refs_6_), channel_id=1, source_target_pairs={{0,1},{1,2},{2,3},{3,0},{4,5},{5,6},{6,7},{7,4},{8,9},{9,10},{10,1... | collective-permute-start | bytes 294920 | tf_op jit(solution)/shard_map/ppermute | solution.py:203
  60.5 7.2 %collective-permute-start.9 = (bf16[4,96,128]{2,1,0:T(8,128)(2,1)S(1)}, bf16[4,96,128]{2,1,0:T(8,128)(2,1)S(1)}, u32[]{:S(2)}, u32[]{:S(2)}) collective-permute-start(bf16[4,96,128]{2,1,0:T(8,128)(2,1)S(1)} %shard_map.69.refs_6_), channel_id=1, source_target_pairs={{0,2},{1,3},{2,0},{3,1},{4,6},{5,7},{6,4},{7,5},{8,10},{9,11},{10,... | collective-permute-start | bytes 294920 | tf_op jit(solution)/shard_map/ppermute | solution.py:203

commit v7 on v6

--- a/solution.py
+++ b/solution.py
@@ -13,63 +13,56 @@
 SMEM = pl.BlockSpec(memory_space=pltpu.SMEM)
 
 
-def partial_kernel(place_ref, owners_ref, adjoint_ref, probes_ref, out_ref, masked, wide):
-    step = pl.program_id(0)
-    y_count = pl.num_programs(0)
-    z_count = out_ref.shape[1]
+def split_kernel(source_ref, out_ref, sems):
+    pieces, _, points = out_ref.shape
+    copies = [
+        pltpu.make_async_copy(source_ref.at[:, pl.ds(i * points, points)], out_ref.at[i], sems.at[i])
+        for i in range(pieces)
+    ]
+    for copy in copies:
+        copy.start()
+    for copy in copies:
+        copy.wait()
+
+
+def split(source, pieces):
+    rows, points = source.shape
+    return pl.pallas_call(
+        split_kernel,
+        out_shape=jax.ShapeDtypeStruct((pieces, rows, points // pieces), source.dtype),
+        in_specs=[pl.BlockSpec(memory_space=pl.ANY)],
+        out_specs=VMEM,
+        scratch_shapes=[pltpu.SemaphoreType.DMA((pieces,))],
+        compiler_params=pltpu.CompilerParams(vmem_limit_bytes=56 * MIB),
+        cost_estimate=pl.CostEstimate(flops=0, bytes_accessed=2 * MIB, transcendentals=0),
+    )(source)
+
+
+def partial_kernel(y_count, offset, other, place_ref, owners_ref, adjoint_ref, wide_ref, *refs):
+    out_ref, masked = refs[-2:]
     samples = adjoint_ref.shape[0]
-    vectors = probes_ref.shape[0]
-
-    @pl.when(step == 0)
-    def _():
-        wide[:vectors, :] = probes_ref[...]
-        wide[vectors:, :] = probes_ref[128:, :]
-
+    z_count = out_ref.shape[0]
     own = owners_ref[...]
     adjoint = adjoint_ref[...]
-    y = lax.rem(place_ref[0] + step, y_count)
-    for offset in range(z_count):
-        owner = (offset * y_count + y) * 2 + place_ref[1]
-        hot = jnp.where(own == owner, 1.0, 0.0).astype(jnp.bfloat16)
-        masked[offset * samples:(offset + 1) * samples, :] = adjoint * hot
+    y = lax.rem(place_ref[0] + offset, y_count)
+    core = 1 - place_ref[1] if other else place_ref[1]
+    for z in range(z_count):
+        hot = jnp.where(own == (z * y_count + y) * 2 + core, 1.0, 0.0).astype(jnp.bfloat16)
+        masked[z * samples:(z + 1) * samples, :] = adjoint * hot
     product = lax.dot_general(
-        masked[...], wide[...], (((1,), (1,)), ((), ())), preferred_element_type=jnp.float32
+        masked[...], wide_ref[...], (((1,), (1,)), ((), ())), preferred_element_type=jnp.float32
     )
     half = samples // 2
     low = lax.broadcasted_iota(jnp.int32, (half, 128), 1) < 64
-    for offset in range(z_count):
-        block = product[offset * samples:(offset + 1) * samples, :]
-        out_ref[0, offset, :samples, :] = block[:, :128]
-        out_ref[0, offset, samples:, :] = jnp.where(low, block[:half, 128:], block[half:, 128:])
-
-
-def partial_coeffs(place, owners, adjoint, probes):
-    samples, rows = adjoint.shape
-    vectors = probes.shape[0]
-    y_count, z_count = lax.axis_size("y"), lax.axis_size(Z_AXES)
-    packed = samples * vectors // 128
-    return pl.pallas_call(
-        partial_kernel,
-        grid=(y_count,),
-        in_specs=[
-            SMEM,
-            pl.BlockSpec((1, rows), lambda i: (0, 0)),
-            pl.BlockSpec((samples, rows), lambda i: (0, 0)),
-            pl.BlockSpec((vectors, rows), lambda i: (0, 0)),
-        ],
-        out_specs=pl.BlockSpec((1, z_count, packed, 128), lambda i: (i, 0, 0, 0)),
-        out_shape=jax.ShapeDtypeStruct((y_count, z_count, packed, 128), jnp.float32),
-        scratch_shapes=[
-            pltpu.VMEM((z_count * samples, rows), jnp.bfloat16),
-            pltpu.VMEM((256, rows), jnp.bfloat16),
-        ],
-        compiler_params=pltpu.CompilerParams(vmem_limit_bytes=24 * MIB),
-        cost_estimate=pl.CostEstimate(
-            flops=2 * y_count * z_count * samples * rows * 256,
-            bytes_accessed=3 * MIB,
-            transcendentals=0,
-        ),
-    )(place, owners, adjoint, probes)
+    for z in range(z_count):
+        block = product[z * samples:(z + 1) * samples, :]
+        head = block[:, :128]
+        tail = jnp.where(low, block[:half, 128:], block[half:, 128:])
+        if not other:
+            head = head + refs[0][z, :samples, :]
+            tail = tail + refs[0][z, samples:, :]
+        out_ref[z, :samples, :] = head.astype(out_ref.dtype)
+        out_ref[z, samples:, :] = tail.astype(out_ref.dtype)
 
 
 def local_call(kernel, out_shape, *args, smem=0, scratch=(), flops=0):
@@ -82,12 +75,6 @@
         compiler_params=pltpu.CompilerParams(vmem_limit_bytes=24 * MIB),
         cost_estimate=pl.CostEstimate(flops=flops, bytes_accessed=2 * MIB, transcendentals=0),
     )(*args)
-
-
-def merge_kernel(kept_ref, came_ref, own_ref, *out_refs):
-    own_ref[...] = kept_ref[0] + came_ref[0]
-    for offset, out_ref in enumerate(out_refs, 1):
-        out_ref[...] = (kept_ref[offset] + came_ref[offset]).astype(out_ref.dtype)
 
 
 def halve_kernel(place_ref, *refs):
@@ -214,20 +201,41 @@
     smp = lax.axis_index("smp")
     y, core = lax.axis_index("y"), lax.axis_index("core")
 
-    pieces = forward_samples.reshape(samples, members, piece).transpose(1, 0, 2)
+    pieces = split(forward_samples, members)
     own, probes = owners.T, probe_values.T
     pieces, own = lax.optimization_barrier((pieces, own))
     pieces = lax.all_to_all(pieces, GROUP, 0, 0, tiled=True)
 
-    sent = partial_coeffs(jnp.stack([y, 1 - core]), own, adjoint_samples, probes)
-    came = lax.ppermute(sent, "core", [(0, 1), (1, 0)])
-    kept = partial_coeffs(jnp.stack([y, core]), own, adjoint_samples, probes)
-    shape = kept.shape[1:]
-    shapes = [jax.ShapeDtypeStruct(shape, jnp.float32)]
-    shapes += [jax.ShapeDtypeStruct(shape, jnp.bfloat16)] * (y_count - 1)
-    sums = local_call(merge_kernel, shapes, kept, came)
-    came = exchange(dict(enumerate(sums[1:], 1)), "y", lambda i, k: i + k)
-    sums = [sums[0]] + came
+    wide = jnp.concatenate([probes, probes[128:]], axis=0)
+    shape = (lax.axis_size(Z_AXES), samples * vectors // 128, 128)
+    place = jnp.stack([y, core])
+
+    def partial(offset, other, kind, *came):
+        return local_call(
+            lambda *refs: partial_kernel(y_count, offset, other, *refs),
+            jax.ShapeDtypeStruct(shape, kind),
+            place,
+            own,
+            adjoint_samples,
+            wide,
+            *came,
+            smem=1,
+            scratch=[pltpu.VMEM((shape[0] * samples, own.shape[1]), jnp.bfloat16)],
+            flops=2 * shape[0] * samples * own.shape[1] * 256,
+        )
+
+    order = sorted(range(y_count), key=lambda k: (k == 0, abs(k - y_count // 2)))
+    came = {}
+    for offset in order:
+        sent = partial(offset, True, jnp.float32)
+        came[offset] = lax.ppermute(sent, "core", [(0, 1), (1, 0)])
+    sums = []
+    for offset in order:
+        kind = jnp.bfloat16 if offset else jnp.float32
+        merged = partial(offset, False, kind, came[offset])
+        route = [(i, (i + offset) % y_count) for i in range(y_count)]
+        sums.append(lax.ppermute(merged, "y", route) if offset else merged)
+    sums = sums[-1:] + sums[:-1]
     shape = (groups,) + shape[1:]
     shapes = [jax.ShapeDtypeStruct(shape, jnp.float32), jax.ShapeDtypeStruct(shape, jnp.bfloat16)]
     zl = lax.axis_index("zl")

time: 97.6 us -> 95.8 us (0.982)
  Pallas kernels: 10.2 us -> 17.4 us
  waiting for transfers between devices: 27.4 us -> 20.4 us
  blocking collectives: 27.1 us -> 24.2 us
  local copies, waits for them, and re-layouts: 3.29 us -> 1.86 us
  starting transfers between devices: 28.1 us -> 29.5 us
    pallas_call x5 -> x12, Pallas kernels: 2.9 us -> 15 us  [local_call(): pl.pallas_call(kernel, out_shape=out_shape, in_specs=[SMEM] * smem + [VME...]
    ppermute x9 -> x6, waiting for transfers between devices: 21.7 us -> 11.9 us  [exchange(): came[offset] = lax.ppermute(pieces[offset], axis, pairs)]
    ppermute x1 -> x7, starting transfers between devices: 0.09 us -> 5.67 us  [the longest x3 4.41 us: body(): sums.append(lax.ppermute(merged, 'y', route) if offset else merged)]
    ppermute x1 -> x7, waiting for transfers between devices: 0.01 us -> 5 us  [the longest x3 4.99 us: body(): sums.append(lax.ppermute(merged, 'y', route) if offset else merged)]
    pallas_call x2 -> x1, Pallas kernels: 7.34 us -> 2.36 us  [split(): pl.pallas_call(split_kernel, out_shape=jax.ShapeDtypeStruct((pieces, rows...]
    ppermute x9 -> x6, starting transfers between devices: 16.7 us -> 12.5 us  [exchange(): came[offset] = lax.ppermute(pieces[offset], axis, pairs)]
    all_to_all x1, blocking collectives: 27.1 us -> 24.2 us  [body(): result = lax.all_to_all(result, GROUP, 0, 0, tiled=True)]
    reshape x1 -> x0, local copies, waits for them, and re-layouts: 2.32 us -> none  [body(): pieces = forward_samples.reshape(samples, members, piece).transpose(1, 0, 2)]
  transfers between devices with their start and end apart: 12 -> 15, of which waited for: 9 -> 8; matrix products, arithmetic and copies ran while one was open for 0% -> 0% of each run, Pallas kernels for 9% -> 14%
where the time goes in v7:
time: 95.8 us; the launch traced here: 94.4 us
  starting transfers between devices  29.5 us (31%)
  blocking collectives  24.2 us (25%)
  waiting for transfers between devices  20.4 us (21%)
  Pallas kernels  17.4 us (18%)
  local copies, waits for them, and re-layouts  1.86 us (2%)
    all_to_all x1, blocking collectives, body(): result = lax.all_to_all(result, GROUP, 0, 0, tiled=True)  24.2 us
    pallas_call x12, Pallas kernels, local_call(): pl.pallas_call(kernel, out_shape=out_shape, in_specs=[SMEM] * smem + [VME...  15 us
    ppermute x6, starting transfers between devices, exchange(): came[offset] = lax.ppermute(pieces[offset], axis, pairs)  12.5 us
    ppermute x6, waiting for transfers between devices, exchange(): came[offset] = lax.ppermute(pieces[offset], axis, pairs)  11.9 us
    all_to_all x1, starting transfers between devices, body(): pieces = lax.all_to_all(pieces, GROUP, 0, 0, tiled=True)  10.3 us
    ppermute x3, waiting for transfers between devices, body(): sums.append(lax.ppermute(merged, 'y', route) if offset else merged)  4.99 us
    ppermute x3, starting transfers between devices, body(): sums.append(lax.ppermute(merged, 'y', route) if offset else merged)  4.41 us
    ppermute x1, waiting for transfers between devices, body(): came = lax.ppermute(sent, 'zl', [(0, 1), (1, 0)])  3.53 us
  transfers between devices with their start and end apart: 15, of which 8 were waited for; matrix products, arithmetic and copies ran while one was open for 0% of the time, Pallas kernels for 14%

profile of v7, /device:TPU:40, one launch (start us, length us, event | category | flops | bytes accessed | tf_op | source)
XLA Modules:
  0.0 94.4 jit_solution(14193629621434246368)
XLA Ops:
  0.0 2.4 %shard_map.64 = bf16[16,64,512]{2,1,0:T(8,128)(2,1)} custom-call(bf16[64,8192]{1,0:T(8,128)(2,1)} %source_ref.1), custom_call_target="tpu_custom_call" | custom-call | bytes 2097152 | tf_op jit(solution)/shard_map/pallas_call | solution.py:30
  2.4 0.0 copy-start.3
  2.4 10.3 %all-to-all-start = ((bf16[16,64,512]{2,1,0:T(8,128)(2,1)}), bf16[16,64,512]{2,1,0:T(8,128)(2,1)S(1)}, u32[]{:S(2)}, u32[]{:S(2)}) async-start(bf16[16,64,512]{2,1,0:T(8,128)(2,1)} %shard_map.64), calls=%async_computation | async-start | bytes 2097152 | tf_op jit(solution)/shard_map/all_to_all | solution.py:207
  12.7 0.1 pad_add_fusion.1.refs_0_
  12.8 0.1 pad_maximum_fusion.refs_3_
  12.9 0.9 copy-done
  13.7 1.3 %shard_map.69 = f32[8,96,128]{2,1,0:T(8,128)S(1)} custom-call(s32[2]{0:T(128)S(1)} %pad_add_fusion.1.refs_0_, s32[1,2048]{1,0:T(1,128)S(1)} %bitcast.10, bf16[64,2048]{1,0:T(8,128)(2,1)S(1)} %copy-done, bf16[256,2048]{1,0:T(8,128)(2,1)S(1)} %pad_maximum_fusion.refs_3_), custom_call_target="tpu_custom_call" | custom-call | flops 536870912 | bytes 2097152 | tf_op jit(solution)/shard_map/pallas_call | solution.py:69
  15.0 0.1 collective-permute-start.3
  15.1 1.3 %shard_map.71 = f32[8,96,128]{2,1,0:T(8,128)S(1)} custom-call(s32[2]{0:T(128)S(1)} %pad_add_fusion.1.refs_0_, s32[1,2048]{1,0:T(1,128)S(1)} %bitcast.11, bf16[64,2048]{1,0:T(8,128)(2,1)S(1)} %copy-done, bf16[256,2048]{1,0:T(8,128)(2,1)S(1)} %pad_maximum_fusion.refs_3_), custom_call_target="tpu_custom_call" | custom-call | flops 536870912 | bytes 2097152 | tf_op jit(solution)/shard_map/pallas_call | solution.py:69
  16.4 0.6 collective-permute-start.5
  17.0 1.3 %shard_map.67 = f32[8,96,128]{2,1,0:T(8,128)S(1)} custom-call(s32[2]{0:T(128)S(1)} %pad_add_fusion.1.refs_0_, s32[1,2048]{1,0:T(1,128)S(1)} %bitcast.12, bf16[64,2048]{1,0:T(8,128)(2,1)S(1)} %copy-done, bf16[256,2048]{1,0:T(8,128)(2,1)S(1)} %pad_maximum_fusion.refs_3_), custom_call_target="tpu_custom_call" | custom-call | flops 536870912 | bytes 2097152 | tf_op jit(solution)/shard_map/pallas_call | solution.py:69
  18.3 0.1 collective-permute-start.1
  18.4 2.0 %shard_map.65 = f32[8,96,128]{2,1,0:T(8,128)} custom-call(s32[2]{0:T(128)S(1)} %pad_add_fusion.1.refs_0_, s32[1,2048]{1,0:T(1,128)S(1)} %bitcast.13, bf16[64,2048]{1,0:T(8,128)(2,1)S(1)} %copy-done, bf16[256,2048]{1,0:T(8,128)(2,1)S(1)} %pad_maximum_fusion.refs_3_), custom_call_target="tpu_custom_call" | custom-call | flops 536870912 | bytes 2097152 | tf_op jit(solution)/shard_map/pallas_call | solution.py:69
  20.4 0.5 collective-permute-start
  20.9 0.0 collective-permute-done.3.refs_4_
  20.9 1.3 %shard_map.70 = bf16[8,96,128]{2,1,0:T(8,128)(2,1)S(1)} custom-call(s32[2]{0:T(128)S(1)} %pad_add_fusion.1.refs_0_, s32[1,2048]{1,0:T(1,128)S(1)} %bitcast.14, bf16[64,2048]{1,0:T(8,128)(2,1)S(1)} %copy-done, bf16[256,2048]{1,0:T(8,128)(2,1)S(1)} %pad_maximum_fusion.refs_3_, f32[8,96,128]{2,1,0:T(8,128)S(1)} %collective-permute-done.3.refs_4_), custom_call_target="tpu_custom_call" | custom-call | flops 536870912 | bytes 2097152 | tf_op jit(solution)/shard_map/pallas_call | solution.py:69
  22.2 1.7 %collective-permute-start.4 = (bf16[8,96,128]{2,1,0:T(8,128)(2,1)S(1)}, bf16[8,96,128]{2,1,0:T(8,128)(2,1)S(1)}, u32[]{:S(2)}, u32[]{:S(2)}) collective-permute-start(bf16[8,96,128]{2,1,0:T(8,128)(2,1)S(1)} %shard_map.70), channel_id=1, source_target_pairs={{0,8},{8,16},{16,24},{24,0},{1,9},{9,17},{17,25},{25,1},{2,10},{10... | collective-permute-start | bytes 589832 | tf_op jit(solution)/shard_map/ppermute | solution.py:237
  23.9 0.0 collective-permute-done.5.refs_4_
  23.9 2.0 %shard_map.72 = bf16[8,96,128]{2,1,0:T(8,128)(2,1)} custom-call(s32[2]{0:T(128)S(1)} %pad_add_fusion.1.refs_0_, s32[1,2048]{1,0:T(1,128)S(1)} %bitcast.15, bf16[64,2048]{1,0:T(8,128)(2,1)S(1)} %copy-done, bf16[256,2048]{1,0:T(8,128)(2,1)S(1)} %pad_maximum_fusion.refs_3_, f32[8,96,128]{2,1,0:T(8,128)S(1)} %collective-permute-done.5.refs_4_), custom_call_target="tpu_custom_call" | custom-call | flops 536870912 | bytes 2097152 | tf_op jit(solution)/shard_map/pallas_call | solution.py:69
  25.8 0.4 collective-permute-start.6
  26.3 0.0 collective-permute-done.1.refs_4_
  26.3 2.0 %shard_map.68 = bf16[8,96,128]{2,1,0:T(8,128)(2,1)} custom-call(s32[2]{0:T(128)S(1)} %pad_add_fusion.1.refs_0_, s32[1,2048]{1,0:T(1,128)S(1)} %bitcast.16, bf16[64,2048]{1,0:T(8,128)(2,1)S(1)} %copy-done, bf16[256,2048]{1,0:T(8,128)(2,1)S(1)} %pad_maximum_fusion.refs_3_, f32[8,96,128]{2,1,0:T(8,128)S(1)} %collective-permute-done.1.refs_4_), custom_call_target="tpu_custom_call" | custom-call | flops 536870912 | bytes 2097152 | tf_op jit(solution)/shard_map/pallas_call | solution.py:69
  28.3 2.3 %collective-permute-start.2 = (bf16[8,96,128]{2,1,0:T(8,128)(2,1)}, bf16[8,96,128]{2,1,0:T(8,128)(2,1)S(1)}, u32[]{:S(2)}, u32[]{:S(2)}) collective-permute-start(bf16[8,96,128]{2,1,0:T(8,128)(2,1)} %shard_map.68), channel_id=1, source_target_pairs={{0,16},{8,24},{16,0},{24,8},{1,17},{9,25},{17,1},{25,9},{2,18},{10... | collective-permute-start | bytes 589832 | tf_op jit(solution)/shard_map/ppermute | solution.py:237
  31.2 0.0 copy-start.1
  31.2 1.3 %shard_map.66.refs_0_ = f32[8,96,128]{2,1,0:T(8,128)S(1)} custom-call(s32[2]{0:T(128)S(1)} %pad_add_fusion.1.refs_0_, s32[1,2048]{1,0:T(1,128)S(1)} %bitcast.17, bf16[64,2048]{1,0:T(8,128)(2,1)S(1)} %copy-done, bf16[256,2048]{1,0:T(8,128)(2,1)S(1)} %pad_maximum_fusion.refs_3_, f32[8,96,128]{2,1,0:T(8,128)S(1)} %collective-permute-done.refs_4_), custom_call_target="tpu_custom_call" | custom-call | flops 536870912 | bytes 2097152 | tf_op jit(solution)/shard_map/pallas_call | solution.py:69
  32.5 0.6 collective-permute-done.6.refs_3_
  33.1 4.4 %collective-permute-done.2.refs_1_ = bf16[8,96,128]{2,1,0:T(8,128)(2,1)S(1)} collective-permute-done((bf16[8,96,128]{2,1,0:T(8,128)(2,1)}, bf16[8,96,128]{2,1,0:T(8,128)(2,1)S(1)}, u32[]{:S(2)}, u32[]{:S(2)}) %collective-permute-start.2) | collective-permute-done | bytes 196640 | tf_op jit(solution)/shard_map/ppermute | solution.py:237
  37.5 0.1 shard_map.73
  37.6 1.1 %collective-permute-start.7 = (bf16[4,96,128]{2,1,0:T(8,128)(2,1)S(1)}, bf16[4,96,128]{2,1,0:T(8,128)(2,1)S(1)}, u32[]{:S(2)}, u32[]{:S(2)}) collective-permute-start(bf16[4,96,128]{2,1,0:T(8,128)(2,1)S(1)} %get-tuple-element.20), channel_id=1, source_target_pairs={{0,32},{32,0},{1,33},{33,1},{2,34},{34,2},{3,35},{35,3},{4,36},{36... | collective-permute-start | bytes 294920 | tf_op jit(solution)/shard_map/ppermute | solution.py:243
  38.7 0.1 pad_add_fusion.place_ref.refs_0_
  38.8 3.5 %collective-permute-done.7.came_ref = bf16[4,96,128]{2,1,0:T(8,128)(2,1)S(1)} collective-permute-done((bf16[4,96,128]{2,1,0:T(8,128)(2,1)S(1)}, bf16[4,96,128]{2,1,0:T(8,128)(2,1)S(1)}, u32[]{:S(2)}, u32[]{:S(2)}) %collective-permute-start.7) | collective-permute-done | bytes 98336 | tf_op jit(solution)/shard_map/ppermute | solution.py:243
  42.3 0.6 shard_map.74
  42.9 4.1 %collective-permute-start.10 = (bf16[416,128]{1,0:T(8,128)(2,1)S(1)}, bf16[416,128]{1,0:T(8,128)(2,1)S(1)}, u32[]{:S(2)}, u32[]{:S(2)}) collective-permute-start(bf16[416,128]{1,0:T(8,128)(2,1)S(1)} %get-tuple-element.29), channel_id=1, source_target_pairs={{0,192},{64,128},{128,64},{192,0},{1,193},{65,129},{129,65},{193,1... | collective-permute-start | bytes 319496 | tf_op jit(solution)/shard_map/ppermute | solution.py:190
  47.1 2.4 %collective-permute-start.8 = (bf16[416,128]{1,0:T(8,128)(2,1)S(1)}, bf16[416,128]{1,0:T(8,128)(2,1)S(1)}, u32[]{:S(2)}, u32[]{:S(2)}) collective-permute-start(bf16[416,128]{1,0:T(8,128)(2,1)S(1)} %get-tuple-element.27), channel_id=1, source_target_pairs={{0,64},{64,0},{128,192},{192,128},{1,65},{65,1},{129,193},{193,129... | collective-permute-start | bytes 319496 | tf_op jit(solution)/shard_map/ppermute | solution.py:190
  49.4 0.1 collective-permute-start.9
  49.5 1.4 %collective-permute-done.10.refs_2_.refs_5_ = bf16[416,128]{1,0:T(8,128)(2,1)S(1)} collective-permute-done((bf16[416,128]{1,0:T(8,128)(2,1)S(1)}, bf16[416,128]{1,0:T(8,128)(2,1)S(1)}, u32[]{:S(2)}, u32[]{:S(2)}) %collective-permute-start.10) | collective-permute-done | bytes 106528 | tf_op jit(solution)/shard_map/ppermute | solution.py:190
  50.9 5.7 %collective-permute-done.8.refs_0_.refs_3_ = bf16[416,128]{1,0:T(8,128)(2,1)S(1)} collective-permute-done((bf16[416,128]{1,0:T(8,128)(2,1)S(1)}, bf16[416,128]{1,0:T(8,128)(2,1)S(1)}, u32[]{:S(2)}, u32[]{:S(2)}) %collective-permute-start.8) | collective-permute-done | bytes 106528 | tf_op jit(solution)/shard_map/ppermute | solution.py:190
  56.6 1.7 %collective-permute-done.9.refs_1_.refs_4_ = bf16[416,128]{1,0:T(8,128)(2,1)S(1)} collective-permute-done((bf16[416,128]{1,0:T(8,128)(2,1)S(1)}, bf16[416,128]{1,0:T(8,128)(2,1)S(1)}, u32[]{:S(2)}, u32[]{:S(2)}) %collective-permute-start.9) | collective-permute-done | bytes 106528 | tf_op jit(solution)/shard_map/ppermute | solution.py:190
  58.3 0.6 shard_map.75.refs_6_
  58.9 2.1 %collective-permute-start.11 = (bf16[4,96,128]{2,1,0:T(8,128)(2,1)S(1)}, bf16[4,96,128]{2,1,0:T(8,128)(2,1)S(1)}, u32[]{:S(2)}, u32[]{:S(2)}) collective-permute-start(bf16[4,96,128]{2,1,0:T(8,128)(2,1)S(1)} %shard_map.75.refs_6_), channel_id=1, source_target_pairs={{0,1},{1,2},{2,3},{3,0},{4,5},{5,6},{6,7},{7,4},{8,9},{9,10},{10,1... | collective-permute-start | bytes 294920 | tf_op jit(solution)/shard_map/ppermute | solution.py:190
  61.0 2.4 %collective-permute-start.12 = (bf16[4,96,128]{2,1,0:T(8,128)(2,1)S(1)}, bf16[4,96,128]{2,1,0:T(8,128)(2,1)S(1)}, u32[]{:S(2)}, u32[]{:S(2)}) collective-permute-start(bf16[4,96,128]{2,1,0:T(8,128)(2,1)S(1)} %shard_map.75.refs_6_), channel_id=1, source_target_pairs={{0,2},{1,3},{2,0},{3,1},{4,6},{5,7},{6,4},{7,5},{8,10},{9,11},{10,... | collective-permute-start | bytes 294920 | tf_op jit(solution)/shard_map/ppermute | solution.py:190
  63.3 1.5 %collective-permute-start.13 = (bf16[4,96,128]{2,1,0:T(8,128)(2,1)S(1)}, bf16[4,96,128]{2,1,0:T(8,128)(2,1)S(1)}, u32[]{:S(2)}, u32[]{:S(2)}) collective-permute-start(bf16[4,96,128]{2,1,0:T(8,128)(2,1)S(1)} %shard_map.75.refs_6_), channel_id=1, source_target_pairs={{0,3},{1,0},{2,1},{3,2},{4,7},{5,4},{6,5},{7,6},{8,11},{9,8},{10,9... | collective-permute-start | bytes 294920 | tf_op jit(solution)/shard_map/ppermute | solution.py:190
  64.8 0.0 collective-permute-done.11.refs_7_
  64.8 2.3 %collective-permute-done.12.refs_8_ = bf16[4,96,128]{2,1,0:T(8,128)(2,1)S(1)} collective-permute-done((bf16[4,96,128]{2,1,0:T(8,128)(2,1)S(1)}, bf16[4,96,128]{2,1,0:T(8,128)(2,1)S(1)}, u32[]{:S(2)}, u32[]{:S(2)}) %collective-permute-start.12) | collective-permute-done | bytes 98336 | tf_op jit(solution)/shard_map/ppermute | solution.py:190
  67.1 0.9 collective-permute-done.13.refs_9_
  68.0 1.3 %shard_map.76 = bf16[16,48,512]{2,1,0:T(8,128)(2,1)S(1)} custom-call(s32[3]{0:T(128)S(1)} %pad_add_fusion.place_ref.refs_0_, bf16[16,64,512]{2,1,0:T(8,128)(2,1)S(1)} %all-to-all-done.refs_1_, bf16[32,128]{1,0:T(8,128)(2,1)S(1)} %get-tuple-element.26.extra_ref.refs_2_, bf16[416,128]{1,0:T(8,128)(2,1)S(1)} %collective-permute-done.8.refs_0_.refs_3_, ...), custom_call_target="tpu_custom_call" | custom-call | flops 201326592 | bytes 2097152 | tf_op jit(solution)/shard_map/pallas_call | solution.py:69
  69.3 24.2 %all_to_all.10 = bf16[16,48,512]{2,1,0:T(8,128)(2,1)S(1)} all-to-all(bf16[16,48,512]{2,1,0:T(8,128)(2,1)S(1)} %shard_map.76), channel_id=1, replica_groups=mesh['zg'=4,'zl'=2,'y'=4,'core'=2,'smp'=4] {'zg','smp'}, dimensions={0} | all-to-all | bytes 1572864 | tf_op jit(solution)/shard_map/all_to_all | solution.py:286
  93.4 1.0 %copy.8 = bf16[16,6,8,512]{3,2,0,1:T(8,128)(2,1)} copy(bf16[16,6,8,512]{3,2,1,0:T(8,128)(2,1)S(1)} %bitcast.18) | data formatting | bytes 1572864 | tf_op jit(solution)/shard_map/reshape | solution.py:287
  (9 shorter events, 0.0 us)
Async XLA Ops:
  2.4 10.3 %copy-start.3 = (bf16[2048,192]{0,1:T(8,128)(2,1)S(1)}, bf16[2048,192]{0,1:T(8,128)(2,1)}, u32[]{:S(2)}) copy-start(bf16[2048,192]{0,1:T(8,128)(2,1)} %param.8) | copy-start | bytes 2359300
  2.4 40.6 %all-to-all-start = ((bf16[16,64,512]{2,1,0:T(8,128)(2,1)}), bf16[16,64,512]{2,1,0:T(8,128)(2,1)S(1)}, u32[]{:S(2)}, u32[]{:S(2)}) async-start(bf16[16,64,512]{2,1,0:T(8,128)(2,1)} %shard_map.64), calls=%async_computation | async-start | bytes 2097152 | tf_op jit(solution)/shard_map/all_to_all | solution.py:207
  12.8 1.0 %copy-start = (bf16[64,2048]{1,0:T(8,128)(2,1)S(1)}, bf16[64,2048]{1,0:T(8,128)(2,1)}, u32[]{:S(2)}) copy-start(bf16[64,2048]{1,0:T(8,128)(2,1)} %refs_2_.15) | copy-start | bytes 786436
  12.8 1.0 %copy-start.2 = (s32[2048,1]{0,1:T(1,128)S(1)}, s32[2048,1]{0,1:T(1,128)}, u32[]{:S(2)}) copy-start(s32[2048,1]{0,1:T(1,128)} %param.9) | copy-start | bytes 24580
  15.0 5.9 %collective-permute-start.3 = (f32[8,96,128]{2,1,0:T(8,128)S(1)}, f32[8,96,128]{2,1,0:T(8,128)S(1)}, u32[]{:S(2)}, u32[]{:S(2)}) collective-permute-start(f32[8,96,128]{2,1,0:T(8,128)S(1)} %shard_map.69), channel_id=1, source_target_pairs={{0,4},{4,0},{1,5},{5,1},{2,6},{6,2},{3,7},{7,3},{8,12},{12,8},{9,1... | collective-permute-start | bytes 1179656 | tf_op jit(solution)/shard_map/ppermute | solution.py:231
  16.4 7.5 %collective-permute-start.5 = (f32[8,96,128]{2,1,0:T(8,128)S(1)}, f32[8,96,128]{2,1,0:T(8,128)S(1)}, u32[]{:S(2)}, u32[]{:S(2)}) collective-permute-start(f32[8,96,128]{2,1,0:T(8,128)S(1)} %shard_map.71), channel_id=1, source_target_pairs={{0,4},{4,0},{1,5},{5,1},{2,6},{6,2},{3,7},{7,3},{8,12},{12,8},{9,1... | collective-permute-start | bytes 1179656 | tf_op jit(solution)/shard_map/ppermute | solution.py:231
  18.3 8.0 %collective-permute-start.1 = (f32[8,96,128]{2,1,0:T(8,128)S(1)}, f32[8,96,128]{2,1,0:T(8,128)S(1)}, u32[]{:S(2)}, u32[]{:S(2)}) collective-permute-start(f32[8,96,128]{2,1,0:T(8,128)S(1)} %shard_map.67), channel_id=1, source_target_pairs={{0,4},{4,0},{1,5},{5,1},{2,6},{6,2},{3,7},{7,3},{8,12},{12,8},{9,1... | collective-permute-start | bytes 1179656 | tf_op jit(solution)/shard_map/ppermute | solution.py:231
  20.4 10.8 %collective-permute-start = (f32[8,96,128]{2,1,0:T(8,128)}, f32[8,96,128]{2,1,0:T(8,128)S(1)}, u32[]{:S(2)}, u32[]{:S(2)}) collective-permute-start(f32[8,96,128]{2,1,0:T(8,128)} %shard_map.65), channel_id=1, source_target_pairs={{0,4},{4,0},{1,5},{5,1},{2,6},{6,2},{3,7},{7,3},{8,12},{12,8},{9,1... | collective-permute-start | bytes 1179656 | tf_op jit(solution)/shard_map/ppermute | solution.py:231
  22.2 10.3 %collective-permute-start.4 = (bf16[8,96,128]{2,1,0:T(8,128)(2,1)S(1)}, bf16[8,96,128]{2,1,0:T(8,128)(2,1)S(1)}, u32[]{:S(2)}, u32[]{:S(2)}) collective-permute-start(bf16[8,96,128]{2,1,0:T(8,128)(2,1)S(1)} %shard_map.70), channel_id=1, source_target_pairs={{0,8},{8,16},{16,24},{24,0},{1,9},{9,17},{17,25},{25,1},{2,10},{10... | collective-permute-start | bytes 589832 | tf_op jit(solution)/shard_map/ppermute | solution.py:237
  25.8 7.3 %collective-permute-start.6 = (bf16[8,96,128]{2,1,0:T(8,128)(2,1)}, bf16[8,96,128]{2,1,0:T(8,128)(2,1)S(1)}, u32[]{:S(2)}, u32[]{:S(2)}) collective-permute-start(bf16[8,96,128]{2,1,0:T(8,128)(2,1)} %shard_map.72), channel_id=1, source_target_pairs={{0,24},{8,0},{16,8},{24,16},{1,25},{9,1},{17,9},{25,17},{2,26},{10... | collective-permute-start | bytes 589832 | tf_op jit(solution)/shard_map/ppermute | solution.py:237
  28.3 9.3 %collective-permute-start.2 = (bf16[8,96,128]{2,1,0:T(8,128)(2,1)}, bf16[8,96,128]{2,1,0:T(8,128)(2,1)S(1)}, u32[]{:S(2)}, u32[]{:S(2)}) collective-permute-start(bf16[8,96,128]{2,1,0:T(8,128)(2,1)} %shard_map.68), channel_id=1, source_target_pairs={{0,16},{8,24},{16,0},{24,8},{1,17},{9,25},{17,1},{25,9},{2,18},{10... | collective-permute-start | bytes 589832 | tf_op jit(solution)/shard_map/ppermute | solution.py:237
  31.2 11.1 %copy-start.1 = (f32[2,8192]{1,0:T(2,128)S(1)}, f32[2,8192]{1,0:T(2,128)}, u32[]{:S(2)}) copy-start(f32[2,8192]{1,0:T(2,128)} %twiddle_ref.1) | copy-start | bytes 196612
  37.6 4.7 %collective-permute-start.7 = (bf16[4,96,128]{2,1,0:T(8,128)(2,1)S(1)}, bf16[4,96,128]{2,1,0:T(8,128)(2,1)S(1)}, u32[]{:S(2)}, u32[]{:S(2)}) collective-permute-start(bf16[4,96,128]{2,1,0:T(8,128)(2,1)S(1)} %get-tuple-element.20), channel_id=1, source_target_pairs={{0,32},{32,0},{1,33},{33,1},{2,34},{34,2},{3,35},{35,3},{4,36},{36... | collective-permute-start | bytes 294920 | tf_op jit(solution)/shard_map/ppermute | solution.py:243
  42.9 7.9 %collective-permute-start.10 = (bf16[416,128]{1,0:T(8,128)(2,1)S(1)}, bf16[416,128]{1,0:T(8,128)(2,1)S(1)}, u32[]{:S(2)}, u32[]{:S(2)}) collective-permute-start(bf16[416,128]{1,0:T(8,128)(2,1)S(1)} %get-tuple-element.29), channel_id=1, source_target_pairs={{0,192},{64,128},{128,64},{192,0},{1,193},{65,129},{129,65},{193,1... | collective-permute-start | bytes 319496 | tf_op jit(solution)/shard_map/ppermute | solution.py:190
  47.1 9.5 %collective-permute-start.8 = (bf16[416,128]{1,0:T(8,128)(2,1)S(1)}, bf16[416,128]{1,0:T(8,128)(2,1)S(1)}, u32[]{:S(2)}, u32[]{:S(2)}) collective-permute-start(bf16[416,128]{1,0:T(8,128)(2,1)S(1)} %get-tuple-element.27), channel_id=1, source_target_pairs={{0,64},{64,0},{128,192},{192,128},{1,65},{65,1},{129,193},{193,129... | collective-permute-start | bytes 319496 | tf_op jit(solution)/shard_map/ppermute | solution.py:190
  49.4 8.9 %collective-permute-start.9 = (bf16[416,128]{1,0:T(8,128)(2,1)S(1)}, bf16[416,128]{1,0:T(8,128)(2,1)S(1)}, u32[]{:S(2)}, u32[]{:S(2)}) collective-permute-start(bf16[416,128]{1,0:T(8,128)(2,1)S(1)} %get-tuple-element.28), channel_id=1, source_target_pairs={{0,128},{64,192},{128,0},{192,64},{1,129},{65,193},{129,1},{193,65... | collective-permute-start | bytes 319496 | tf_op jit(solution)/shard_map/ppermute | solution.py:190
  58.9 5.9 %collective-permute-start.11 = (bf16[4,96,128]{2,1,0:T(8,128)(2,1)S(1)}, bf16[4,96,128]{2,1,0:T(8,128)(2,1)S(1)}, u32[]{:S(2)}, u32[]{:S(2)}) collective-permute-start(bf16[4,96,128]{2,1,0:T(8,128)(2,1)S(1)} %shard_map.75.refs_6_), channel_id=1, source_target_pairs={{0,1},{1,2},{2,3},{3,0},{4,5},{5,6},{6,7},{7,4},{8,9},{9,10},{10,1... | collective-permute-start | bytes 294920 | tf_op jit(solution)/shard_map/ppermute | solution.py:190
  61.0 6.1 %collective-permute-start.12 = (bf16[4,96,128]{2,1,0:T(8,128)(2,1)S(1)}, bf16[4,96,128]{2,1,0:T(8,128)(2,1)S(1)}, u32[]{:S(2)}, u32[]{:S(2)}) collective-permute-start(bf16[4,96,128]{2,1,0:T(8,128)(2,1)S(1)} %shard_map.75.refs_6_), channel_id=1, source_target_pairs={{0,2},{1,3},{2,0},{3,1},{4,6},{5,7},{6,4},{7,5},{8,10},{9,11},{10,... | collective-permute-start | bytes 294920 | tf_op jit(solution)/shard_map/ppermute | solution.py:190
  63.3 4.6 %collective-permute-start.13 = (bf16[4,96,128]{2,1,0:T(8,128)(2,1)S(1)}, bf16[4,96,128]{2,1,0:T(8,128)(2,1)S(1)}, u32[]{:S(2)}, u32[]{:S(2)}) collective-permute-start(bf16[4,96,128]{2,1,0:T(8,128)(2,1)S(1)} %shard_map.75.refs_6_), channel_id=1, source_target_pairs={{0,3},{1,0},{2,1},{3,2},{4,7},{5,4},{6,5},{7,6},{8,11},{9,8},{10,9... | collective-permute-start | bytes 294920 | tf_op jit(solution)/shard_map/ppermute | solution.py:190

commit v8 on v7

--- a/solution.py
+++ b/solution.py
@@ -31,14 +31,40 @@
         split_kernel,
         out_shape=jax.ShapeDtypeStruct((pieces, rows, points // pieces), source.dtype),
         in_specs=[pl.BlockSpec(memory_space=pl.ANY)],
-        out_specs=VMEM,
+        out_specs=pl.BlockSpec(memory_space=pl.ANY),
         scratch_shapes=[pltpu.SemaphoreType.DMA((pieces,))],
         compiler_params=pltpu.CompilerParams(vmem_limit_bytes=56 * MIB),
         cost_estimate=pl.CostEstimate(flops=0, bytes_accessed=2 * MIB, transcendentals=0),
     )(source)
 
 
-def partial_kernel(y_count, offset, other, place_ref, owners_ref, adjoint_ref, wide_ref, *refs):
+def join_kernel(parts, pieces_ref, out_ref, sems):
+    pieces, _, points = pieces_ref.shape
+    copies = []
+    for i in range(pieces):
+        place = (i % (pieces // parts)) * parts + i // (pieces // parts)
+        target = out_ref.at[:, pl.ds(place * points, points)]
+        copies.append(pltpu.make_async_copy(pieces_ref.at[i], target, sems.at[i]))
+    for copy in copies:
+        copy.start()
+    for copy in copies:
+        copy.wait()
+
+
+def join(pieces, parts):
+    count, rows, points = pieces.shape
+    return pl.pallas_call(
+        lambda *refs: join_kernel(parts, *refs),
+        out_shape=jax.ShapeDtypeStruct((rows, count * points), pieces.dtype),
+        in_specs=[VMEM],
+        out_specs=pl.BlockSpec(memory_space=pl.ANY),
+        scratch_shapes=[pltpu.SemaphoreType.DMA((count,))],
+        compiler_params=pltpu.CompilerParams(vmem_limit_bytes=12 * MIB),
+        cost_estimate=pl.CostEstimate(flops=0, bytes_accessed=2 * MIB, transcendentals=0),
+    )(pieces)
+
+
+def partial_kernel(y_count, offset, other, place_ref, owners_ref, adjoint_ref, probes_ref, *refs):
     out_ref, masked = refs[-2:]
     samples = adjoint_ref.shape[0]
     z_count = out_ref.shape[0]
@@ -50,14 +76,13 @@
         hot = jnp.where(own == (z * y_count + y) * 2 + core, 1.0, 0.0).astype(jnp.bfloat16)
         masked[z * samples:(z + 1) * samples, :] = adjoint * hot
     product = lax.dot_general(
-        masked[...], wide_ref[...], (((1,), (1,)), ((), ())), preferred_element_type=jnp.float32
+        masked[...], probes_ref[...], (((1,), (1,)), ((), ())), preferred_element_type=jnp.float32
     )
     half = samples // 2
-    low = lax.broadcasted_iota(jnp.int32, (half, 128), 1) < 64
     for z in range(z_count):
         block = product[z * samples:(z + 1) * samples, :]
         head = block[:, :128]
-        tail = jnp.where(low, block[:half, 128:], block[half:, 128:])
+        tail = jnp.concatenate([block[:half, 128:], block[half:, 128:]], axis=1)
         if not other:
             head = head + refs[0][z, :samples, :]
             tail = tail + refs[0][z, samples:, :]
@@ -72,7 +97,7 @@
         in_specs=[SMEM] * smem + [VMEM] * (len(args) - smem),
         out_specs=jax.tree.map(lambda _: VMEM, out_shape),
         scratch_shapes=list(scratch),
-        compiler_params=pltpu.CompilerParams(vmem_limit_bytes=24 * MIB),
+        compiler_params=pltpu.CompilerParams(vmem_limit_bytes=12 * MIB),
         cost_estimate=pl.CostEstimate(flops=flops, bytes_accessed=2 * MIB, transcendentals=0),
     )(*args)
 
@@ -140,19 +165,20 @@
 
 
 def field_kernel(blocks, parts, place_ref, samples_ref, extra_ref, *refs):
-    offers, weight_refs = refs[:blocks - 1], refs[blocks - 1:-2]
-    out_ref, field = refs[-2:]
+    offers, weight_refs = refs[:blocks - 1], refs[blocks - 1:-3]
+    out_ref, field, every = refs[-3:]
     zg, smp = place_ref[0], place_ref[1]
     vectors, points = field.shape[1:]
     samples = samples_ref.shape[1]
-    packed = weight_refs[0].shape[1]
+    packed = every.shape[2]
+    for p in range(parts):
+        every[lax.rem(smp - p + parts, parts)] = weight_refs[p][...]
     factors = []
     for c in range(blocks):
-        head, tail, columns, grid = [], [], [], []
+        head, tail, columns = [], [], []
         for p in range(parts):
-            grid.append(samples_ref[(zg ^ c) * parts + lax.rem(smp - p + parts, parts)])
-            head.append(weight_refs[p][c, :samples, :])
-            rest = weight_refs[p][c, samples:, :]
+            head.append(every[p, c, :samples, :])
+            rest = every[p, c, samples:, :]
             tail += [rest[:, :64], rest[:, 64:]]
         extra = offers[c - 1][blocks * packed:, :] if c else extra_ref[...]
         extra = extra.astype(jnp.float32)
@@ -160,7 +186,7 @@
             terms = extra[column * 8:column * 8 + 8]
             columns.append(terms[0:2] + terms[2:4] + terms[4:6])
         factors.append(jnp.concatenate(columns, axis=1))
-        grid = jnp.concatenate(grid, axis=0)
+        grid = samples_ref[pl.ds((zg ^ c) * parts, parts)].reshape(parts * samples, points)
         head = jnp.concatenate(head, axis=0)
         tail = jnp.concatenate(tail, axis=0)
         field[c, :128, :] = lax.dot_general(
@@ -179,7 +205,7 @@
                 for c in range(blocks)
             ]
         for c in range(blocks):
-            out_ref[(zg ^ c) * parts + p] = level[c].astype(jnp.bfloat16)
+            out_ref[p * blocks + (zg ^ c)] = level[c].astype(jnp.bfloat16)
 
 
 def exchange(pieces, axis, route):
@@ -206,7 +232,6 @@
     pieces, own = lax.optimization_barrier((pieces, own))
     pieces = lax.all_to_all(pieces, GROUP, 0, 0, tiled=True)
 
-    wide = jnp.concatenate([probes, probes[128:]], axis=0)
     shape = (lax.axis_size(Z_AXES), samples * vectors // 128, 128)
     place = jnp.stack([y, core])
 
@@ -217,7 +242,7 @@
             place,
             own,
             adjoint_samples,
-            wide,
+            probes,
             *came,
             smem=1,
             scratch=[pltpu.VMEM((shape[0] * samples, own.shape[1]), jnp.bfloat16)],
@@ -225,17 +250,19 @@
         )
 
     order = sorted(range(y_count), key=lambda k: (k == 0, abs(k - y_count // 2)))
-    came = {}
-    for offset in order:
-        sent = partial(offset, True, jnp.float32)
-        came[offset] = lax.ppermute(sent, "core", [(0, 1), (1, 0)])
-    sums = []
-    for offset in order:
-        kind = jnp.bfloat16 if offset else jnp.float32
-        merged = partial(offset, False, kind, came[offset])
-        route = [(i, (i + offset) % y_count) for i in range(y_count)]
-        sums.append(lax.ppermute(merged, "y", route) if offset else merged)
-    sums = sums[-1:] + sums[:-1]
+    came, sums = {}, {}
+    steps = [(offset, True) for offset in order[:-1]] + [(offset, False) for offset in order[:-1]]
+    for offset, other in steps + [(0, True), (0, False)]:
+        if other:
+            sent = partial(offset, True, jnp.float32)
+            came[offset] = lax.ppermute(sent, "core", [(0, 1), (1, 0)])
+        elif offset:
+            merged = partial(offset, False, jnp.bfloat16, came[offset])
+            route = [(i, (i + offset) % y_count) for i in range(y_count)]
+            sums[offset] = lax.ppermute(merged, "y", route)
+        else:
+            sums[offset] = partial(offset, False, jnp.float32, came[offset])
+    sums = [sums[offset] for offset in range(y_count)]
     shape = (groups,) + shape[1:]
     shapes = [jax.ShapeDtypeStruct(shape, jnp.float32), jax.ShapeDtypeStruct(shape, jnp.bfloat16)]
     zl = lax.axis_index("zl")
@@ -280,11 +307,14 @@
         weights,
         *others,
         smem=1,
-        scratch=[pltpu.VMEM((groups, vectors, piece), jnp.float32)],
+        scratch=[
+            pltpu.VMEM((groups, vectors, piece), jnp.float32),
+            pltpu.VMEM((parts,) + shape, jnp.bfloat16),
+        ],
         flops=2 * members * samples * vectors * piece,
     )
-    result = lax.all_to_all(result, GROUP, 0, 0, tiled=True)
-    return result.transpose(1, 0, 2).reshape(vectors // parts, points)
+    result = lax.all_to_all(result, ("smp", "zg"), 0, 0, tiled=True)
+    return join(result, parts)
 
 
 def solution(mesh):

time: 95.8 us -> 130 us (1.36)
  Pallas kernels: 17.4 us -> 49.4 us
  blocking collectives: 24.2 us -> 26.6 us
  waiting for transfers between devices: 20.4 us -> 22.1 us
    pallas_call x1, Pallas kernels: 2.36 us -> 33 us  [split(): pl.pallas_call(split_kernel, out_shape=jax.ShapeDtypeStruct((pieces, rows...]
    all_to_all x1, blocking collectives: 24.2 us -> 26.6 us  [body(): result = lax.all_to_all(result, ('smp', 'zg'), 0, 0, tiled=True)]
    ppermute x6, waiting for transfers between devices: 11.9 us -> 13.4 us  [exchange(): came[offset] = lax.ppermute(pieces[offset], axis, pairs)]
  transfers between devices with their start and end apart: 15 -> 15, of which waited for: 8 -> 9; matrix products, arithmetic and copies ran while one was open for 0% -> 0% of each run, Pallas kernels for 14% -> 10%
where the time goes in v8:
time: 130 us
  Pallas kernels  49.4 us (38%)
  starting transfers between devices  29.8 us (23%)
  blocking collectives  26.6 us (20%)
  waiting for transfers between devices  22.1 us (17%)
    pallas_call x1, Pallas kernels, split(): pl.pallas_call(split_kernel, out_shape=jax.ShapeDtypeStruct((pieces, rows...  33 us
    all_to_all x1, blocking collectives, body(): result = lax.all_to_all(result, ('smp', 'zg'), 0, 0, tiled=True)  26.6 us
    pallas_call x12, Pallas kernels, local_call(): pl.pallas_call(kernel, out_shape=out_shape, in_specs=[SMEM] * smem + [VME...  15.4 us
    ppermute x6, waiting for transfers between devices, exchange(): came[offset] = lax.ppermute(pieces[offset], axis, pairs)  13.4 us
    ppermute x6, starting transfers between devices, exchange(): came[offset] = lax.ppermute(pieces[offset], axis, pairs)  12.2 us
    all_to_all x1, starting transfers between devices, body(): pieces = lax.all_to_all(pieces, GROUP, 0, 0, tiled=True)  10.3 us
    ppermute x3, waiting for transfers between devices, body(): sums[offset] = lax.ppermute(merged, 'y', route)  5.11 us
    ppermute x3, starting transfers between devices, body(): sums[offset] = lax.ppermute(merged, 'y', route)  4.93 us
  transfers between devices with their start and end apart: 15, of which 9 were waited for; matrix products, arithmetic and copies ran while one was open for 0% of the time, Pallas kernels for 10%

profile of v8, /device:TPU:40, one launch (start us, length us, event | category | flops | bytes accessed | tf_op | source)
XLA Modules:
  0.0 129.6 jit_solution(3467733885084233939)
XLA Ops:
  0.0 33.0 %shard_map.64 = bf16[16,64,512]{2,1,0:T(8,128)(2,1)} custom-call(bf16[64,8192]{1,0:T(8,128)(2,1)} %source_ref.1), custom_call_target="tpu_custom_call" | custom-call | bytes 2097152 | tf_op jit(solution)/shard_map/pallas_call | solution.py:30
  33.0 0.0 copy-start.1
  33.0 0.0 copy-start.2
  33.0 10.3 %all-to-all-start = ((bf16[16,64,512]{2,1,0:T(8,128)(2,1)}), bf16[16,64,512]{2,1,0:T(8,128)(2,1)S(1)}, u32[]{:S(2)}, u32[]{:S(2)}) async-start(bf16[16,64,512]{2,1,0:T(8,128)(2,1)} %shard_map.64), calls=%async_computation | async-start | bytes 2097152 | tf_op jit(solution)/shard_map/all_to_all | solution.py:233
  43.3 0.0 copy-start.3
  43.3 0.1 pad_add_fusion.1.refs_0_
  43.4 0.6 copy-done.3
  44.0 1.3 %shard_map.67 = f32[8,96,128]{2,1,0:T(8,128)S(1)} custom-call(s32[2]{0:T(128)S(1)} %pad_add_fusion.1.refs_0_, s32[1,2048]{1,0:T(1,128)S(1)} %bitcast.15, bf16[64,2048]{1,0:T(8,128)(2,1)S(1)} %copy-done.2, bf16[192,2048]{1,0:T(8,128)(2,1)S(1)} %bitcast.7), custom_call_target="tpu_custom_call" | custom-call | flops 536870912 | bytes 2097152 | tf_op jit(solution)/shard_map/pallas_call | solution.py:94
  45.4 0.1 collective-permute-start.1
  45.4 1.3 %shard_map.69 = f32[8,96,128]{2,1,0:T(8,128)S(1)} custom-call(s32[2]{0:T(128)S(1)} %pad_add_fusion.1.refs_0_, s32[1,2048]{1,0:T(1,128)S(1)} %bitcast.16, bf16[64,2048]{1,0:T(8,128)(2,1)S(1)} %copy-done.2, bf16[192,2048]{1,0:T(8,128)(2,1)S(1)} %bitcast.8), custom_call_target="tpu_custom_call" | custom-call | flops 536870912 | bytes 2097152 | tf_op jit(solution)/shard_map/pallas_call | solution.py:94
  46.8 0.6 collective-permute-start.3
  47.4 1.3 %shard_map.71 = f32[8,96,128]{2,1,0:T(8,128)S(1)} custom-call(s32[2]{0:T(128)S(1)} %pad_add_fusion.1.refs_0_, s32[1,2048]{1,0:T(1,128)S(1)} %bitcast.17, bf16[64,2048]{1,0:T(8,128)(2,1)S(1)} %copy-done.2, bf16[192,2048]{1,0:T(8,128)(2,1)S(1)} %bitcast.9), custom_call_target="tpu_custom_call" | custom-call | flops 536870912 | bytes 2097152 | tf_op jit(solution)/shard_map/pallas_call | solution.py:94
  48.7 0.1 collective-permute-start.5
  48.8 1.3 %shard_map.65 = f32[8,96,128]{2,1,0:T(8,128)S(1)} custom-call(s32[2]{0:T(128)S(1)} %pad_add_fusion.1.refs_0_, s32[1,2048]{1,0:T(1,128)S(1)} %bitcast.18, bf16[64,2048]{1,0:T(8,128)(2,1)S(1)} %copy-done.2, bf16[192,2048]{1,0:T(8,128)(2,1)S(1)} %bitcast.10), custom_call_target="tpu_custom_call" | custom-call | flops 536870912 | bytes 2097152 | tf_op jit(solution)/shard_map/pallas_call | solution.py:94
  50.1 0.6 collective-permute-start
  50.7 2.0 %shard_map.68 = bf16[8,96,128]{2,1,0:T(8,128)(2,1)} custom-call(s32[2]{0:T(128)S(1)} %pad_add_fusion.1.refs_0_, s32[1,2048]{1,0:T(1,128)S(1)} %bitcast.19, bf16[64,2048]{1,0:T(8,128)(2,1)S(1)} %copy-done.2, bf16[192,2048]{1,0:T(8,128)(2,1)S(1)} %bitcast.11, f32[8,96,128]{2,1,0:T(8,128)S(1)} %collective-permute-done.1.refs_4_), custom_call_target="tpu_custom_call" | custom-call | flops 536870912 | bytes 2097152 | tf_op jit(solution)/shard_map/pallas_call | solution.py:94
  52.7 1.6 %collective-permute-start.2 = (bf16[8,96,128]{2,1,0:T(8,128)(2,1)}, bf16[8,96,128]{2,1,0:T(8,128)(2,1)S(1)}, u32[]{:S(2)}, u32[]{:S(2)}) collective-permute-start(bf16[8,96,128]{2,1,0:T(8,128)(2,1)} %shard_map.68), channel_id=1, source_target_pairs={{0,8},{8,16},{16,24},{24,0},{1,9},{9,17},{17,25},{25,1},{2,10},{10... | collective-permute-start | bytes 589832 | tf_op jit(solution)/shard_map/ppermute | solution.py:262
  54.3 0.0 collective-permute-done.3.refs_4_
  54.3 2.0 %shard_map.70 = bf16[8,96,128]{2,1,0:T(8,128)(2,1)} custom-call(s32[2]{0:T(128)S(1)} %pad_add_fusion.1.refs_0_, s32[1,2048]{1,0:T(1,128)S(1)} %bitcast.20, bf16[64,2048]{1,0:T(8,128)(2,1)S(1)} %copy-done.2, bf16[192,2048]{1,0:T(8,128)(2,1)S(1)} %bitcast.12, f32[8,96,128]{2,1,0:T(8,128)S(1)} %collective-permute-done.3.refs_4_), custom_call_target="tpu_custom_call" | custom-call | flops 536870912 | bytes 2097152 | tf_op jit(solution)/shard_map/pallas_call | solution.py:94
  56.3 1.0 collective-permute-start.4
  57.3 2.0 %shard_map.72 = bf16[8,96,128]{2,1,0:T(8,128)(2,1)} custom-call(s32[2]{0:T(128)S(1)} %pad_add_fusion.1.refs_0_, s32[1,2048]{1,0:T(1,128)S(1)} %bitcast.21, bf16[64,2048]{1,0:T(8,128)(2,1)S(1)} %copy-done.2, bf16[192,2048]{1,0:T(8,128)(2,1)S(1)} %bitcast.13, f32[8,96,128]{2,1,0:T(8,128)S(1)} %collective-permute-done.5.refs_4_), custom_call_target="tpu_custom_call" | custom-call | flops 536870912 | bytes 2097152 | tf_op jit(solution)/shard_map/pallas_call | solution.py:94
  59.3 2.4 %collective-permute-start.6 = (bf16[8,96,128]{2,1,0:T(8,128)(2,1)}, bf16[8,96,128]{2,1,0:T(8,128)(2,1)S(1)}, u32[]{:S(2)}, u32[]{:S(2)}) collective-permute-start(bf16[8,96,128]{2,1,0:T(8,128)(2,1)} %shard_map.72), channel_id=1, source_target_pairs={{0,24},{8,0},{16,8},{24,16},{1,25},{9,1},{17,9},{25,17},{2,26},{10... | collective-permute-start | bytes 589832 | tf_op jit(solution)/shard_map/ppermute | solution.py:262
  62.3 0.0 collective-permute-done.refs_4_
  62.3 1.3 %shard_map.66.refs_0_ = f32[8,96,128]{2,1,0:T(8,128)S(1)} custom-call(s32[2]{0:T(128)S(1)} %pad_add_fusion.1.refs_0_, s32[1,2048]{1,0:T(1,128)S(1)} %bitcast.22, bf16[64,2048]{1,0:T(8,128)(2,1)S(1)} %copy-done.2, bf16[192,2048]{1,0:T(8,128)(2,1)S(1)} %bitcast.14, f32[8,96,128]{2,1,0:T(8,128)S(1)} %collective-permute-done.refs_4_), custom_call_target="tpu_custom_call" | custom-call | flops 536870912 | bytes 2097152 | tf_op jit(solution)/shard_map/pallas_call | solution.py:94
  63.7 2.2 %collective-permute-done.4.refs_2_ = bf16[8,96,128]{2,1,0:T(8,128)(2,1)S(1)} collective-permute-done((bf16[8,96,128]{2,1,0:T(8,128)(2,1)}, bf16[8,96,128]{2,1,0:T(8,128)(2,1)S(1)}, u32[]{:S(2)}, u32[]{:S(2)}) %collective-permute-start.4) | collective-permute-done | bytes 196640 | tf_op jit(solution)/shard_map/ppermute | solution.py:262
  65.9 2.9 %collective-permute-done.6.refs_3_ = bf16[8,96,128]{2,1,0:T(8,128)(2,1)S(1)} collective-permute-done((bf16[8,96,128]{2,1,0:T(8,128)(2,1)}, bf16[8,96,128]{2,1,0:T(8,128)(2,1)S(1)}, u32[]{:S(2)}, u32[]{:S(2)}) %collective-permute-start.6) | collective-permute-done | bytes 196640 | tf_op jit(solution)/shard_map/ppermute | solution.py:262
  68.8 0.1 shard_map.73
  68.9 1.1 collective-permute-start.7
  70.0 0.1 pad_add_fusion.place_ref.refs_0_
  70.1 3.6 %collective-permute-done.7.came_ref = bf16[4,96,128]{2,1,0:T(8,128)(2,1)S(1)} collective-permute-done((bf16[4,96,128]{2,1,0:T(8,128)(2,1)S(1)}, bf16[4,96,128]{2,1,0:T(8,128)(2,1)S(1)}, u32[]{:S(2)}, u32[]{:S(2)}) %collective-permute-start.7) | collective-permute-done | bytes 98336 | tf_op jit(solution)/shard_map/ppermute | solution.py:270
  73.7 0.6 shard_map.74
  74.3 0.0 all-to-all-done.refs_1_
  74.3 4.1 %collective-permute-start.10 = (bf16[416,128]{1,0:T(8,128)(2,1)S(1)}, bf16[416,128]{1,0:T(8,128)(2,1)S(1)}, u32[]{:S(2)}, u32[]{:S(2)}) collective-permute-start(bf16[416,128]{1,0:T(8,128)(2,1)S(1)} %get-tuple-element.29), channel_id=1, source_target_pairs={{0,192},{64,128},{128,64},{192,0},{1,193},{65,129},{129,65},{193,1... | collective-permute-start | bytes 319496 | tf_op jit(solution)/shard_map/ppermute | solution.py:216
  78.4 2.4 %collective-permute-start.8 = (bf16[416,128]{1,0:T(8,128)(2,1)S(1)}, bf16[416,128]{1,0:T(8,128)(2,1)S(1)}, u32[]{:S(2)}, u32[]{:S(2)}) collective-permute-start(bf16[416,128]{1,0:T(8,128)(2,1)S(1)} %get-tuple-element.27), channel_id=1, source_target_pairs={{0,64},{64,0},{128,192},{192,128},{1,65},{65,1},{129,193},{193,129... | collective-permute-start | bytes 319496 | tf_op jit(solution)/shard_map/ppermute | solution.py:216
  80.8 0.1 collective-permute-start.9
  80.9 3.6 %collective-permute-done.10.refs_2_.refs_5_ = bf16[416,128]{1,0:T(8,128)(2,1)S(1)} collective-permute-done((bf16[416,128]{1,0:T(8,128)(2,1)S(1)}, bf16[416,128]{1,0:T(8,128)(2,1)S(1)}, u32[]{:S(2)}, u32[]{:S(2)}) %collective-permute-start.10) | collective-permute-done | bytes 106528 | tf_op jit(solution)/shard_map/ppermute | solution.py:216
  84.4 4.5 %collective-permute-done.8.refs_0_.refs_3_ = bf16[416,128]{1,0:T(8,128)(2,1)S(1)} collective-permute-done((bf16[416,128]{1,0:T(8,128)(2,1)S(1)}, bf16[416,128]{1,0:T(8,128)(2,1)S(1)}, u32[]{:S(2)}, u32[]{:S(2)}) %collective-permute-start.8) | collective-permute-done | bytes 106528 | tf_op jit(solution)/shard_map/ppermute | solution.py:216
  88.9 2.2 %collective-permute-done.9.refs_1_.refs_4_ = bf16[416,128]{1,0:T(8,128)(2,1)S(1)} collective-permute-done((bf16[416,128]{1,0:T(8,128)(2,1)S(1)}, bf16[416,128]{1,0:T(8,128)(2,1)S(1)}, u32[]{:S(2)}, u32[]{:S(2)}) %collective-permute-start.9) | collective-permute-done | bytes 106528 | tf_op jit(solution)/shard_map/ppermute | solution.py:216
  91.1 0.6 shard_map.75.refs_6_
  91.7 1.5 %collective-permute-start.11 = (bf16[4,96,128]{2,1,0:T(8,128)(2,1)S(1)}, bf16[4,96,128]{2,1,0:T(8,128)(2,1)S(1)}, u32[]{:S(2)}, u32[]{:S(2)}) collective-permute-start(bf16[4,96,128]{2,1,0:T(8,128)(2,1)S(1)} %shard_map.75.refs_6_), channel_id=1, source_target_pairs={{0,1},{1,2},{2,3},{3,0},{4,5},{5,6},{6,7},{7,4},{8,9},{9,10},{10,1... | collective-permute-start | bytes 294920 | tf_op jit(solution)/shard_map/ppermute | solution.py:216
  93.2 2.7 %collective-permute-start.12 = (bf16[4,96,128]{2,1,0:T(8,128)(2,1)S(1)}, bf16[4,96,128]{2,1,0:T(8,128)(2,1)S(1)}, u32[]{:S(2)}, u32[]{:S(2)}) collective-permute-start(bf16[4,96,128]{2,1,0:T(8,128)(2,1)S(1)} %shard_map.75.refs_6_), channel_id=1, source_target_pairs={{0,2},{1,3},{2,0},{3,1},{4,6},{5,7},{6,4},{7,5},{8,10},{9,11},{10,... | collective-permute-start | bytes 294920 | tf_op jit(solution)/shard_map/ppermute | solution.py:216
  95.9 1.5 %collective-permute-start.13 = (bf16[4,96,128]{2,1,0:T(8,128)(2,1)S(1)}, bf16[4,96,128]{2,1,0:T(8,128)(2,1)S(1)}, u32[]{:S(2)}, u32[]{:S(2)}) collective-permute-start(bf16[4,96,128]{2,1,0:T(8,128)(2,1)S(1)} %shard_map.75.refs_6_), channel_id=1, source_target_pairs={{0,3},{1,0},{2,1},{3,2},{4,7},{5,4},{6,5},{7,6},{8,11},{9,8},{10,9... | collective-permute-start | bytes 294920 | tf_op jit(solution)/shard_map/ppermute | solution.py:216
  97.3 0.3 collective-permute-done.11.refs_7_
  97.6 1.9 %collective-permute-done.12.refs_8_ = bf16[4,96,128]{2,1,0:T(8,128)(2,1)S(1)} collective-permute-done((bf16[4,96,128]{2,1,0:T(8,128)(2,1)S(1)}, bf16[4,96,128]{2,1,0:T(8,128)(2,1)S(1)}, u32[]{:S(2)}, u32[]{:S(2)}) %collective-permute-start.12) | collective-permute-done | bytes 98336 | tf_op jit(solution)/shard_map/ppermute | solution.py:216
  99.5 1.0 collective-permute-done.13.refs_9_
  100.5 1.3 %shard_map.76 = bf16[16,48,512]{2,1,0:T(8,128)(2,1)S(1)} custom-call(s32[3]{0:T(128)S(1)} %pad_add_fusion.place_ref.refs_0_, bf16[16,64,512]{2,1,0:T(8,128)(2,1)S(1)} %all-to-all-done.refs_1_, bf16[32,128]{1,0:T(8,128)(2,1)S(1)} %get-tuple-element.26.extra_ref.refs_2_, bf16[416,128]{1,0:T(8,128)(2,1)S(1)} %collective-permute-done.8.refs_0_.refs_3_, ...), custom_call_target="tpu_custom_call" | custom-call | flops 201326592 | bytes 2097152 | tf_op jit(solution)/shard_map/pallas_call | solution.py:94
  101.8 26.6 %all_to_all.10.refs_0_ = bf16[16,48,512]{2,1,0:T(8,128)(2,1)S(1)} all-to-all(bf16[16,48,512]{2,1,0:T(8,128)(2,1)S(1)} %shard_map.76), channel_id=1, replica_groups=mesh['zg'=4,'zl'=2,'y'=4,'core'=2,'smp'=4] {'smp','zg'}, dimensions={0} | all-to-all | bytes 1572864 | tf_op jit(solution)/shard_map/all_to_all | solution.py:316
  128.4 1.0 shard_map.77
  (7 shorter events, 0.0 us)
Async XLA Ops:
  33.0 10.4 %copy-start.1 = (bf16[2048,192]{0,1:T(8,128)(2,1)S(1)}, bf16[2048,192]{0,1:T(8,128)(2,1)}, u32[]{:S(2)}) copy-start(bf16[2048,192]{0,1:T(8,128)(2,1)} %param.8) | copy-start | bytes 2359300
  33.0 10.4 %copy-start.2 = (bf16[64,2048]{1,0:T(8,128)(2,1)S(1)}, bf16[64,2048]{1,0:T(8,128)(2,1)}, u32[]{:S(2)}) copy-start(bf16[64,2048]{1,0:T(8,128)(2,1)} %refs_2_.15) | copy-start | bytes 786436
  33.0 41.3 %all-to-all-start = ((bf16[16,64,512]{2,1,0:T(8,128)(2,1)}), bf16[16,64,512]{2,1,0:T(8,128)(2,1)S(1)}, u32[]{:S(2)}, u32[]{:S(2)}) async-start(bf16[16,64,512]{2,1,0:T(8,128)(2,1)} %shard_map.64), calls=%async_computation | async-start | bytes 2097152 | tf_op jit(solution)/shard_map/all_to_all | solution.py:233
  43.3 0.7 copy-start.3
  45.4 5.3 %collective-permute-start.1 = (f32[8,96,128]{2,1,0:T(8,128)S(1)}, f32[8,96,128]{2,1,0:T(8,128)S(1)}, u32[]{:S(2)}, u32[]{:S(2)}) collective-permute-start(f32[8,96,128]{2,1,0:T(8,128)S(1)} %shard_map.67), channel_id=1, source_target_pairs={{0,4},{4,0},{1,5},{5,1},{2,6},{6,2},{3,7},{7,3},{8,12},{12,8},{9,1... | collective-permute-start | bytes 1179656 | tf_op jit(solution)/shard_map/ppermute | solution.py:258
  46.8 7.5 %collective-permute-start.3 = (f32[8,96,128]{2,1,0:T(8,128)S(1)}, f32[8,96,128]{2,1,0:T(8,128)S(1)}, u32[]{:S(2)}, u32[]{:S(2)}) collective-permute-start(f32[8,96,128]{2,1,0:T(8,128)S(1)} %shard_map.69), channel_id=1, source_target_pairs={{0,4},{4,0},{1,5},{5,1},{2,6},{6,2},{3,7},{7,3},{8,12},{12,8},{9,1... | collective-permute-start | bytes 1179656 | tf_op jit(solution)/shard_map/ppermute | solution.py:258
  48.7 8.6 %collective-permute-start.5 = (f32[8,96,128]{2,1,0:T(8,128)S(1)}, f32[8,96,128]{2,1,0:T(8,128)S(1)}, u32[]{:S(2)}, u32[]{:S(2)}) collective-permute-start(f32[8,96,128]{2,1,0:T(8,128)S(1)} %shard_map.71), channel_id=1, source_target_pairs={{0,4},{4,0},{1,5},{5,1},{2,6},{6,2},{3,7},{7,3},{8,12},{12,8},{9,1... | collective-permute-start | bytes 1179656 | tf_op jit(solution)/shard_map/ppermute | solution.py:258
  50.1 12.2 %collective-permute-start = (f32[8,96,128]{2,1,0:T(8,128)S(1)}, f32[8,96,128]{2,1,0:T(8,128)S(1)}, u32[]{:S(2)}, u32[]{:S(2)}) collective-permute-start(f32[8,96,128]{2,1,0:T(8,128)S(1)} %shard_map.65), channel_id=1, source_target_pairs={{0,4},{4,0},{1,5},{5,1},{2,6},{6,2},{3,7},{7,3},{8,12},{12,8},{9,1... | collective-permute-start | bytes 1179656 | tf_op jit(solution)/shard_map/ppermute | solution.py:258
  52.7 11.0 %collective-permute-start.2 = (bf16[8,96,128]{2,1,0:T(8,128)(2,1)}, bf16[8,96,128]{2,1,0:T(8,128)(2,1)S(1)}, u32[]{:S(2)}, u32[]{:S(2)}) collective-permute-start(bf16[8,96,128]{2,1,0:T(8,128)(2,1)} %shard_map.68), channel_id=1, source_target_pairs={{0,8},{8,16},{16,24},{24,0},{1,9},{9,17},{17,25},{25,1},{2,10},{10... | collective-permute-start | bytes 589832 | tf_op jit(solution)/shard_map/ppermute | solution.py:262
  56.3 9.5 %collective-permute-start.4 = (bf16[8,96,128]{2,1,0:T(8,128)(2,1)}, bf16[8,96,128]{2,1,0:T(8,128)(2,1)S(1)}, u32[]{:S(2)}, u32[]{:S(2)}) collective-permute-start(bf16[8,96,128]{2,1,0:T(8,128)(2,1)} %shard_map.70), channel_id=1, source_target_pairs={{0,16},{8,24},{16,0},{24,8},{1,17},{9,25},{17,1},{25,9},{2,18},{10... | collective-permute-start | bytes 589832 | tf_op jit(solution)/shard_map/ppermute | solution.py:262
  59.3 9.5 %collective-permute-start.6 = (bf16[8,96,128]{2,1,0:T(8,128)(2,1)}, bf16[8,96,128]{2,1,0:T(8,128)(2,1)S(1)}, u32[]{:S(2)}, u32[]{:S(2)}) collective-permute-start(bf16[8,96,128]{2,1,0:T(8,128)(2,1)} %shard_map.72), channel_id=1, source_target_pairs={{0,24},{8,0},{16,8},{24,16},{1,25},{9,1},{17,9},{25,17},{2,26},{10... | collective-permute-start | bytes 589832 | tf_op jit(solution)/shard_map/ppermute | solution.py:262
  68.8 4.9 %copy-start = (f32[2,8192]{1,0:T(2,128)S(1)}, f32[2,8192]{1,0:T(2,128)}, u32[]{:S(2)}) copy-start(f32[2,8192]{1,0:T(2,128)} %twiddle_ref.1) | copy-start | bytes 196612
  68.9 4.8 %collective-permute-start.7 = (bf16[4,96,128]{2,1,0:T(8,128)(2,1)S(1)}, bf16[4,96,128]{2,1,0:T(8,128)(2,1)S(1)}, u32[]{:S(2)}, u32[]{:S(2)}) collective-permute-start(bf16[4,96,128]{2,1,0:T(8,128)(2,1)S(1)} %get-tuple-element.20), channel_id=1, source_target_pairs={{0,32},{32,0},{1,33},{33,1},{2,34},{34,2},{3,35},{35,3},{4,36},{36... | collective-permute-start | bytes 294920 | tf_op jit(solution)/shard_map/ppermute | solution.py:270
  74.3 10.1 %collective-permute-start.10 = (bf16[416,128]{1,0:T(8,128)(2,1)S(1)}, bf16[416,128]{1,0:T(8,128)(2,1)S(1)}, u32[]{:S(2)}, u32[]{:S(2)}) collective-permute-start(bf16[416,128]{1,0:T(8,128)(2,1)S(1)} %get-tuple-element.29), channel_id=1, source_target_pairs={{0,192},{64,128},{128,64},{192,0},{1,193},{65,129},{129,65},{193,1... | collective-permute-start | bytes 319496 | tf_op jit(solution)/shard_map/ppermute | solution.py:216
  78.4 10.5 %collective-permute-start.8 = (bf16[416,128]{1,0:T(8,128)(2,1)S(1)}, bf16[416,128]{1,0:T(8,128)(2,1)S(1)}, u32[]{:S(2)}, u32[]{:S(2)}) collective-permute-start(bf16[416,128]{1,0:T(8,128)(2,1)S(1)} %get-tuple-element.27), channel_id=1, source_target_pairs={{0,64},{64,0},{128,192},{192,128},{1,65},{65,1},{129,193},{193,129... | collective-permute-start | bytes 319496 | tf_op jit(solution)/shard_map/ppermute | solution.py:216
  80.8 10.3 %collective-permute-start.9 = (bf16[416,128]{1,0:T(8,128)(2,1)S(1)}, bf16[416,128]{1,0:T(8,128)(2,1)S(1)}, u32[]{:S(2)}, u32[]{:S(2)}) collective-permute-start(bf16[416,128]{1,0:T(8,128)(2,1)S(1)} %get-tuple-element.28), channel_id=1, source_target_pairs={{0,128},{64,192},{128,0},{192,64},{1,129},{65,193},{129,1},{193,65... | collective-permute-start | bytes 319496 | tf_op jit(solution)/shard_map/ppermute | solution.py:216
  91.7 5.9 %collective-permute-start.11 = (bf16[4,96,128]{2,1,0:T(8,128)(2,1)S(1)}, bf16[4,96,128]{2,1,0:T(8,128)(2,1)S(1)}, u32[]{:S(2)}, u32[]{:S(2)}) collective-permute-start(bf16[4,96,128]{2,1,0:T(8,128)(2,1)S(1)} %shard_map.75.refs_6_), channel_id=1, source_target_pairs={{0,1},{1,2},{2,3},{3,0},{4,5},{5,6},{6,7},{7,4},{8,9},{9,10},{10,1... | collective-permute-start | bytes 294920 | tf_op jit(solution)/shard_map/ppermute | solution.py:216
  93.2 6.3 %collective-permute-start.12 = (bf16[4,96,128]{2,1,0:T(8,128)(2,1)S(1)}, bf16[4,96,128]{2,1,0:T(8,128)(2,1)S(1)}, u32[]{:S(2)}, u32[]{:S(2)}) collective-permute-start(bf16[4,96,128]{2,1,0:T(8,128)(2,1)S(1)} %shard_map.75.refs_6_), channel_id=1, source_target_pairs={{0,2},{1,3},{2,0},{3,1},{4,6},{5,7},{6,4},{7,5},{8,10},{9,11},{10,... | collective-permute-start | bytes 294920 | tf_op jit(solution)/shard_map/ppermute | solution.py:216
  95.9 4.6 %collective-permute-start.13 = (bf16[4,96,128]{2,1,0:T(8,128)(2,1)S(1)}, bf16[4,96,128]{2,1,0:T(8,128)(2,1)S(1)}, u32[]{:S(2)}, u32[]{:S(2)}) collective-permute-start(bf16[4,96,128]{2,1,0:T(8,128)(2,1)S(1)} %shard_map.75.refs_6_), channel_id=1, source_target_pairs={{0,3},{1,0},{2,1},{3,2},{4,7},{5,4},{6,5},{7,6},{8,11},{9,8},{10,9... | collective-permute-start | bytes 294920 | tf_op jit(solution)/shard_map/ppermute | solution.py:216

commit v9 on v6

--- a/solution.py
+++ b/solution.py
@@ -13,59 +13,72 @@
 SMEM = pl.BlockSpec(memory_space=pltpu.SMEM)
 
 
-def partial_kernel(place_ref, owners_ref, adjoint_ref, probes_ref, out_ref, masked, wide):
+def split_kernel(source_ref, out_ref):
+    points = out_ref.shape[2]
+    for i in range(out_ref.shape[0]):
+        out_ref[i] = source_ref[:, i * points:(i + 1) * points]
+
+
+def split(source, pieces):
+    rows, points = source.shape
+    steps = 4
+    return pl.pallas_call(
+        split_kernel,
+        grid=(steps,),
+        out_shape=jax.ShapeDtypeStruct((pieces, rows, points // pieces), source.dtype),
+        in_specs=[pl.BlockSpec((rows, points // steps), lambda i: (0, i))],
+        out_specs=pl.BlockSpec((pieces // steps, rows, points // pieces), lambda i: (i, 0, 0)),
+        compiler_params=pltpu.CompilerParams(vmem_limit_bytes=56 * MIB),
+        cost_estimate=pl.CostEstimate(flops=0, bytes_accessed=2 * MIB, transcendentals=0),
+    )(source)
+
+
+def partial_kernel(y_count, offsets, other, place_ref, owners_ref, adjoint_ref, probes_ref, *refs):
+    out_ref, masked = refs
     step = pl.program_id(0)
-    y_count = pl.num_programs(0)
+    samples = adjoint_ref.shape[0]
     z_count = out_ref.shape[1]
-    samples = adjoint_ref.shape[0]
-    vectors = probes_ref.shape[0]
-
-    @pl.when(step == 0)
-    def _():
-        wide[:vectors, :] = probes_ref[...]
-        wide[vectors:, :] = probes_ref[128:, :]
-
     own = owners_ref[...]
     adjoint = adjoint_ref[...]
-    y = lax.rem(place_ref[0] + step, y_count)
-    for offset in range(z_count):
-        owner = (offset * y_count + y) * 2 + place_ref[1]
-        hot = jnp.where(own == owner, 1.0, 0.0).astype(jnp.bfloat16)
-        masked[offset * samples:(offset + 1) * samples, :] = adjoint * hot
+    offset = offsets[-1]
+    for i, value in enumerate(offsets[:-1]):
+        offset = jnp.where(step == i, value, offset)
+    y = lax.rem(place_ref[0] + offset, y_count)
+    core = 1 - place_ref[1] if other else place_ref[1]
+    for z in range(z_count):
+        hot = jnp.where(own == (z * y_count + y) * 2 + core, 1.0, 0.0).astype(jnp.bfloat16)
+        masked[z * samples:(z + 1) * samples, :] = adjoint * hot
     product = lax.dot_general(
-        masked[...], wide[...], (((1,), (1,)), ((), ())), preferred_element_type=jnp.float32
+        masked[...], probes_ref[...], (((1,), (1,)), ((), ())), preferred_element_type=jnp.float32
     )
     half = samples // 2
-    low = lax.broadcasted_iota(jnp.int32, (half, 128), 1) < 64
-    for offset in range(z_count):
-        block = product[offset * samples:(offset + 1) * samples, :]
-        out_ref[0, offset, :samples, :] = block[:, :128]
-        out_ref[0, offset, samples:, :] = jnp.where(low, block[:half, 128:], block[half:, 128:])
-
-
-def partial_coeffs(place, owners, adjoint, probes):
+    for z in range(z_count):
+        block = product[z * samples:(z + 1) * samples, :]
+        out_ref[0, z, :samples, :] = block[:, :128]
+        tail = jnp.concatenate([block[:half, 128:], block[half:, 128:]], axis=1)
+        out_ref[0, z, samples:, :] = tail
+
+
+def partial_coeffs(offsets, other, place, owners, adjoint, probes):
     samples, rows = adjoint.shape
     vectors = probes.shape[0]
     y_count, z_count = lax.axis_size("y"), lax.axis_size(Z_AXES)
-    packed = samples * vectors // 128
+    shape = (len(offsets), z_count, samples * vectors // 128, 128)
     return pl.pallas_call(
-        partial_kernel,
-        grid=(y_count,),
+        lambda *refs: partial_kernel(y_count, offsets, other, *refs),
+        grid=(len(offsets),),
         in_specs=[
             SMEM,
             pl.BlockSpec((1, rows), lambda i: (0, 0)),
             pl.BlockSpec((samples, rows), lambda i: (0, 0)),
             pl.BlockSpec((vectors, rows), lambda i: (0, 0)),
         ],
-        out_specs=pl.BlockSpec((1, z_count, packed, 128), lambda i: (i, 0, 0, 0)),
-        out_shape=jax.ShapeDtypeStruct((y_count, z_count, packed, 128), jnp.float32),
-        scratch_shapes=[
-            pltpu.VMEM((z_count * samples, rows), jnp.bfloat16),
-            pltpu.VMEM((256, rows), jnp.bfloat16),
-        ],
-        compiler_params=pltpu.CompilerParams(vmem_limit_bytes=24 * MIB),
+        out_specs=pl.BlockSpec((1,) + shape[1:], lambda i: (i, 0, 0, 0)),
+        out_shape=jax.ShapeDtypeStruct(shape, jnp.float32),
+        scratch_shapes=[pltpu.VMEM((z_count * samples, rows), jnp.bfloat16)],
+        compiler_params=pltpu.CompilerParams(vmem_limit_bytes=12 * MIB),
         cost_estimate=pl.CostEstimate(
-            flops=2 * y_count * z_count * samples * rows * 256,
+            flops=2 * len(offsets) * z_count * samples * rows * 256,
             bytes_accessed=3 * MIB,
             transcendentals=0,
         ),
@@ -79,15 +92,14 @@
         in_specs=[SMEM] * smem + [VMEM] * (len(args) - smem),
         out_specs=jax.tree.map(lambda _: VMEM, out_shape),
         scratch_shapes=list(scratch),
-        compiler_params=pltpu.CompilerParams(vmem_limit_bytes=24 * MIB),
+        compiler_params=pltpu.CompilerParams(vmem_limit_bytes=12 * MIB),
         cost_estimate=pl.CostEstimate(flops=flops, bytes_accessed=2 * MIB, transcendentals=0),
     )(*args)
 
 
-def merge_kernel(kept_ref, came_ref, own_ref, *out_refs):
-    own_ref[...] = kept_ref[0] + came_ref[0]
-    for offset, out_ref in enumerate(out_refs, 1):
-        out_ref[...] = (kept_ref[offset] + came_ref[offset]).astype(out_ref.dtype)
+def merge_kernel(kept_ref, came_ref, *out_refs):
+    for i, out_ref in enumerate(out_refs):
+        out_ref[...] = (kept_ref[i] + came_ref[i]).astype(out_ref.dtype)
 
 
 def halve_kernel(place_ref, *refs):
@@ -135,7 +147,7 @@
 
 
 def weights_kernel(place_ref, own_ref, extra_ref, *refs):
-    offers, out_ref = refs[:-1], refs[-1]
+    offers, (out_ref, rows_ref) = refs[:-2], refs[-2:]
     blocks, packed, lanes = own_ref.shape
     samples = packed * 2 // 3
     row = lax.broadcasted_iota(jnp.int32, (packed, lanes), 0)
@@ -148,32 +160,32 @@
         for offer in offers:
             total = total + offer[block * packed:(block + 1) * packed, :].astype(jnp.float32)
         extra = offers[block - 1][blocks * packed:, :] if block else extra_ref[...]
+        rows_ref[block] = extra
         rank = extra.astype(jnp.float32)[6:7]
         out_ref[block] = jnp.where(sample < rank, total, 0.0).astype(jnp.bfloat16)
 
 
-def field_kernel(blocks, parts, place_ref, samples_ref, extra_ref, *refs):
-    offers, weight_refs = refs[:blocks - 1], refs[blocks - 1:-2]
-    out_ref, field = refs[-2:]
+def field_kernel(blocks, parts, place_ref, samples_ref, rows_ref, *refs):
+    weight_refs = refs[:-3]
+    out_ref, field, every = refs[-3:]
     zg, smp = place_ref[0], place_ref[1]
     vectors, points = field.shape[1:]
     samples = samples_ref.shape[1]
-    packed = weight_refs[0].shape[1]
+    for p in range(parts):
+        every[lax.rem(smp - p + parts, parts)] = weight_refs[p][...]
     factors = []
     for c in range(blocks):
-        head, tail, columns, grid = [], [], [], []
+        head, tail, columns = [], [], []
         for p in range(parts):
-            grid.append(samples_ref[(zg ^ c) * parts + lax.rem(smp - p + parts, parts)])
-            head.append(weight_refs[p][c, :samples, :])
-            rest = weight_refs[p][c, samples:, :]
+            head.append(every[p, c, :samples, :])
+            rest = every[p, c, samples:, :]
             tail += [rest[:, :64], rest[:, 64:]]
-        extra = offers[c - 1][blocks * packed:, :] if c else extra_ref[...]
-        extra = extra.astype(jnp.float32)
+        extra = rows_ref[c].astype(jnp.float32)
         for column in range(extra.shape[0] // 8):
             terms = extra[column * 8:column * 8 + 8]
             columns.append(terms[0:2] + terms[2:4] + terms[4:6])
         factors.append(jnp.concatenate(columns, axis=1))
-        grid = jnp.concatenate(grid, axis=0)
+        grid = samples_ref[pl.ds((zg ^ c) * parts, parts)].reshape(parts * samples, points)
         head = jnp.concatenate(head, axis=0)
         tail = jnp.concatenate(tail, axis=0)
         field[c, :128, :] = lax.dot_general(
@@ -214,20 +226,26 @@
     smp = lax.axis_index("smp")
     y, core = lax.axis_index("y"), lax.axis_index("core")
 
-    pieces = forward_samples.reshape(samples, members, piece).transpose(1, 0, 2)
+    pieces = split(forward_samples, members)
     own, probes = owners.T, probe_values.T
     pieces, own = lax.optimization_barrier((pieces, own))
     pieces = lax.all_to_all(pieces, GROUP, 0, 0, tiled=True)
 
-    sent = partial_coeffs(jnp.stack([y, 1 - core]), own, adjoint_samples, probes)
+    place = jnp.stack([y, core])
+    order = sorted(range(y_count), key=lambda k: (k == 0, abs(k - y_count // 2)))
+    sent = partial_coeffs(order, True, place, own, adjoint_samples, probes)
     came = lax.ppermute(sent, "core", [(0, 1), (1, 0)])
-    kept = partial_coeffs(jnp.stack([y, core]), own, adjoint_samples, probes)
-    shape = kept.shape[1:]
-    shapes = [jax.ShapeDtypeStruct(shape, jnp.float32)]
-    shapes += [jax.ShapeDtypeStruct(shape, jnp.bfloat16)] * (y_count - 1)
-    sums = local_call(merge_kernel, shapes, kept, came)
-    came = exchange(dict(enumerate(sums[1:], 1)), "y", lambda i, k: i + k)
-    sums = [sums[0]] + came
+    shape = sent.shape[1:]
+    kept = partial_coeffs(order, False, place, own, adjoint_samples, probes)
+    kinds = [jnp.bfloat16 if offset else jnp.float32 for offset in order]
+    merged = local_call(
+        merge_kernel, [jax.ShapeDtypeStruct(shape, kind) for kind in kinds], kept, came
+    )
+    sums = {}
+    for offset, value in zip(order, merged):
+        route = [(i, (i + offset) % y_count) for i in range(y_count)]
+        sums[offset] = lax.ppermute(value, "y", route) if offset else value
+    sums = [sums[offset] for offset in range(y_count)]
     shape = (groups,) + shape[1:]
     shapes = [jax.ShapeDtypeStruct(shape, jnp.float32), jax.ShapeDtypeStruct(shape, jnp.bfloat16)]
     zl = lax.axis_index("zl")
@@ -252,9 +270,11 @@
     )
     *offers, pieces = lax.optimization_barrier((*offers, pieces))
     offers = exchange(dict(enumerate(offers, 1)), "zg", lambda i, k: i ^ k)
-    weights = local_call(
+    shapes = [jax.ShapeDtypeStruct(shape, jnp.bfloat16)]
+    shapes += [jax.ShapeDtypeStruct((groups,) + extra.shape, jnp.bfloat16)]
+    weights, factors = local_call(
         weights_kernel,
-        jax.ShapeDtypeStruct(shape, jnp.bfloat16),
+        shapes,
         place,
         partial,
         extra,
@@ -267,12 +287,14 @@
         jax.ShapeDtypeStruct((members, vectors // parts, piece), jnp.bfloat16),
         place,
         pieces,
-        extra,
-        *offers,
+        factors,
         weights,
         *others,
         smem=1,
-        scratch=[pltpu.VMEM((groups, vectors, piece), jnp.float32)],
+        scratch=[
+            pltpu.VMEM((groups, vectors, piece), jnp.float32),
+            pltpu.VMEM((parts,) + shape, jnp.bfloat16),
+        ],
         flops=2 * members * samples * vectors * piece,
     )
     result = lax.all_to_all(result, GROUP, 0, 0, tiled=True)

time: 97.6 us -> 98.7 us (1.011)
  Pallas kernels: 10.2 us -> 13.7 us
  local copies, waits for them, and re-layouts: 3.29 us -> 0.97 us
    ppermute x0 -> x3, waiting for transfers between devices: none -> 8.04 us  [body(): sums[offset] = lax.ppermute(value, 'y', route) if offset else value]
    ppermute x9 -> x6, waiting for transfers between devices: 21.7 us -> 13.7 us  [exchange(): came[offset] = lax.ppermute(pieces[offset], axis, pairs)]
    ppermute x9 -> x6, starting transfers between devices: 16.7 us -> 11.6 us  [exchange(): came[offset] = lax.ppermute(pieces[offset], axis, pairs)]
    ppermute x0 -> x3, starting transfers between devices: none -> 5 us  [body(): sums[offset] = lax.ppermute(value, 'y', route) if offset else value]
    pallas_call x2 -> x3, Pallas kernels: 7.34 us -> 10.9 us  [the longest x2 7.5 us: partial_coeffs(): pl.pallas_call(lambda *refs: partial_kernel(y_count, offsets, other, *ref...]
    reshape x1 -> x0, local copies, waits for them, and re-layouts: 2.32 us -> none  [body(): pieces = forward_samples.reshape(samples, members, piece).transpose(1, 0, 2)]
where the time goes in v9:
time: 98.7 us; the launch traced here: 98.1 us
  starting transfers between devices  28.1 us (28%)
  waiting for transfers between devices  27.4 us (28%)
  blocking collectives  27.1 us (27%)
  Pallas kernels  13.7 us (14%)
    all_to_all x1, blocking collectives, body(): result = lax.all_to_all(result, GROUP, 0, 0, tiled=True)  27.1 us
    ppermute x6, waiting for transfers between devices, exchange(): came[offset] = lax.ppermute(pieces[offset], axis, pairs)  13.7 us
    ppermute x6, starting transfers between devices, exchange(): came[offset] = lax.ppermute(pieces[offset], axis, pairs)  11.6 us
    all_to_all x1, starting transfers between devices, body(): pieces = lax.all_to_all(pieces, GROUP, 0, 0, tiled=True)  10.3 us
    ppermute x3, waiting for transfers between devices, body(): sums[offset] = lax.ppermute(value, 'y', route) if offset else value  8.04 us
    pallas_call x2, Pallas kernels, partial_coeffs(): pl.pallas_call(lambda *refs: partial_kernel(y_count, offsets, other, *ref...  7.5 us
    ppermute x1, waiting for transfers between devices, body(): came = lax.ppermute(sent, 'zl', [(0, 1), (1, 0)])  5.09 us
    ppermute x3, starting transfers between devices, body(): sums[offset] = lax.ppermute(value, 'y', route) if offset else value  5 us
  transfers between devices with their start and end apart: 12, of which 9 were waited for; matrix products, arithmetic and copies ran while one was open for 0% of the time, Pallas kernels for 9%

profile of v9, /device:TPU:40, one launch (start us, length us, event | category | flops | bytes accessed | tf_op | source)
XLA Modules:
  0.0 98.1 jit_solution(9742414329854574718)
XLA Ops:
  0.0 3.3 %shard_map.64 = bf16[16,64,512]{2,1,0:T(8,128)(2,1)} custom-call(bf16[64,8192]{1,0:T(8,128)(2,1)} %source_ref.1), custom_call_target="tpu_custom_call" | custom-call | bytes 2097152 | tf_op jit(solution)/shard_map/pallas_call | solution.py:25
  3.3 0.0 copy-start.1
  3.4 0.0 copy-start.2
  3.4 0.0 copy-start.3
  3.4 10.3 %all-to-all-start = ((bf16[16,64,512]{2,1,0:T(8,128)(2,1)}), bf16[16,64,512]{2,1,0:T(8,128)(2,1)S(1)}, u32[]{:S(2)}, u32[]{:S(2)}) async-start(bf16[16,64,512]{2,1,0:T(8,128)(2,1)} %shard_map.64), calls=%async_computation | async-start | bytes 2097152 | tf_op jit(solution)/shard_map/all_to_all | solution.py:232
  13.6 0.1 pad_add_fusion.1.refs_0_
  13.7 0.0 copy-done.1
  13.7 0.0 copy-done.2
  13.7 0.0 copy-done.3
  13.7 3.8 %shard_map.66 = f32[4,8,96,128]{3,2,1,0:T(8,128)S(1)} custom-call(s32[2]{0:T(128)S(1)} %pad_add_fusion.1.refs_0_, s32[1,2048]{1,0:T(1,128)S(1)} %bitcast.12, bf16[64,2048]{1,0:T(8,128)(2,1)S(1)} %copy-done.2, bf16[192,2048]{1,0:T(8,128)(2,1)S(1)} %bitcast.10), custom_call_target="tpu_custom_call" | custom-call | flops 2147483648 | bytes 3145728 | tf_op jit(solution)/shard_map/pallas_call | solution.py:67
  17.5 0.1 collective-permute-start
  17.6 3.8 %shard_map.65.kept_ref = f32[4,8,96,128]{3,2,1,0:T(8,128)S(1)} custom-call(s32[2]{0:T(128)S(1)} %pad_add_fusion.1.refs_0_, s32[1,2048]{1,0:T(1,128)S(1)} %bitcast.13, bf16[64,2048]{1,0:T(8,128)(2,1)S(1)} %copy-done.2, bf16[192,2048]{1,0:T(8,128)(2,1)S(1)} %bitcast.11), custom_call_target="tpu_custom_call" | custom-call | flops 2147483648 | bytes 3145728 | tf_op jit(solution)/shard_map/pallas_call | solution.py:67
  21.3 0.0 copy-start
  21.4 0.0 collective-permute-done.came_ref
  21.4 0.1 shard_map.67
  21.5 1.6 %collective-permute-start.1 = (bf16[8,96,128]{2,1,0:T(8,128)(2,1)S(1)}, bf16[8,96,128]{2,1,0:T(8,128)(2,1)S(1)}, u32[]{:S(2)}, u32[]{:S(2)}) collective-permute-start(bf16[8,96,128]{2,1,0:T(8,128)(2,1)S(1)} %get-tuple-element.26), channel_id=1, source_target_pairs={{0,8},{8,16},{16,24},{24,0},{1,9},{9,17},{17,25},{25,1},{2,10},{10... | collective-permute-start | bytes 589832 | tf_op jit(solution)/shard_map/ppermute | solution.py:247
  23.2 1.0 collective-permute-start.2
  24.1 2.4 %collective-permute-start.3 = (bf16[8,96,128]{2,1,0:T(8,128)(2,1)S(1)}, bf16[8,96,128]{2,1,0:T(8,128)(2,1)S(1)}, u32[]{:S(2)}, u32[]{:S(2)}) collective-permute-start(bf16[8,96,128]{2,1,0:T(8,128)(2,1)S(1)} %get-tuple-element.28), channel_id=1, source_target_pairs={{0,24},{8,0},{16,8},{24,16},{1,25},{9,1},{17,9},{25,17},{2,26},{10... | collective-permute-start | bytes 589832 | tf_op jit(solution)/shard_map/ppermute | solution.py:247
  27.2 2.1 %collective-permute-done.1.refs_1_ = bf16[8,96,128]{2,1,0:T(8,128)(2,1)S(1)} collective-permute-done((bf16[8,96,128]{2,1,0:T(8,128)(2,1)S(1)}, bf16[8,96,128]{2,1,0:T(8,128)(2,1)S(1)}, u32[]{:S(2)}, u32[]{:S(2)}) %collective-permute-start.1) | collective-permute-done | bytes 196640 | tf_op jit(solution)/shard_map/ppermute | solution.py:247
  29.3 3.2 %collective-permute-done.2.refs_2_ = bf16[8,96,128]{2,1,0:T(8,128)(2,1)S(1)} collective-permute-done((bf16[8,96,128]{2,1,0:T(8,128)(2,1)S(1)}, bf16[8,96,128]{2,1,0:T(8,128)(2,1)S(1)}, u32[]{:S(2)}, u32[]{:S(2)}) %collective-permute-start.2) | collective-permute-done | bytes 196640 | tf_op jit(solution)/shard_map/ppermute | solution.py:247
  32.5 2.8 %collective-permute-done.3.refs_3_ = bf16[8,96,128]{2,1,0:T(8,128)(2,1)S(1)} collective-permute-done((bf16[8,96,128]{2,1,0:T(8,128)(2,1)S(1)}, bf16[8,96,128]{2,1,0:T(8,128)(2,1)S(1)}, u32[]{:S(2)}, u32[]{:S(2)}) %collective-permute-start.3) | collective-permute-done | bytes 196640 | tf_op jit(solution)/shard_map/ppermute | solution.py:247
  35.2 0.1 shard_map.68
  35.3 1.1 %collective-permute-start.4 = (bf16[4,96,128]{2,1,0:T(8,128)(2,1)S(1)}, bf16[4,96,128]{2,1,0:T(8,128)(2,1)S(1)}, u32[]{:S(2)}, u32[]{:S(2)}) collective-permute-start(bf16[4,96,128]{2,1,0:T(8,128)(2,1)S(1)} %get-tuple-element.30), channel_id=1, source_target_pairs={{0,32},{32,0},{1,33},{33,1},{2,34},{34,2},{3,35},{35,3},{4,36},{36... | collective-permute-start | bytes 294920 | tf_op jit(solution)/shard_map/ppermute | solution.py:253
  36.4 0.1 pad_add_fusion.place_ref.refs_0_
  36.5 5.1 %collective-permute-done.4.came_ref = bf16[4,96,128]{2,1,0:T(8,128)(2,1)S(1)} collective-permute-done((bf16[4,96,128]{2,1,0:T(8,128)(2,1)S(1)}, bf16[4,96,128]{2,1,0:T(8,128)(2,1)S(1)}, u32[]{:S(2)}, u32[]{:S(2)}) %collective-permute-start.4) | collective-permute-done | bytes 98336 | tf_op jit(solution)/shard_map/ppermute | solution.py:253
  41.6 0.0 copy-done
  41.6 0.6 shard_map.69
  42.2 0.6 all-to-all-done.refs_1_
  42.8 0.8 collective-permute-start.5
  43.5 4.1 %collective-permute-start.6 = (bf16[416,128]{1,0:T(8,128)(2,1)S(1)}, bf16[416,128]{1,0:T(8,128)(2,1)S(1)}, u32[]{:S(2)}, u32[]{:S(2)}) collective-permute-start(bf16[416,128]{1,0:T(8,128)(2,1)S(1)} %get-tuple-element.39), channel_id=1, source_target_pairs={{0,128},{64,192},{128,0},{192,64},{1,129},{65,193},{129,1},{193,65... | collective-permute-start | bytes 319496 | tf_op jit(solution)/shard_map/ppermute | solution.py:215
  47.6 1.7 %collective-permute-start.7 = (bf16[416,128]{1,0:T(8,128)(2,1)S(1)}, bf16[416,128]{1,0:T(8,128)(2,1)S(1)}, u32[]{:S(2)}, u32[]{:S(2)}) collective-permute-start(bf16[416,128]{1,0:T(8,128)(2,1)S(1)} %get-tuple-element.40), channel_id=1, source_target_pairs={{0,192},{64,128},{128,64},{192,0},{1,193},{65,129},{129,65},{193,1... | collective-permute-start | bytes 319496 | tf_op jit(solution)/shard_map/ppermute | solution.py:215
  49.3 0.3 collective-permute-done.5.refs_0_
  49.6 4.2 %collective-permute-done.6.refs_1_ = bf16[416,128]{1,0:T(8,128)(2,1)S(1)} collective-permute-done((bf16[416,128]{1,0:T(8,128)(2,1)S(1)}, bf16[416,128]{1,0:T(8,128)(2,1)S(1)}, u32[]{:S(2)}, u32[]{:S(2)}) %collective-permute-start.6) | collective-permute-done | bytes 106528 | tf_op jit(solution)/shard_map/ppermute | solution.py:215
  53.8 4.2 %collective-permute-done.7.refs_2_ = bf16[416,128]{1,0:T(8,128)(2,1)S(1)} collective-permute-done((bf16[416,128]{1,0:T(8,128)(2,1)S(1)}, bf16[416,128]{1,0:T(8,128)(2,1)S(1)}, u32[]{:S(2)}, u32[]{:S(2)}) %collective-permute-start.7) | collective-permute-done | bytes 106528 | tf_op jit(solution)/shard_map/ppermute | solution.py:215
  58.0 0.6 shard_map.70
  58.6 2.9 %collective-permute-start.10 = (bf16[4,96,128]{2,1,0:T(8,128)(2,1)S(1)}, bf16[4,96,128]{2,1,0:T(8,128)(2,1)S(1)}, u32[]{:S(2)}, u32[]{:S(2)}) collective-permute-start(bf16[4,96,128]{2,1,0:T(8,128)(2,1)S(1)} %get-tuple-element.42.refs_3_), channel_id=1, source_target_pairs={{0,3},{1,0},{2,1},{3,2},{4,7},{5,4},{6,5},{7,6},{8,11},{9,8},{10,9... | collective-permute-start | bytes 294920 | tf_op jit(solution)/shard_map/ppermute | solution.py:215
  61.5 0.0 collective-permute-start.8
  61.5 2.3 %collective-permute-start.9 = (bf16[4,96,128]{2,1,0:T(8,128)(2,1)S(1)}, bf16[4,96,128]{2,1,0:T(8,128)(2,1)S(1)}, u32[]{:S(2)}, u32[]{:S(2)}) collective-permute-start(bf16[4,96,128]{2,1,0:T(8,128)(2,1)S(1)} %get-tuple-element.42.refs_3_), channel_id=1, source_target_pairs={{0,2},{1,3},{2,0},{3,1},{4,6},{5,7},{6,4},{7,5},{8,10},{9,11},{10,... | collective-permute-start | bytes 294920 | tf_op jit(solution)/shard_map/ppermute | solution.py:215
  63.8 0.0 collective-permute-done.10.refs_6_
  63.8 4.9 %collective-permute-done.8.refs_4_ = bf16[4,96,128]{2,1,0:T(8,128)(2,1)S(1)} collective-permute-done((bf16[4,96,128]{2,1,0:T(8,128)(2,1)S(1)}, bf16[4,96,128]{2,1,0:T(8,128)(2,1)S(1)}, u32[]{:S(2)}, u32[]{:S(2)}) %collective-permute-start.8) | collective-permute-done | bytes 98336 | tf_op jit(solution)/shard_map/ppermute | solution.py:215
  68.7 0.0 collective-permute-done.9.refs_5_
  68.7 1.4 %shard_map.71 = bf16[16,48,512]{2,1,0:T(8,128)(2,1)S(1)} custom-call(s32[3]{0:T(128)S(1)} %pad_add_fusion.place_ref.refs_0_, bf16[16,64,512]{2,1,0:T(8,128)(2,1)S(1)} %all-to-all-done.refs_1_, bf16[4,32,128]{2,1,0:T(8,128)(2,1)S(1)} %get-tuple-element.41.refs_2_, bf16[4,96,128]{2,1,0:T(8,128)(2,1)S(1)} %get-tuple-element.42.refs_3_, ...), custom_call_target="tpu_custom_call" | custom-call | flops 201326592 | bytes 2097152 | tf_op jit(solution)/shard_map/pallas_call | solution.py:89
  70.0 27.1 %all_to_all.10 = bf16[16,48,512]{2,1,0:T(8,128)(2,1)S(1)} all-to-all(bf16[16,48,512]{2,1,0:T(8,128)(2,1)S(1)} %shard_map.71), channel_id=1, replica_groups=mesh['zg'=4,'zl'=2,'y'=4,'core'=2,'smp'=4] {'zg','smp'}, dimensions={0} | all-to-all | bytes 1572864 | tf_op jit(solution)/shard_map/all_to_all | solution.py:300
  97.1 1.0 copy.8
Async XLA Ops:
  3.3 10.4 %copy-start.1 = (bf16[2048,192]{0,1:T(8,128)(2,1)S(1)}, bf16[2048,192]{0,1:T(8,128)(2,1)}, u32[]{:S(2)}) copy-start(bf16[2048,192]{0,1:T(8,128)(2,1)} %param.8) | copy-start | bytes 2359300
  3.4 10.4 %copy-start.2 = (bf16[64,2048]{1,0:T(8,128)(2,1)S(1)}, bf16[64,2048]{1,0:T(8,128)(2,1)}, u32[]{:S(2)}) copy-start(bf16[64,2048]{1,0:T(8,128)(2,1)} %refs_2_.3) | copy-start | bytes 786436
  3.4 10.4 %copy-start.3 = (s32[2048,1]{0,1:T(1,128)S(1)}, s32[2048,1]{0,1:T(1,128)}, u32[]{:S(2)}) copy-start(s32[2048,1]{0,1:T(1,128)} %param.9) | copy-start | bytes 24580
  3.4 39.4 %all-to-all-start = ((bf16[16,64,512]{2,1,0:T(8,128)(2,1)}), bf16[16,64,512]{2,1,0:T(8,128)(2,1)S(1)}, u32[]{:S(2)}, u32[]{:S(2)}) async-start(bf16[16,64,512]{2,1,0:T(8,128)(2,1)} %shard_map.64), calls=%async_computation | async-start | bytes 2097152 | tf_op jit(solution)/shard_map/all_to_all | solution.py:232
  17.5 3.9 %collective-permute-start = (f32[4,8,96,128]{3,2,1,0:T(8,128)S(1)}, f32[4,8,96,128]{3,2,1,0:T(8,128)S(1)}, u32[]{:S(2)}, u32[]{:S(2)}) collective-permute-start(f32[4,8,96,128]{3,2,1,0:T(8,128)S(1)} %shard_map.66), channel_id=1, source_target_pairs={{0,4},{4,0},{1,5},{5,1},{2,6},{6,2},{3,7},{7,3},{8,12},{12,8},{9,1... | collective-permute-start | bytes 4718600 | tf_op jit(solution)/shard_map/ppermute | solution.py:237
  21.3 20.2 %copy-start = (f32[2,8192]{1,0:T(2,128)S(1)}, f32[2,8192]{1,0:T(2,128)}, u32[]{:S(2)}) copy-start(f32[2,8192]{1,0:T(2,128)} %twiddle_ref.1) | copy-start | bytes 196612
  21.5 7.8 %collective-permute-start.1 = (bf16[8,96,128]{2,1,0:T(8,128)(2,1)S(1)}, bf16[8,96,128]{2,1,0:T(8,128)(2,1)S(1)}, u32[]{:S(2)}, u32[]{:S(2)}) collective-permute-start(bf16[8,96,128]{2,1,0:T(8,128)(2,1)S(1)} %get-tuple-element.26), channel_id=1, source_target_pairs={{0,8},{8,16},{16,24},{24,0},{1,9},{9,17},{17,25},{25,1},{2,10},{10... | collective-permute-start | bytes 589832 | tf_op jit(solution)/shard_map/ppermute | solution.py:247
  23.2 9.3 %collective-permute-start.2 = (bf16[8,96,128]{2,1,0:T(8,128)(2,1)S(1)}, bf16[8,96,128]{2,1,0:T(8,128)(2,1)S(1)}, u32[]{:S(2)}, u32[]{:S(2)}) collective-permute-start(bf16[8,96,128]{2,1,0:T(8,128)(2,1)S(1)} %get-tuple-element.27), channel_id=1, source_target_pairs={{0,16},{8,24},{16,0},{24,8},{1,17},{9,25},{17,1},{25,9},{2,18},{10... | collective-permute-start | bytes 589832 | tf_op jit(solution)/shard_map/ppermute | solution.py:247
  24.1 11.1 %collective-permute-start.3 = (bf16[8,96,128]{2,1,0:T(8,128)(2,1)S(1)}, bf16[8,96,128]{2,1,0:T(8,128)(2,1)S(1)}, u32[]{:S(2)}, u32[]{:S(2)}) collective-permute-start(bf16[8,96,128]{2,1,0:T(8,128)(2,1)S(1)} %get-tuple-element.28), channel_id=1, source_target_pairs={{0,24},{8,0},{16,8},{24,16},{1,25},{9,1},{17,9},{25,17},{2,26},{10... | collective-permute-start | bytes 589832 | tf_op jit(solution)/shard_map/ppermute | solution.py:247
  35.3 6.3 %collective-permute-start.4 = (bf16[4,96,128]{2,1,0:T(8,128)(2,1)S(1)}, bf16[4,96,128]{2,1,0:T(8,128)(2,1)S(1)}, u32[]{:S(2)}, u32[]{:S(2)}) collective-permute-start(bf16[4,96,128]{2,1,0:T(8,128)(2,1)S(1)} %get-tuple-element.30), channel_id=1, source_target_pairs={{0,32},{32,0},{1,33},{33,1},{2,34},{34,2},{3,35},{35,3},{4,36},{36... | collective-permute-start | bytes 294920 | tf_op jit(solution)/shard_map/ppermute | solution.py:253
  42.8 6.8 %collective-permute-start.5 = (bf16[416,128]{1,0:T(8,128)(2,1)S(1)}, bf16[416,128]{1,0:T(8,128)(2,1)S(1)}, u32[]{:S(2)}, u32[]{:S(2)}) collective-permute-start(bf16[416,128]{1,0:T(8,128)(2,1)S(1)} %get-tuple-element.38), channel_id=1, source_target_pairs={{0,64},{64,0},{128,192},{192,128},{1,65},{65,1},{129,193},{193,129... | collective-permute-start | bytes 319496 | tf_op jit(solution)/shard_map/ppermute | solution.py:215
  43.5 10.3 %collective-permute-start.6 = (bf16[416,128]{1,0:T(8,128)(2,1)S(1)}, bf16[416,128]{1,0:T(8,128)(2,1)S(1)}, u32[]{:S(2)}, u32[]{:S(2)}) collective-permute-start(bf16[416,128]{1,0:T(8,128)(2,1)S(1)} %get-tuple-element.39), channel_id=1, source_target_pairs={{0,128},{64,192},{128,0},{192,64},{1,129},{65,193},{129,1},{193,65... | collective-permute-start | bytes 319496 | tf_op jit(solution)/shard_map/ppermute | solution.py:215
  47.6 10.4 %collective-permute-start.7 = (bf16[416,128]{1,0:T(8,128)(2,1)S(1)}, bf16[416,128]{1,0:T(8,128)(2,1)S(1)}, u32[]{:S(2)}, u32[]{:S(2)}) collective-permute-start(bf16[416,128]{1,0:T(8,128)(2,1)S(1)} %get-tuple-element.40), channel_id=1, source_target_pairs={{0,192},{64,128},{128,64},{192,0},{1,193},{65,129},{129,65},{193,1... | collective-permute-start | bytes 319496 | tf_op jit(solution)/shard_map/ppermute | solution.py:215
  58.6 5.1 %collective-permute-start.10 = (bf16[4,96,128]{2,1,0:T(8,128)(2,1)S(1)}, bf16[4,96,128]{2,1,0:T(8,128)(2,1)S(1)}, u32[]{:S(2)}, u32[]{:S(2)}) collective-permute-start(bf16[4,96,128]{2,1,0:T(8,128)(2,1)S(1)} %get-tuple-element.42.refs_3_), channel_id=1, source_target_pairs={{0,3},{1,0},{2,1},{3,2},{4,7},{5,4},{6,5},{7,6},{8,11},{9,8},{10,9... | collective-permute-start | bytes 294920 | tf_op jit(solution)/shard_map/ppermute | solution.py:215
  61.5 7.2 %collective-permute-start.8 = (bf16[4,96,128]{2,1,0:T(8,128)(2,1)S(1)}, bf16[4,96,128]{2,1,0:T(8,128)(2,1)S(1)}, u32[]{:S(2)}, u32[]{:S(2)}) collective-permute-start(bf16[4,96,128]{2,1,0:T(8,128)(2,1)S(1)} %get-tuple-element.42.refs_3_), channel_id=1, source_target_pairs={{0,1},{1,2},{2,3},{3,0},{4,5},{5,6},{6,7},{7,4},{8,9},{9,10},{10,1... | collective-permute-start | bytes 294920 | tf_op jit(solution)/shard_map/ppermute | solution.py:215
  61.5 7.2 %collective-permute-start.9 = (bf16[4,96,128]{2,1,0:T(8,128)(2,1)S(1)}, bf16[4,96,128]{2,1,0:T(8,128)(2,1)S(1)}, u32[]{:S(2)}, u32[]{:S(2)}) collective-permute-start(bf16[4,96,128]{2,1,0:T(8,128)(2,1)S(1)} %get-tuple-element.42.refs_3_), channel_id=1, source_target_pairs={{0,2},{1,3},{2,0},{3,1},{4,6},{5,7},{6,4},{7,5},{8,10},{9,11},{10,... | collective-permute-start | bytes 294920 | tf_op jit(solution)/shard_map/ppermute | solution.py:215

commit v10 on v9

--- a/solution.py
+++ b/solution.py
@@ -13,79 +13,35 @@
 SMEM = pl.BlockSpec(memory_space=pltpu.SMEM)
 
 
-def split_kernel(source_ref, out_ref):
-    points = out_ref.shape[2]
-    for i in range(out_ref.shape[0]):
-        out_ref[i] = source_ref[:, i * points:(i + 1) * points]
-
-
-def split(source, pieces):
-    rows, points = source.shape
-    steps = 4
-    return pl.pallas_call(
-        split_kernel,
-        grid=(steps,),
-        out_shape=jax.ShapeDtypeStruct((pieces, rows, points // pieces), source.dtype),
-        in_specs=[pl.BlockSpec((rows, points // steps), lambda i: (0, i))],
-        out_specs=pl.BlockSpec((pieces // steps, rows, points // pieces), lambda i: (i, 0, 0)),
-        compiler_params=pltpu.CompilerParams(vmem_limit_bytes=56 * MIB),
-        cost_estimate=pl.CostEstimate(flops=0, bytes_accessed=2 * MIB, transcendentals=0),
-    )(source)
-
-
-def partial_kernel(y_count, offsets, other, place_ref, owners_ref, adjoint_ref, probes_ref, *refs):
-    out_ref, masked = refs
-    step = pl.program_id(0)
-    samples = adjoint_ref.shape[0]
-    z_count = out_ref.shape[1]
-    own = owners_ref[...]
-    adjoint = adjoint_ref[...]
-    offset = offsets[-1]
-    for i, value in enumerate(offsets[:-1]):
-        offset = jnp.where(step == i, value, offset)
+def partial_kernel(y_count, offset, place_ref, *refs):
+    out_ref, masked = refs[-2:]
+    z_count = out_ref.shape[0]
     y = lax.rem(place_ref[0] + offset, y_count)
-    core = 1 - place_ref[1] if other else place_ref[1]
-    for z in range(z_count):
-        hot = jnp.where(own == (z * y_count + y) * 2 + core, 1.0, 0.0).astype(jnp.bfloat16)
-        masked[z * samples:(z + 1) * samples, :] = adjoint * hot
-    product = lax.dot_general(
-        masked[...], probes_ref[...], (((1,), (1,)), ((), ())), preferred_element_type=jnp.float32
-    )
+    product = None
+    for owners_ref, adjoint_ref, probes_ref in (refs[0:3], refs[3:6]):
+        own = owners_ref[...]
+        adjoint = adjoint_ref[...]
+        samples = adjoint.shape[0]
+        for z in range(z_count):
+            owner = (z * y_count + y) * 2 + place_ref[1]
+            hot = jnp.where(own == owner, 1.0, 0.0).astype(jnp.bfloat16)
+            masked[z * samples:(z + 1) * samples, :] = adjoint * hot
+        term = lax.dot_general(
+            masked[...],
+            probes_ref[...],
+            (((1,), (1,)), ((), ())),
+            preferred_element_type=jnp.float32,
+        )
+        product = term if product is None else product + term
     half = samples // 2
     for z in range(z_count):
         block = product[z * samples:(z + 1) * samples, :]
-        out_ref[0, z, :samples, :] = block[:, :128]
         tail = jnp.concatenate([block[:half, 128:], block[half:, 128:]], axis=1)
-        out_ref[0, z, samples:, :] = tail
-
-
-def partial_coeffs(offsets, other, place, owners, adjoint, probes):
-    samples, rows = adjoint.shape
-    vectors = probes.shape[0]
-    y_count, z_count = lax.axis_size("y"), lax.axis_size(Z_AXES)
-    shape = (len(offsets), z_count, samples * vectors // 128, 128)
-    return pl.pallas_call(
-        lambda *refs: partial_kernel(y_count, offsets, other, *refs),
-        grid=(len(offsets),),
-        in_specs=[
-            SMEM,
-            pl.BlockSpec((1, rows), lambda i: (0, 0)),
-            pl.BlockSpec((samples, rows), lambda i: (0, 0)),
-            pl.BlockSpec((vectors, rows), lambda i: (0, 0)),
-        ],
-        out_specs=pl.BlockSpec((1,) + shape[1:], lambda i: (i, 0, 0, 0)),
-        out_shape=jax.ShapeDtypeStruct(shape, jnp.float32),
-        scratch_shapes=[pltpu.VMEM((z_count * samples, rows), jnp.bfloat16)],
-        compiler_params=pltpu.CompilerParams(vmem_limit_bytes=12 * MIB),
-        cost_estimate=pl.CostEstimate(
-            flops=2 * len(offsets) * z_count * samples * rows * 256,
-            bytes_accessed=3 * MIB,
-            transcendentals=0,
-        ),
-    )(place, owners, adjoint, probes)
-
-
-def local_call(kernel, out_shape, *args, smem=0, scratch=(), flops=0):
+        out_ref[z, :samples, :] = block[:, :128].astype(out_ref.dtype)
+        out_ref[z, samples:, :] = tail.astype(out_ref.dtype)
+
+
+def local_call(kernel, out_shape, *args, smem=0, scratch=(), flops=0, moved=2 * MIB):
     return pl.pallas_call(
         kernel,
         out_shape=out_shape,
@@ -93,13 +49,8 @@
         out_specs=jax.tree.map(lambda _: VMEM, out_shape),
         scratch_shapes=list(scratch),
         compiler_params=pltpu.CompilerParams(vmem_limit_bytes=12 * MIB),
-        cost_estimate=pl.CostEstimate(flops=flops, bytes_accessed=2 * MIB, transcendentals=0),
+        cost_estimate=pl.CostEstimate(flops=flops, bytes_accessed=moved, transcendentals=0),
     )(*args)
-
-
-def merge_kernel(kept_ref, came_ref, *out_refs):
-    for i, out_ref in enumerate(out_refs):
-        out_ref[...] = (kept_ref[i] + came_ref[i]).astype(out_ref.dtype)
 
 
 def halve_kernel(place_ref, *refs):
@@ -226,23 +177,27 @@
     smp = lax.axis_index("smp")
     y, core = lax.axis_index("y"), lax.axis_index("core")
 
-    pieces = split(forward_samples, members)
+    pieces = forward_samples.reshape(samples, members, piece).transpose(1, 0, 2)
     own, probes = owners.T, probe_values.T
-    pieces, own = lax.optimization_barrier((pieces, own))
+    rows = (own, adjoint_samples, probes)
+    came = [lax.ppermute(x, "core", [(0, 1), (1, 0)]) for x in rows]
+    pieces, *came = lax.optimization_barrier((pieces, *came))
+    rows = (own, adjoint_samples, probes, *came)
     pieces = lax.all_to_all(pieces, GROUP, 0, 0, tiled=True)
 
     place = jnp.stack([y, core])
-    order = sorted(range(y_count), key=lambda k: (k == 0, abs(k - y_count // 2)))
-    sent = partial_coeffs(order, True, place, own, adjoint_samples, probes)
-    came = lax.ppermute(sent, "core", [(0, 1), (1, 0)])
-    shape = sent.shape[1:]
-    kept = partial_coeffs(order, False, place, own, adjoint_samples, probes)
-    kinds = [jnp.bfloat16 if offset else jnp.float32 for offset in order]
-    merged = local_call(
-        merge_kernel, [jax.ShapeDtypeStruct(shape, kind) for kind in kinds], kept, came
-    )
+    shape = (lax.axis_size(Z_AXES), samples * vectors // 128, 128)
     sums = {}
-    for offset, value in zip(order, merged):
+    for offset in sorted(range(y_count), key=lambda k: (k == 0, abs(k - y_count // 2))):
+        value = local_call(
+            lambda *refs, offset=offset: partial_kernel(y_count, offset, *refs),
+            jax.ShapeDtypeStruct(shape, jnp.bfloat16 if offset else jnp.float32),
+            place,
+            *rows,
+            smem=1,
+            scratch=[pltpu.VMEM((shape[0] * samples, own.shape[1]), jnp.bfloat16)],
+            flops=16 * shape[0] * samples * own.shape[1] * 256,
+        )
         route = [(i, (i + offset) % y_count) for i in range(y_count)]
         sums[offset] = lax.ppermute(value, "y", route) if offset else value
     sums = [sums[offset] for offset in range(y_count)]

time: 98.7 us -> 98.8 us (level)
  Pallas kernels: 13.7 us -> 10.1 us
  local copies, waits for them, and re-layouts: 0.97 us -> 3.3 us
  blocking collectives: 27.1 us -> 28.9 us
  waiting for transfers between devices: 27.4 us -> 25.7 us
  starting transfers between devices: 28.1 us -> 29.4 us
    pallas_call x3 -> x0, Pallas kernels: 10.9 us -> none  [the longest x2 7.5 us: partial_coeffs(): pl.pallas_call(lambda *refs: partial_kernel(y_count, offsets, other, *ref...]
    pallas_call x5 -> x8, Pallas kernels: 2.8 us -> 10.1 us  [local_call(): pl.pallas_call(kernel, out_shape=out_shape, in_specs=[SMEM] * smem + [VME...]
    ppermute x3, waiting for transfers between devices: 8.04 us -> 4.26 us  [body(): sums[offset] = lax.ppermute(value, 'y', route) if offset else value]
    all_to_all x1, waiting for transfers between devices: 0.6 us -> 3.62 us  [body(): pieces = lax.all_to_all(pieces, GROUP, 0, 0, tiled=True)]
    reshape x0 -> x1, local copies, waits for them, and re-layouts: none -> 2.32 us  [body(): pieces = forward_samples.reshape(samples, members, piece).transpose(1, 0, 2)]
    ppermute x6, waiting for transfers between devices: 13.7 us -> 11.4 us  [exchange(): came[offset] = lax.ppermute(pieces[offset], axis, pairs)]
    all_to_all x1, blocking collectives: 27.1 us -> 28.9 us  [body(): result = lax.all_to_all(result, GROUP, 0, 0, tiled=True)]
    ppermute x1, waiting for transfers between devices: 5.09 us -> 6.42 us  [body(): came = lax.ppermute(sent, 'zl', [(0, 1), (1, 0)])]
  transfers between devices with their start and end apart: 12 -> 14, of which waited for: 9 -> 8; matrix products, arithmetic and copies ran while one was open for 0% -> 3% of each run, Pallas kernels for 9% -> 8%
where the time goes in v10:
time: 98.8 us; the launch traced here: 98.3 us
  starting transfers between devices  29.4 us (30%)
  blocking collectives  28.9 us (29%)
  waiting for transfers between devices  25.7 us (26%)
  Pallas kernels  10.1 us (10%)
  local copies, waits for them, and re-layouts  3.3 us (3%)
    all_to_all x1, blocking collectives, body(): result = lax.all_to_all(result, GROUP, 0, 0, tiled=True)  28.9 us
    ppermute x6, starting transfers between devices, exchange(): came[offset] = lax.ppermute(pieces[offset], axis, pairs)  12.4 us
    ppermute x6, waiting for transfers between devices, exchange(): came[offset] = lax.ppermute(pieces[offset], axis, pairs)  11.4 us
    all_to_all x1, starting transfers between devices, body(): pieces = lax.all_to_all(pieces, GROUP, 0, 0, tiled=True)  10.3 us
    pallas_call x8, Pallas kernels, local_call(): pl.pallas_call(kernel, out_shape=out_shape, in_specs=[SMEM] * smem + [VME...  10.1 us
    ppermute x1, waiting for transfers between devices, body(): came = lax.ppermute(sent, 'zl', [(0, 1), (1, 0)])  6.42 us
    ppermute x3, starting transfers between devices, body(): sums[offset] = lax.ppermute(value, 'y', route) if offset else value  5.15 us
    ppermute x3, waiting for transfers between devices, body(): sums[offset] = lax.ppermute(value, 'y', route) if offset else value  4.26 us
  transfers between devices with their start and end apart: 14, of which 8 were waited for; matrix products, arithmetic and copies ran while one was open for 3% of the time, Pallas kernels for 8%

profile of v10, /device:TPU:40, one launch (start us, length us, event | category | flops | bytes accessed | tf_op | source)
XLA Modules:
  0.0 98.3 jit_solution(915238488377260558)
XLA Ops:
  0.0 0.0 collective-permute-start.2
  0.0 0.5 collective-permute-start.1
  0.5 0.0 collective-permute-start
  0.5 2.3 %copy.12 = bf16[8,16,8,512]{3,2,0,1:T(8,128)(2,1)} copy(bf16[8,16,8,512]{3,2,1,0:T(8,128)(2,1)} %bitcast.29) | data formatting | bytes 2097152 | tf_op jit(solution)/shard_map/reshape | solution.py:180
  2.8 0.0 collective-permute-done.refs_4_
  2.9 0.0 collective-permute-done.1.refs_5_
  2.9 0.0 collective-permute-done.2.refs_6_
  2.9 0.0 copy-start.1
  2.9 0.0 copy-start.2
  2.9 10.3 %all-to-all-start = ((bf16[16,64,512]{2,1,0:T(8,128)(2,1)}), bf16[16,64,512]{2,1,0:T(8,128)(2,1)S(1)}, u32[]{:S(2)}, u32[]{:S(2)}) async-start(bf16[16,64,512]{2,1,0:T(8,128)(2,1)} %bitcast.27), calls=%async_computation | async-start | bytes 2097152 | tf_op jit(solution)/shard_map/all_to_all | solution.py:186
  13.2 0.0 copy-start.3
  13.9 0.1 pad_add_fusion.1.refs_0_
  13.9 0.0 copy-done.1
  13.9 0.0 copy-done.2
  13.9 0.0 copy-done.3
  14.0 1.9 %shard_map.67 = bf16[8,96,128]{2,1,0:T(8,128)(2,1)S(1)} custom-call(s32[2]{0:T(128)S(1)} %pad_add_fusion.1.refs_0_, s32[1,2048]{1,0:T(1,128)S(1)} %bitcast.23, bf16[64,2048]{1,0:T(8,128)(2,1)S(1)} %copy-done.2, bf16[192,2048]{1,0:T(8,128)(2,1)S(1)} %bitcast.18, s32[1,2048]{1,0:T(1,128)S(1)} %collective-permute-done.refs_4_, ...), custom_call_target="tpu_custom_call" | custom-call | flops 4294967296 | bytes 2097152 | tf_op jit(solution)/shard_map/pallas_call | solution.py:45
  15.8 0.5 collective-permute-start.5
  16.4 1.9 %shard_map.66 = bf16[8,96,128]{2,1,0:T(8,128)(2,1)S(1)} custom-call(s32[2]{0:T(128)S(1)} %pad_add_fusion.1.refs_0_, s32[1,2048]{1,0:T(1,128)S(1)} %bitcast.24, bf16[64,2048]{1,0:T(8,128)(2,1)S(1)} %copy-done.2, bf16[192,2048]{1,0:T(8,128)(2,1)S(1)} %bitcast.19, s32[1,2048]{1,0:T(1,128)S(1)} %collective-permute-done.refs_4_, ...), custom_call_target="tpu_custom_call" | custom-call | flops 4294967296 | bytes 2097152 | tf_op jit(solution)/shard_map/pallas_call | solution.py:45
  18.2 2.7 %collective-permute-start.4 = (bf16[8,96,128]{2,1,0:T(8,128)(2,1)S(1)}, bf16[8,96,128]{2,1,0:T(8,128)(2,1)S(1)}, u32[]{:S(2)}, u32[]{:S(2)}) collective-permute-start(bf16[8,96,128]{2,1,0:T(8,128)(2,1)S(1)} %shard_map.66), channel_id=1, source_target_pairs={{0,16},{8,24},{16,0},{24,8},{1,17},{9,25},{17,1},{25,9},{2,18},{10... | collective-permute-start | bytes 589832 | tf_op jit(solution)/shard_map/ppermute | solution.py:202
  20.9 1.9 %shard_map.65 = bf16[8,96,128]{2,1,0:T(8,128)(2,1)S(1)} custom-call(s32[2]{0:T(128)S(1)} %pad_add_fusion.1.refs_0_, s32[1,2048]{1,0:T(1,128)S(1)} %bitcast.25, bf16[64,2048]{1,0:T(8,128)(2,1)S(1)} %copy-done.2, bf16[192,2048]{1,0:T(8,128)(2,1)S(1)} %bitcast.20, s32[1,2048]{1,0:T(1,128)S(1)} %collective-permute-done.refs_4_, ...), custom_call_target="tpu_custom_call" | custom-call | flops 4294967296 | bytes 2097152 | tf_op jit(solution)/shard_map/pallas_call | solution.py:45
  22.8 2.0 %collective-permute-start.3 = (bf16[8,96,128]{2,1,0:T(8,128)(2,1)S(1)}, bf16[8,96,128]{2,1,0:T(8,128)(2,1)S(1)}, u32[]{:S(2)}, u32[]{:S(2)}) collective-permute-start(bf16[8,96,128]{2,1,0:T(8,128)(2,1)S(1)} %shard_map.65), channel_id=1, source_target_pairs={{0,8},{8,16},{16,24},{24,0},{1,9},{9,17},{17,25},{25,1},{2,10},{10... | collective-permute-start | bytes 589832 | tf_op jit(solution)/shard_map/ppermute | solution.py:202
  24.7 1.9 %shard_map.64.refs_0_ = f32[8,96,128]{2,1,0:T(8,128)S(1)} custom-call(s32[2]{0:T(128)S(1)} %pad_add_fusion.1.refs_0_, s32[1,2048]{1,0:T(1,128)S(1)} %bitcast.26, bf16[64,2048]{1,0:T(8,128)(2,1)S(1)} %copy-done.2, bf16[192,2048]{1,0:T(8,128)(2,1)S(1)} %bitcast.21, s32[1,2048]{1,0:T(1,128)S(1)} %collective-permute-done.refs_4_, ...), custom_call_target="tpu_custom_call" | custom-call | flops 4294967296 | bytes 2097152 | tf_op jit(solution)/shard_map/pallas_call | solution.py:45
  26.6 0.0 collective-permute-done.5.refs_3_
  26.6 1.5 %collective-permute-done.4.refs_2_ = bf16[8,96,128]{2,1,0:T(8,128)(2,1)S(1)} collective-permute-done((bf16[8,96,128]{2,1,0:T(8,128)(2,1)S(1)}, bf16[8,96,128]{2,1,0:T(8,128)(2,1)S(1)}, u32[]{:S(2)}, u32[]{:S(2)}) %collective-permute-start.4) | collective-permute-done | bytes 196640 | tf_op jit(solution)/shard_map/ppermute | solution.py:202
  28.1 2.7 %collective-permute-done.3.refs_1_ = bf16[8,96,128]{2,1,0:T(8,128)(2,1)S(1)} collective-permute-done((bf16[8,96,128]{2,1,0:T(8,128)(2,1)S(1)}, bf16[8,96,128]{2,1,0:T(8,128)(2,1)S(1)}, u32[]{:S(2)}, u32[]{:S(2)}) %collective-permute-start.3) | collective-permute-done | bytes 196640 | tf_op jit(solution)/shard_map/ppermute | solution.py:202
  30.9 0.1 shard_map.68
  31.0 1.1 %collective-permute-start.6 = (bf16[4,96,128]{2,1,0:T(8,128)(2,1)S(1)}, bf16[4,96,128]{2,1,0:T(8,128)(2,1)S(1)}, u32[]{:S(2)}, u32[]{:S(2)}) collective-permute-start(bf16[4,96,128]{2,1,0:T(8,128)(2,1)S(1)} %get-tuple-element.26), channel_id=1, source_target_pairs={{0,32},{32,0},{1,33},{33,1},{2,34},{34,2},{3,35},{35,3},{4,36},{36... | collective-permute-start | bytes 294920 | tf_op jit(solution)/shard_map/ppermute | solution.py:208
  32.0 0.1 pad_add_fusion.place_ref.refs_0_
  32.1 6.4 %collective-permute-done.6.came_ref = bf16[4,96,128]{2,1,0:T(8,128)(2,1)S(1)} collective-permute-done((bf16[4,96,128]{2,1,0:T(8,128)(2,1)S(1)}, bf16[4,96,128]{2,1,0:T(8,128)(2,1)S(1)}, u32[]{:S(2)}, u32[]{:S(2)}) %collective-permute-start.6) | collective-permute-done | bytes 98336 | tf_op jit(solution)/shard_map/ppermute | solution.py:208
  38.5 0.0 copy-done
  38.5 0.6 shard_map.69
  39.2 3.6 %all-to-all-done.refs_1_ = bf16[16,64,512]{2,1,0:T(8,128)(2,1)S(1)} async-done(((bf16[16,64,512]{2,1,0:T(8,128)(2,1)}), bf16[16,64,512]{2,1,0:T(8,128)(2,1)S(1)}, u32[]{:S(2)}, u32[]{:S(2)}) %all-to-all-start) | async-done | bytes 1048608 | tf_op jit(solution)/shard_map/all_to_all | solution.py:186
  42.8 0.4 collective-permute-start.7
  43.1 4.1 %collective-permute-start.8 = (bf16[416,128]{1,0:T(8,128)(2,1)S(1)}, bf16[416,128]{1,0:T(8,128)(2,1)S(1)}, u32[]{:S(2)}, u32[]{:S(2)}) collective-permute-start(bf16[416,128]{1,0:T(8,128)(2,1)S(1)} %get-tuple-element.35), channel_id=1, source_target_pairs={{0,128},{64,192},{128,0},{192,64},{1,129},{65,193},{129,1},{193,65... | collective-permute-start | bytes 319496 | tf_op jit(solution)/shard_map/ppermute | solution.py:166
  47.2 2.0 %collective-permute-start.9 = (bf16[416,128]{1,0:T(8,128)(2,1)S(1)}, bf16[416,128]{1,0:T(8,128)(2,1)S(1)}, u32[]{:S(2)}, u32[]{:S(2)}) collective-permute-start(bf16[416,128]{1,0:T(8,128)(2,1)S(1)} %get-tuple-element.36), channel_id=1, source_target_pairs={{0,192},{64,128},{128,64},{192,0},{1,193},{65,129},{129,65},{193,1... | collective-permute-start | bytes 319496 | tf_op jit(solution)/shard_map/ppermute | solution.py:166
  49.3 0.0 collective-permute-done.7.refs_0_
  49.3 7.1 %collective-permute-done.8.refs_1_ = bf16[416,128]{1,0:T(8,128)(2,1)S(1)} collective-permute-done((bf16[416,128]{1,0:T(8,128)(2,1)S(1)}, bf16[416,128]{1,0:T(8,128)(2,1)S(1)}, u32[]{:S(2)}, u32[]{:S(2)}) %collective-permute-start.8) | collective-permute-done | bytes 106528 | tf_op jit(solution)/shard_map/ppermute | solution.py:166
  56.4 1.2 %collective-permute-done.9.refs_2_ = bf16[416,128]{1,0:T(8,128)(2,1)S(1)} collective-permute-done((bf16[416,128]{1,0:T(8,128)(2,1)S(1)}, bf16[416,128]{1,0:T(8,128)(2,1)S(1)}, u32[]{:S(2)}, u32[]{:S(2)}) %collective-permute-start.9) | collective-permute-done | bytes 106528 | tf_op jit(solution)/shard_map/ppermute | solution.py:166
  57.6 0.6 shard_map.70
  58.2 1.5 %collective-permute-start.10 = (bf16[4,96,128]{2,1,0:T(8,128)(2,1)S(1)}, bf16[4,96,128]{2,1,0:T(8,128)(2,1)S(1)}, u32[]{:S(2)}, u32[]{:S(2)}) collective-permute-start(bf16[4,96,128]{2,1,0:T(8,128)(2,1)S(1)} %get-tuple-element.38.refs_3_), channel_id=1, source_target_pairs={{0,1},{1,2},{2,3},{3,0},{4,5},{5,6},{6,7},{7,4},{8,9},{9,10},{10,1... | collective-permute-start | bytes 294920 | tf_op jit(solution)/shard_map/ppermute | solution.py:166
  59.8 2.8 %collective-permute-start.11 = (bf16[4,96,128]{2,1,0:T(8,128)(2,1)S(1)}, bf16[4,96,128]{2,1,0:T(8,128)(2,1)S(1)}, u32[]{:S(2)}, u32[]{:S(2)}) collective-permute-start(bf16[4,96,128]{2,1,0:T(8,128)(2,1)S(1)} %get-tuple-element.38.refs_3_), channel_id=1, source_target_pairs={{0,2},{1,3},{2,0},{3,1},{4,6},{5,7},{6,4},{7,5},{8,10},{9,11},{10,... | collective-permute-start | bytes 294920 | tf_op jit(solution)/shard_map/ppermute | solution.py:166
  62.5 1.6 %collective-permute-start.12 = (bf16[4,96,128]{2,1,0:T(8,128)(2,1)S(1)}, bf16[4,96,128]{2,1,0:T(8,128)(2,1)S(1)}, u32[]{:S(2)}, u32[]{:S(2)}) collective-permute-start(bf16[4,96,128]{2,1,0:T(8,128)(2,1)S(1)} %get-tuple-element.38.refs_3_), channel_id=1, source_target_pairs={{0,3},{1,0},{2,1},{3,2},{4,7},{5,4},{6,5},{7,6},{8,11},{9,8},{10,9... | collective-permute-start | bytes 294920 | tf_op jit(solution)/shard_map/ppermute | solution.py:166
  64.1 0.0 collective-permute-done.10.refs_4_
  64.1 2.1 %collective-permute-done.11.refs_5_ = bf16[4,96,128]{2,1,0:T(8,128)(2,1)S(1)} collective-permute-done((bf16[4,96,128]{2,1,0:T(8,128)(2,1)S(1)}, bf16[4,96,128]{2,1,0:T(8,128)(2,1)S(1)}, u32[]{:S(2)}, u32[]{:S(2)}) %collective-permute-start.11) | collective-permute-done | bytes 98336 | tf_op jit(solution)/shard_map/ppermute | solution.py:166
  66.2 1.0 collective-permute-done.12.refs_6_
  67.2 1.3 %shard_map.71 = bf16[16,48,512]{2,1,0:T(8,128)(2,1)S(1)} custom-call(s32[3]{0:T(128)S(1)} %pad_add_fusion.place_ref.refs_0_, bf16[16,64,512]{2,1,0:T(8,128)(2,1)S(1)} %all-to-all-done.refs_1_, bf16[4,32,128]{2,1,0:T(8,128)(2,1)S(1)} %get-tuple-element.37.refs_2_, bf16[4,96,128]{2,1,0:T(8,128)(2,1)S(1)} %get-tuple-element.38.refs_3_, ...), custom_call_target="tpu_custom_call" | custom-call | flops 201326592 | bytes 2097152 | tf_op jit(solution)/shard_map/pallas_call | solution.py:45
  68.5 28.9 %all_to_all.10 = bf16[16,48,512]{2,1,0:T(8,128)(2,1)S(1)} all-to-all(bf16[16,48,512]{2,1,0:T(8,128)(2,1)S(1)} %shard_map.71), channel_id=1, replica_groups=mesh['zg'=4,'zl'=2,'y'=4,'core'=2,'smp'=4] {'zg','smp'}, dimensions={0} | all-to-all | bytes 1572864 | tf_op jit(solution)/shard_map/all_to_all | solution.py:255
  97.4 1.0 copy.10
  (1 shorter events, 0.0 us)
Async XLA Ops:
  0.0 2.9 %collective-permute-start.2 = (bf16[192,2048]{1,0:T(8,128)(2,1)}, bf16[192,2048]{1,0:T(8,128)(2,1)S(1)}, u32[]{:S(2)}, u32[]{:S(2)}) collective-permute-start(bf16[192,2048]{1,0:T(8,128)(2,1)} %bitcast.17), channel_id=1, source_target_pairs={{0,4},{4,0},{1,5},{5,1},{2,6},{6,2},{3,7},{7,3},{8,12},{12,8},{9,1... | collective-permute-start | bytes 2359304 | tf_op jit(solution)/shard_map/ppermute | solution.py:183
  0.0 2.9 %collective-permute-start.1 = (bf16[64,2048]{1,0:T(8,128)(2,1)}, bf16[64,2048]{1,0:T(8,128)(2,1)S(1)}, u32[]{:S(2)}, u32[]{:S(2)}) collective-permute-start(bf16[64,2048]{1,0:T(8,128)(2,1)} %refs_2_.7), channel_id=1, source_target_pairs={{0,4},{4,0},{1,5},{5,1},{2,6},{6,2},{3,7},{7,3},{8,12},{12,8},{9,1... | collective-permute-start | bytes 786440 | tf_op jit(solution)/shard_map/ppermute | solution.py:183
  0.5 2.4 %collective-permute-start = (s32[1,2048]{1,0:T(1,128)}, s32[1,2048]{1,0:T(1,128)S(1)}, u32[]{:S(2)}, u32[]{:S(2)}) collective-permute-start(s32[1,2048]{1,0:T(1,128)} %bitcast.22), channel_id=1, source_target_pairs={{0,4},{4,0},{1,5},{5,1},{2,6},{6,2},{3,7},{7,3},{8,12},{12,8},{9,1... | collective-permute-start | bytes 24584 | tf_op jit(solution)/shard_map/ppermute | solution.py:183
  2.9 11.1 %copy-start.1 = (bf16[2048,192]{0,1:T(8,128)(2,1)S(1)}, bf16[2048,192]{0,1:T(8,128)(2,1)}, u32[]{:S(2)}) copy-start(bf16[2048,192]{0,1:T(8,128)(2,1)} %param.8) | copy-start | bytes 2359300
  2.9 11.1 %copy-start.2 = (bf16[64,2048]{1,0:T(8,128)(2,1)S(1)}, bf16[64,2048]{1,0:T(8,128)(2,1)}, u32[]{:S(2)}) copy-start(bf16[64,2048]{1,0:T(8,128)(2,1)} %refs_2_.7) | copy-start | bytes 786436
  2.9 39.9 %all-to-all-start = ((bf16[16,64,512]{2,1,0:T(8,128)(2,1)}), bf16[16,64,512]{2,1,0:T(8,128)(2,1)S(1)}, u32[]{:S(2)}, u32[]{:S(2)}) async-start(bf16[16,64,512]{2,1,0:T(8,128)(2,1)} %bitcast.27), calls=%async_computation | async-start | bytes 2097152 | tf_op jit(solution)/shard_map/all_to_all | solution.py:186
  13.2 0.8 copy-start.3
  15.8 10.8 %collective-permute-start.5 = (bf16[8,96,128]{2,1,0:T(8,128)(2,1)S(1)}, bf16[8,96,128]{2,1,0:T(8,128)(2,1)S(1)}, u32[]{:S(2)}, u32[]{:S(2)}) collective-permute-start(bf16[8,96,128]{2,1,0:T(8,128)(2,1)S(1)} %shard_map.67), channel_id=1, source_target_pairs={{0,24},{8,0},{16,8},{24,16},{1,25},{9,1},{17,9},{25,17},{2,26},{10... | collective-permute-start | bytes 589832 | tf_op jit(solution)/shard_map/ppermute | solution.py:202
  18.2 9.9 %collective-permute-start.4 = (bf16[8,96,128]{2,1,0:T(8,128)(2,1)S(1)}, bf16[8,96,128]{2,1,0:T(8,128)(2,1)S(1)}, u32[]{:S(2)}, u32[]{:S(2)}) collective-permute-start(bf16[8,96,128]{2,1,0:T(8,128)(2,1)S(1)} %shard_map.66), channel_id=1, source_target_pairs={{0,16},{8,24},{16,0},{24,8},{1,17},{9,25},{17,1},{25,9},{2,18},{10... | collective-permute-start | bytes 589832 | tf_op jit(solution)/shard_map/ppermute | solution.py:202
  22.8 8.1 %collective-permute-start.3 = (bf16[8,96,128]{2,1,0:T(8,128)(2,1)S(1)}, bf16[8,96,128]{2,1,0:T(8,128)(2,1)S(1)}, u32[]{:S(2)}, u32[]{:S(2)}) collective-permute-start(bf16[8,96,128]{2,1,0:T(8,128)(2,1)S(1)} %shard_map.65), channel_id=1, source_target_pairs={{0,8},{8,16},{16,24},{24,0},{1,9},{9,17},{17,25},{25,1},{2,10},{10... | collective-permute-start | bytes 589832 | tf_op jit(solution)/shard_map/ppermute | solution.py:202
  30.9 7.7 %copy-start = (f32[2,8192]{1,0:T(2,128)S(1)}, f32[2,8192]{1,0:T(2,128)}, u32[]{:S(2)}) copy-start(f32[2,8192]{1,0:T(2,128)} %twiddle_ref.1) | copy-start | bytes 196612
  31.0 7.6 %collective-permute-start.6 = (bf16[4,96,128]{2,1,0:T(8,128)(2,1)S(1)}, bf16[4,96,128]{2,1,0:T(8,128)(2,1)S(1)}, u32[]{:S(2)}, u32[]{:S(2)}) collective-permute-start(bf16[4,96,128]{2,1,0:T(8,128)(2,1)S(1)} %get-tuple-element.26), channel_id=1, source_target_pairs={{0,32},{32,0},{1,33},{33,1},{2,34},{34,2},{3,35},{35,3},{4,36},{36... | collective-permute-start | bytes 294920 | tf_op jit(solution)/shard_map/ppermute | solution.py:208
  42.8 6.5 %collective-permute-start.7 = (bf16[416,128]{1,0:T(8,128)(2,1)S(1)}, bf16[416,128]{1,0:T(8,128)(2,1)S(1)}, u32[]{:S(2)}, u32[]{:S(2)}) collective-permute-start(bf16[416,128]{1,0:T(8,128)(2,1)S(1)} %get-tuple-element.34), channel_id=1, source_target_pairs={{0,64},{64,0},{128,192},{192,128},{1,65},{65,1},{129,193},{193,129... | collective-permute-start | bytes 319496 | tf_op jit(solution)/shard_map/ppermute | solution.py:166
  43.1 13.3 %collective-permute-start.8 = (bf16[416,128]{1,0:T(8,128)(2,1)S(1)}, bf16[416,128]{1,0:T(8,128)(2,1)S(1)}, u32[]{:S(2)}, u32[]{:S(2)}) collective-permute-start(bf16[416,128]{1,0:T(8,128)(2,1)S(1)} %get-tuple-element.35), channel_id=1, source_target_pairs={{0,128},{64,192},{128,0},{192,64},{1,129},{65,193},{129,1},{193,65... | collective-permute-start | bytes 319496 | tf_op jit(solution)/shard_map/ppermute | solution.py:166
  47.2 10.4 %collective-permute-start.9 = (bf16[416,128]{1,0:T(8,128)(2,1)S(1)}, bf16[416,128]{1,0:T(8,128)(2,1)S(1)}, u32[]{:S(2)}, u32[]{:S(2)}) collective-permute-start(bf16[416,128]{1,0:T(8,128)(2,1)S(1)} %get-tuple-element.36), channel_id=1, source_target_pairs={{0,192},{64,128},{128,64},{192,0},{1,193},{65,129},{129,65},{193,1... | collective-permute-start | bytes 319496 | tf_op jit(solution)/shard_map/ppermute | solution.py:166
  58.2 5.9 %collective-permute-start.10 = (bf16[4,96,128]{2,1,0:T(8,128)(2,1)S(1)}, bf16[4,96,128]{2,1,0:T(8,128)(2,1)S(1)}, u32[]{:S(2)}, u32[]{:S(2)}) collective-permute-start(bf16[4,96,128]{2,1,0:T(8,128)(2,1)S(1)} %get-tuple-element.38.refs_3_), channel_id=1, source_target_pairs={{0,1},{1,2},{2,3},{3,0},{4,5},{5,6},{6,7},{7,4},{8,9},{9,10},{10,1... | collective-permute-start | bytes 294920 | tf_op jit(solution)/shard_map/ppermute | solution.py:166
  59.8 6.4 %collective-permute-start.11 = (bf16[4,96,128]{2,1,0:T(8,128)(2,1)S(1)}, bf16[4,96,128]{2,1,0:T(8,128)(2,1)S(1)}, u32[]{:S(2)}, u32[]{:S(2)}) collective-permute-start(bf16[4,96,128]{2,1,0:T(8,128)(2,1)S(1)} %get-tuple-element.38.refs_3_), channel_id=1, source_target_pairs={{0,2},{1,3},{2,0},{3,1},{4,6},{5,7},{6,4},{7,5},{8,10},{9,11},{10,... | collective-permute-start | bytes 294920 | tf_op jit(solution)/shard_map/ppermute | solution.py:166
  62.5 4.6 %collective-permute-start.12 = (bf16[4,96,128]{2,1,0:T(8,128)(2,1)S(1)}, bf16[4,96,128]{2,1,0:T(8,128)(2,1)S(1)}, u32[]{:S(2)}, u32[]{:S(2)}) collective-permute-start(bf16[4,96,128]{2,1,0:T(8,128)(2,1)S(1)} %get-tuple-element.38.refs_3_), channel_id=1, source_target_pairs={{0,3},{1,0},{2,1},{3,2},{4,7},{5,4},{6,5},{7,6},{8,11},{9,8},{10,9... | collective-permute-start | bytes 294920 | tf_op jit(solution)/shard_map/ppermute | solution.py:166

commit v11 on v10

--- a/solution.py
+++ b/solution.py
@@ -51,6 +51,40 @@
         compiler_params=pltpu.CompilerParams(vmem_limit_bytes=12 * MIB),
         cost_estimate=pl.CostEstimate(flops=flops, bytes_accessed=moved, transcendentals=0),
     )(*args)
+
+
+def join_kernel(place_ref, pieces_ref, out_ref, sems):
+    count, _, points = pieces_ref.shape
+    copies = []
+    for i in range(count):
+        place = jnp.where(place_ref[3] == 1, count - 1 - i, i)
+        target = out_ref.at[:, pl.ds(pl.multiple_of(place * points, points), points)]
+        copies.append(pltpu.make_async_copy(pieces_ref.at[i], target, sems.at[i]))
+    for copy in copies:
+        copy.start()
+    for copy in copies:
+        copy.wait()
+
+
+def join(place, pieces):
+    count, rows, points = pieces.shape
+    return pl.pallas_call(
+        join_kernel,
+        out_shape=jax.ShapeDtypeStruct((rows, count * points), pieces.dtype),
+        in_specs=[SMEM, VMEM],
+        out_specs=pl.BlockSpec(memory_space=pl.ANY),
+        scratch_shapes=[pltpu.SemaphoreType.DMA((count,))],
+        compiler_params=pltpu.CompilerParams(vmem_limit_bytes=12 * MIB),
+        cost_estimate=pl.CostEstimate(flops=0, bytes_accessed=2 * MIB, transcendentals=0),
+    )(place, pieces)
+
+
+def reversed_groups(zg, zl, y, core, smp):
+    groups = []
+    for rest in range(zl * y * core):
+        members = [((g * zl * y * core) + rest) * smp + p for g in range(zg) for p in range(smp)]
+        groups.append(members[::-1] if rest % core else members)
+    return groups
 
 
 def halve_kernel(place_ref, *refs):
@@ -155,7 +189,9 @@
                 for c in range(blocks)
             ]
         for c in range(blocks):
-            out_ref[(zg ^ c) * parts + p] = level[c].astype(jnp.bfloat16)
+            member = (zg ^ c) * parts + p
+            position = jnp.where(place_ref[3] == 1, blocks * parts - 1 - member, member)
+            out_ref[position] = level[c].astype(jnp.bfloat16)
 
 
 def exchange(pieces, axis, route):
@@ -212,7 +248,7 @@
     offer = (groups * shape[1] + tail, shape[2])
     shapes += [jax.ShapeDtypeStruct(offer, jnp.bfloat16)] * (groups - 1)
     zg = lax.axis_index("zg")
-    place = jnp.stack([zg, smp, block_ranks[0]])
+    place = jnp.stack([zg, smp, block_ranks[0], core])
     partial, extra, *offers = local_call(
         offer_kernel,
         shapes,
@@ -252,8 +288,10 @@
         ],
         flops=2 * members * samples * vectors * piece,
     )
-    result = lax.all_to_all(result, GROUP, 0, 0, tiled=True)
-    return result.transpose(1, 0, 2).reshape(vectors // parts, points)
+    axes = BLK + ("smp",)
+    lists = reversed_groups(*(lax.axis_size(axis) for axis in axes))
+    result = lax.all_to_all(result, axes, 0, 0, tiled=True, axis_index_groups=lists)
+    return join(place, result)
 
 
 def solution(mesh):

time: 98.8 us -> 97.1 us (0.983)
  blocking collectives: 28.9 us -> 26 us
  Pallas kernels: 10.1 us -> 11.7 us
    all_to_all x1, blocking collectives: 28.9 us -> 26 us  [body(): lax.all_to_all(result, axes, 0, 0, tiled=True, axis_index_groups=lists)]
    pallas_call x0 -> x1, Pallas kernels: none -> 1.55 us  [join(): pl.pallas_call(join_kernel, out_shape=jax.ShapeDtypeStruct((rows, count *...]
  transfers between devices with their start and end apart: 14 -> 14, of which waited for: 8 -> 8; matrix products, arithmetic and copies ran while one was open for 3% -> 3% of each run, Pallas kernels for 8% -> 9%
where the time goes in v11:
time: 97.1 us; the launch traced here: 96 us
  starting transfers between devices  29.4 us (30%)
  blocking collectives  26 us (27%)
  waiting for transfers between devices  25.7 us (26%)
  Pallas kernels  11.7 us (12%)
  local copies, waits for them, and re-layouts  2.34 us (2%)
    all_to_all x1, blocking collectives, body(): lax.all_to_all(result, axes, 0, 0, tiled=True, axis_index_groups=lists)  26 us
    ppermute x6, starting transfers between devices, exchange(): came[offset] = lax.ppermute(pieces[offset], axis, pairs)  12.4 us
    ppermute x6, waiting for transfers between devices, exchange(): came[offset] = lax.ppermute(pieces[offset], axis, pairs)  11.4 us
    all_to_all x1, starting transfers between devices, body(): pieces = lax.all_to_all(pieces, GROUP, 0, 0, tiled=True)  10.3 us
    pallas_call x8, Pallas kernels, local_call(): pl.pallas_call(kernel, out_shape=out_shape, in_specs=[SMEM] * smem + [VME...  10.1 us
    ppermute x1, waiting for transfers between devices, body(): came = lax.ppermute(sent, 'zl', [(0, 1), (1, 0)])  6.42 us
    ppermute x3, starting transfers between devices, body(): sums[offset] = lax.ppermute(value, 'y', route) if offset else value  5.16 us
    ppermute x3, waiting for transfers between devices, body(): sums[offset] = lax.ppermute(value, 'y', route) if offset else value  4.25 us
  transfers between devices with their start and end apart: 14, of which 8 were waited for; matrix products, arithmetic and copies ran while one was open for 3% of the time, Pallas kernels for 9%

profile of v11, /device:TPU:40, one launch (start us, length us, event | category | flops | bytes accessed | tf_op | source)
XLA Modules:
  0.0 96.0 jit_solution(3444416234273652401)
XLA Ops:
  0.0 0.0 collective-permute-start.2
  0.0 0.5 collective-permute-start.1
  0.5 0.0 collective-permute-start
  0.5 2.3 %copy.10 = bf16[8,16,8,512]{3,2,0,1:T(8,128)(2,1)} copy(bf16[8,16,8,512]{3,2,1,0:T(8,128)(2,1)} %bitcast.25) | data formatting | bytes 2097152 | tf_op jit(solution)/shard_map/reshape | solution.py:216
  2.8 0.0 collective-permute-done.refs_4_
  2.9 0.0 collective-permute-done.1.refs_5_
  2.9 0.0 collective-permute-done.2.refs_6_
  2.9 0.0 copy-start.1
  2.9 0.0 copy-start.2
  2.9 10.3 %all-to-all-start = ((bf16[16,64,512]{2,1,0:T(8,128)(2,1)}), bf16[16,64,512]{2,1,0:T(8,128)(2,1)S(1)}, u32[]{:S(2)}, u32[]{:S(2)}) async-start(bf16[16,64,512]{2,1,0:T(8,128)(2,1)} %bitcast.24), calls=%async_computation | async-start | bytes 2097152 | tf_op jit(solution)/shard_map/all_to_all | solution.py:222
  13.2 0.0 copy-start.3
  13.9 0.1 pad_add_fusion.1.refs_0_
  13.9 0.0 copy-done.1
  13.9 0.0 copy-done.2
  14.0 0.0 copy-done.3
  14.0 1.9 %shard_map.67 = bf16[8,96,128]{2,1,0:T(8,128)(2,1)S(1)} custom-call(s32[2]{0:T(128)S(1)} %pad_add_fusion.1.refs_0_, s32[1,2048]{1,0:T(1,128)S(1)} %bitcast.20, bf16[64,2048]{1,0:T(8,128)(2,1)S(1)} %copy-done.2, bf16[192,2048]{1,0:T(8,128)(2,1)S(1)} %bitcast.15, s32[1,2048]{1,0:T(1,128)S(1)} %collective-permute-done.refs_4_, ...), custom_call_target="tpu_custom_call" | custom-call | flops 4294967296 | bytes 2097152 | tf_op jit(solution)/shard_map/pallas_call | solution.py:45
  15.8 0.5 collective-permute-start.5
  16.4 1.9 %shard_map.66 = bf16[8,96,128]{2,1,0:T(8,128)(2,1)S(1)} custom-call(s32[2]{0:T(128)S(1)} %pad_add_fusion.1.refs_0_, s32[1,2048]{1,0:T(1,128)S(1)} %bitcast.21, bf16[64,2048]{1,0:T(8,128)(2,1)S(1)} %copy-done.2, bf16[192,2048]{1,0:T(8,128)(2,1)S(1)} %bitcast.16, s32[1,2048]{1,0:T(1,128)S(1)} %collective-permute-done.refs_4_, ...), custom_call_target="tpu_custom_call" | custom-call | flops 4294967296 | bytes 2097152 | tf_op jit(solution)/shard_map/pallas_call | solution.py:45
  18.2 2.7 %collective-permute-start.4 = (bf16[8,96,128]{2,1,0:T(8,128)(2,1)S(1)}, bf16[8,96,128]{2,1,0:T(8,128)(2,1)S(1)}, u32[]{:S(2)}, u32[]{:S(2)}) collective-permute-start(bf16[8,96,128]{2,1,0:T(8,128)(2,1)S(1)} %shard_map.66), channel_id=1, source_target_pairs={{0,16},{8,24},{16,0},{24,8},{1,17},{9,25},{17,1},{25,9},{2,18},{10... | collective-permute-start | bytes 589832 | tf_op jit(solution)/shard_map/ppermute | solution.py:238
  20.9 1.9 %shard_map.65 = bf16[8,96,128]{2,1,0:T(8,128)(2,1)S(1)} custom-call(s32[2]{0:T(128)S(1)} %pad_add_fusion.1.refs_0_, s32[1,2048]{1,0:T(1,128)S(1)} %bitcast.22, bf16[64,2048]{1,0:T(8,128)(2,1)S(1)} %copy-done.2, bf16[192,2048]{1,0:T(8,128)(2,1)S(1)} %bitcast.17, s32[1,2048]{1,0:T(1,128)S(1)} %collective-permute-done.refs_4_, ...), custom_call_target="tpu_custom_call" | custom-call | flops 4294967296 | bytes 2097152 | tf_op jit(solution)/shard_map/pallas_call | solution.py:45
  22.8 2.0 %collective-permute-start.3 = (bf16[8,96,128]{2,1,0:T(8,128)(2,1)S(1)}, bf16[8,96,128]{2,1,0:T(8,128)(2,1)S(1)}, u32[]{:S(2)}, u32[]{:S(2)}) collective-permute-start(bf16[8,96,128]{2,1,0:T(8,128)(2,1)S(1)} %shard_map.65), channel_id=1, source_target_pairs={{0,8},{8,16},{16,24},{24,0},{1,9},{9,17},{17,25},{25,1},{2,10},{10... | collective-permute-start | bytes 589832 | tf_op jit(solution)/shard_map/ppermute | solution.py:238
  24.7 1.9 %shard_map.64.refs_0_ = f32[8,96,128]{2,1,0:T(8,128)S(1)} custom-call(s32[2]{0:T(128)S(1)} %pad_add_fusion.1.refs_0_, s32[1,2048]{1,0:T(1,128)S(1)} %bitcast.23, bf16[64,2048]{1,0:T(8,128)(2,1)S(1)} %copy-done.2, bf16[192,2048]{1,0:T(8,128)(2,1)S(1)} %bitcast.18, s32[1,2048]{1,0:T(1,128)S(1)} %collective-permute-done.refs_4_, ...), custom_call_target="tpu_custom_call" | custom-call | flops 4294967296 | bytes 2097152 | tf_op jit(solution)/shard_map/pallas_call | solution.py:45
  26.6 0.0 collective-permute-done.5.refs_3_
  26.6 1.5 %collective-permute-done.4.refs_2_ = bf16[8,96,128]{2,1,0:T(8,128)(2,1)S(1)} collective-permute-done((bf16[8,96,128]{2,1,0:T(8,128)(2,1)S(1)}, bf16[8,96,128]{2,1,0:T(8,128)(2,1)S(1)}, u32[]{:S(2)}, u32[]{:S(2)}) %collective-permute-start.4) | collective-permute-done | bytes 196640 | tf_op jit(solution)/shard_map/ppermute | solution.py:238
  28.1 2.7 %collective-permute-done.3.refs_1_ = bf16[8,96,128]{2,1,0:T(8,128)(2,1)S(1)} collective-permute-done((bf16[8,96,128]{2,1,0:T(8,128)(2,1)S(1)}, bf16[8,96,128]{2,1,0:T(8,128)(2,1)S(1)}, u32[]{:S(2)}, u32[]{:S(2)}) %collective-permute-start.3) | collective-permute-done | bytes 196640 | tf_op jit(solution)/shard_map/ppermute | solution.py:238
  30.9 0.1 shard_map.68
  31.0 1.1 %collective-permute-start.6 = (bf16[4,96,128]{2,1,0:T(8,128)(2,1)S(1)}, bf16[4,96,128]{2,1,0:T(8,128)(2,1)S(1)}, u32[]{:S(2)}, u32[]{:S(2)}) collective-permute-start(bf16[4,96,128]{2,1,0:T(8,128)(2,1)S(1)} %get-tuple-element.26), channel_id=1, source_target_pairs={{0,32},{32,0},{1,33},{33,1},{2,34},{34,2},{3,35},{35,3},{4,36},{36... | collective-permute-start | bytes 294920 | tf_op jit(solution)/shard_map/ppermute | solution.py:244
  32.0 0.1 pad_add_fusion.place_ref.refs_0_
  32.1 6.4 %collective-permute-done.6.came_ref = bf16[4,96,128]{2,1,0:T(8,128)(2,1)S(1)} collective-permute-done((bf16[4,96,128]{2,1,0:T(8,128)(2,1)S(1)}, bf16[4,96,128]{2,1,0:T(8,128)(2,1)S(1)}, u32[]{:S(2)}, u32[]{:S(2)}) %collective-permute-start.6) | collective-permute-done | bytes 98336 | tf_op jit(solution)/shard_map/ppermute | solution.py:244
  38.5 0.0 copy-done
  38.5 0.6 shard_map.69
  39.2 3.6 %all-to-all-done.refs_1_ = bf16[16,64,512]{2,1,0:T(8,128)(2,1)S(1)} async-done(((bf16[16,64,512]{2,1,0:T(8,128)(2,1)}), bf16[16,64,512]{2,1,0:T(8,128)(2,1)S(1)}, u32[]{:S(2)}, u32[]{:S(2)}) %all-to-all-start) | async-done | bytes 1048608 | tf_op jit(solution)/shard_map/all_to_all | solution.py:222
  42.8 0.4 collective-permute-start.7
  43.1 4.1 %collective-permute-start.8 = (bf16[416,128]{1,0:T(8,128)(2,1)S(1)}, bf16[416,128]{1,0:T(8,128)(2,1)S(1)}, u32[]{:S(2)}, u32[]{:S(2)}) collective-permute-start(bf16[416,128]{1,0:T(8,128)(2,1)S(1)} %get-tuple-element.35), channel_id=1, source_target_pairs={{0,128},{64,192},{128,0},{192,64},{1,129},{65,193},{129,1},{193,65... | collective-permute-start | bytes 319496 | tf_op jit(solution)/shard_map/ppermute | solution.py:202
  47.2 2.0 %collective-permute-start.9 = (bf16[416,128]{1,0:T(8,128)(2,1)S(1)}, bf16[416,128]{1,0:T(8,128)(2,1)S(1)}, u32[]{:S(2)}, u32[]{:S(2)}) collective-permute-start(bf16[416,128]{1,0:T(8,128)(2,1)S(1)} %get-tuple-element.36), channel_id=1, source_target_pairs={{0,192},{64,128},{128,64},{192,0},{1,193},{65,129},{129,65},{193,1... | collective-permute-start | bytes 319496 | tf_op jit(solution)/shard_map/ppermute | solution.py:202
  49.3 0.0 collective-permute-done.7.refs_0_
  49.3 7.1 %collective-permute-done.8.refs_1_ = bf16[416,128]{1,0:T(8,128)(2,1)S(1)} collective-permute-done((bf16[416,128]{1,0:T(8,128)(2,1)S(1)}, bf16[416,128]{1,0:T(8,128)(2,1)S(1)}, u32[]{:S(2)}, u32[]{:S(2)}) %collective-permute-start.8) | collective-permute-done | bytes 106528 | tf_op jit(solution)/shard_map/ppermute | solution.py:202
  56.4 1.2 %collective-permute-done.9.refs_2_ = bf16[416,128]{1,0:T(8,128)(2,1)S(1)} collective-permute-done((bf16[416,128]{1,0:T(8,128)(2,1)S(1)}, bf16[416,128]{1,0:T(8,128)(2,1)S(1)}, u32[]{:S(2)}, u32[]{:S(2)}) %collective-permute-start.9) | collective-permute-done | bytes 106528 | tf_op jit(solution)/shard_map/ppermute | solution.py:202
  57.6 0.6 shard_map.70
  58.2 1.5 %collective-permute-start.10 = (bf16[4,96,128]{2,1,0:T(8,128)(2,1)S(1)}, bf16[4,96,128]{2,1,0:T(8,128)(2,1)S(1)}, u32[]{:S(2)}, u32[]{:S(2)}) collective-permute-start(bf16[4,96,128]{2,1,0:T(8,128)(2,1)S(1)} %get-tuple-element.38.refs_3_), channel_id=1, source_target_pairs={{0,1},{1,2},{2,3},{3,0},{4,5},{5,6},{6,7},{7,4},{8,9},{9,10},{10,1... | collective-permute-start | bytes 294920 | tf_op jit(solution)/shard_map/ppermute | solution.py:202
  59.8 2.8 %collective-permute-start.11 = (bf16[4,96,128]{2,1,0:T(8,128)(2,1)S(1)}, bf16[4,96,128]{2,1,0:T(8,128)(2,1)S(1)}, u32[]{:S(2)}, u32[]{:S(2)}) collective-permute-start(bf16[4,96,128]{2,1,0:T(8,128)(2,1)S(1)} %get-tuple-element.38.refs_3_), channel_id=1, source_target_pairs={{0,2},{1,3},{2,0},{3,1},{4,6},{5,7},{6,4},{7,5},{8,10},{9,11},{10,... | collective-permute-start | bytes 294920 | tf_op jit(solution)/shard_map/ppermute | solution.py:202
  62.5 1.6 %collective-permute-start.12 = (bf16[4,96,128]{2,1,0:T(8,128)(2,1)S(1)}, bf16[4,96,128]{2,1,0:T(8,128)(2,1)S(1)}, u32[]{:S(2)}, u32[]{:S(2)}) collective-permute-start(bf16[4,96,128]{2,1,0:T(8,128)(2,1)S(1)} %get-tuple-element.38.refs_3_), channel_id=1, source_target_pairs={{0,3},{1,0},{2,1},{3,2},{4,7},{5,4},{6,5},{7,6},{8,11},{9,8},{10,9... | collective-permute-start | bytes 294920 | tf_op jit(solution)/shard_map/ppermute | solution.py:202
  64.1 0.0 collective-permute-done.10.refs_4_
  64.1 2.1 %collective-permute-done.11.refs_5_ = bf16[4,96,128]{2,1,0:T(8,128)(2,1)S(1)} collective-permute-done((bf16[4,96,128]{2,1,0:T(8,128)(2,1)S(1)}, bf16[4,96,128]{2,1,0:T(8,128)(2,1)S(1)}, u32[]{:S(2)}, u32[]{:S(2)}) %collective-permute-start.11) | collective-permute-done | bytes 98336 | tf_op jit(solution)/shard_map/ppermute | solution.py:202
  66.2 1.0 %collective-permute-done.12.refs_6_ = bf16[4,96,128]{2,1,0:T(8,128)(2,1)S(1)} collective-permute-done((bf16[4,96,128]{2,1,0:T(8,128)(2,1)S(1)}, bf16[4,96,128]{2,1,0:T(8,128)(2,1)S(1)}, u32[]{:S(2)}, u32[]{:S(2)}) %collective-permute-start.12) | collective-permute-done | bytes 98336 | tf_op jit(solution)/shard_map/ppermute | solution.py:202
  67.2 1.3 %shard_map.71 = bf16[16,48,512]{2,1,0:T(8,128)(2,1)S(1)} custom-call(s32[4]{0:T(128)S(1)} %pad_add_fusion.place_ref.refs_0_, bf16[16,64,512]{2,1,0:T(8,128)(2,1)S(1)} %all-to-all-done.refs_1_, bf16[4,32,128]{2,1,0:T(8,128)(2,1)S(1)} %get-tuple-element.37.refs_2_, bf16[4,96,128]{2,1,0:T(8,128)(2,1)S(1)} %get-tuple-element.38.refs_3_, ...), custom_call_target="tpu_custom_call" | custom-call | flops 201326592 | bytes 2097152 | tf_op jit(solution)/shard_map/pallas_call | solution.py:45
  68.5 26.0 %all_to_all.10.pieces_ref = bf16[16,48,512]{2,1,0:T(8,128)(2,1)S(1)} all-to-all(bf16[16,48,512]{2,1,0:T(8,128)(2,1)S(1)} %shard_map.71), channel_id=1, replica_groups={{0,1,2,3,64,65,66,67,128,129,130,131,192,193,194,195},{199,198,197,196,..., dimensions={0} | all-to-all | bytes 1572864 | tf_op jit(solution)/shard_map/all_to_all | solution.py:293
  94.5 1.5 %shard_map.72 = bf16[48,8192]{1,0:T(8,128)(2,1)} custom-call(s32[4]{0:T(128)S(1)} %pad_add_fusion.place_ref.refs_0_, bf16[16,48,512]{2,1,0:T(8,128)(2,1)S(1)} %all_to_all.10.pieces_ref), custom_call_target="tpu_custom_call" | custom-call | bytes 2097152 | tf_op jit(solution)/shard_map/pallas_call | solution.py:71
  (1 shorter events, 0.0 us)
Async XLA Ops:
  0.0 2.9 %collective-permute-start.2 = (bf16[192,2048]{1,0:T(8,128)(2,1)}, bf16[192,2048]{1,0:T(8,128)(2,1)S(1)}, u32[]{:S(2)}, u32[]{:S(2)}) collective-permute-start(bf16[192,2048]{1,0:T(8,128)(2,1)} %bitcast.14), channel_id=1, source_target_pairs={{0,4},{4,0},{1,5},{5,1},{2,6},{6,2},{3,7},{7,3},{8,12},{12,8},{9,1... | collective-permute-start | bytes 2359304 | tf_op jit(solution)/shard_map/ppermute | solution.py:219
  0.0 2.9 %collective-permute-start.1 = (bf16[64,2048]{1,0:T(8,128)(2,1)}, bf16[64,2048]{1,0:T(8,128)(2,1)S(1)}, u32[]{:S(2)}, u32[]{:S(2)}) collective-permute-start(bf16[64,2048]{1,0:T(8,128)(2,1)} %refs_2_.7), channel_id=1, source_target_pairs={{0,4},{4,0},{1,5},{5,1},{2,6},{6,2},{3,7},{7,3},{8,12},{12,8},{9,1... | collective-permute-start | bytes 786440 | tf_op jit(solution)/shard_map/ppermute | solution.py:219
  0.5 2.4 %collective-permute-start = (s32[1,2048]{1,0:T(1,128)}, s32[1,2048]{1,0:T(1,128)S(1)}, u32[]{:S(2)}, u32[]{:S(2)}) collective-permute-start(s32[1,2048]{1,0:T(1,128)} %bitcast.19), channel_id=1, source_target_pairs={{0,4},{4,0},{1,5},{5,1},{2,6},{6,2},{3,7},{7,3},{8,12},{12,8},{9,1... | collective-permute-start | bytes 24584 | tf_op jit(solution)/shard_map/ppermute | solution.py:219
  2.9 11.1 %copy-start.1 = (bf16[2048,192]{0,1:T(8,128)(2,1)S(1)}, bf16[2048,192]{0,1:T(8,128)(2,1)}, u32[]{:S(2)}) copy-start(bf16[2048,192]{0,1:T(8,128)(2,1)} %param.8) | copy-start | bytes 2359300
  2.9 11.1 %copy-start.2 = (bf16[64,2048]{1,0:T(8,128)(2,1)S(1)}, bf16[64,2048]{1,0:T(8,128)(2,1)}, u32[]{:S(2)}) copy-start(bf16[64,2048]{1,0:T(8,128)(2,1)} %refs_2_.7) | copy-start | bytes 786436
  2.9 39.9 %all-to-all-start = ((bf16[16,64,512]{2,1,0:T(8,128)(2,1)}), bf16[16,64,512]{2,1,0:T(8,128)(2,1)S(1)}, u32[]{:S(2)}, u32[]{:S(2)}) async-start(bf16[16,64,512]{2,1,0:T(8,128)(2,1)} %bitcast.24), calls=%async_computation | async-start | bytes 2097152 | tf_op jit(solution)/shard_map/all_to_all | solution.py:222
  13.2 0.8 copy-start.3
  15.8 10.8 %collective-permute-start.5 = (bf16[8,96,128]{2,1,0:T(8,128)(2,1)S(1)}, bf16[8,96,128]{2,1,0:T(8,128)(2,1)S(1)}, u32[]{:S(2)}, u32[]{:S(2)}) collective-permute-start(bf16[8,96,128]{2,1,0:T(8,128)(2,1)S(1)} %shard_map.67), channel_id=1, source_target_pairs={{0,24},{8,0},{16,8},{24,16},{1,25},{9,1},{17,9},{25,17},{2,26},{10... | collective-permute-start | bytes 589832 | tf_op jit(solution)/shard_map/ppermute | solution.py:238
  18.2 9.9 %collective-permute-start.4 = (bf16[8,96,128]{2,1,0:T(8,128)(2,1)S(1)}, bf16[8,96,128]{2,1,0:T(8,128)(2,1)S(1)}, u32[]{:S(2)}, u32[]{:S(2)}) collective-permute-start(bf16[8,96,128]{2,1,0:T(8,128)(2,1)S(1)} %shard_map.66), channel_id=1, source_target_pairs={{0,16},{8,24},{16,0},{24,8},{1,17},{9,25},{17,1},{25,9},{2,18},{10... | collective-permute-start | bytes 589832 | tf_op jit(solution)/shard_map/ppermute | solution.py:238
  22.8 8.1 %collective-permute-start.3 = (bf16[8,96,128]{2,1,0:T(8,128)(2,1)S(1)}, bf16[8,96,128]{2,1,0:T(8,128)(2,1)S(1)}, u32[]{:S(2)}, u32[]{:S(2)}) collective-permute-start(bf16[8,96,128]{2,1,0:T(8,128)(2,1)S(1)} %shard_map.65), channel_id=1, source_target_pairs={{0,8},{8,16},{16,24},{24,0},{1,9},{9,17},{17,25},{25,1},{2,10},{10... | collective-permute-start | bytes 589832 | tf_op jit(solution)/shard_map/ppermute | solution.py:238
  30.9 7.7 %copy-start = (f32[2,8192]{1,0:T(2,128)S(1)}, f32[2,8192]{1,0:T(2,128)}, u32[]{:S(2)}) copy-start(f32[2,8192]{1,0:T(2,128)} %twiddle_ref.1) | copy-start | bytes 196612
  31.0 7.6 %collective-permute-start.6 = (bf16[4,96,128]{2,1,0:T(8,128)(2,1)S(1)}, bf16[4,96,128]{2,1,0:T(8,128)(2,1)S(1)}, u32[]{:S(2)}, u32[]{:S(2)}) collective-permute-start(bf16[4,96,128]{2,1,0:T(8,128)(2,1)S(1)} %get-tuple-element.26), channel_id=1, source_target_pairs={{0,32},{32,0},{1,33},{33,1},{2,34},{34,2},{3,35},{35,3},{4,36},{36... | collective-permute-start | bytes 294920 | tf_op jit(solution)/shard_map/ppermute | solution.py:244
  42.8 6.5 %collective-permute-start.7 = (bf16[416,128]{1,0:T(8,128)(2,1)S(1)}, bf16[416,128]{1,0:T(8,128)(2,1)S(1)}, u32[]{:S(2)}, u32[]{:S(2)}) collective-permute-start(bf16[416,128]{1,0:T(8,128)(2,1)S(1)} %get-tuple-element.34), channel_id=1, source_target_pairs={{0,64},{64,0},{128,192},{192,128},{1,65},{65,1},{129,193},{193,129... | collective-permute-start | bytes 319496 | tf_op jit(solution)/shard_map/ppermute | solution.py:202
  43.1 13.3 %collective-permute-start.8 = (bf16[416,128]{1,0:T(8,128)(2,1)S(1)}, bf16[416,128]{1,0:T(8,128)(2,1)S(1)}, u32[]{:S(2)}, u32[]{:S(2)}) collective-permute-start(bf16[416,128]{1,0:T(8,128)(2,1)S(1)} %get-tuple-element.35), channel_id=1, source_target_pairs={{0,128},{64,192},{128,0},{192,64},{1,129},{65,193},{129,1},{193,65... | collective-permute-start | bytes 319496 | tf_op jit(solution)/shard_map/ppermute | solution.py:202
  47.2 10.4 %collective-permute-start.9 = (bf16[416,128]{1,0:T(8,128)(2,1)S(1)}, bf16[416,128]{1,0:T(8,128)(2,1)S(1)}, u32[]{:S(2)}, u32[]{:S(2)}) collective-permute-start(bf16[416,128]{1,0:T(8,128)(2,1)S(1)} %get-tuple-element.36), channel_id=1, source_target_pairs={{0,192},{64,128},{128,64},{192,0},{1,193},{65,129},{129,65},{193,1... | collective-permute-start | bytes 319496 | tf_op jit(solution)/shard_map/ppermute | solution.py:202
  58.2 5.9 %collective-permute-start.10 = (bf16[4,96,128]{2,1,0:T(8,128)(2,1)S(1)}, bf16[4,96,128]{2,1,0:T(8,128)(2,1)S(1)}, u32[]{:S(2)}, u32[]{:S(2)}) collective-permute-start(bf16[4,96,128]{2,1,0:T(8,128)(2,1)S(1)} %get-tuple-element.38.refs_3_), channel_id=1, source_target_pairs={{0,1},{1,2},{2,3},{3,0},{4,5},{5,6},{6,7},{7,4},{8,9},{9,10},{10,1... | collective-permute-start | bytes 294920 | tf_op jit(solution)/shard_map/ppermute | solution.py:202
  59.8 6.4 %collective-permute-start.11 = (bf16[4,96,128]{2,1,0:T(8,128)(2,1)S(1)}, bf16[4,96,128]{2,1,0:T(8,128)(2,1)S(1)}, u32[]{:S(2)}, u32[]{:S(2)}) collective-permute-start(bf16[4,96,128]{2,1,0:T(8,128)(2,1)S(1)} %get-tuple-element.38.refs_3_), channel_id=1, source_target_pairs={{0,2},{1,3},{2,0},{3,1},{4,6},{5,7},{6,4},{7,5},{8,10},{9,11},{10,... | collective-permute-start | bytes 294920 | tf_op jit(solution)/shard_map/ppermute | solution.py:202
  62.5 4.6 %collective-permute-start.12 = (bf16[4,96,128]{2,1,0:T(8,128)(2,1)S(1)}, bf16[4,96,128]{2,1,0:T(8,128)(2,1)S(1)}, u32[]{:S(2)}, u32[]{:S(2)}) collective-permute-start(bf16[4,96,128]{2,1,0:T(8,128)(2,1)S(1)} %get-tuple-element.38.refs_3_), channel_id=1, source_target_pairs={{0,3},{1,0},{2,1},{3,2},{4,7},{5,4},{6,5},{7,6},{8,11},{9,8},{10,9... | collective-permute-start | bytes 294920 | tf_op jit(solution)/shard_map/ppermute | solution.py:202

commit v12 on v10

--- a/solution.py
+++ b/solution.py
@@ -53,6 +53,18 @@
     )(*args)
 
 
+def place_of(member, count, core):
+    return jnp.where(core == 1, count - 1 - member, member)
+
+
+def reversed_groups(zg, zl, y, core, smp):
+    groups = []
+    for rest in range(zl * y * core):
+        members = [((g * zl * y * core) + rest) * smp + p for g in range(zg) for p in range(smp)]
+        groups.append(members[::-1] if rest % core else members)
+    return groups
+
+
 def halve_kernel(place_ref, *refs):
     kept_ref, sent_ref = refs[-2:]
     for block in range(kept_ref.shape[0]):
@@ -74,7 +86,7 @@
     rank = jnp.full((8 - 3 * levels, lanes), rank.astype(jnp.float32))
     for distance in range(blocks):
         partner = zg ^ distance
-        start = (partner * blocks + smp) * piece
+        start = place_of(partner * blocks + smp, blocks * blocks, place_ref[3]) * piece
         rows = []
         for column in range(piece // lanes):
             left = twiddle_ref[:, pl.ds(pl.multiple_of(start + column * lanes, lanes), lanes)]
@@ -123,7 +135,7 @@
     vectors, points = field.shape[1:]
     samples = samples_ref.shape[1]
     for p in range(parts):
-        every[lax.rem(smp - p + parts, parts)] = weight_refs[p][...]
+        every[place_of(lax.rem(smp - p + parts, parts), parts, place_ref[3])] = weight_refs[p][...]
     factors = []
     for c in range(blocks):
         head, tail, columns = [], [], []
@@ -136,7 +148,8 @@
             terms = extra[column * 8:column * 8 + 8]
             columns.append(terms[0:2] + terms[2:4] + terms[4:6])
         factors.append(jnp.concatenate(columns, axis=1))
-        grid = samples_ref[pl.ds((zg ^ c) * parts, parts)].reshape(parts * samples, points)
+        first = place_of(zg ^ c, blocks, place_ref[3]) * parts
+        grid = samples_ref[pl.ds(first, parts)].reshape(parts * samples, points)
         head = jnp.concatenate(head, axis=0)
         tail = jnp.concatenate(tail, axis=0)
         field[c, :128, :] = lax.dot_general(
@@ -155,7 +168,8 @@
                 for c in range(blocks)
             ]
         for c in range(blocks):
-            out_ref[(zg ^ c) * parts + p] = level[c].astype(jnp.bfloat16)
+            target = place_of((zg ^ c) * parts + p, blocks * parts, place_ref[3])
+            out_ref[target] = level[c].astype(jnp.bfloat16)
 
 
 def exchange(pieces, axis, route):
@@ -183,7 +197,9 @@
     came = [lax.ppermute(x, "core", [(0, 1), (1, 0)]) for x in rows]
     pieces, *came = lax.optimization_barrier((pieces, *came))
     rows = (own, adjoint_samples, probes, *came)
-    pieces = lax.all_to_all(pieces, GROUP, 0, 0, tiled=True)
+    axes = BLK + ("smp",)
+    lists = reversed_groups(*(lax.axis_size(axis) for axis in axes))
+    pieces = lax.all_to_all(pieces, axes, 0, 0, tiled=True, axis_index_groups=lists)
 
     place = jnp.stack([y, core])
     shape = (lax.axis_size(Z_AXES), samples * vectors // 128, 128)
@@ -212,7 +228,7 @@
     offer = (groups * shape[1] + tail, shape[2])
     shapes += [jax.ShapeDtypeStruct(offer, jnp.bfloat16)] * (groups - 1)
     zg = lax.axis_index("zg")
-    place = jnp.stack([zg, smp, block_ranks[0]])
+    place = jnp.stack([zg, smp, block_ranks[0], core])
     partial, extra, *offers = local_call(
         offer_kernel,
         shapes,
@@ -252,7 +268,7 @@
         ],
         flops=2 * members * samples * vectors * piece,
     )
-    result = lax.all_to_all(result, GROUP, 0, 0, tiled=True)
+    result = lax.all_to_all(result, axes, 0, 0, tiled=True, axis_index_groups=lists)
     return result.transpose(1, 0, 2).reshape(vectors // parts, points)
 
 

time: 98.8 us -> 98 us (level); the launches traced: 98.3 us -> 96.5 us
    all_to_all x1, waiting for transfers between devices: 3.62 us -> 0.01 us  [body(): lax.all_to_all(pieces, axes, 0, 0, tiled=True, axis_index_groups=lists)]
    ppermute x6, waiting for transfers between devices: 11.4 us -> 12.5 us  [exchange(): came[offset] = lax.ppermute(pieces[offset], axis, pairs)]
where the time goes in v12:
time: 98 us; the launch traced here: 96.5 us
  starting transfers between devices  28.8 us (29%)
  blocking collectives  28.3 us (29%)
  waiting for transfers between devices  25.1 us (26%)
  Pallas kernels  10.2 us (10%)
  local copies, waits for them, and re-layouts  3.3 us (3%)
    all_to_all x1, blocking collectives, body(): lax.all_to_all(result, axes, 0, 0, tiled=True, axis_index_groups=lists)  28.3 us
    ppermute x6, waiting for transfers between devices, exchange(): came[offset] = lax.ppermute(pieces[offset], axis, pairs)  12.5 us
    ppermute x6, starting transfers between devices, exchange(): came[offset] = lax.ppermute(pieces[offset], axis, pairs)  11.8 us
    all_to_all x1, starting transfers between devices, body(): lax.all_to_all(pieces, axes, 0, 0, tiled=True, axis_index_groups=lists)  10.3 us
    pallas_call x8, Pallas kernels, local_call(): pl.pallas_call(kernel, out_shape=out_shape, in_specs=[SMEM] * smem + [VME...  10.2 us
    ppermute x1, waiting for transfers between devices, body(): came = lax.ppermute(sent, 'zl', [(0, 1), (1, 0)])  7.27 us
    ppermute x3, waiting for transfers between devices, body(): sums[offset] = lax.ppermute(value, 'y', route) if offset else value  5.24 us
    ppermute x3, starting transfers between devices, body(): sums[offset] = lax.ppermute(value, 'y', route) if offset else value  5.16 us
  transfers between devices with their start and end apart: 14, of which 8 were waited for; matrix products, arithmetic and copies ran while one was open for 3% of the time, Pallas kernels for 8%

profile of v12, /device:TPU:40, one launch (start us, length us, event | category | flops | bytes accessed | tf_op | source)
XLA Modules:
  0.0 96.5 jit_solution(10229733729036709948)
XLA Ops:
  0.0 0.0 collective-permute-start.2
  0.0 0.5 collective-permute-start.1
  0.5 0.0 collective-permute-start
  0.5 2.3 %copy.12 = bf16[8,16,8,512]{3,2,0,1:T(8,128)(2,1)} copy(bf16[8,16,8,512]{3,2,1,0:T(8,128)(2,1)} %bitcast.29) | data formatting | bytes 2097152 | tf_op jit(solution)/shard_map/reshape | solution.py:194
  2.8 0.0 collective-permute-done.refs_4_
  2.9 0.0 collective-permute-done.1.refs_5_
  2.9 0.0 collective-permute-done.2.refs_6_
  2.9 0.0 copy-start.1
  2.9 0.0 copy-start.2
  2.9 10.3 %all-to-all-start = ((bf16[16,64,512]{2,1,0:T(8,128)(2,1)}), bf16[16,64,512]{2,1,0:T(8,128)(2,1)S(1)}, u32[]{:S(2)}, u32[]{:S(2)}) async-start(bf16[16,64,512]{2,1,0:T(8,128)(2,1)} %bitcast.27), calls=%async_computation | async-start | bytes 2097152 | tf_op jit(solution)/shard_map/all_to_all | solution.py:202
  13.2 0.0 copy-start.3
  13.9 0.1 pad_add_fusion.1.refs_0_
  13.9 0.0 copy-done.1
  13.9 0.0 copy-done.2
  14.0 0.0 copy-done.3
  14.0 1.9 %shard_map.67 = bf16[8,96,128]{2,1,0:T(8,128)(2,1)S(1)} custom-call(s32[2]{0:T(128)S(1)} %pad_add_fusion.1.refs_0_, s32[1,2048]{1,0:T(1,128)S(1)} %bitcast.23, bf16[64,2048]{1,0:T(8,128)(2,1)S(1)} %copy-done.2, bf16[192,2048]{1,0:T(8,128)(2,1)S(1)} %bitcast.18, s32[1,2048]{1,0:T(1,128)S(1)} %collective-permute-done.refs_4_, ...), custom_call_target="tpu_custom_call" | custom-call | flops 4294967296 | bytes 2097152 | tf_op jit(solution)/shard_map/pallas_call | solution.py:45
  15.8 0.5 collective-permute-start.5
  16.4 1.9 %shard_map.66 = bf16[8,96,128]{2,1,0:T(8,128)(2,1)S(1)} custom-call(s32[2]{0:T(128)S(1)} %pad_add_fusion.1.refs_0_, s32[1,2048]{1,0:T(1,128)S(1)} %bitcast.24, bf16[64,2048]{1,0:T(8,128)(2,1)S(1)} %copy-done.2, bf16[192,2048]{1,0:T(8,128)(2,1)S(1)} %bitcast.19, s32[1,2048]{1,0:T(1,128)S(1)} %collective-permute-done.refs_4_, ...), custom_call_target="tpu_custom_call" | custom-call | flops 4294967296 | bytes 2097152 | tf_op jit(solution)/shard_map/pallas_call | solution.py:45
  18.2 2.7 %collective-permute-start.4 = (bf16[8,96,128]{2,1,0:T(8,128)(2,1)S(1)}, bf16[8,96,128]{2,1,0:T(8,128)(2,1)S(1)}, u32[]{:S(2)}, u32[]{:S(2)}) collective-permute-start(bf16[8,96,128]{2,1,0:T(8,128)(2,1)S(1)} %shard_map.66), channel_id=1, source_target_pairs={{0,16},{8,24},{16,0},{24,8},{1,17},{9,25},{17,1},{25,9},{2,18},{10... | collective-permute-start | bytes 589832 | tf_op jit(solution)/shard_map/ppermute | solution.py:218
  20.9 1.9 %shard_map.65 = bf16[8,96,128]{2,1,0:T(8,128)(2,1)S(1)} custom-call(s32[2]{0:T(128)S(1)} %pad_add_fusion.1.refs_0_, s32[1,2048]{1,0:T(1,128)S(1)} %bitcast.25, bf16[64,2048]{1,0:T(8,128)(2,1)S(1)} %copy-done.2, bf16[192,2048]{1,0:T(8,128)(2,1)S(1)} %bitcast.20, s32[1,2048]{1,0:T(1,128)S(1)} %collective-permute-done.refs_4_, ...), custom_call_target="tpu_custom_call" | custom-call | flops 4294967296 | bytes 2097152 | tf_op jit(solution)/shard_map/pallas_call | solution.py:45
  22.8 2.0 %collective-permute-start.3 = (bf16[8,96,128]{2,1,0:T(8,128)(2,1)S(1)}, bf16[8,96,128]{2,1,0:T(8,128)(2,1)S(1)}, u32[]{:S(2)}, u32[]{:S(2)}) collective-permute-start(bf16[8,96,128]{2,1,0:T(8,128)(2,1)S(1)} %shard_map.65), channel_id=1, source_target_pairs={{0,8},{8,16},{16,24},{24,0},{1,9},{9,17},{17,25},{25,1},{2,10},{10... | collective-permute-start | bytes 589832 | tf_op jit(solution)/shard_map/ppermute | solution.py:218
  24.7 1.9 %shard_map.64.refs_0_ = f32[8,96,128]{2,1,0:T(8,128)S(1)} custom-call(s32[2]{0:T(128)S(1)} %pad_add_fusion.1.refs_0_, s32[1,2048]{1,0:T(1,128)S(1)} %bitcast.26, bf16[64,2048]{1,0:T(8,128)(2,1)S(1)} %copy-done.2, bf16[192,2048]{1,0:T(8,128)(2,1)S(1)} %bitcast.21, s32[1,2048]{1,0:T(1,128)S(1)} %collective-permute-done.refs_4_, ...), custom_call_target="tpu_custom_call" | custom-call | flops 4294967296 | bytes 2097152 | tf_op jit(solution)/shard_map/pallas_call | solution.py:45
  26.6 0.0 collective-permute-done.5.refs_3_
  26.6 2.1 %collective-permute-done.4.refs_2_ = bf16[8,96,128]{2,1,0:T(8,128)(2,1)S(1)} collective-permute-done((bf16[8,96,128]{2,1,0:T(8,128)(2,1)S(1)}, bf16[8,96,128]{2,1,0:T(8,128)(2,1)S(1)}, u32[]{:S(2)}, u32[]{:S(2)}) %collective-permute-start.4) | collective-permute-done | bytes 196640 | tf_op jit(solution)/shard_map/ppermute | solution.py:218
  28.7 3.1 %collective-permute-done.3.refs_1_ = bf16[8,96,128]{2,1,0:T(8,128)(2,1)S(1)} collective-permute-done((bf16[8,96,128]{2,1,0:T(8,128)(2,1)S(1)}, bf16[8,96,128]{2,1,0:T(8,128)(2,1)S(1)}, u32[]{:S(2)}, u32[]{:S(2)}) %collective-permute-start.3) | collective-permute-done | bytes 196640 | tf_op jit(solution)/shard_map/ppermute | solution.py:218
  31.8 0.1 shard_map.68
  31.9 1.1 %collective-permute-start.6 = (bf16[4,96,128]{2,1,0:T(8,128)(2,1)S(1)}, bf16[4,96,128]{2,1,0:T(8,128)(2,1)S(1)}, u32[]{:S(2)}, u32[]{:S(2)}) collective-permute-start(bf16[4,96,128]{2,1,0:T(8,128)(2,1)S(1)} %get-tuple-element.26), channel_id=1, source_target_pairs={{0,32},{32,0},{1,33},{33,1},{2,34},{34,2},{3,35},{35,3},{4,36},{36... | collective-permute-start | bytes 294920 | tf_op jit(solution)/shard_map/ppermute | solution.py:224
  33.0 0.1 pad_add_fusion.place_ref.refs_0_
  33.1 7.3 %collective-permute-done.6.came_ref = bf16[4,96,128]{2,1,0:T(8,128)(2,1)S(1)} collective-permute-done((bf16[4,96,128]{2,1,0:T(8,128)(2,1)S(1)}, bf16[4,96,128]{2,1,0:T(8,128)(2,1)S(1)}, u32[]{:S(2)}, u32[]{:S(2)}) %collective-permute-start.6) | collective-permute-done | bytes 98336 | tf_op jit(solution)/shard_map/ppermute | solution.py:224
  40.4 0.0 copy-done
  40.4 0.6 shard_map.69
  41.0 0.0 all-to-all-done.refs_1_
  41.0 2.2 %collective-permute-start.7 = (bf16[416,128]{1,0:T(8,128)(2,1)S(1)}, bf16[416,128]{1,0:T(8,128)(2,1)S(1)}, u32[]{:S(2)}, u32[]{:S(2)}) collective-permute-start(bf16[416,128]{1,0:T(8,128)(2,1)S(1)} %get-tuple-element.34), channel_id=1, source_target_pairs={{0,64},{64,0},{128,192},{192,128},{1,65},{65,1},{129,193},{193,129... | collective-permute-start | bytes 319496 | tf_op jit(solution)/shard_map/ppermute | solution.py:180
  43.2 1.4 %collective-permute-start.8 = (bf16[416,128]{1,0:T(8,128)(2,1)S(1)}, bf16[416,128]{1,0:T(8,128)(2,1)S(1)}, u32[]{:S(2)}, u32[]{:S(2)}) collective-permute-start(bf16[416,128]{1,0:T(8,128)(2,1)S(1)} %get-tuple-element.35), channel_id=1, source_target_pairs={{0,128},{64,192},{128,0},{192,64},{1,129},{65,193},{129,1},{193,65... | collective-permute-start | bytes 319496 | tf_op jit(solution)/shard_map/ppermute | solution.py:180
  44.6 3.0 %collective-permute-start.9 = (bf16[416,128]{1,0:T(8,128)(2,1)S(1)}, bf16[416,128]{1,0:T(8,128)(2,1)S(1)}, u32[]{:S(2)}, u32[]{:S(2)}) collective-permute-start(bf16[416,128]{1,0:T(8,128)(2,1)S(1)} %get-tuple-element.36), channel_id=1, source_target_pairs={{0,192},{64,128},{128,64},{192,0},{1,193},{65,129},{129,65},{193,1... | collective-permute-start | bytes 319496 | tf_op jit(solution)/shard_map/ppermute | solution.py:180
  47.6 5.0 %collective-permute-done.7.refs_0_ = bf16[416,128]{1,0:T(8,128)(2,1)S(1)} collective-permute-done((bf16[416,128]{1,0:T(8,128)(2,1)S(1)}, bf16[416,128]{1,0:T(8,128)(2,1)S(1)}, u32[]{:S(2)}, u32[]{:S(2)}) %collective-permute-start.7) | collective-permute-done | bytes 106528 | tf_op jit(solution)/shard_map/ppermute | solution.py:180
  52.6 2.8 %collective-permute-done.8.refs_1_ = bf16[416,128]{1,0:T(8,128)(2,1)S(1)} collective-permute-done((bf16[416,128]{1,0:T(8,128)(2,1)S(1)}, bf16[416,128]{1,0:T(8,128)(2,1)S(1)}, u32[]{:S(2)}, u32[]{:S(2)}) %collective-permute-start.8) | collective-permute-done | bytes 106528 | tf_op jit(solution)/shard_map/ppermute | solution.py:180
  55.5 1.7 %collective-permute-done.9.refs_2_ = bf16[416,128]{1,0:T(8,128)(2,1)S(1)} collective-permute-done((bf16[416,128]{1,0:T(8,128)(2,1)S(1)}, bf16[416,128]{1,0:T(8,128)(2,1)S(1)}, u32[]{:S(2)}, u32[]{:S(2)}) %collective-permute-start.9) | collective-permute-done | bytes 106528 | tf_op jit(solution)/shard_map/ppermute | solution.py:180
  57.1 0.6 shard_map.70
  57.7 1.7 %collective-permute-start.10 = (bf16[4,96,128]{2,1,0:T(8,128)(2,1)S(1)}, bf16[4,96,128]{2,1,0:T(8,128)(2,1)S(1)}, u32[]{:S(2)}, u32[]{:S(2)}) collective-permute-start(bf16[4,96,128]{2,1,0:T(8,128)(2,1)S(1)} %get-tuple-element.38.refs_3_), channel_id=1, source_target_pairs={{0,1},{1,2},{2,3},{3,0},{4,5},{5,6},{6,7},{7,4},{8,9},{9,10},{10,1... | collective-permute-start | bytes 294920 | tf_op jit(solution)/shard_map/ppermute | solution.py:180
  59.4 1.0 %collective-permute-start.11 = (bf16[4,96,128]{2,1,0:T(8,128)(2,1)S(1)}, bf16[4,96,128]{2,1,0:T(8,128)(2,1)S(1)}, u32[]{:S(2)}, u32[]{:S(2)}) collective-permute-start(bf16[4,96,128]{2,1,0:T(8,128)(2,1)S(1)} %get-tuple-element.38.refs_3_), channel_id=1, source_target_pairs={{0,2},{1,3},{2,0},{3,1},{4,6},{5,7},{6,4},{7,5},{8,10},{9,11},{10,... | collective-permute-start | bytes 294920 | tf_op jit(solution)/shard_map/ppermute | solution.py:180
  60.4 2.5 %collective-permute-start.12 = (bf16[4,96,128]{2,1,0:T(8,128)(2,1)S(1)}, bf16[4,96,128]{2,1,0:T(8,128)(2,1)S(1)}, u32[]{:S(2)}, u32[]{:S(2)}) collective-permute-start(bf16[4,96,128]{2,1,0:T(8,128)(2,1)S(1)} %get-tuple-element.38.refs_3_), channel_id=1, source_target_pairs={{0,3},{1,0},{2,1},{3,2},{4,7},{5,4},{6,5},{7,6},{8,11},{9,8},{10,9... | collective-permute-start | bytes 294920 | tf_op jit(solution)/shard_map/ppermute | solution.py:180
  63.0 2.8 %collective-permute-done.10.refs_4_ = bf16[4,96,128]{2,1,0:T(8,128)(2,1)S(1)} collective-permute-done((bf16[4,96,128]{2,1,0:T(8,128)(2,1)S(1)}, bf16[4,96,128]{2,1,0:T(8,128)(2,1)S(1)}, u32[]{:S(2)}, u32[]{:S(2)}) %collective-permute-start.10) | collective-permute-done | bytes 98336 | tf_op jit(solution)/shard_map/ppermute | solution.py:180
  65.7 0.0 collective-permute-done.11.refs_5_
  65.7 0.2 collective-permute-done.12.refs_6_
  65.9 1.4 %shard_map.71 = bf16[16,48,512]{2,1,0:T(8,128)(2,1)S(1)} custom-call(s32[4]{0:T(128)S(1)} %pad_add_fusion.place_ref.refs_0_, bf16[16,64,512]{2,1,0:T(8,128)(2,1)S(1)} %all-to-all-done.refs_1_, bf16[4,32,128]{2,1,0:T(8,128)(2,1)S(1)} %get-tuple-element.37.refs_2_, bf16[4,96,128]{2,1,0:T(8,128)(2,1)S(1)} %get-tuple-element.38.refs_3_, ...), custom_call_target="tpu_custom_call" | custom-call | flops 201326592 | bytes 2097152 | tf_op jit(solution)/shard_map/pallas_call | solution.py:45
  67.3 28.3 %all_to_all.10 = bf16[16,48,512]{2,1,0:T(8,128)(2,1)S(1)} all-to-all(bf16[16,48,512]{2,1,0:T(8,128)(2,1)S(1)} %shard_map.71), channel_id=1, replica_groups={{0,1,2,3,64,65,66,67,128,129,130,131,192,193,194,195},{199,198,197,196,..., dimensions={0} | all-to-all | bytes 1572864 | tf_op jit(solution)/shard_map/all_to_all | solution.py:271
  95.6 1.0 copy.10
  (1 shorter events, 0.0 us)
Async XLA Ops:
  0.0 2.9 %collective-permute-start.2 = (bf16[192,2048]{1,0:T(8,128)(2,1)}, bf16[192,2048]{1,0:T(8,128)(2,1)S(1)}, u32[]{:S(2)}, u32[]{:S(2)}) collective-permute-start(bf16[192,2048]{1,0:T(8,128)(2,1)} %bitcast.17), channel_id=1, source_target_pairs={{0,4},{4,0},{1,5},{5,1},{2,6},{6,2},{3,7},{7,3},{8,12},{12,8},{9,1... | collective-permute-start | bytes 2359304 | tf_op jit(solution)/shard_map/ppermute | solution.py:197
  0.0 2.9 %collective-permute-start.1 = (bf16[64,2048]{1,0:T(8,128)(2,1)}, bf16[64,2048]{1,0:T(8,128)(2,1)S(1)}, u32[]{:S(2)}, u32[]{:S(2)}) collective-permute-start(bf16[64,2048]{1,0:T(8,128)(2,1)} %refs_2_.7), channel_id=1, source_target_pairs={{0,4},{4,0},{1,5},{5,1},{2,6},{6,2},{3,7},{7,3},{8,12},{12,8},{9,1... | collective-permute-start | bytes 786440 | tf_op jit(solution)/shard_map/ppermute | solution.py:197
  0.5 2.4 %collective-permute-start = (s32[1,2048]{1,0:T(1,128)}, s32[1,2048]{1,0:T(1,128)S(1)}, u32[]{:S(2)}, u32[]{:S(2)}) collective-permute-start(s32[1,2048]{1,0:T(1,128)} %bitcast.22), channel_id=1, source_target_pairs={{0,4},{4,0},{1,5},{5,1},{2,6},{6,2},{3,7},{7,3},{8,12},{12,8},{9,1... | collective-permute-start | bytes 24584 | tf_op jit(solution)/shard_map/ppermute | solution.py:197
  2.9 11.1 %copy-start.1 = (bf16[2048,192]{0,1:T(8,128)(2,1)S(1)}, bf16[2048,192]{0,1:T(8,128)(2,1)}, u32[]{:S(2)}) copy-start(bf16[2048,192]{0,1:T(8,128)(2,1)} %param.8) | copy-start | bytes 2359300
  2.9 11.1 %copy-start.2 = (bf16[64,2048]{1,0:T(8,128)(2,1)S(1)}, bf16[64,2048]{1,0:T(8,128)(2,1)}, u32[]{:S(2)}) copy-start(bf16[64,2048]{1,0:T(8,128)(2,1)} %refs_2_.7) | copy-start | bytes 786436
  2.9 38.1 %all-to-all-start = ((bf16[16,64,512]{2,1,0:T(8,128)(2,1)}), bf16[16,64,512]{2,1,0:T(8,128)(2,1)S(1)}, u32[]{:S(2)}, u32[]{:S(2)}) async-start(bf16[16,64,512]{2,1,0:T(8,128)(2,1)} %bitcast.27), calls=%async_computation | async-start | bytes 2097152 | tf_op jit(solution)/shard_map/all_to_all | solution.py:202
  13.2 0.8 copy-start.3
  15.8 10.8 %collective-permute-start.5 = (bf16[8,96,128]{2,1,0:T(8,128)(2,1)S(1)}, bf16[8,96,128]{2,1,0:T(8,128)(2,1)S(1)}, u32[]{:S(2)}, u32[]{:S(2)}) collective-permute-start(bf16[8,96,128]{2,1,0:T(8,128)(2,1)S(1)} %shard_map.67), channel_id=1, source_target_pairs={{0,24},{8,0},{16,8},{24,16},{1,25},{9,1},{17,9},{25,17},{2,26},{10... | collective-permute-start | bytes 589832 | tf_op jit(solution)/shard_map/ppermute | solution.py:218
  18.2 10.5 %collective-permute-start.4 = (bf16[8,96,128]{2,1,0:T(8,128)(2,1)S(1)}, bf16[8,96,128]{2,1,0:T(8,128)(2,1)S(1)}, u32[]{:S(2)}, u32[]{:S(2)}) collective-permute-start(bf16[8,96,128]{2,1,0:T(8,128)(2,1)S(1)} %shard_map.66), channel_id=1, source_target_pairs={{0,16},{8,24},{16,0},{24,8},{1,17},{9,25},{17,1},{25,9},{2,18},{10... | collective-permute-start | bytes 589832 | tf_op jit(solution)/shard_map/ppermute | solution.py:218
  22.8 9.1 %collective-permute-start.3 = (bf16[8,96,128]{2,1,0:T(8,128)(2,1)S(1)}, bf16[8,96,128]{2,1,0:T(8,128)(2,1)S(1)}, u32[]{:S(2)}, u32[]{:S(2)}) collective-permute-start(bf16[8,96,128]{2,1,0:T(8,128)(2,1)S(1)} %shard_map.65), channel_id=1, source_target_pairs={{0,8},{8,16},{16,24},{24,0},{1,9},{9,17},{17,25},{25,1},{2,10},{10... | collective-permute-start | bytes 589832 | tf_op jit(solution)/shard_map/ppermute | solution.py:218
  31.8 8.5 %copy-start = (f32[2,8192]{1,0:T(2,128)S(1)}, f32[2,8192]{1,0:T(2,128)}, u32[]{:S(2)}) copy-start(f32[2,8192]{1,0:T(2,128)} %twiddle_ref.1) | copy-start | bytes 196612
  31.9 8.4 %collective-permute-start.6 = (bf16[4,96,128]{2,1,0:T(8,128)(2,1)S(1)}, bf16[4,96,128]{2,1,0:T(8,128)(2,1)S(1)}, u32[]{:S(2)}, u32[]{:S(2)}) collective-permute-start(bf16[4,96,128]{2,1,0:T(8,128)(2,1)S(1)} %get-tuple-element.26), channel_id=1, source_target_pairs={{0,32},{32,0},{1,33},{33,1},{2,34},{34,2},{3,35},{35,3},{4,36},{36... | collective-permute-start | bytes 294920 | tf_op jit(solution)/shard_map/ppermute | solution.py:224
  41.0 11.6 %collective-permute-start.7 = (bf16[416,128]{1,0:T(8,128)(2,1)S(1)}, bf16[416,128]{1,0:T(8,128)(2,1)S(1)}, u32[]{:S(2)}, u32[]{:S(2)}) collective-permute-start(bf16[416,128]{1,0:T(8,128)(2,1)S(1)} %get-tuple-element.34), channel_id=1, source_target_pairs={{0,64},{64,0},{128,192},{192,128},{1,65},{65,1},{129,193},{193,129... | collective-permute-start | bytes 319496 | tf_op jit(solution)/shard_map/ppermute | solution.py:180
  43.2 12.2 %collective-permute-start.8 = (bf16[416,128]{1,0:T(8,128)(2,1)S(1)}, bf16[416,128]{1,0:T(8,128)(2,1)S(1)}, u32[]{:S(2)}, u32[]{:S(2)}) collective-permute-start(bf16[416,128]{1,0:T(8,128)(2,1)S(1)} %get-tuple-element.35), channel_id=1, source_target_pairs={{0,128},{64,192},{128,0},{192,64},{1,129},{65,193},{129,1},{193,65... | collective-permute-start | bytes 319496 | tf_op jit(solution)/shard_map/ppermute | solution.py:180
  44.6 12.5 %collective-permute-start.9 = (bf16[416,128]{1,0:T(8,128)(2,1)S(1)}, bf16[416,128]{1,0:T(8,128)(2,1)S(1)}, u32[]{:S(2)}, u32[]{:S(2)}) collective-permute-start(bf16[416,128]{1,0:T(8,128)(2,1)S(1)} %get-tuple-element.36), channel_id=1, source_target_pairs={{0,192},{64,128},{128,64},{192,0},{1,193},{65,129},{129,65},{193,1... | collective-permute-start | bytes 319496 | tf_op jit(solution)/shard_map/ppermute | solution.py:180
  57.7 8.0 %collective-permute-start.10 = (bf16[4,96,128]{2,1,0:T(8,128)(2,1)S(1)}, bf16[4,96,128]{2,1,0:T(8,128)(2,1)S(1)}, u32[]{:S(2)}, u32[]{:S(2)}) collective-permute-start(bf16[4,96,128]{2,1,0:T(8,128)(2,1)S(1)} %get-tuple-element.38.refs_3_), channel_id=1, source_target_pairs={{0,1},{1,2},{2,3},{3,0},{4,5},{5,6},{6,7},{7,4},{8,9},{9,10},{10,1... | collective-permute-start | bytes 294920 | tf_op jit(solution)/shard_map/ppermute | solution.py:180
  59.4 6.3 %collective-permute-start.11 = (bf16[4,96,128]{2,1,0:T(8,128)(2,1)S(1)}, bf16[4,96,128]{2,1,0:T(8,128)(2,1)S(1)}, u32[]{:S(2)}, u32[]{:S(2)}) collective-permute-start(bf16[4,96,128]{2,1,0:T(8,128)(2,1)S(1)} %get-tuple-element.38.refs_3_), channel_id=1, source_target_pairs={{0,2},{1,3},{2,0},{3,1},{4,6},{5,7},{6,4},{7,5},{8,10},{9,11},{10,... | collective-permute-start | bytes 294920 | tf_op jit(solution)/shard_map/ppermute | solution.py:180
  60.4 5.5 %collective-permute-start.12 = (bf16[4,96,128]{2,1,0:T(8,128)(2,1)S(1)}, bf16[4,96,128]{2,1,0:T(8,128)(2,1)S(1)}, u32[]{:S(2)}, u32[]{:S(2)}) collective-permute-start(bf16[4,96,128]{2,1,0:T(8,128)(2,1)S(1)} %get-tuple-element.38.refs_3_), channel_id=1, source_target_pairs={{0,3},{1,0},{2,1},{3,2},{4,7},{5,4},{6,5},{7,6},{8,11},{9,8},{10,9... | collective-permute-start | bytes 294920 | tf_op jit(solution)/shard_map/ppermute | solution.py:180

commit v13 on v12

--- a/solution.py
+++ b/solution.py
@@ -125,17 +125,18 @@
         extra = offers[block - 1][blocks * packed:, :] if block else extra_ref[...]
         rows_ref[block] = extra
         rank = extra.astype(jnp.float32)[6:7]
-        out_ref[block] = jnp.where(sample < rank, total, 0.0).astype(jnp.bfloat16)
-
-
-def field_kernel(blocks, parts, place_ref, samples_ref, rows_ref, *refs):
-    weight_refs = refs[:-3]
-    out_ref, field, every = refs[-3:]
-    zg, smp = place_ref[0], place_ref[1]
+        weights = jnp.where(sample < rank, total, 0.0).astype(jnp.bfloat16)
+        for part in range(out_ref.shape[0]):
+            out_ref[part, block] = weights
+
+
+def field_kernel(blocks, parts, place_ref, samples_ref, rows_ref, weights_ref, *refs):
+    out_ref, field, every = refs
+    zg = place_ref[0]
     vectors, points = field.shape[1:]
     samples = samples_ref.shape[1]
     for p in range(parts):
-        every[place_of(lax.rem(smp - p + parts, parts), parts, place_ref[3])] = weight_refs[p][...]
+        every[place_of(p, parts, place_ref[3])] = weights_ref[p]
     factors = []
     for c in range(blocks):
         head, tail, columns = [], [], []
@@ -241,7 +242,7 @@
     )
     *offers, pieces = lax.optimization_barrier((*offers, pieces))
     offers = exchange(dict(enumerate(offers, 1)), "zg", lambda i, k: i ^ k)
-    shapes = [jax.ShapeDtypeStruct(shape, jnp.bfloat16)]
+    shapes = [jax.ShapeDtypeStruct((parts,) + shape, jnp.bfloat16)]
     shapes += [jax.ShapeDtypeStruct((groups,) + extra.shape, jnp.bfloat16)]
     weights, factors = local_call(
         weights_kernel,
@@ -252,7 +253,7 @@
         *offers,
         smem=1,
     )
-    others = exchange({p: weights for p in range(1, parts)}, "smp", lambda i, k: i + k)
+    weights = lax.all_to_all(weights, "smp", 0, 0, tiled=True)
     result = local_call(
         lambda *refs: field_kernel(groups, parts, *refs),
         jax.ShapeDtypeStruct((members, vectors // parts, piece), jnp.bfloat16),
@@ -260,7 +261,6 @@
         pieces,
         factors,
         weights,
-        *others,
         smem=1,
         scratch=[
             pltpu.VMEM((groups, vectors, piece), jnp.float32),

time: 98 us -> 99.5 us (1.015)
  blocking collectives: 28.3 us -> 37.5 us
  starting transfers between devices: 28.8 us -> 23.6 us
  waiting for transfers between devices: 25.1 us -> 22.1 us
    all_to_all x0 -> x1, blocking collectives: none -> 11.8 us  [body(): weights = lax.all_to_all(weights, 'smp', 0, 0, tiled=True)]
    ppermute x6 -> x3, starting transfers between devices: 11.8 us -> 6.58 us  [exchange(): came[offset] = lax.ppermute(pieces[offset], axis, pairs)]
    ppermute x6 -> x3, waiting for transfers between devices: 12.5 us -> 9.53 us  [exchange(): came[offset] = lax.ppermute(pieces[offset], axis, pairs)]
    all_to_all x1, blocking collectives: 28.3 us -> 25.7 us  [body(): lax.all_to_all(result, axes, 0, 0, tiled=True, axis_index_groups=lists)]
  transfers between devices with their start and end apart: 14 -> 11, of which waited for: 8 -> 6; matrix products, arithmetic and copies ran while one was open for 3% -> 3% of each run, Pallas kernels for 8% -> 8%
where the time goes in v13:
time: 99.5 us; the launch traced here: 97.6 us
  blocking collectives  37.5 us (38%)
  starting transfers between devices  23.6 us (24%)
  waiting for transfers between devices  22.1 us (22%)
  Pallas kernels  10.2 us (10%)
  local copies, waits for them, and re-layouts  3.29 us (3%)
    all_to_all x1, blocking collectives, body(): lax.all_to_all(result, axes, 0, 0, tiled=True, axis_index_groups=lists)  25.7 us
    all_to_all x1, blocking collectives, body(): weights = lax.all_to_all(weights, 'smp', 0, 0, tiled=True)  11.8 us
    all_to_all x1, starting transfers between devices, body(): lax.all_to_all(pieces, axes, 0, 0, tiled=True, axis_index_groups=lists)  10.3 us
    pallas_call x8, Pallas kernels, local_call(): pl.pallas_call(kernel, out_shape=out_shape, in_specs=[SMEM] * smem + [VME...  10.2 us
    ppermute x3, waiting for transfers between devices, exchange(): came[offset] = lax.ppermute(pieces[offset], axis, pairs)  9.53 us
    ppermute x1, waiting for transfers between devices, body(): came = lax.ppermute(sent, 'zl', [(0, 1), (1, 0)])  7.28 us
    ppermute x3, starting transfers between devices, exchange(): came[offset] = lax.ppermute(pieces[offset], axis, pairs)  6.58 us
    ppermute x3, waiting for transfers between devices, body(): sums[offset] = lax.ppermute(value, 'y', route) if offset else value  5.24 us
  transfers between devices with their start and end apart: 11, of which 6 were waited for; matrix products, arithmetic and copies ran while one was open for 3% of the time, Pallas kernels for 8%

profile of v13, /device:TPU:40, one launch (start us, length us, event | category | flops | bytes accessed | tf_op | source)
XLA Modules:
  0.0 97.6 jit_solution(9338896656597786746)
XLA Ops:
  0.0 0.0 collective-permute-start.2
  0.0 0.5 collective-permute-start.1
  0.5 0.0 collective-permute-start
  0.5 2.3 %copy.12 = bf16[8,16,8,512]{3,2,0,1:T(8,128)(2,1)} copy(bf16[8,16,8,512]{3,2,1,0:T(8,128)(2,1)} %bitcast.29) | data formatting | bytes 2097152 | tf_op jit(solution)/shard_map/reshape | solution.py:195
  2.8 0.0 collective-permute-done.refs_4_
  2.9 0.0 collective-permute-done.1.refs_5_
  2.9 0.0 collective-permute-done.2.refs_6_
  2.9 0.0 copy-start.1
  2.9 0.0 copy-start.2
  2.9 10.3 %all-to-all-start = ((bf16[16,64,512]{2,1,0:T(8,128)(2,1)}), bf16[16,64,512]{2,1,0:T(8,128)(2,1)S(1)}, u32[]{:S(2)}, u32[]{:S(2)}) async-start(bf16[16,64,512]{2,1,0:T(8,128)(2,1)} %bitcast.27), calls=%async_computation | async-start | bytes 2097152 | tf_op jit(solution)/shard_map/all_to_all | solution.py:203
  13.2 0.0 copy-start.3
  13.9 0.1 pad_add_fusion.1.refs_0_
  13.9 0.0 copy-done.1
  13.9 0.0 copy-done.2
  14.0 0.0 copy-done.3
  14.0 1.9 %shard_map.67 = bf16[8,96,128]{2,1,0:T(8,128)(2,1)S(1)} custom-call(s32[2]{0:T(128)S(1)} %pad_add_fusion.1.refs_0_, s32[1,2048]{1,0:T(1,128)S(1)} %bitcast.23, bf16[64,2048]{1,0:T(8,128)(2,1)S(1)} %copy-done.2, bf16[192,2048]{1,0:T(8,128)(2,1)S(1)} %bitcast.18, s32[1,2048]{1,0:T(1,128)S(1)} %collective-permute-done.refs_4_, ...), custom_call_target="tpu_custom_call" | custom-call | flops 4294967296 | bytes 2097152 | tf_op jit(solution)/shard_map/pallas_call | solution.py:45
  15.8 0.5 collective-permute-start.5
  16.4 1.9 %shard_map.66 = bf16[8,96,128]{2,1,0:T(8,128)(2,1)S(1)} custom-call(s32[2]{0:T(128)S(1)} %pad_add_fusion.1.refs_0_, s32[1,2048]{1,0:T(1,128)S(1)} %bitcast.24, bf16[64,2048]{1,0:T(8,128)(2,1)S(1)} %copy-done.2, bf16[192,2048]{1,0:T(8,128)(2,1)S(1)} %bitcast.19, s32[1,2048]{1,0:T(1,128)S(1)} %collective-permute-done.refs_4_, ...), custom_call_target="tpu_custom_call" | custom-call | flops 4294967296 | bytes 2097152 | tf_op jit(solution)/shard_map/pallas_call | solution.py:45
  18.2 2.7 %collective-permute-start.4 = (bf16[8,96,128]{2,1,0:T(8,128)(2,1)S(1)}, bf16[8,96,128]{2,1,0:T(8,128)(2,1)S(1)}, u32[]{:S(2)}, u32[]{:S(2)}) collective-permute-start(bf16[8,96,128]{2,1,0:T(8,128)(2,1)S(1)} %shard_map.66), channel_id=1, source_target_pairs={{0,16},{8,24},{16,0},{24,8},{1,17},{9,25},{17,1},{25,9},{2,18},{10... | collective-permute-start | bytes 589832 | tf_op jit(solution)/shard_map/ppermute | solution.py:219
  20.9 1.9 %shard_map.65 = bf16[8,96,128]{2,1,0:T(8,128)(2,1)S(1)} custom-call(s32[2]{0:T(128)S(1)} %pad_add_fusion.1.refs_0_, s32[1,2048]{1,0:T(1,128)S(1)} %bitcast.25, bf16[64,2048]{1,0:T(8,128)(2,1)S(1)} %copy-done.2, bf16[192,2048]{1,0:T(8,128)(2,1)S(1)} %bitcast.20, s32[1,2048]{1,0:T(1,128)S(1)} %collective-permute-done.refs_4_, ...), custom_call_target="tpu_custom_call" | custom-call | flops 4294967296 | bytes 2097152 | tf_op jit(solution)/shard_map/pallas_call | solution.py:45
  22.8 2.0 %collective-permute-start.3 = (bf16[8,96,128]{2,1,0:T(8,128)(2,1)S(1)}, bf16[8,96,128]{2,1,0:T(8,128)(2,1)S(1)}, u32[]{:S(2)}, u32[]{:S(2)}) collective-permute-start(bf16[8,96,128]{2,1,0:T(8,128)(2,1)S(1)} %shard_map.65), channel_id=1, source_target_pairs={{0,8},{8,16},{16,24},{24,0},{1,9},{9,17},{17,25},{25,1},{2,10},{10... | collective-permute-start | bytes 589832 | tf_op jit(solution)/shard_map/ppermute | solution.py:219
  24.7 1.9 %shard_map.64.refs_0_ = f32[8,96,128]{2,1,0:T(8,128)S(1)} custom-call(s32[2]{0:T(128)S(1)} %pad_add_fusion.1.refs_0_, s32[1,2048]{1,0:T(1,128)S(1)} %bitcast.26, bf16[64,2048]{1,0:T(8,128)(2,1)S(1)} %copy-done.2, bf16[192,2048]{1,0:T(8,128)(2,1)S(1)} %bitcast.21, s32[1,2048]{1,0:T(1,128)S(1)} %collective-permute-done.refs_4_, ...), custom_call_target="tpu_custom_call" | custom-call | flops 4294967296 | bytes 2097152 | tf_op jit(solution)/shard_map/pallas_call | solution.py:45
  26.6 0.0 collective-permute-done.5.refs_3_
  26.6 2.1 %collective-permute-done.4.refs_2_ = bf16[8,96,128]{2,1,0:T(8,128)(2,1)S(1)} collective-permute-done((bf16[8,96,128]{2,1,0:T(8,128)(2,1)S(1)}, bf16[8,96,128]{2,1,0:T(8,128)(2,1)S(1)}, u32[]{:S(2)}, u32[]{:S(2)}) %collective-permute-start.4) | collective-permute-done | bytes 196640 | tf_op jit(solution)/shard_map/ppermute | solution.py:219
  28.7 3.1 %collective-permute-done.3.refs_1_ = bf16[8,96,128]{2,1,0:T(8,128)(2,1)S(1)} collective-permute-done((bf16[8,96,128]{2,1,0:T(8,128)(2,1)S(1)}, bf16[8,96,128]{2,1,0:T(8,128)(2,1)S(1)}, u32[]{:S(2)}, u32[]{:S(2)}) %collective-permute-start.3) | collective-permute-done | bytes 196640 | tf_op jit(solution)/shard_map/ppermute | solution.py:219
  31.8 0.0 copy-start
  31.8 0.1 shard_map.68
  31.9 1.1 %collective-permute-start.6 = (bf16[4,96,128]{2,1,0:T(8,128)(2,1)S(1)}, bf16[4,96,128]{2,1,0:T(8,128)(2,1)S(1)}, u32[]{:S(2)}, u32[]{:S(2)}) collective-permute-start(bf16[4,96,128]{2,1,0:T(8,128)(2,1)S(1)} %get-tuple-element.26), channel_id=1, source_target_pairs={{0,32},{32,0},{1,33},{33,1},{2,34},{34,2},{3,35},{35,3},{4,36},{36... | collective-permute-start | bytes 294920 | tf_op jit(solution)/shard_map/ppermute | solution.py:225
  33.0 0.1 pad_add_fusion.place_ref.refs_0_
  33.1 7.3 %collective-permute-done.6.came_ref = bf16[4,96,128]{2,1,0:T(8,128)(2,1)S(1)} collective-permute-done((bf16[4,96,128]{2,1,0:T(8,128)(2,1)S(1)}, bf16[4,96,128]{2,1,0:T(8,128)(2,1)S(1)}, u32[]{:S(2)}, u32[]{:S(2)}) %collective-permute-start.6) | collective-permute-done | bytes 98336 | tf_op jit(solution)/shard_map/ppermute | solution.py:225
  40.4 0.0 copy-done
  40.4 0.6 shard_map.69
  41.0 0.0 all-to-all-done.refs_1_
  41.0 2.2 %collective-permute-start.7 = (bf16[416,128]{1,0:T(8,128)(2,1)S(1)}, bf16[416,128]{1,0:T(8,128)(2,1)S(1)}, u32[]{:S(2)}, u32[]{:S(2)}) collective-permute-start(bf16[416,128]{1,0:T(8,128)(2,1)S(1)} %get-tuple-element.34), channel_id=1, source_target_pairs={{0,64},{64,0},{128,192},{192,128},{1,65},{65,1},{129,193},{193,129... | collective-permute-start | bytes 319496 | tf_op jit(solution)/shard_map/ppermute | solution.py:181
  43.2 1.4 %collective-permute-start.8 = (bf16[416,128]{1,0:T(8,128)(2,1)S(1)}, bf16[416,128]{1,0:T(8,128)(2,1)S(1)}, u32[]{:S(2)}, u32[]{:S(2)}) collective-permute-start(bf16[416,128]{1,0:T(8,128)(2,1)S(1)} %get-tuple-element.35), channel_id=1, source_target_pairs={{0,128},{64,192},{128,0},{192,64},{1,129},{65,193},{129,1},{193,65... | collective-permute-start | bytes 319496 | tf_op jit(solution)/shard_map/ppermute | solution.py:181
  44.6 3.0 %collective-permute-start.9 = (bf16[416,128]{1,0:T(8,128)(2,1)S(1)}, bf16[416,128]{1,0:T(8,128)(2,1)S(1)}, u32[]{:S(2)}, u32[]{:S(2)}) collective-permute-start(bf16[416,128]{1,0:T(8,128)(2,1)S(1)} %get-tuple-element.36), channel_id=1, source_target_pairs={{0,192},{64,128},{128,64},{192,0},{1,193},{65,129},{129,65},{193,1... | collective-permute-start | bytes 319496 | tf_op jit(solution)/shard_map/ppermute | solution.py:181
  47.6 5.0 %collective-permute-done.7.refs_0_ = bf16[416,128]{1,0:T(8,128)(2,1)S(1)} collective-permute-done((bf16[416,128]{1,0:T(8,128)(2,1)S(1)}, bf16[416,128]{1,0:T(8,128)(2,1)S(1)}, u32[]{:S(2)}, u32[]{:S(2)}) %collective-permute-start.7) | collective-permute-done | bytes 106528 | tf_op jit(solution)/shard_map/ppermute | solution.py:181
  52.6 2.8 %collective-permute-done.8.refs_1_ = bf16[416,128]{1,0:T(8,128)(2,1)S(1)} collective-permute-done((bf16[416,128]{1,0:T(8,128)(2,1)S(1)}, bf16[416,128]{1,0:T(8,128)(2,1)S(1)}, u32[]{:S(2)}, u32[]{:S(2)}) %collective-permute-start.8) | collective-permute-done | bytes 106528 | tf_op jit(solution)/shard_map/ppermute | solution.py:181
  55.4 1.7 %collective-permute-done.9.refs_2_ = bf16[416,128]{1,0:T(8,128)(2,1)S(1)} collective-permute-done((bf16[416,128]{1,0:T(8,128)(2,1)S(1)}, bf16[416,128]{1,0:T(8,128)(2,1)S(1)}, u32[]{:S(2)}, u32[]{:S(2)}) %collective-permute-start.9) | collective-permute-done | bytes 106528 | tf_op jit(solution)/shard_map/ppermute | solution.py:181
  57.1 0.6 shard_map.70
  57.7 11.8 %all_to_all.15.refs_3_ = bf16[4,4,96,128]{3,2,1,0:T(8,128)(2,1)S(1)} all-to-all(bf16[4,4,96,128]{3,2,1,0:T(8,128)(2,1)S(1)} %get-tuple-element.38), channel_id=1, replica_groups=mesh['zg'=4,'zl'=2,'y'=4,'core'=2,'smp'=4] {'smp'}, dimensions={0} | all-to-all | bytes 786432 | tf_op jit(solution)/shard_map/all_to_all | solution.py:256
  69.5 1.4 %shard_map.71 = bf16[16,48,512]{2,1,0:T(8,128)(2,1)S(1)} custom-call(s32[4]{0:T(128)S(1)} %pad_add_fusion.place_ref.refs_0_, bf16[16,64,512]{2,1,0:T(8,128)(2,1)S(1)} %all-to-all-done.refs_1_, bf16[4,32,128]{2,1,0:T(8,128)(2,1)S(1)} %get-tuple-element.37.refs_2_, bf16[4,4,96,128]{3,2,1,0:T(8,128)(2,1)S(1)} %all_to_all.15.refs_3_), custom_call_target="tpu_custom_call" | custom-call | flops 201326592 | bytes 2097152 | tf_op jit(solution)/shard_map/pallas_call | solution.py:45
  70.9 25.7 %all_to_all.16 = bf16[16,48,512]{2,1,0:T(8,128)(2,1)S(1)} all-to-all(bf16[16,48,512]{2,1,0:T(8,128)(2,1)S(1)} %shard_map.71), channel_id=1, replica_groups={{0,1,2,3,64,65,66,67,128,129,130,131,192,193,194,195},{199,198,197,196,..., dimensions={0} | all-to-all | bytes 1572864 | tf_op jit(solution)/shard_map/all_to_all | solution.py:271
  96.6 1.0 copy.10
Async XLA Ops:
  0.0 2.9 %collective-permute-start.2 = (bf16[192,2048]{1,0:T(8,128)(2,1)}, bf16[192,2048]{1,0:T(8,128)(2,1)S(1)}, u32[]{:S(2)}, u32[]{:S(2)}) collective-permute-start(bf16[192,2048]{1,0:T(8,128)(2,1)} %bitcast.17), channel_id=1, source_target_pairs={{0,4},{4,0},{1,5},{5,1},{2,6},{6,2},{3,7},{7,3},{8,12},{12,8},{9,1... | collective-permute-start | bytes 2359304 | tf_op jit(solution)/shard_map/ppermute | solution.py:198
  0.0 2.9 %collective-permute-start.1 = (bf16[64,2048]{1,0:T(8,128)(2,1)}, bf16[64,2048]{1,0:T(8,128)(2,1)S(1)}, u32[]{:S(2)}, u32[]{:S(2)}) collective-permute-start(bf16[64,2048]{1,0:T(8,128)(2,1)} %refs_2_.7), channel_id=1, source_target_pairs={{0,4},{4,0},{1,5},{5,1},{2,6},{6,2},{3,7},{7,3},{8,12},{12,8},{9,1... | collective-permute-start | bytes 786440 | tf_op jit(solution)/shard_map/ppermute | solution.py:198
  0.5 2.4 %collective-permute-start = (s32[1,2048]{1,0:T(1,128)}, s32[1,2048]{1,0:T(1,128)S(1)}, u32[]{:S(2)}, u32[]{:S(2)}) collective-permute-start(s32[1,2048]{1,0:T(1,128)} %bitcast.22), channel_id=1, source_target_pairs={{0,4},{4,0},{1,5},{5,1},{2,6},{6,2},{3,7},{7,3},{8,12},{12,8},{9,1... | collective-permute-start | bytes 24584 | tf_op jit(solution)/shard_map/ppermute | solution.py:198
  2.9 11.1 %copy-start.1 = (bf16[2048,192]{0,1:T(8,128)(2,1)S(1)}, bf16[2048,192]{0,1:T(8,128)(2,1)}, u32[]{:S(2)}) copy-start(bf16[2048,192]{0,1:T(8,128)(2,1)} %param.8) | copy-start | bytes 2359300
  2.9 11.1 %copy-start.2 = (bf16[64,2048]{1,0:T(8,128)(2,1)S(1)}, bf16[64,2048]{1,0:T(8,128)(2,1)}, u32[]{:S(2)}) copy-start(bf16[64,2048]{1,0:T(8,128)(2,1)} %refs_2_.7) | copy-start | bytes 786436
  2.9 38.1 %all-to-all-start = ((bf16[16,64,512]{2,1,0:T(8,128)(2,1)}), bf16[16,64,512]{2,1,0:T(8,128)(2,1)S(1)}, u32[]{:S(2)}, u32[]{:S(2)}) async-start(bf16[16,64,512]{2,1,0:T(8,128)(2,1)} %bitcast.27), calls=%async_computation | async-start | bytes 2097152 | tf_op jit(solution)/shard_map/all_to_all | solution.py:203
  13.2 0.8 copy-start.3
  15.8 10.8 %collective-permute-start.5 = (bf16[8,96,128]{2,1,0:T(8,128)(2,1)S(1)}, bf16[8,96,128]{2,1,0:T(8,128)(2,1)S(1)}, u32[]{:S(2)}, u32[]{:S(2)}) collective-permute-start(bf16[8,96,128]{2,1,0:T(8,128)(2,1)S(1)} %shard_map.67), channel_id=1, source_target_pairs={{0,24},{8,0},{16,8},{24,16},{1,25},{9,1},{17,9},{25,17},{2,26},{10... | collective-permute-start | bytes 589832 | tf_op jit(solution)/shard_map/ppermute | solution.py:219
  18.2 10.5 %collective-permute-start.4 = (bf16[8,96,128]{2,1,0:T(8,128)(2,1)S(1)}, bf16[8,96,128]{2,1,0:T(8,128)(2,1)S(1)}, u32[]{:S(2)}, u32[]{:S(2)}) collective-permute-start(bf16[8,96,128]{2,1,0:T(8,128)(2,1)S(1)} %shard_map.66), channel_id=1, source_target_pairs={{0,16},{8,24},{16,0},{24,8},{1,17},{9,25},{17,1},{25,9},{2,18},{10... | collective-permute-start | bytes 589832 | tf_op jit(solution)/shard_map/ppermute | solution.py:219
  22.8 9.1 %collective-permute-start.3 = (bf16[8,96,128]{2,1,0:T(8,128)(2,1)S(1)}, bf16[8,96,128]{2,1,0:T(8,128)(2,1)S(1)}, u32[]{:S(2)}, u32[]{:S(2)}) collective-permute-start(bf16[8,96,128]{2,1,0:T(8,128)(2,1)S(1)} %shard_map.65), channel_id=1, source_target_pairs={{0,8},{8,16},{16,24},{24,0},{1,9},{9,17},{17,25},{25,1},{2,10},{10... | collective-permute-start | bytes 589832 | tf_op jit(solution)/shard_map/ppermute | solution.py:219
  31.8 8.6 %copy-start = (f32[2,8192]{1,0:T(2,128)S(1)}, f32[2,8192]{1,0:T(2,128)}, u32[]{:S(2)}) copy-start(f32[2,8192]{1,0:T(2,128)} %twiddle_ref.1) | copy-start | bytes 196612
  31.9 8.4 %collective-permute-start.6 = (bf16[4,96,128]{2,1,0:T(8,128)(2,1)S(1)}, bf16[4,96,128]{2,1,0:T(8,128)(2,1)S(1)}, u32[]{:S(2)}, u32[]{:S(2)}) collective-permute-start(bf16[4,96,128]{2,1,0:T(8,128)(2,1)S(1)} %get-tuple-element.26), channel_id=1, source_target_pairs={{0,32},{32,0},{1,33},{33,1},{2,34},{34,2},{3,35},{35,3},{4,36},{36... | collective-permute-start | bytes 294920 | tf_op jit(solution)/shard_map/ppermute | solution.py:225
  41.0 11.6 %collective-permute-start.7 = (bf16[416,128]{1,0:T(8,128)(2,1)S(1)}, bf16[416,128]{1,0:T(8,128)(2,1)S(1)}, u32[]{:S(2)}, u32[]{:S(2)}) collective-permute-start(bf16[416,128]{1,0:T(8,128)(2,1)S(1)} %get-tuple-element.34), channel_id=1, source_target_pairs={{0,64},{64,0},{128,192},{192,128},{1,65},{65,1},{129,193},{193,129... | collective-permute-start | bytes 319496 | tf_op jit(solution)/shard_map/ppermute | solution.py:181
  43.2 12.2 %collective-permute-start.8 = (bf16[416,128]{1,0:T(8,128)(2,1)S(1)}, bf16[416,128]{1,0:T(8,128)(2,1)S(1)}, u32[]{:S(2)}, u32[]{:S(2)}) collective-permute-start(bf16[416,128]{1,0:T(8,128)(2,1)S(1)} %get-tuple-element.35), channel_id=1, source_target_pairs={{0,128},{64,192},{128,0},{192,64},{1,129},{65,193},{129,1},{193,65... | collective-permute-start | bytes 319496 | tf_op jit(solution)/shard_map/ppermute | solution.py:181
  44.6 12.5 %collective-permute-start.9 = (bf16[416,128]{1,0:T(8,128)(2,1)S(1)}, bf16[416,128]{1,0:T(8,128)(2,1)S(1)}, u32[]{:S(2)}, u32[]{:S(2)}) collective-permute-start(bf16[416,128]{1,0:T(8,128)(2,1)S(1)} %get-tuple-element.36), channel_id=1, source_target_pairs={{0,192},{64,128},{128,64},{192,0},{1,193},{65,129},{129,65},{193,1... | collective-permute-start | bytes 319496 | tf_op jit(solution)/shard_map/ppermute | solution.py:181

commit v14 on v7

--- a/solution.py
+++ b/solution.py
@@ -72,7 +72,7 @@
         in_specs=[SMEM] * smem + [VMEM] * (len(args) - smem),
         out_specs=jax.tree.map(lambda _: VMEM, out_shape),
         scratch_shapes=list(scratch),
-        compiler_params=pltpu.CompilerParams(vmem_limit_bytes=24 * MIB),
+        compiler_params=pltpu.CompilerParams(vmem_limit_bytes=12 * MIB),
         cost_estimate=pl.CostEstimate(flops=flops, bytes_accessed=2 * MIB, transcendentals=0),
     )(*args)
 
@@ -221,7 +221,7 @@
             *came,
             smem=1,
             scratch=[pltpu.VMEM((shape[0] * samples, own.shape[1]), jnp.bfloat16)],
-            flops=2 * shape[0] * samples * own.shape[1] * 256,
+            flops=4 * shape[0] * samples * own.shape[1] * 256,
         )
 
     order = sorted(range(y_count), key=lambda k: (k == 0, abs(k - y_count // 2)))

time: 95.8 us -> 95.8 us (level)
  local copies, waits for them, and re-layouts: 1.86 us -> 2.84 us
    ppermute x3, waiting for transfers between devices: 4.99 us -> 4.01 us  [body(): sums.append(lax.ppermute(merged, 'y', route) if offset else merged)]
    unnamed x8 -> x10, local copies, waits for them, and re-layouts: 0.89 us -> 1.87 us
  transfers between devices with their start and end apart: 15 -> 15, of which waited for: 8 -> 7; matrix products, arithmetic and copies ran while one was open for 0% -> 0% of each run, Pallas kernels for 14% -> 14%
where the time goes in v14:
time: 95.8 us; the launch traced here: 94.4 us
  starting transfers between devices  29.5 us (31%)
  blocking collectives  24.1 us (25%)
  waiting for transfers between devices  19.5 us (20%)
  Pallas kernels  17.3 us (18%)
  local copies, waits for them, and re-layouts  2.84 us (3%)
    all_to_all x1, blocking collectives, body(): result = lax.all_to_all(result, GROUP, 0, 0, tiled=True)  24.1 us
    pallas_call x12, Pallas kernels, local_call(): pl.pallas_call(kernel, out_shape=out_shape, in_specs=[SMEM] * smem + [VME...  14.9 us
    ppermute x6, starting transfers between devices, exchange(): came[offset] = lax.ppermute(pieces[offset], axis, pairs)  12.5 us
    ppermute x6, waiting for transfers between devices, exchange(): came[offset] = lax.ppermute(pieces[offset], axis, pairs)  11.9 us
    all_to_all x1, starting transfers between devices, body(): pieces = lax.all_to_all(pieces, GROUP, 0, 0, tiled=True)  10.3 us
    ppermute x3, starting transfers between devices, body(): sums.append(lax.ppermute(merged, 'y', route) if offset else merged)  4.32 us
    ppermute x3, waiting for transfers between devices, body(): sums.append(lax.ppermute(merged, 'y', route) if offset else merged)  4.01 us
    ppermute x1, waiting for transfers between devices, body(): came = lax.ppermute(sent, 'zl', [(0, 1), (1, 0)])  3.54 us
  transfers between devices with their start and end apart: 15, of which 7 were waited for; matrix products, arithmetic and copies ran while one was open for 0% of the time, Pallas kernels for 14%

profile of v14, /device:TPU:40, one launch (start us, length us, event | category | flops | bytes accessed | tf_op | source)
XLA Modules:
  0.0 94.4 jit_solution(14409872747777190646)
XLA Ops:
  0.0 2.4 %shard_map.64 = bf16[16,64,512]{2,1,0:T(8,128)(2,1)} custom-call(bf16[64,8192]{1,0:T(8,128)(2,1)} %source_ref.1), custom_call_target="tpu_custom_call" | custom-call | bytes 2097152 | tf_op jit(solution)/shard_map/pallas_call | solution.py:30
  2.4 0.0 copy-start.4
  2.4 10.3 %all-to-all-start = ((bf16[16,64,512]{2,1,0:T(8,128)(2,1)}), bf16[16,64,512]{2,1,0:T(8,128)(2,1)S(1)}, u32[]{:S(2)}, u32[]{:S(2)}) async-start(bf16[16,64,512]{2,1,0:T(8,128)(2,1)} %shard_map.64), calls=%async_computation | async-start | bytes 2097152 | tf_op jit(solution)/shard_map/all_to_all | solution.py:207
  12.7 0.1 pad_add_fusion.1.refs_0_
  12.8 0.1 pad_maximum_fusion.refs_3_
  12.9 0.9 copy-done.1
  13.8 1.3 %shard_map.69 = f32[8,96,128]{2,1,0:T(8,128)S(1)} custom-call(s32[2]{0:T(128)S(1)} %pad_add_fusion.1.refs_0_, s32[1,2048]{1,0:T(1,128)S(1)} %bitcast.10, bf16[64,2048]{1,0:T(8,128)(2,1)S(1)} %copy-done.1, bf16[256,2048]{1,0:T(8,128)(2,1)S(1)} %pad_maximum_fusion.refs_3_), custom_call_target="tpu_custom_call" | custom-call | flops 1073741824 | bytes 2097152 | tf_op jit(solution)/shard_map/pallas_call | solution.py:69
  15.0 0.1 collective-permute-start.3
  15.1 1.3 %shard_map.71 = f32[8,96,128]{2,1,0:T(8,128)S(1)} custom-call(s32[2]{0:T(128)S(1)} %pad_add_fusion.1.refs_0_, s32[1,2048]{1,0:T(1,128)S(1)} %bitcast.11, bf16[64,2048]{1,0:T(8,128)(2,1)S(1)} %copy-done.1, bf16[256,2048]{1,0:T(8,128)(2,1)S(1)} %pad_maximum_fusion.refs_3_), custom_call_target="tpu_custom_call" | custom-call | flops 1073741824 | bytes 2097152 | tf_op jit(solution)/shard_map/pallas_call | solution.py:69
  16.4 0.6 collective-permute-start.5
  17.0 1.3 %shard_map.67 = f32[8,96,128]{2,1,0:T(8,128)S(1)} custom-call(s32[2]{0:T(128)S(1)} %pad_add_fusion.1.refs_0_, s32[1,2048]{1,0:T(1,128)S(1)} %bitcast.12, bf16[64,2048]{1,0:T(8,128)(2,1)S(1)} %copy-done.1, bf16[256,2048]{1,0:T(8,128)(2,1)S(1)} %pad_maximum_fusion.refs_3_), custom_call_target="tpu_custom_call" | custom-call | flops 1073741824 | bytes 2097152 | tf_op jit(solution)/shard_map/pallas_call | solution.py:69
  18.3 0.1 collective-permute-start.1
  18.4 1.3 %shard_map.65 = f32[8,96,128]{2,1,0:T(8,128)S(1)} custom-call(s32[2]{0:T(128)S(1)} %pad_add_fusion.1.refs_0_, s32[1,2048]{1,0:T(1,128)S(1)} %bitcast.13, bf16[64,2048]{1,0:T(8,128)(2,1)S(1)} %copy-done.1, bf16[256,2048]{1,0:T(8,128)(2,1)S(1)} %pad_maximum_fusion.refs_3_), custom_call_target="tpu_custom_call" | custom-call | flops 1073741824 | bytes 2097152 | tf_op jit(solution)/shard_map/pallas_call | solution.py:69
  19.7 0.6 collective-permute-start
  20.3 0.0 collective-permute-done.3.refs_4_
  20.3 2.0 %shard_map.70 = bf16[8,96,128]{2,1,0:T(8,128)(2,1)} custom-call(s32[2]{0:T(128)S(1)} %pad_add_fusion.1.refs_0_, s32[1,2048]{1,0:T(1,128)S(1)} %bitcast.14, bf16[64,2048]{1,0:T(8,128)(2,1)S(1)} %copy-done.1, bf16[256,2048]{1,0:T(8,128)(2,1)S(1)} %pad_maximum_fusion.refs_3_, f32[8,96,128]{2,1,0:T(8,128)S(1)} %collective-permute-done.3.refs_4_), custom_call_target="tpu_custom_call" | custom-call | flops 1073741824 | bytes 2097152 | tf_op jit(solution)/shard_map/pallas_call | solution.py:69
  22.3 1.6 %collective-permute-start.4 = (bf16[8,96,128]{2,1,0:T(8,128)(2,1)}, bf16[8,96,128]{2,1,0:T(8,128)(2,1)S(1)}, u32[]{:S(2)}, u32[]{:S(2)}) collective-permute-start(bf16[8,96,128]{2,1,0:T(8,128)(2,1)} %shard_map.70), channel_id=1, source_target_pairs={{0,8},{8,16},{16,24},{24,0},{1,9},{9,17},{17,25},{25,1},{2,10},{10... | collective-permute-start | bytes 589832 | tf_op jit(solution)/shard_map/ppermute | solution.py:237
  23.8 0.0 collective-permute-done.5.refs_4_
  23.8 2.0 %shard_map.72 = bf16[8,96,128]{2,1,0:T(8,128)(2,1)} custom-call(s32[2]{0:T(128)S(1)} %pad_add_fusion.1.refs_0_, s32[1,2048]{1,0:T(1,128)S(1)} %bitcast.15, bf16[64,2048]{1,0:T(8,128)(2,1)S(1)} %copy-done.1, bf16[256,2048]{1,0:T(8,128)(2,1)S(1)} %pad_maximum_fusion.refs_3_, f32[8,96,128]{2,1,0:T(8,128)S(1)} %collective-permute-done.5.refs_4_), custom_call_target="tpu_custom_call" | custom-call | flops 1073741824 | bytes 2097152 | tf_op jit(solution)/shard_map/pallas_call | solution.py:69
  25.8 0.4 collective-permute-start.6
  26.3 0.0 collective-permute-done.1.refs_4_
  26.3 2.0 %shard_map.68 = bf16[8,96,128]{2,1,0:T(8,128)(2,1)} custom-call(s32[2]{0:T(128)S(1)} %pad_add_fusion.1.refs_0_, s32[1,2048]{1,0:T(1,128)S(1)} %bitcast.16, bf16[64,2048]{1,0:T(8,128)(2,1)S(1)} %copy-done.1, bf16[256,2048]{1,0:T(8,128)(2,1)S(1)} %pad_maximum_fusion.refs_3_, f32[8,96,128]{2,1,0:T(8,128)S(1)} %collective-permute-done.1.refs_4_), custom_call_target="tpu_custom_call" | custom-call | flops 1073741824 | bytes 2097152 | tf_op jit(solution)/shard_map/pallas_call | solution.py:69
  28.2 2.3 %collective-permute-start.2 = (bf16[8,96,128]{2,1,0:T(8,128)(2,1)}, bf16[8,96,128]{2,1,0:T(8,128)(2,1)S(1)}, u32[]{:S(2)}, u32[]{:S(2)}) collective-permute-start(bf16[8,96,128]{2,1,0:T(8,128)(2,1)} %shard_map.68), channel_id=1, source_target_pairs={{0,16},{8,24},{16,0},{24,8},{1,17},{9,25},{17,1},{25,9},{2,18},{10... | collective-permute-start | bytes 589832 | tf_op jit(solution)/shard_map/ppermute | solution.py:237
  31.2 0.0 copy-start
  31.2 0.0 copy-start.2
  31.2 1.0 %copy-done.2 = bf16[64,2048]{1,0:T(8,128)(2,1)S(1)} copy-done((bf16[64,2048]{1,0:T(8,128)(2,1)S(1)}, bf16[64,2048]{1,0:T(8,128)(2,1)}, u32[]{:S(2)}) %copy-start.2) | copy-done | bytes 262168
  32.2 1.3 %shard_map.66.refs_0_ = f32[8,96,128]{2,1,0:T(8,128)S(1)} custom-call(s32[2]{0:T(128)S(1)} %pad_add_fusion.1.refs_0_, s32[1,2048]{1,0:T(1,128)S(1)} %bitcast.17, bf16[64,2048]{1,0:T(8,128)(2,1)S(1)} %copy-done.2, bf16[256,2048]{1,0:T(8,128)(2,1)S(1)} %pad_maximum_fusion.refs_3_, f32[8,96,128]{2,1,0:T(8,128)S(1)} %collective-permute-done.refs_4_), custom_call_target="tpu_custom_call" | custom-call | flops 1073741824 | bytes 2097152 | tf_op jit(solution)/shard_map/pallas_call | solution.py:69
  33.5 4.0 %collective-permute-done.2.refs_1_ = bf16[8,96,128]{2,1,0:T(8,128)(2,1)S(1)} collective-permute-done((bf16[8,96,128]{2,1,0:T(8,128)(2,1)}, bf16[8,96,128]{2,1,0:T(8,128)(2,1)S(1)}, u32[]{:S(2)}, u32[]{:S(2)}) %collective-permute-start.2) | collective-permute-done | bytes 196640 | tf_op jit(solution)/shard_map/ppermute | solution.py:237
  37.5 0.1 shard_map.73
  37.6 1.1 %collective-permute-start.7 = (bf16[4,96,128]{2,1,0:T(8,128)(2,1)S(1)}, bf16[4,96,128]{2,1,0:T(8,128)(2,1)S(1)}, u32[]{:S(2)}, u32[]{:S(2)}) collective-permute-start(bf16[4,96,128]{2,1,0:T(8,128)(2,1)S(1)} %get-tuple-element.20), channel_id=1, source_target_pairs={{0,32},{32,0},{1,33},{33,1},{2,34},{34,2},{3,35},{35,3},{4,36},{36... | collective-permute-start | bytes 294920 | tf_op jit(solution)/shard_map/ppermute | solution.py:243
  38.7 0.1 pad_add_fusion.place_ref.refs_0_
  38.8 3.5 %collective-permute-done.7.came_ref = bf16[4,96,128]{2,1,0:T(8,128)(2,1)S(1)} collective-permute-done((bf16[4,96,128]{2,1,0:T(8,128)(2,1)S(1)}, bf16[4,96,128]{2,1,0:T(8,128)(2,1)S(1)}, u32[]{:S(2)}, u32[]{:S(2)}) %collective-permute-start.7) | collective-permute-done | bytes 98336 | tf_op jit(solution)/shard_map/ppermute | solution.py:243
  42.3 0.6 shard_map.74
  42.9 4.1 %collective-permute-start.10 = (bf16[416,128]{1,0:T(8,128)(2,1)S(1)}, bf16[416,128]{1,0:T(8,128)(2,1)S(1)}, u32[]{:S(2)}, u32[]{:S(2)}) collective-permute-start(bf16[416,128]{1,0:T(8,128)(2,1)S(1)} %get-tuple-element.29), channel_id=1, source_target_pairs={{0,192},{64,128},{128,64},{192,0},{1,193},{65,129},{129,65},{193,1... | collective-permute-start | bytes 319496 | tf_op jit(solution)/shard_map/ppermute | solution.py:190
  47.0 2.4 %collective-permute-start.8 = (bf16[416,128]{1,0:T(8,128)(2,1)S(1)}, bf16[416,128]{1,0:T(8,128)(2,1)S(1)}, u32[]{:S(2)}, u32[]{:S(2)}) collective-permute-start(bf16[416,128]{1,0:T(8,128)(2,1)S(1)} %get-tuple-element.27), channel_id=1, source_target_pairs={{0,64},{64,0},{128,192},{192,128},{1,65},{65,1},{129,193},{193,129... | collective-permute-start | bytes 319496 | tf_op jit(solution)/shard_map/ppermute | solution.py:190
  49.4 0.1 collective-permute-start.9
  49.5 1.4 %collective-permute-done.10.refs_2_.refs_5_ = bf16[416,128]{1,0:T(8,128)(2,1)S(1)} collective-permute-done((bf16[416,128]{1,0:T(8,128)(2,1)S(1)}, bf16[416,128]{1,0:T(8,128)(2,1)S(1)}, u32[]{:S(2)}, u32[]{:S(2)}) %collective-permute-start.10) | collective-permute-done | bytes 106528 | tf_op jit(solution)/shard_map/ppermute | solution.py:190
  50.9 5.7 %collective-permute-done.8.refs_0_.refs_3_ = bf16[416,128]{1,0:T(8,128)(2,1)S(1)} collective-permute-done((bf16[416,128]{1,0:T(8,128)(2,1)S(1)}, bf16[416,128]{1,0:T(8,128)(2,1)S(1)}, u32[]{:S(2)}, u32[]{:S(2)}) %collective-permute-start.8) | collective-permute-done | bytes 106528 | tf_op jit(solution)/shard_map/ppermute | solution.py:190
  56.6 1.7 %collective-permute-done.9.refs_1_.refs_4_ = bf16[416,128]{1,0:T(8,128)(2,1)S(1)} collective-permute-done((bf16[416,128]{1,0:T(8,128)(2,1)S(1)}, bf16[416,128]{1,0:T(8,128)(2,1)S(1)}, u32[]{:S(2)}, u32[]{:S(2)}) %collective-permute-start.9) | collective-permute-done | bytes 106528 | tf_op jit(solution)/shard_map/ppermute | solution.py:190
  58.3 0.6 shard_map.75.refs_6_
  58.9 2.1 %collective-permute-start.11 = (bf16[4,96,128]{2,1,0:T(8,128)(2,1)S(1)}, bf16[4,96,128]{2,1,0:T(8,128)(2,1)S(1)}, u32[]{:S(2)}, u32[]{:S(2)}) collective-permute-start(bf16[4,96,128]{2,1,0:T(8,128)(2,1)S(1)} %shard_map.75.refs_6_), channel_id=1, source_target_pairs={{0,1},{1,2},{2,3},{3,0},{4,5},{5,6},{6,7},{7,4},{8,9},{9,10},{10,1... | collective-permute-start | bytes 294920 | tf_op jit(solution)/shard_map/ppermute | solution.py:190
  60.9 2.4 %collective-permute-start.12 = (bf16[4,96,128]{2,1,0:T(8,128)(2,1)S(1)}, bf16[4,96,128]{2,1,0:T(8,128)(2,1)S(1)}, u32[]{:S(2)}, u32[]{:S(2)}) collective-permute-start(bf16[4,96,128]{2,1,0:T(8,128)(2,1)S(1)} %shard_map.75.refs_6_), channel_id=1, source_target_pairs={{0,2},{1,3},{2,0},{3,1},{4,6},{5,7},{6,4},{7,5},{8,10},{9,11},{10,... | collective-permute-start | bytes 294920 | tf_op jit(solution)/shard_map/ppermute | solution.py:190
  63.3 1.5 %collective-permute-start.13 = (bf16[4,96,128]{2,1,0:T(8,128)(2,1)S(1)}, bf16[4,96,128]{2,1,0:T(8,128)(2,1)S(1)}, u32[]{:S(2)}, u32[]{:S(2)}) collective-permute-start(bf16[4,96,128]{2,1,0:T(8,128)(2,1)S(1)} %shard_map.75.refs_6_), channel_id=1, source_target_pairs={{0,3},{1,0},{2,1},{3,2},{4,7},{5,4},{6,5},{7,6},{8,11},{9,8},{10,9... | collective-permute-start | bytes 294920 | tf_op jit(solution)/shard_map/ppermute | solution.py:190
  64.8 2.3 %collective-permute-done.12.refs_8_ = bf16[4,96,128]{2,1,0:T(8,128)(2,1)S(1)} collective-permute-done((bf16[4,96,128]{2,1,0:T(8,128)(2,1)S(1)}, bf16[4,96,128]{2,1,0:T(8,128)(2,1)S(1)}, u32[]{:S(2)}, u32[]{:S(2)}) %collective-permute-start.12) | collective-permute-done | bytes 98336 | tf_op jit(solution)/shard_map/ppermute | solution.py:190
  67.1 0.9 collective-permute-done.13.refs_9_
  67.9 1.3 %shard_map.76 = bf16[16,48,512]{2,1,0:T(8,128)(2,1)S(1)} custom-call(s32[3]{0:T(128)S(1)} %pad_add_fusion.place_ref.refs_0_, bf16[16,64,512]{2,1,0:T(8,128)(2,1)S(1)} %all-to-all-done.refs_1_, bf16[32,128]{1,0:T(8,128)(2,1)S(1)} %get-tuple-element.26.extra_ref.refs_2_, bf16[416,128]{1,0:T(8,128)(2,1)S(1)} %collective-permute-done.8.refs_0_.refs_3_, ...), custom_call_target="tpu_custom_call" | custom-call | flops 201326592 | bytes 2097152 | tf_op jit(solution)/shard_map/pallas_call | solution.py:69
  69.3 24.1 %all_to_all.10 = bf16[16,48,512]{2,1,0:T(8,128)(2,1)S(1)} all-to-all(bf16[16,48,512]{2,1,0:T(8,128)(2,1)S(1)} %shard_map.76), channel_id=1, replica_groups=mesh['zg'=4,'zl'=2,'y'=4,'core'=2,'smp'=4] {'zg','smp'}, dimensions={0} | all-to-all | bytes 1572864 | tf_op jit(solution)/shard_map/all_to_all | solution.py:286
  93.4 1.0 %copy.8 = bf16[16,6,8,512]{3,2,0,1:T(8,128)(2,1)} copy(bf16[16,6,8,512]{3,2,1,0:T(8,128)(2,1)S(1)} %bitcast.18) | data formatting | bytes 1572864 | tf_op jit(solution)/shard_map/reshape | solution.py:287
  (11 shorter events, 0.0 us)
Async XLA Ops:
  2.4 10.3 %copy-start.4 = (bf16[2048,192]{0,1:T(8,128)(2,1)S(1)}, bf16[2048,192]{0,1:T(8,128)(2,1)}, u32[]{:S(2)}) copy-start(bf16[2048,192]{0,1:T(8,128)(2,1)} %param.8) | copy-start | bytes 2359300
  2.4 40.5 %all-to-all-start = ((bf16[16,64,512]{2,1,0:T(8,128)(2,1)}), bf16[16,64,512]{2,1,0:T(8,128)(2,1)S(1)}, u32[]{:S(2)}, u32[]{:S(2)}) async-start(bf16[16,64,512]{2,1,0:T(8,128)(2,1)} %shard_map.64), calls=%async_computation | async-start | bytes 2097152 | tf_op jit(solution)/shard_map/all_to_all | solution.py:207
  12.8 1.0 %copy-start.1 = (bf16[64,2048]{1,0:T(8,128)(2,1)S(1)}, bf16[64,2048]{1,0:T(8,128)(2,1)}, u32[]{:S(2)}) copy-start(bf16[64,2048]{1,0:T(8,128)(2,1)} %refs_2_.15) | copy-start | bytes 786436
  12.8 1.0 %copy-start.3 = (s32[2048,1]{0,1:T(1,128)S(1)}, s32[2048,1]{0,1:T(1,128)}, u32[]{:S(2)}) copy-start(s32[2048,1]{0,1:T(1,128)} %param.9) | copy-start | bytes 24580
  15.0 5.2 %collective-permute-start.3 = (f32[8,96,128]{2,1,0:T(8,128)S(1)}, f32[8,96,128]{2,1,0:T(8,128)S(1)}, u32[]{:S(2)}, u32[]{:S(2)}) collective-permute-start(f32[8,96,128]{2,1,0:T(8,128)S(1)} %shard_map.69), channel_id=1, source_target_pairs={{0,4},{4,0},{1,5},{5,1},{2,6},{6,2},{3,7},{7,3},{8,12},{12,8},{9,1... | collective-permute-start | bytes 1179656 | tf_op jit(solution)/shard_map/ppermute | solution.py:231
  16.4 7.4 %collective-permute-start.5 = (f32[8,96,128]{2,1,0:T(8,128)S(1)}, f32[8,96,128]{2,1,0:T(8,128)S(1)}, u32[]{:S(2)}, u32[]{:S(2)}) collective-permute-start(f32[8,96,128]{2,1,0:T(8,128)S(1)} %shard_map.71), channel_id=1, source_target_pairs={{0,4},{4,0},{1,5},{5,1},{2,6},{6,2},{3,7},{7,3},{8,12},{12,8},{9,1... | collective-permute-start | bytes 1179656 | tf_op jit(solution)/shard_map/ppermute | solution.py:231
  18.3 8.0 %collective-permute-start.1 = (f32[8,96,128]{2,1,0:T(8,128)S(1)}, f32[8,96,128]{2,1,0:T(8,128)S(1)}, u32[]{:S(2)}, u32[]{:S(2)}) collective-permute-start(f32[8,96,128]{2,1,0:T(8,128)S(1)} %shard_map.67), channel_id=1, source_target_pairs={{0,4},{4,0},{1,5},{5,1},{2,6},{6,2},{3,7},{7,3},{8,12},{12,8},{9,1... | collective-permute-start | bytes 1179656 | tf_op jit(solution)/shard_map/ppermute | solution.py:231
  19.7 11.5 %collective-permute-start = (f32[8,96,128]{2,1,0:T(8,128)S(1)}, f32[8,96,128]{2,1,0:T(8,128)S(1)}, u32[]{:S(2)}, u32[]{:S(2)}) collective-permute-start(f32[8,96,128]{2,1,0:T(8,128)S(1)} %shard_map.65), channel_id=1, source_target_pairs={{0,4},{4,0},{1,5},{5,1},{2,6},{6,2},{3,7},{7,3},{8,12},{12,8},{9,1... | collective-permute-start | bytes 1179656 | tf_op jit(solution)/shard_map/ppermute | solution.py:231
  22.3 11.2 %collective-permute-start.4 = (bf16[8,96,128]{2,1,0:T(8,128)(2,1)}, bf16[8,96,128]{2,1,0:T(8,128)(2,1)S(1)}, u32[]{:S(2)}, u32[]{:S(2)}) collective-permute-start(bf16[8,96,128]{2,1,0:T(8,128)(2,1)} %shard_map.70), channel_id=1, source_target_pairs={{0,8},{8,16},{16,24},{24,0},{1,9},{9,17},{17,25},{25,1},{2,10},{10... | collective-permute-start | bytes 589832 | tf_op jit(solution)/shard_map/ppermute | solution.py:237
  25.8 7.7 %collective-permute-start.6 = (bf16[8,96,128]{2,1,0:T(8,128)(2,1)}, bf16[8,96,128]{2,1,0:T(8,128)(2,1)S(1)}, u32[]{:S(2)}, u32[]{:S(2)}) collective-permute-start(bf16[8,96,128]{2,1,0:T(8,128)(2,1)} %shard_map.72), channel_id=1, source_target_pairs={{0,24},{8,0},{16,8},{24,16},{1,25},{9,1},{17,9},{25,17},{2,26},{10... | collective-permute-start | bytes 589832 | tf_op jit(solution)/shard_map/ppermute | solution.py:237
  28.2 9.3 %collective-permute-start.2 = (bf16[8,96,128]{2,1,0:T(8,128)(2,1)}, bf16[8,96,128]{2,1,0:T(8,128)(2,1)S(1)}, u32[]{:S(2)}, u32[]{:S(2)}) collective-permute-start(bf16[8,96,128]{2,1,0:T(8,128)(2,1)} %shard_map.68), channel_id=1, source_target_pairs={{0,16},{8,24},{16,0},{24,8},{1,17},{9,25},{17,1},{25,9},{2,18},{10... | collective-permute-start | bytes 589832 | tf_op jit(solution)/shard_map/ppermute | solution.py:237
  31.2 11.1 %copy-start = (f32[2,8192]{1,0:T(2,128)S(1)}, f32[2,8192]{1,0:T(2,128)}, u32[]{:S(2)}) copy-start(f32[2,8192]{1,0:T(2,128)} %twiddle_ref.1) | copy-start | bytes 196612
  31.2 1.0 %copy-start.2 = (bf16[64,2048]{1,0:T(8,128)(2,1)S(1)}, bf16[64,2048]{1,0:T(8,128)(2,1)}, u32[]{:S(2)}) copy-start(bf16[64,2048]{1,0:T(8,128)(2,1)} %refs_2_.15) | copy-start | bytes 786436
  37.6 4.7 %collective-permute-start.7 = (bf16[4,96,128]{2,1,0:T(8,128)(2,1)S(1)}, bf16[4,96,128]{2,1,0:T(8,128)(2,1)S(1)}, u32[]{:S(2)}, u32[]{:S(2)}) collective-permute-start(bf16[4,96,128]{2,1,0:T(8,128)(2,1)S(1)} %get-tuple-element.20), channel_id=1, source_target_pairs={{0,32},{32,0},{1,33},{33,1},{2,34},{34,2},{3,35},{35,3},{4,36},{36... | collective-permute-start | bytes 294920 | tf_op jit(solution)/shard_map/ppermute | solution.py:243
  42.9 7.9 %collective-permute-start.10 = (bf16[416,128]{1,0:T(8,128)(2,1)S(1)}, bf16[416,128]{1,0:T(8,128)(2,1)S(1)}, u32[]{:S(2)}, u32[]{:S(2)}) collective-permute-start(bf16[416,128]{1,0:T(8,128)(2,1)S(1)} %get-tuple-element.29), channel_id=1, source_target_pairs={{0,192},{64,128},{128,64},{192,0},{1,193},{65,129},{129,65},{193,1... | collective-permute-start | bytes 319496 | tf_op jit(solution)/shard_map/ppermute | solution.py:190
  47.0 9.5 %collective-permute-start.8 = (bf16[416,128]{1,0:T(8,128)(2,1)S(1)}, bf16[416,128]{1,0:T(8,128)(2,1)S(1)}, u32[]{:S(2)}, u32[]{:S(2)}) collective-permute-start(bf16[416,128]{1,0:T(8,128)(2,1)S(1)} %get-tuple-element.27), channel_id=1, source_target_pairs={{0,64},{64,0},{128,192},{192,128},{1,65},{65,1},{129,193},{193,129... | collective-permute-start | bytes 319496 | tf_op jit(solution)/shard_map/ppermute | solution.py:190
  49.4 8.9 %collective-permute-start.9 = (bf16[416,128]{1,0:T(8,128)(2,1)S(1)}, bf16[416,128]{1,0:T(8,128)(2,1)S(1)}, u32[]{:S(2)}, u32[]{:S(2)}) collective-permute-start(bf16[416,128]{1,0:T(8,128)(2,1)S(1)} %get-tuple-element.28), channel_id=1, source_target_pairs={{0,128},{64,192},{128,0},{192,64},{1,129},{65,193},{129,1},{193,65... | collective-permute-start | bytes 319496 | tf_op jit(solution)/shard_map/ppermute | solution.py:190
  58.9 5.9 %collective-permute-start.11 = (bf16[4,96,128]{2,1,0:T(8,128)(2,1)S(1)}, bf16[4,96,128]{2,1,0:T(8,128)(2,1)S(1)}, u32[]{:S(2)}, u32[]{:S(2)}) collective-permute-start(bf16[4,96,128]{2,1,0:T(8,128)(2,1)S(1)} %shard_map.75.refs_6_), channel_id=1, source_target_pairs={{0,1},{1,2},{2,3},{3,0},{4,5},{5,6},{6,7},{7,4},{8,9},{9,10},{10,1... | collective-permute-start | bytes 294920 | tf_op jit(solution)/shard_map/ppermute | solution.py:190
  60.9 6.1 %collective-permute-start.12 = (bf16[4,96,128]{2,1,0:T(8,128)(2,1)S(1)}, bf16[4,96,128]{2,1,0:T(8,128)(2,1)S(1)}, u32[]{:S(2)}, u32[]{:S(2)}) collective-permute-start(bf16[4,96,128]{2,1,0:T(8,128)(2,1)S(1)} %shard_map.75.refs_6_), channel_id=1, source_target_pairs={{0,2},{1,3},{2,0},{3,1},{4,6},{5,7},{6,4},{7,5},{8,10},{9,11},{10,... | collective-permute-start | bytes 294920 | tf_op jit(solution)/shard_map/ppermute | solution.py:190
  63.3 4.6 %collective-permute-start.13 = (bf16[4,96,128]{2,1,0:T(8,128)(2,1)S(1)}, bf16[4,96,128]{2,1,0:T(8,128)(2,1)S(1)}, u32[]{:S(2)}, u32[]{:S(2)}) collective-permute-start(bf16[4,96,128]{2,1,0:T(8,128)(2,1)S(1)} %shard_map.75.refs_6_), channel_id=1, source_target_pairs={{0,3},{1,0},{2,1},{3,2},{4,7},{5,4},{6,5},{7,6},{8,11},{9,8},{10,9... | collective-permute-start | bytes 294920 | tf_op jit(solution)/shard_map/ppermute | solution.py:190
